TPU v7x, 32 devices: a whole 2x2x4 slice. The times are simulated.
32 devices in a mesh: sub: 16 (over z, y, x), tm: 2 (over core).
Axes of the slice: x: 2, y: 2, z: 4, core: 2. Of those that a mesh axis runs over, the one named last changes fastest.
Arguments:
- data: bfloat16 [1, 16384, 512], P(None, 'sub', 'tm'), may hold values from -6 to 6
- delays: int32 [16384], P('sub'), may hold values from 0 to 15, as said below
- offsets: int32 [2048, 1024], P('sub'), may hold values from 0 to 96, as said below
- widths: int32 [8], replicated, may hold values from 1 to 128, as said below
Outputs:
- boxcars: float32 [2048, 1, 8, 512], P('sub', None, None, 'tm')
Inputs may be any that keep to these rules, and one draw needn't show every extreme that they name: `delays`: some channel has delay 16 - 1. `offsets`: some entry equals 96 and some entry equals 0. `widths`: some entry equals 128.
All inputs are finite; a program needn't handle non-finite values.
Results may differ from a plain program's by a relative error of at most 0.0048.
Values may be sent and summed in bfloat16 or wider, within the bound.
No kernel may reach another device: no remote copies, remote signals or barrier semaphores. Data moves between devices by JAX's collectives and lax.ppermute only.
A program may use at most 64 MiB of HBM per device.

v0:
```python
import math

import jax
import jax.numpy as jnp
from jax import lax
from jax.sharding import PartitionSpec as P

WMAX = 128
DCH = 16
OMAX = 96


def passed_along(value, axis, steps):
    count = lax.axis_size(axis)
    initial, last = (max(0, -steps), min(count, count - steps))
    return lax.ppermute(value, axis, [(source, source + steps) for source in range(initial, last)])


def series_of(padded_series_block, delays, sub_count, count):
    chans = padded_series_block.shape[1]
    per_sub = chans // sub_count
    owner = jnp.arange(chans, dtype=jnp.int32) // per_sub
    member = owner[None, :] == jnp.arange(sub_count, dtype=jnp.int32)[:, None]
    running = jnp.zeros((padded_series_block.shape[0], sub_count, count), jnp.float32)
    for delay in range(DCH):
        select = (member & (delays[None, :] == delay)).astype(jnp.bfloat16)
        running = running + jnp.einsum(
            "sc,bct->bst",
            select,
            padded_series_block[:, :, delay : delay + count],
            preferred_element_type=jnp.float32,
        )
    return running.astype(jnp.bfloat16)


def hankel_of(series, length):
    return jnp.stack([series[:, :, lag : lag + length] for lag in range(OMAX + 1)], axis=2)


def project(lag_rows, hankel, scale):
    onehot = (lag_rows[:, :, None] == jnp.arange(OMAX + 1, dtype=jnp.int32)[None, None, :]).astype(
        jnp.bfloat16
    )
    return jnp.einsum("msk,bskt->mbt", onehot, hankel, preferred_element_type=jnp.float32) * scale


def per_device(data, delays, offsets, widths):
    beams, chans, length = data.shape
    dm_dev = offsets.shape[0]
    nsub = offsets.shape[1]
    groups = lax.axis_size("sub")
    sub_dev = nsub // groups
    scale = 1.0 / math.sqrt(chans * groups)
    extra = 0
    out_len = length + extra
    trailing_rows = passed_along(data[:, :, : OMAX + DCH - 1 + extra], "tm", -1)
    series = series_of(
        jnp.concatenate([data, trailing_rows], axis=2), delays, sub_dev, out_len + OMAX
    )
    table = lax.all_to_all(offsets, "sub", split_axis=1, concat_axis=0, tiled=True)
    hankel = hankel_of(series, out_len)
    block = math.gcd(lax.axis_size("sub") * dm_dev, 256)

    def one_block(block_index):
        lag_rows = lax.dynamic_slice_in_dim(table, block_index * block, block, 0)
        return project(lag_rows, hankel, scale)

    blocks = lax.map(one_block, jnp.arange(lax.axis_size("sub") * dm_dev // block, dtype=jnp.int32))
    channel_totals = lax.psum_scatter(
        blocks.reshape(lax.axis_size("sub") * dm_dev, beams, out_len),
        "sub",
        scatter_dimension=0,
        tiled=True,
    )
    dedispersed = channel_totals.astype(jnp.bfloat16)
    later_rows = passed_along(dedispersed[:, :, : WMAX - 1], "tm", -1)
    padded_series_block = jnp.concatenate([dedispersed, later_rows], axis=2)
    lag = (
        jnp.arange(padded_series_block.shape[2], dtype=jnp.int32)[:, None]
        - jnp.arange(length, dtype=jnp.int32)[None, :]
    )
    subband_weight_matrix = ((lag[None] >= 0) & (lag[None] < widths[:, None, None])).astype(
        jnp.bfloat16
    )
    filtered = jnp.einsum(
        "syh,qho->syqo",
        padded_series_block,
        subband_weight_matrix,
        preferred_element_type=jnp.float32,
    )
    return filtered / jnp.sqrt(widths.astype(jnp.float32))[None, None, :, None]


def solution(mesh):
    placed = (P(None, "sub", "tm"), P("sub"), P("sub", None), P())
    return jax.shard_map(
        per_device,
        mesh=mesh,
        in_specs=placed,
        out_specs=P("sub", None, None, "tm"),
        check_vma=False,
    )
```

profile of v0, /device:TPU:0, one launch (start us, length us, event | category | flops | bytes accessed | tf_op | source)
XLA Modules:
  0.0 173.3 jit_solution(15338695852809551773)
XLA Ops:
  6.5 1.0 slice.345
  7.5 1.3 collective-permute-start
  8.8 2.0 %copy.11 = s32[128,1024]{0,1:T(8,128)} copy(s32[128,1024]{1,0:T(8,128)} %param.8) | data formatting | bytes 1048576 | tf_op args[2]
  10.9 8.4 %all-to-all-start = ((s32[128,16,64]{0,2,1:T(8,128)}), s32[128,16,64]{0,2,1:T(8,128)}, u32[]{:S(2)}, u32[]{:S(2)}) async-start(s32[128,16,64]{0,2,1:T(8,128)} %bitcast.4), calls=%async_computation | async-start | bytes 1048576 | tf_op jit(solution)/shard_map/all_to_all | solution.py:60
  19.3 1.1 constant_dynamic-update-slice_fusion.1
  20.5 0.4 fusion.44
  21.4 0.4 fusion.46
  21.8 0.4 fusion.47
  22.7 0.4 fusion.49
  23.1 0.4 fusion.50
  24.0 0.4 fusion.52
  24.5 0.4 fusion.53
  25.3 0.4 fusion.55
  25.8 0.4 fusion.56
  26.7 0.4 fusion.58
  35.3 1.8 %copy.13 = bf16[1,64,97,256]{3,2,1,0:T(8,128)(2,1)S(1)} copy(bf16[1,64,97,256]{3,1,2,0:T(8,128)(2,1)S(1)} %constant_dynamic-update-slice_fusion.2) | data formatting | bytes 6356992 | tf_op jit(solution)/shard_map/while | solution.py:68
  37.2 1.9 %copy_bitcast_fusion = s32[2048,64]{0,1:T(8,128)} fusion(s32[128,16,64]{0,2,1:T(8,128)} %all-to-all-done), kind=kLoop, calls=%fused_computation.66 | loop fusion | bytes 1048576 | tf_op jit(solution)/shard_map/all_to_all | solution.py:60
  39.1 38.5 %while.10 = (s32[]{:T(128)}, f32[8,256,1,256]{3,1,2,0:T(8,128)}, s32[8]{0:T(128)S(1)}, s32[2048,64]{0,1:T(8,128)}, bf16[1,64,97,256]{3,2,1,0:T(8,128)(2,1)S(1)},...) while((s32[]{:T(128)}, f32[8,256,1,256]{3,1,2,0:T(8,128)}, s32[8]{0:T(128)S(1)}, s32[2048,64]{0,1:T(8,128)}, ...), condition=%wide.region_1.2_spmd, body=%wide.region_0.1_spmd.sunk | while | flops 815349760 | bytes 3637915 | solution.py:68
  39.1 0.6 dynamic_slice.11
  40.4 0.8 constant_dynamic-slice_fusion.2
  41.2 2.7 %fusion.133 = f32[8,256,1,256]{3,1,2,0:T(8,128)} fusion(f32[8,256,1,256]{3,1,2,0:T(8,128)} %get-tuple-element.115, s32[]{:T(128)} %get-tuple-element.114, bf16[1,64,97,256]{3,2,1,0:T(8,128)(2,1)S(1)} %get-tuple-element.127, s32[256,64]{0,1:T(8,128)S(1)} %constant_dynamic-slice_fusion.2), kind=kOutput, calls=%fused_computation.7.clone.1 | convolution fusion | flops 815349760 | bytes 3506688 | tf_op jit(solution)/shard_map/while/body/eval_jaxpr/msk,bskt->mbt/dot_general | solution.py:44
  43.9 0.6 dynamic_slice.11
  45.2 0.8 constant_dynamic-slice_fusion.2
  46.0 2.7 %fusion.133 = f32[8,256,1,256]{3,1,2,0:T(8,128)} fusion(f32[8,256,1,256]{3,1,2,0:T(8,128)} %get-tuple-element.115, s32[]{:T(128)} %get-tuple-element.114, bf16[1,64,97,256]{3,2,1,0:T(8,128)(2,1)S(1)} %get-tuple-element.127, s32[256,64]{0,1:T(8,128)S(1)} %constant_dynamic-slice_fusion.2), kind=kOutput, calls=%fused_computation.7.clone.1 | convolution fusion | flops 815349760 | bytes 3506688 | tf_op jit(solution)/shard_map/while/body/eval_jaxpr/msk,bskt->mbt/dot_general | solution.py:44
  48.7 0.6 dynamic_slice.11
  50.0 0.8 constant_dynamic-slice_fusion.2
  50.8 2.7 %fusion.133 = f32[8,256,1,256]{3,1,2,0:T(8,128)} fusion(f32[8,256,1,256]{3,1,2,0:T(8,128)} %get-tuple-element.115, s32[]{:T(128)} %get-tuple-element.114, bf16[1,64,97,256]{3,2,1,0:T(8,128)(2,1)S(1)} %get-tuple-element.127, s32[256,64]{0,1:T(8,128)S(1)} %constant_dynamic-slice_fusion.2), kind=kOutput, calls=%fused_computation.7.clone.1 | convolution fusion | flops 815349760 | bytes 3506688 | tf_op jit(solution)/shard_map/while/body/eval_jaxpr/msk,bskt->mbt/dot_general | solution.py:44
  53.5 0.6 dynamic_slice.11
  54.8 0.8 constant_dynamic-slice_fusion.2
  55.7 2.7 %fusion.133 = f32[8,256,1,256]{3,1,2,0:T(8,128)} fusion(f32[8,256,1,256]{3,1,2,0:T(8,128)} %get-tuple-element.115, s32[]{:T(128)} %get-tuple-element.114, bf16[1,64,97,256]{3,2,1,0:T(8,128)(2,1)S(1)} %get-tuple-element.127, s32[256,64]{0,1:T(8,128)S(1)} %constant_dynamic-slice_fusion.2), kind=kOutput, calls=%fused_computation.7.clone.1 | convolution fusion | flops 815349760 | bytes 3506688 | tf_op jit(solution)/shard_map/while/body/eval_jaxpr/msk,bskt->mbt/dot_general | solution.py:44
  58.3 0.6 dynamic_slice.11
  59.6 0.8 constant_dynamic-slice_fusion.2
  60.5 2.7 %fusion.133 = f32[8,256,1,256]{3,1,2,0:T(8,128)} fusion(f32[8,256,1,256]{3,1,2,0:T(8,128)} %get-tuple-element.115, s32[]{:T(128)} %get-tuple-element.114, bf16[1,64,97,256]{3,2,1,0:T(8,128)(2,1)S(1)} %get-tuple-element.127, s32[256,64]{0,1:T(8,128)S(1)} %constant_dynamic-slice_fusion.2), kind=kOutput, calls=%fused_computation.7.clone.1 | convolution fusion | flops 815349760 | bytes 3506688 | tf_op jit(solution)/shard_map/while/body/eval_jaxpr/msk,bskt->mbt/dot_general | solution.py:44
  63.1 0.6 dynamic_slice.11
  64.4 0.8 constant_dynamic-slice_fusion.2
  65.3 2.7 %fusion.133 = f32[8,256,1,256]{3,1,2,0:T(8,128)} fusion(f32[8,256,1,256]{3,1,2,0:T(8,128)} %get-tuple-element.115, s32[]{:T(128)} %get-tuple-element.114, bf16[1,64,97,256]{3,2,1,0:T(8,128)(2,1)S(1)} %get-tuple-element.127, s32[256,64]{0,1:T(8,128)S(1)} %constant_dynamic-slice_fusion.2), kind=kOutput, calls=%fused_computation.7.clone.1 | convolution fusion | flops 815349760 | bytes 3506688 | tf_op jit(solution)/shard_map/while/body/eval_jaxpr/msk,bskt->mbt/dot_general | solution.py:44
  68.0 0.6 dynamic_slice.11
  69.2 0.8 constant_dynamic-slice_fusion.2
  70.1 2.7 %fusion.133 = f32[8,256,1,256]{3,1,2,0:T(8,128)} fusion(f32[8,256,1,256]{3,1,2,0:T(8,128)} %get-tuple-element.115, s32[]{:T(128)} %get-tuple-element.114, bf16[1,64,97,256]{3,2,1,0:T(8,128)(2,1)S(1)} %get-tuple-element.127, s32[256,64]{0,1:T(8,128)S(1)} %constant_dynamic-slice_fusion.2), kind=kOutput, calls=%fused_computation.7.clone.1 | convolution fusion | flops 815349760 | bytes 3506688 | tf_op jit(solution)/shard_map/while/body/eval_jaxpr/msk,bskt->mbt/dot_general | solution.py:44
  72.7 0.6 dynamic_slice.11
  74.0 0.8 constant_dynamic-slice_fusion.2
  74.9 2.7 %fusion.133 = f32[8,256,1,256]{3,1,2,0:T(8,128)} fusion(f32[8,256,1,256]{3,1,2,0:T(8,128)} %get-tuple-element.115, s32[]{:T(128)} %get-tuple-element.114, bf16[1,64,97,256]{3,2,1,0:T(8,128)(2,1)S(1)} %get-tuple-element.127, s32[256,64]{0,1:T(8,128)S(1)} %constant_dynamic-slice_fusion.2), kind=kOutput, calls=%fused_computation.7.clone.1 | convolution fusion | flops 815349760 | bytes 3506688 | tf_op jit(solution)/shard_map/while/body/eval_jaxpr/msk,bskt->mbt/dot_general | solution.py:44
  77.7 82.3 %reduce-scatter.2.cloned.1.call-done = f32[128,1,256]{2,0,1:T(8,128)} async-done(((f32[2048,1,256]{2,0,1:T(8,128)}), f32[128,1,256]{2,0,1:T(8,128)}) %reduce-scatter.2.cloned.1.call-update) | async-done | bytes 131088 | tf_op jit(solution)/shard_map/reduce_scatter | solution.py:69
  160.0 0.9 convert_element_type.7
  160.9 1.3 collective-permute-start.1
  162.2 1.8 %collective-permute-done.1 = bf16[128,1,127]{2,0,1:T(8,128)(2,1)S(1)} collective-permute-done((bf16[128,1,127]{2,0,1:T(8,128)(2,1)S(1)}, bf16[128,1,127]{2,0,1:T(8,128)(2,1)S(1)}, u32[]{:S(2)}, u32[]{:S(2)}) %collective-permute-start.1) | collective-permute-done | bytes 32544 | tf_op jit(solution)/shard_map/ppermute | solution.py:16
  164.0 0.9 fusion.24
  164.9 1.6 copy.14
  (120 shorter events, 10.6 us)
Async XLA Ops:
  6.5 13.8 %copy-start = (s32[1024]{0:T(1024)S(1)}, s32[1024]{0:T(1024)}, u32[]{:S(2)}) copy-start(s32[1024]{0:T(1024)} %param.7) | copy-start | bytes 12292
  7.5 12.9 %collective-permute-start = (bf16[1,1024,111]{2,1,0:T(8,128)(2,1)S(1)}, bf16[1,1024,111]{2,1,0:T(8,128)(2,1)S(1)}, u32[]{:S(2)}, u32[]{:S(2)}) collective-permute-start(bf16[1,1024,111]{2,1,0:T(8,128)(2,1)S(1)} %slice.345), channel_id=1, source_target_pairs={{1,0},{3,2},{5,4},{7,6},{9,8},{11,10},{13,12},{15,14},{17,16},{19,... | collective-permute-start | bytes 681992 | tf_op jit(solution)/shard_map/ppermute | solution.py:16
  10.9 26.3 %all-to-all-start = ((s32[128,16,64]{0,2,1:T(8,128)}), s32[128,16,64]{0,2,1:T(8,128)}, u32[]{:S(2)}, u32[]{:S(2)}) async-start(s32[128,16,64]{0,2,1:T(8,128)} %bitcast.4), calls=%async_computation | async-start | bytes 1048576 | tf_op jit(solution)/shard_map/all_to_all | solution.py:60
  19.2 140.7 %reduce-scatter.2.cloned.1.call-start = ((), (), s32[]{:S(2)}) async-start(), calls=%async_computation.2 | async-start | bytes 2228224 | tf_op jit(solution)/shard_map/reduce_scatter | solution.py:69
  39.1 38.5 %copy-start.1 = (s32[8]{0:T(128)S(1)}, s32[8]{0:T(128)}, u32[]{:S(2)}) copy-start(s32[8]{0:T(128)} %param.9) | copy-start | bytes 100
  160.9 3.1 %collective-permute-start.1 = (bf16[128,1,127]{2,0,1:T(8,128)(2,1)S(1)}, bf16[128,1,127]{2,0,1:T(8,128)(2,1)S(1)}, u32[]{:S(2)}, u32[]{:S(2)}) collective-permute-start(bf16[128,1,127]{2,0,1:T(8,128)(2,1)S(1)} %slice.573), channel_id=1, source_target_pairs={{1,0},{3,2},{5,4},{7,6},{9,8},{11,10},{13,12},{15,14},{17,16},{19,... | collective-permute-start | bytes 97544 | tf_op jit(solution)/shard_map/ppermute | solution.py:16
Sparse Core Ops, SparseCore 0:
  77.7 82.2 reduce-scatter.1
where the time goes:
time: 174 us; the launch traced here: 173 us
  waiting for transfers between devices  84.1 us (48%)
  local copies, waits for them, and re-layouts  29.3 us (17%)
  matrix products  29.1 us (17%)
  between operations  13.7 us (8%)
  starting transfers between devices  11 us (6%)
  loops' own time  5.17 us (3%)
    reduce_scatter x1, waiting for transfers between devices, per_device(): lax.psum_scatter(blocks.reshape(lax.axis_size('sub') * dm_dev, beams, out...  82.3 us
    dot_general x8, matrix products, project(): jnp.einsum('msk,bskt->mbt', onehot, hankel, preferred_element_type=jnp.fl...  21.3 us
    unnamed x102, local copies, waits for them, and re-layouts  10.9 us
    all_to_all x1, starting transfers between devices, per_device(): lax.all_to_all(offsets, 'sub', split_axis=1, concat_axis=0, tiled=True)  8.36 us
    dot_general x16, matrix products, series_of(): jnp.einsum('sc,bct->bst', select, padded_series_block[:, :, delay:delay +...  6.83 us
    dynamic_slice x8, local copies, waits for them, and re-layouts, one_block(): lag_rows = lax.dynamic_slice_in_dim(table, block_index * block, block, 0)  6.8 us
    dynamic_slice x8, local copies, waits for them, and re-layouts, per_device(): lax.map(one_block, jnp.arange(lax.axis_size('sub') * dm_dev // block, dty...  5.19 us
    another operation x1, loops' own time, per_device(): lax.map(one_block, jnp.arange(lax.axis_size('sub') * dm_dev // block, dty...  5.17 us
  transfers between devices with their start and end apart: 4, of which 2 were waited for; matrix products, arithmetic and copies ran while one was open for 11% of the time, Pallas kernels for 0%

commit v1 on v0

v1 whole, which is shorter than its diff:
```python
import functools
import math

import jax
import jax.numpy as jnp
from jax import lax
from jax.experimental import pallas as pl
from jax.experimental.pallas import tpu as pltpu
from jax.sharding import PartitionSpec as P

WMAX = 128
DCH = 16
OMAX = 96
LANES = 128
STEP = 16
VMEM = pl.BlockSpec(memory_space=pltpu.VMEM)
SMEM = pl.BlockSpec(memory_space=pltpu.SMEM)


def passed_back(value, axis):
    count = lax.axis_size(axis)
    return lax.ppermute(value, axis, [(source, source - 1) for source in range(1, count)])


def series_kernel(per_sub, key_ref, data_ref, halo_ref, series_ref):
    chans = data_ref.shape[0]
    span = series_ref.shape[1]
    block = min(chans, 256)
    subs = block // per_sub
    rows = lax.broadcasted_iota(jnp.int32, (DCH * subs, block), 0)
    for at in range(chans // block):
        here = pl.ds(at * block, block)
        member = jnp.where(rows == key_ref[:, here], 1.0, 0.0).astype(jnp.bfloat16)
        values = jnp.concatenate([data_ref[here, :], halo_ref[here, :]], axis=1)
        picked = jnp.dot(member, values, preferred_element_type=jnp.float32)
        total = picked[:subs, :]
        for delay in range(1, DCH):
            total = total + pltpu.roll(picked[delay * subs : (delay + 1) * subs, :], span - delay, 1)
        series_ref[pl.ds(at * subs, subs), :] = total.astype(jnp.bfloat16)


def where_equal(table, value):
    wanted = jnp.full((1, table.shape[1]), value, jnp.int32).astype(jnp.float32).astype(jnp.bfloat16)
    return jnp.where(table == wanted, jnp.bfloat16(1), jnp.bfloat16(0))


def dedisperse_kernel(scale, length, series_ref, offsets_ref, out_ref, head_ref, turned, lags, totals):
    nsub, span = series_ref.shape
    trials = offsets_ref.shape[0]
    for at in range(nsub // LANES):
        here = pl.ds(at * LANES, LANES)
        for first in range(0, span, LANES):
            tile = series_ref[here, pl.ds(first, LANES)].astype(jnp.float32)
            turned[pl.ds(first, LANES), here] = tile.T
        lags[here, :] = offsets_ref[:, here].astype(jnp.float32).T.astype(jnp.bfloat16)
    groups = OMAX // STEP
    rows = length + STEP
    totals[...] = jnp.zeros_like(totals)

    def one_lag(lag, carry):
        shifted = turned[pl.ds(0, length + OMAX - STEP), :].astype(jnp.bfloat16)
        for pair in range(groups // 2):
            chosen = [where_equal(lags[...], lag + STEP * (2 * pair + odd)) for odd in range(2)]
            first = 2 * STEP * pair
            totals[pair] += jnp.dot(
                shifted[first : first + rows],
                jnp.concatenate(chosen, axis=1),
                preferred_element_type=jnp.float32,
            )
        turned[pl.ds(0, span - 8), :] = turned[pl.ds(1, span - 8), :]
        return carry

    lax.fori_loop(0, STEP, one_lag, 0)
    last = where_equal(lags[...], OMAX)
    result = jnp.dot(
        turned[pl.ds(OMAX - STEP, length), :].astype(jnp.bfloat16), last, preferred_element_type=jnp.float32
    )
    for pair in range(groups // 2):
        result = result + totals[pair, pl.ds(0, length), pl.ds(0, trials)]
        result = result + totals[pair, pl.ds(STEP, length), pl.ds(trials, trials)]
    done = (result * scale).T.astype(jnp.bfloat16)
    out_ref[...] = done
    head_ref[...] = done[:, :WMAX]


def boxcar_kernel(widths_ref, main_ref, later_ref, out_ref, mixed):
    trials, length = main_ref.shape
    filters = widths_ref.shape[0]
    values = jnp.concatenate([main_ref[...], later_ref[...]], axis=1)
    shape = (length + WMAX, length)
    lag = lax.broadcasted_iota(jnp.int32, shape, 0) - lax.broadcasted_iota(jnp.int32, shape, 1)
    for at in range(filters):
        width = widths_ref[at]
        band = jnp.where((lag >= 0) & (lag < width), 1.0, 0.0).astype(jnp.bfloat16)
        sums = jnp.dot(values, band, preferred_element_type=jnp.float32)
        root = jnp.sqrt(jnp.full((1, length), width, jnp.int32).astype(jnp.float32))
        scaled = sums / root
        for part in range(length // LANES):
            lanes = slice(part * LANES, (part + 1) * LANES)
            mixed[part, pl.ds(at, trials, stride=filters), :] = scaled[:, lanes]
    for part in range(length // LANES):
        out_ref[:, :, pl.ds(part * LANES, LANES)] = mixed[part].reshape(trials, filters, LANES)


def per_device(data, delays, offsets, widths):
    beams, chans, length = data.shape
    trials, nsub = offsets.shape
    filters = widths.shape[0]
    groups = lax.axis_size("sub")
    sub_dev = nsub // groups
    per_sub = chans // sub_dev
    scale = 1.0 / math.sqrt(chans * groups)
    span = length + LANES
    outs = []
    padded = max(trials, LANES)
    lag_table = jnp.pad(offsets, ((0, padded - trials), (0, 0))) if padded > trials else offsets
    block_subs = min(chans, 256) // per_sub
    channel = jnp.arange(chans, dtype=jnp.int32)
    key = (delays * block_subs + (channel // per_sub) % block_subs)[None, :]
    for beam in range(beams):
        own = data[beam]
        halo = passed_back(own, "tm")
        series = pl.pallas_call(
            functools.partial(series_kernel, per_sub),
            out_shape=jax.ShapeDtypeStruct((sub_dev, span), jnp.bfloat16),
            grid=(1,),
            in_specs=[
                pl.BlockSpec((1, chans), lambda i: (0, 0)),
                pl.BlockSpec((chans, length), lambda i: (0, 0)),
                pl.BlockSpec((chans, LANES), lambda i: (0, 0)),
            ],
            out_specs=pl.BlockSpec((sub_dev, span), lambda i: (0, 0)),
            compiler_params=pltpu.CompilerParams(vmem_limit_bytes=32 << 20),
        )(key, own, halo)
        whole = lax.all_gather(series, "sub", axis=0, tiled=True)
        main, head = pl.pallas_call(
            functools.partial(dedisperse_kernel, scale, length),
            out_shape=[
                jax.ShapeDtypeStruct((padded, length), jnp.bfloat16),
                jax.ShapeDtypeStruct((padded, WMAX), jnp.bfloat16),
            ],
            in_specs=[VMEM, VMEM],
            out_specs=[VMEM, VMEM],
            scratch_shapes=[
                pltpu.VMEM((span, nsub), jnp.float32),
                pltpu.VMEM((nsub, padded), jnp.bfloat16),
                pltpu.VMEM((OMAX // STEP // 2, length + STEP, 2 * padded), jnp.float32),
            ],
            compiler_params=pltpu.CompilerParams(vmem_limit_bytes=40 << 20),
        )(whole, lag_table)
        later = passed_back(head, "tm")
        filtered = pl.pallas_call(
            boxcar_kernel,
            out_shape=jax.ShapeDtypeStruct((padded, filters, length), jnp.float32),
            in_specs=[SMEM, VMEM, VMEM],
            out_specs=VMEM,
            scratch_shapes=[pltpu.VMEM((length // LANES, padded * filters, LANES), jnp.float32)],
            compiler_params=pltpu.CompilerParams(vmem_limit_bytes=32 << 20),
        )(widths, main, later)
        outs.append(filtered.reshape(padded, 1, filters, length)[:trials])
    return outs[0] if beams == 1 else jnp.concatenate(outs, axis=1)


def solution(mesh):
    placed = (P(None, "sub", "tm"), P("sub"), P("sub", None), P())
    return jax.shard_map(
        per_device,
        mesh=mesh,
        in_specs=placed,
        out_specs=P("sub", None, None, "tm"),
        check_vma=False,
    )
```

time: 174 us -> 70.2 us (0.40)
  waiting for transfers between devices: 84.1 us -> 3.83 us
  blocking collectives: 0 us -> 47.5 us
  matrix products: 29.1 us -> 0 us
  local copies, waits for them, and re-layouts: 29.3 us -> 1.05 us
  Pallas kernels: 0 us -> 14.3 us
  between operations: 13.7 us -> 0.05 us
  starting transfers between devices: 11 us -> 2.57 us
  loops' own time: 5.17 us -> 0 us
    reduce_scatter x1 -> x0, waiting for transfers between devices: 82.3 us -> none  [per_device(): lax.psum_scatter(blocks.reshape(lax.axis_size('sub') * dm_dev, beams, out...]
    all_gather x0 -> x1, blocking collectives: none -> 47.5 us  [per_device(): whole = lax.all_gather(series, 'sub', axis=0, tiled=True)]
    dot_general x25 -> x0, matrix products: 29.1 us -> none  [the longest x8 21.3 us: project(): jnp.einsum('msk,bskt->mbt', onehot, hankel, preferred_element_type=jnp.fl...]
    pallas_call x0 -> x3, Pallas kernels: none -> 14.3 us  [the longest x1 11.5 us: per_device(): pl.pallas_call(functools.partial(dedisperse_kernel, scale, length), out_s...]
    dynamic_slice x16 -> x0, local copies, waits for them, and re-layouts: 12 us -> none  [the longest x8 6.8 us: one_block(): lag_rows = lax.dynamic_slice_in_dim(table, block_index * block, block, 0)]
    unnamed x102 -> x6, local copies, waits for them, and re-layouts: 10.9 us -> 1.05 us
    all_to_all x1 -> x0, starting transfers between devices: 8.36 us -> none  [per_device(): lax.all_to_all(offsets, 'sub', split_axis=1, concat_axis=0, tiled=True)]
    another operation x1 -> x0, loops' own time: 5.17 us -> none  [per_device(): lax.map(one_block, jnp.arange(lax.axis_size('sub') * dm_dev // block, dty...]
  transfers between devices with their start and end apart: 4 -> 2, of which waited for: 2 -> 2; matrix products, arithmetic and copies ran while one was open for 11% -> 1% of each run, Pallas kernels for 0% -> 0%
where the time goes in v1:
time: 70.2 us; the launch traced here: 70 us
  blocking collectives  47.5 us (68%)
  Pallas kernels  14.3 us (20%)
  waiting for transfers between devices  3.83 us (5%)
  starting transfers between devices  2.57 us (4%)
  local copies, waits for them, and re-layouts  1.05 us (1%)
    all_gather x1, blocking collectives, per_device(): whole = lax.all_gather(series, 'sub', axis=0, tiled=True)  47.5 us
    pallas_call x1, Pallas kernels, per_device(): pl.pallas_call(functools.partial(dedisperse_kernel, scale, length), out_s...  11.5 us
    ppermute x2, waiting for transfers between devices, passed_back(): lax.ppermute(value, axis, [(source, source - 1) for source in range(1, co...  3.83 us
    ppermute x2, starting transfers between devices, passed_back(): lax.ppermute(value, axis, [(source, source - 1) for source in range(1, co...  2.57 us
    pallas_call x1, Pallas kernels, per_device(): pl.pallas_call(boxcar_kernel, out_shape=jax.ShapeDtypeStruct((padded, fil...  2.07 us
  transfers between devices with their start and end apart: 2, of which 2 were waited for; matrix products, arithmetic and copies ran while one was open for 1% of the time, Pallas kernels for 0%

profile of v1, /device:TPU:0, one launch (start us, length us, event | category | flops | bytes accessed | tf_op | source)
XLA Modules:
  0.0 70.0 jit_solution(6833451052910431553)
XLA Ops:
  0.0 1.3 %collective-permute-start = (bf16[1024,256]{1,0:T(8,128)(2,1)}, bf16[1024,256]{1,0:T(8,128)(2,1)S(1)}, u32[]{:S(2)}, u32[]{:S(2)}) collective-permute-start(bf16[1024,256]{1,0:T(8,128)(2,1)} %bitcast.5), channel_id=1, source_target_pairs={{1,0},{3,2},{5,4},{7,6},{9,8},{11,10},{13,12},{15,14},{17,16},{19,... | collective-permute-start | bytes 1572872 | tf_op jit(solution)/shard_map/ppermute | solution.py:22
  1.3 0.7 fusion.1
  2.0 2.0 %collective-permute-done.halo_ref = bf16[1024,256]{1,0:T(8,128)(2,1)S(1)} collective-permute-done((bf16[1024,256]{1,0:T(8,128)(2,1)}, bf16[1024,256]{1,0:T(8,128)(2,1)S(1)}, u32[]{:S(2)}, u32[]{:S(2)}) %collective-permute-start) | collective-permute-done | bytes 524320 | tf_op jit(solution)/shard_map/ppermute | solution.py:22
  4.0 0.0 copy-start
  4.0 1.0 %copy-done = bf16[1,1024,256]{2,1,0:T(8,128)(2,1)S(1)} copy-done((bf16[1,1024,256]{2,1,0:T(8,128)(2,1)S(1)}, bf16[1,1024,256]{2,1,0:T(8,128)(2,1)}, u32[]{:S(2)}) %copy-start) | copy-done | bytes 524312
  5.0 0.7 shard_map.46
  5.7 0.0 copy-start.1
  5.7 47.5 %all_gather.3.series_ref = bf16[1024,384]{1,0:T(8,128)(2,1)S(1)} all-gather(bf16[64,384]{1,0:T(8,128)(2,1)S(1)} %shard_map.46), channel_id=1, replica_groups=mesh['sub'=16,'tm'=2] {'sub'}, dimensions={0}, use_global_device_ids=true | all-gather | bytes 835584 | tf_op jit(solution)/shard_map/all_gather | solution.py:135
  53.2 0.0 copy-done.1
  53.2 11.5 %shard_map.47 = (bf16[128,256]{1,0:T(8,128)(2,1)S(1)}, bf16[128,128]{1,0:T(8,128)(2,1)S(1)}) custom-call(bf16[1024,384]{1,0:T(8,128)(2,1)S(1)} %all_gather.3.series_ref, s32[128,1024]{1,0:T(8,128)S(1)} %copy-done.1), custom_call_target="tpu_custom_call" | custom-call | tf_op jit(solution)/shard_map/pallas_call | solution.py:136
  64.8 0.0 copy-start.2
  64.8 1.3 %collective-permute-start.1 = (bf16[128,128]{1,0:T(8,128)(2,1)S(1)}, bf16[128,128]{1,0:T(8,128)(2,1)S(1)}, u32[]{:S(2)}, u32[]{:S(2)}) collective-permute-start(bf16[128,128]{1,0:T(8,128)(2,1)S(1)} %get-tuple-element.8), channel_id=1, source_target_pairs={{1,0},{3,2},{5,4},{7,6},{9,8},{11,10},{13,12},{15,14},{17,16},{19,... | collective-permute-start | bytes 98312 | tf_op jit(solution)/shard_map/ppermute | solution.py:22
  66.1 1.8 %collective-permute-done.1.later_ref = bf16[128,128]{1,0:T(8,128)(2,1)S(1)} collective-permute-done((bf16[128,128]{1,0:T(8,128)(2,1)S(1)}, bf16[128,128]{1,0:T(8,128)(2,1)S(1)}, u32[]{:S(2)}, u32[]{:S(2)}) %collective-permute-start.1) | collective-permute-done | bytes 32800 | tf_op jit(solution)/shard_map/ppermute | solution.py:22
  67.9 0.0 copy-done.2
  67.9 2.1 %shard_map.48 = f32[128,8,256]{2,1,0:T(8,128)} custom-call(s32[8]{0:T(128)S(1)} %copy-done.2, bf16[128,256]{1,0:T(8,128)(2,1)S(1)} %get-tuple-element.7.main_ref, bf16[128,128]{1,0:T(8,128)(2,1)S(1)} %collective-permute-done.1.later_ref), custom_call_target="tpu_custom_call" | custom-call | tf_op jit(solution)/shard_map/pallas_call | solution.py:152
Async XLA Ops:
  0.0 4.0 %collective-permute-start = (bf16[1024,256]{1,0:T(8,128)(2,1)}, bf16[1024,256]{1,0:T(8,128)(2,1)S(1)}, u32[]{:S(2)}, u32[]{:S(2)}) collective-permute-start(bf16[1024,256]{1,0:T(8,128)(2,1)} %bitcast.5), channel_id=1, source_target_pairs={{1,0},{3,2},{5,4},{7,6},{9,8},{11,10},{13,12},{15,14},{17,16},{19,... | collective-permute-start | bytes 1572872 | tf_op jit(solution)/shard_map/ppermute | solution.py:22
  4.0 1.0 %copy-start = (bf16[1,1024,256]{2,1,0:T(8,128)(2,1)S(1)}, bf16[1,1024,256]{2,1,0:T(8,128)(2,1)}, u32[]{:S(2)}) copy-start(bf16[1,1024,256]{2,1,0:T(8,128)(2,1)} %param.4) | copy-start | bytes 1572868
  5.7 47.5 %copy-start.1 = (s32[128,1024]{1,0:T(8,128)S(1)}, s32[128,1024]{1,0:T(8,128)}, u32[]{:S(2)}) copy-start(s32[128,1024]{1,0:T(8,128)} %offsets_ref.1) | copy-start | bytes 1572868
  64.8 3.1 %copy-start.2 = (s32[8]{0:T(128)S(1)}, s32[8]{0:T(128)}, u32[]{:S(2)}) copy-start(s32[8]{0:T(128)} %widths_ref.1) | copy-start | bytes 100
  64.8 3.1 %collective-permute-start.1 = (bf16[128,128]{1,0:T(8,128)(2,1)S(1)}, bf16[128,128]{1,0:T(8,128)(2,1)S(1)}, u32[]{:S(2)}, u32[]{:S(2)}) collective-permute-start(bf16[128,128]{1,0:T(8,128)(2,1)S(1)} %get-tuple-element.8), channel_id=1, source_target_pairs={{1,0},{3,2},{5,4},{7,6},{9,8},{11,10},{13,12},{15,14},{17,16},{19,... | collective-permute-start | bytes 98312 | tf_op jit(solution)/shard_map/ppermute | solution.py:22

commit v2 on v1

--- a/solution.py
+++ b/solution.py
@@ -24,7 +24,7 @@
 
 def series_kernel(per_sub, key_ref, data_ref, halo_ref, series_ref):
     chans = data_ref.shape[0]
-    span = series_ref.shape[1]
+    copies, _, span = series_ref.shape
     block = min(chans, 256)
     subs = block // per_sub
     rows = lax.broadcasted_iota(jnp.int32, (DCH * subs, block), 0)
@@ -36,7 +36,9 @@
         total = picked[:subs, :]
         for delay in range(1, DCH):
             total = total + pltpu.roll(picked[delay * subs : (delay + 1) * subs, :], span - delay, 1)
-        series_ref[pl.ds(at * subs, subs), :] = total.astype(jnp.bfloat16)
+        rounded = total.astype(jnp.bfloat16)
+        for copy in range(copies):
+            series_ref[copy, pl.ds(at * subs, subs), :] = rounded
 
 
 def where_equal(table, value):
@@ -122,17 +124,17 @@
         halo = passed_back(own, "tm")
         series = pl.pallas_call(
             functools.partial(series_kernel, per_sub),
-            out_shape=jax.ShapeDtypeStruct((sub_dev, span), jnp.bfloat16),
+            out_shape=jax.ShapeDtypeStruct((groups, sub_dev, span), jnp.bfloat16),
             grid=(1,),
             in_specs=[
                 pl.BlockSpec((1, chans), lambda i: (0, 0)),
                 pl.BlockSpec((chans, length), lambda i: (0, 0)),
                 pl.BlockSpec((chans, LANES), lambda i: (0, 0)),
             ],
-            out_specs=pl.BlockSpec((sub_dev, span), lambda i: (0, 0)),
+            out_specs=pl.BlockSpec((groups, sub_dev, span), lambda i: (0, 0, 0)),
             compiler_params=pltpu.CompilerParams(vmem_limit_bytes=32 << 20),
         )(key, own, halo)
-        whole = lax.all_gather(series, "sub", axis=0, tiled=True)
+        whole = lax.all_to_all(series, "sub", 0, 0, tiled=True).reshape(nsub, span)
         main, head = pl.pallas_call(
             functools.partial(dedisperse_kernel, scale, length),
             out_shape=[

time: 70.2 us -> 52.6 us (0.75)
  blocking collectives: 47.5 us -> 29.8 us
    all_gather x1 -> x0, blocking collectives: 47.5 us -> none  [per_device(): whole = lax.all_gather(series, 'sub', axis=0, tiled=True)]
    all_to_all x0 -> x1, blocking collectives: none -> 29.8 us  [per_device(): whole = lax.all_to_all(series, 'sub', 0, 0, tiled=True).reshape(nsub, span)]
where the time goes in v2:
time: 52.6 us; the launch traced here: 52.3 us
  blocking collectives  29.8 us (57%)
  Pallas kernels  14.3 us (27%)
  waiting for transfers between devices  3.83 us (7%)
  starting transfers between devices  2.57 us (5%)
  local copies, waits for them, and re-layouts  1.05 us (2%)
  other arithmetic  0.69 us (1%)
    all_to_all x1, blocking collectives, per_device(): whole = lax.all_to_all(series, 'sub', 0, 0, tiled=True).reshape(nsub, span)  29.8 us
    pallas_call x1, Pallas kernels, per_device(): pl.pallas_call(functools.partial(dedisperse_kernel, scale, length), out_s...  11.5 us
    ppermute x2, waiting for transfers between devices, passed_back(): lax.ppermute(value, axis, [(source, source - 1) for source in range(1, co...  3.83 us
    ppermute x2, starting transfers between devices, passed_back(): lax.ppermute(value, axis, [(source, source - 1) for source in range(1, co...  2.57 us
    pallas_call x1, Pallas kernels, per_device(): pl.pallas_call(boxcar_kernel, out_shape=jax.ShapeDtypeStruct((padded, fil...  2.07 us
    unnamed x6, local copies, waits for them, and re-layouts  1.05 us
  transfers between devices with their start and end apart: 2, of which 2 were waited for; matrix products, arithmetic and copies ran while one was open for 1% of the time, Pallas kernels for 0%

profile of v2, /device:TPU:0, one launch (start us, length us, event | category | flops | bytes accessed | tf_op | source)
XLA Modules:
  0.0 52.3 jit_solution(9550775306405595972)
XLA Ops:
  0.0 1.3 %collective-permute-start = (bf16[1024,256]{1,0:T(8,128)(2,1)}, bf16[1024,256]{1,0:T(8,128)(2,1)S(1)}, u32[]{:S(2)}, u32[]{:S(2)}) collective-permute-start(bf16[1024,256]{1,0:T(8,128)(2,1)} %bitcast.7), channel_id=1, source_target_pairs={{1,0},{3,2},{5,4},{7,6},{9,8},{11,10},{13,12},{15,14},{17,16},{19,... | collective-permute-start | bytes 1572872 | tf_op jit(solution)/shard_map/ppermute | solution.py:22
  1.3 0.7 %fusion.1 = s32[1024]{0:T(1024)S(1)} fusion(s32[1024]{0:T(1024)} %param.5), kind=kLoop, calls=%fused_computation.8 | loop fusion | flops 21504 | bytes 8192 | tf_op jit(solution)/shard_map/add | solution.py:121
  2.0 2.0 %collective-permute-done.halo_ref = bf16[1024,256]{1,0:T(8,128)(2,1)S(1)} collective-permute-done((bf16[1024,256]{1,0:T(8,128)(2,1)}, bf16[1024,256]{1,0:T(8,128)(2,1)S(1)}, u32[]{:S(2)}, u32[]{:S(2)}) %collective-permute-start) | collective-permute-done | bytes 524320 | tf_op jit(solution)/shard_map/ppermute | solution.py:22
  4.0 0.0 copy-start
  4.0 1.0 %copy-done = bf16[1,1024,256]{2,1,0:T(8,128)(2,1)S(1)} copy-done((bf16[1,1024,256]{2,1,0:T(8,128)(2,1)S(1)}, bf16[1,1024,256]{2,1,0:T(8,128)(2,1)}, u32[]{:S(2)}) %copy-start) | copy-done | bytes 524312
  5.0 0.7 %shard_map.46 = bf16[16,64,384]{2,1,0:T(8,128)(2,1)S(1)} custom-call(s32[1,1024]{1,0:T(1,128)S(1)} %bitcast.9, bf16[1024,256]{1,0:T(8,128)(2,1)S(1)} %bitcast.8, bf16[1024,256]{1,0:T(8,128)(2,1)S(1)} %collective-permute-done.halo_ref), custom_call_target="tpu_custom_call" | custom-call | tf_op jit(solution)/shard_map/pallas_call | solution.py:125
  5.7 0.0 copy-start.1
  5.8 29.8 %all_to_all.5 = bf16[16,64,384]{2,1,0:T(8,128)(2,1)S(1)} all-to-all(bf16[16,64,384]{2,1,0:T(8,128)(2,1)S(1)} %shard_map.46), channel_id=1, replica_groups=mesh['sub'=16,'tm'=2] {'sub'}, dimensions={0} | all-to-all | bytes 1572864 | tf_op jit(solution)/shard_map/all_to_all | solution.py:137
  35.6 0.0 copy-done.1
  35.6 11.5 %shard_map.47 = (bf16[128,256]{1,0:T(8,128)(2,1)S(1)}, bf16[128,128]{1,0:T(8,128)(2,1)S(1)}) custom-call(bf16[1024,384]{1,0:T(8,128)(2,1)S(1)} %bitcast.6, s32[128,1024]{1,0:T(8,128)S(1)} %copy-done.1), custom_call_target="tpu_custom_call" | custom-call | tf_op jit(solution)/shard_map/pallas_call | solution.py:138
  47.1 0.0 copy-start.2
  47.1 1.3 %collective-permute-start.1 = (bf16[128,128]{1,0:T(8,128)(2,1)S(1)}, bf16[128,128]{1,0:T(8,128)(2,1)S(1)}, u32[]{:S(2)}, u32[]{:S(2)}) collective-permute-start(bf16[128,128]{1,0:T(8,128)(2,1)S(1)} %get-tuple-element.8), channel_id=1, source_target_pairs={{1,0},{3,2},{5,4},{7,6},{9,8},{11,10},{13,12},{15,14},{17,16},{19,... | collective-permute-start | bytes 98312 | tf_op jit(solution)/shard_map/ppermute | solution.py:22
  48.5 1.8 %collective-permute-done.1.later_ref = bf16[128,128]{1,0:T(8,128)(2,1)S(1)} collective-permute-done((bf16[128,128]{1,0:T(8,128)(2,1)S(1)}, bf16[128,128]{1,0:T(8,128)(2,1)S(1)}, u32[]{:S(2)}, u32[]{:S(2)}) %collective-permute-start.1) | collective-permute-done | bytes 32800 | tf_op jit(solution)/shard_map/ppermute | solution.py:22
  50.3 0.0 copy-done.2
  50.3 2.1 %shard_map.48 = f32[128,8,256]{2,1,0:T(8,128)} custom-call(s32[8]{0:T(128)S(1)} %copy-done.2, bf16[128,256]{1,0:T(8,128)(2,1)S(1)} %get-tuple-element.7.main_ref, bf16[128,128]{1,0:T(8,128)(2,1)S(1)} %collective-permute-done.1.later_ref), custom_call_target="tpu_custom_call" | custom-call | tf_op jit(solution)/shard_map/pallas_call | solution.py:154
Async XLA Ops:
  0.0 4.0 %collective-permute-start = (bf16[1024,256]{1,0:T(8,128)(2,1)}, bf16[1024,256]{1,0:T(8,128)(2,1)S(1)}, u32[]{:S(2)}, u32[]{:S(2)}) collective-permute-start(bf16[1024,256]{1,0:T(8,128)(2,1)} %bitcast.7), channel_id=1, source_target_pairs={{1,0},{3,2},{5,4},{7,6},{9,8},{11,10},{13,12},{15,14},{17,16},{19,... | collective-permute-start | bytes 1572872 | tf_op jit(solution)/shard_map/ppermute | solution.py:22
  4.0 1.0 %copy-start = (bf16[1,1024,256]{2,1,0:T(8,128)(2,1)S(1)}, bf16[1,1024,256]{2,1,0:T(8,128)(2,1)}, u32[]{:S(2)}) copy-start(bf16[1,1024,256]{2,1,0:T(8,128)(2,1)} %param.4) | copy-start | bytes 1572868
  5.7 29.8 %copy-start.1 = (s32[128,1024]{1,0:T(8,128)S(1)}, s32[128,1024]{1,0:T(8,128)}, u32[]{:S(2)}) copy-start(s32[128,1024]{1,0:T(8,128)} %offsets_ref.1) | copy-start | bytes 1572868
  47.1 3.1 %copy-start.2 = (s32[8]{0:T(128)S(1)}, s32[8]{0:T(128)}, u32[]{:S(2)}) copy-start(s32[8]{0:T(128)} %widths_ref.1) | copy-start | bytes 100
  47.1 3.1 %collective-permute-start.1 = (bf16[128,128]{1,0:T(8,128)(2,1)S(1)}, bf16[128,128]{1,0:T(8,128)(2,1)S(1)}, u32[]{:S(2)}, u32[]{:S(2)}) collective-permute-start(bf16[128,128]{1,0:T(8,128)(2,1)S(1)} %get-tuple-element.8), channel_id=1, source_target_pairs={{1,0},{3,2},{5,4},{7,6},{9,8},{11,10},{13,12},{15,14},{17,16},{19,... | collective-permute-start | bytes 98312 | tf_op jit(solution)/shard_map/ppermute | solution.py:22

commit v3 on v1

v3 whole, which is shorter than its diff:
```python
import functools
import math

import jax
import jax.numpy as jnp
from jax import lax
from jax.experimental import pallas as pl
from jax.experimental.pallas import tpu as pltpu
from jax.sharding import PartitionSpec as P

WMAX = 128
DCH = 16
OMAX = 96
LANES = 128
STEP = 16
TOGETHER = 4
VMEM = pl.BlockSpec(memory_space=pltpu.VMEM)
SMEM = pl.BlockSpec(memory_space=pltpu.SMEM)
LIMIT = pltpu.CompilerParams(vmem_limit_bytes=32 << 20)


def passed_back(value, axis):
    count = lax.axis_size(axis)
    return lax.ppermute(value, axis, [(source, source - 1) for source in range(1, count)])


def exchanged(value, axis, flip):
    count = lax.axis_size(axis)
    return lax.ppermute(value, axis, [(source, source ^ flip) for source in range(count)])


def series_kernel(per_sub, key_ref, data_ref, halo_ref, series_ref):
    chans = data_ref.shape[0]
    span = series_ref.shape[1]
    block = min(chans, 256)
    subs = block // per_sub
    rows = lax.broadcasted_iota(jnp.int32, (DCH * subs, block), 0)
    for at in range(chans // block):
        here = pl.ds(at * block, block)
        member = jnp.where(rows == key_ref[:, here], 1.0, 0.0).astype(jnp.bfloat16)
        values = jnp.concatenate([data_ref[here, :], halo_ref[here, :]], axis=1)
        picked = jnp.dot(member, values, preferred_element_type=jnp.float32)
        total = picked[:subs, :]
        for delay in range(1, DCH):
            total = total + pltpu.roll(picked[delay * subs : (delay + 1) * subs, :], span - delay, 1)
        series_ref[pl.ds(at * subs, subs), :] = total.astype(jnp.bfloat16)


def turn_offsets_kernel(offsets_ref, lags_ref):
    for at in range(offsets_ref.shape[1] // LANES):
        here = pl.ds(at * LANES, LANES)
        lags_ref[here, :] = offsets_ref[:, here].astype(jnp.float32).T.astype(jnp.bfloat16)


def turn_series_kernel(outer, place_ref, *refs):
    blocks, turned_ref, ordered = refs[:outer], refs[outer], refs[outer + 1]
    subs, span = blocks[0].shape
    me = place_ref[0]
    for flip in range(outer):
        start = pl.multiple_of((me ^ flip) * subs, subs)
        ordered[pl.ds(start, subs), :] = blocks[flip][...].astype(jnp.float32)
    rows = turned_ref.shape[0]
    for at in range(outer * subs // LANES):
        here = pl.ds(at * LANES, LANES)
        for first in range(0, rows, LANES):
            count = min(LANES, rows - first)
            tile = ordered[here, pl.ds(first, LANES)].T
            turned_ref[pl.ds(first, count), here] = tile[:count].astype(jnp.bfloat16)


def where_equal(table, value):
    wanted = jnp.full((1, table.shape[1]), value, jnp.int32).astype(jnp.float32).astype(jnp.bfloat16)
    return jnp.where(table == wanted, jnp.bfloat16(1), jnp.bfloat16(0))


def partial_sums(outer, flip, place_ref, turned_ref, lags_ref, moving, lags, totals):
    span, nsub = turned_ref.shape
    length = span - OMAX
    subs = nsub // outer
    trials = lags_ref.shape[1]
    inner = lags_ref.shape[0] // nsub
    column = place_ref[1] ^ flip
    for row in range(outer):
        start = pl.multiple_of((row * inner + column) * subs, subs)
        lags[pl.ds(row * subs, subs), :] = lags_ref[pl.ds(start, subs), :]
    moving[pl.ds(0, span), :] = turned_ref[...].astype(jnp.float32)
    pairs = OMAX // STEP // 2
    rows = length + STEP
    reach = length + OMAX - STEP
    totals[...] = jnp.zeros_like(totals)

    def some_lags(step, carry):
        shifted = jnp.concatenate(
            [moving[pl.ds(at, reach), :].astype(jnp.bfloat16) for at in range(TOGETHER)], axis=1
        )
        for pair in range(pairs):
            chosen = jnp.concatenate(
                [
                    jnp.concatenate(
                        [
                            where_equal(lags[...], step * TOGETHER + at + STEP * (2 * pair + odd))
                            for odd in range(2)
                        ],
                        axis=1,
                    )
                    for at in range(TOGETHER)
                ],
                axis=0,
            )
            first = 2 * STEP * pair
            totals[pair] += jnp.dot(
                shifted[first : first + rows], chosen, preferred_element_type=jnp.float32
            )
        moving[pl.ds(0, span), :] = moving[pl.ds(TOGETHER, span), :]
        return carry

    lax.fori_loop(0, STEP // TOGETHER, some_lags, 0)
    result = jnp.dot(
        moving[pl.ds(OMAX - STEP, length), :].astype(jnp.bfloat16),
        where_equal(lags[...], OMAX),
        preferred_element_type=jnp.float32,
    )
    for pair in range(pairs):
        result = result + totals[pair, pl.ds(0, length), pl.ds(0, trials)]
        result = result + totals[pair, pl.ds(STEP, length), pl.ds(trials, trials)]
    return result


def first_sums_kernel(outer, place_ref, turned_ref, lags_ref, sums_ref, *scratch):
    sums_ref[...] = partial_sums(outer, 0, place_ref, turned_ref, lags_ref, *scratch)


def more_sums_kernel(outer, flip, place_ref, turned_ref, lags_ref, before_ref, sums_ref, *scratch):
    sums_ref[...] = before_ref[...] + partial_sums(outer, flip, place_ref, turned_ref, lags_ref, *scratch)


def last_sums_kernel(
    outer, flip, scale, place_ref, turned_ref, lags_ref, before_ref, out_ref, head_ref, *scratch
):
    sums = before_ref[...] + partial_sums(outer, flip, place_ref, turned_ref, lags_ref, *scratch)
    done = (sums * scale).T.astype(jnp.bfloat16)
    out_ref[...] = done
    head_ref[...] = done[:, :WMAX]


def boxcar_kernel(widths_ref, main_ref, later_ref, out_ref, mixed):
    trials, length = main_ref.shape
    filters = widths_ref.shape[0]
    values = jnp.concatenate([main_ref[...], later_ref[...]], axis=1)
    shape = (length + WMAX, length)
    lag = lax.broadcasted_iota(jnp.int32, shape, 0) - lax.broadcasted_iota(jnp.int32, shape, 1)
    for at in range(filters):
        width = widths_ref[at]
        band = jnp.where((lag >= 0) & (lag < width), 1.0, 0.0).astype(jnp.bfloat16)
        sums = jnp.dot(values, band, preferred_element_type=jnp.float32)
        root = jnp.sqrt(jnp.full((1, length), width, jnp.int32).astype(jnp.float32))
        scaled = sums / root
        for part in range(length // LANES):
            lanes = slice(part * LANES, (part + 1) * LANES)
            mixed[part, pl.ds(at, trials, stride=filters), :] = scaled[:, lanes]
    for part in range(length // LANES):
        out_ref[:, :, pl.ds(part * LANES, LANES)] = mixed[part].reshape(trials, filters, LANES)


def one_beam(own, key, lags, widths, place, groups, outer, per_sub, scale):
    chans, length = own.shape
    sub_dev = chans // per_sub
    inner = groups // outer
    padded = lags.shape[1]
    filters = widths.shape[0]
    halo = passed_back(own, "tm")
    series = pl.pallas_call(
        functools.partial(series_kernel, per_sub),
        out_shape=jax.ShapeDtypeStruct((sub_dev, length + LANES), jnp.bfloat16),
        grid=(1,),
        in_specs=[
            pl.BlockSpec((1, chans), lambda i: (0, 0)),
            pl.BlockSpec((chans, length), lambda i: (0, 0)),
            pl.BlockSpec((chans, LANES), lambda i: (0, 0)),
        ],
        out_specs=pl.BlockSpec((sub_dev, length + LANES), lambda i: (0, 0)),
        compiler_params=LIMIT,
    )(key, own, halo)
    line = [series] + [exchanged(series, "sub", flip * inner) for flip in range(1, outer)]
    span = length + OMAX
    nsub = outer * sub_dev
    turned = pl.pallas_call(
        functools.partial(turn_series_kernel, outer),
        out_shape=jax.ShapeDtypeStruct((span, nsub), jnp.bfloat16),
        in_specs=[SMEM] + [VMEM] * outer,
        out_specs=VMEM,
        scratch_shapes=[pltpu.VMEM((nsub, length + LANES), jnp.float32)],
        compiler_params=LIMIT,
    )(place, *line)
    blocks = [turned] + [exchanged(turned, "sub", flip) for flip in range(1, inner)]
    scratch = [
        pltpu.VMEM((span + 8, nsub), jnp.float32),
        pltpu.VMEM((nsub, padded), jnp.bfloat16),
        pltpu.VMEM((OMAX // STEP // 2, length + STEP, 2 * padded), jnp.float32),
    ]
    sums_shape = jax.ShapeDtypeStruct((length, padded), jnp.float32)
    flops = 2 * span * nsub * padded * (OMAX + 1)
    cost = pl.CostEstimate(flops=flops, bytes_accessed=1 << 20, transcendentals=0)
    common = dict(scratch_shapes=scratch, compiler_params=LIMIT, cost_estimate=cost)
    sums = pl.pallas_call(
        functools.partial(first_sums_kernel, outer),
        out_shape=sums_shape,
        in_specs=[SMEM, VMEM, VMEM],
        out_specs=VMEM,
        **common,
    )(place, turned, lags)
    for flip in range(1, inner - 1):
        sums = pl.pallas_call(
            functools.partial(more_sums_kernel, outer, flip),
            out_shape=sums_shape,
            in_specs=[SMEM, VMEM, VMEM, VMEM],
            out_specs=VMEM,
            **common,
        )(place, blocks[flip], lags, sums)
    main, head = pl.pallas_call(
        functools.partial(last_sums_kernel, outer, inner - 1, scale),
        out_shape=[
            jax.ShapeDtypeStruct((padded, length), jnp.bfloat16),
            jax.ShapeDtypeStruct((padded, WMAX), jnp.bfloat16),
        ],
        in_specs=[SMEM, VMEM, VMEM, VMEM],
        out_specs=[VMEM, VMEM],
        **common,
    )(place, blocks[inner - 1], lags, sums)
    later = passed_back(head, "tm")
    return pl.pallas_call(
        boxcar_kernel,
        out_shape=jax.ShapeDtypeStruct((padded, filters, length), jnp.float32),
        in_specs=[SMEM, VMEM, VMEM],
        out_specs=VMEM,
        scratch_shapes=[pltpu.VMEM((length // LANES, padded * filters, LANES), jnp.float32)],
        compiler_params=LIMIT,
    )(widths, main, later)


def per_device(data, delays, offsets, widths):
    beams, chans, length = data.shape
    trials, nsub = offsets.shape
    groups = lax.axis_size("sub")
    outer = 1 << (groups.bit_length() // 2)
    outer = outer if groups % (outer * outer) == 0 else outer // 2
    inner = groups // outer
    per_sub = chans // (nsub // groups)
    scale = 1.0 / math.sqrt(chans * groups)
    padded = max(trials, LANES)
    lag_table = jnp.pad(offsets, ((0, padded - trials), (0, 0))) if padded > trials else offsets
    block_subs = min(chans, 256) // per_sub
    channel = jnp.arange(chans, dtype=jnp.int32)
    key = (delays * block_subs + (channel // per_sub) % block_subs)[None, :]
    me = lax.axis_index("sub")
    place = jnp.stack([me // inner, me % inner]).astype(jnp.int32)
    lags = pl.pallas_call(
        turn_offsets_kernel,
        out_shape=jax.ShapeDtypeStruct((nsub, padded), jnp.bfloat16),
        in_specs=[VMEM],
        out_specs=VMEM,
        compiler_params=LIMIT,
    )(lag_table)
    outs = [
        one_beam(data[beam], key, lags, widths, place, groups, outer, per_sub, scale)[:trials, None]
        for beam in range(beams)
    ]
    return outs[0] if beams == 1 else jnp.concatenate(outs, axis=1)


def solution(mesh):
    placed = (P(None, "sub", "tm"), P("sub"), P("sub", None), P())
    return jax.shard_map(
        per_device,
        mesh=mesh,
        in_specs=placed,
        out_specs=P("sub", None, None, "tm"),
        check_vma=False,
    )
```

time: 70.2 us -> 39.7 us (0.57)
  blocking collectives: 47.5 us -> 0 us
  starting transfers between devices: 2.57 us -> 11.9 us
  waiting for transfers between devices: 3.83 us -> 8.58 us
  Pallas kernels: 14.3 us -> 17.1 us
    all_gather x1 -> x0, blocking collectives: 47.5 us -> none  [per_device(): whole = lax.all_gather(series, 'sub', axis=0, tiled=True)]
    ppermute x0 -> x6, starting transfers between devices: none -> 9.31 us  [exchanged(): lax.ppermute(value, axis, [(source, source ^ flip) for source in range(co...]
    ppermute x0 -> x6, waiting for transfers between devices: none -> 4.77 us  [exchanged(): lax.ppermute(value, axis, [(source, source ^ flip) for source in range(co...]
    pallas_call x3 -> x8, Pallas kernels: 14.3 us -> 17.1 us  [the longest x2 6.73 us: one_beam(): pl.pallas_call(functools.partial(more_sums_kernel, outer, flip), out_shap...]
    unnamed x6 -> x8, local copies, waits for them, and re-layouts: 1.05 us -> 1.72 us
  transfers between devices with their start and end apart: 2 -> 8, of which waited for: 2 -> 6; matrix products, arithmetic and copies ran while one was open for 1% -> 0% of each run, Pallas kernels for 0% -> 26%
where the time goes in v3:
time: 39.7 us; the launch traced here: 39.5 us
  Pallas kernels  17.1 us (43%)
  starting transfers between devices  11.9 us (30%)
  waiting for transfers between devices  8.58 us (22%)
  local copies, waits for them, and re-layouts  1.72 us (4%)
    ppermute x6, starting transfers between devices, exchanged(): lax.ppermute(value, axis, [(source, source ^ flip) for source in range(co...  9.31 us
    pallas_call x2, Pallas kernels, one_beam(): pl.pallas_call(functools.partial(more_sums_kernel, outer, flip), out_shap...  6.73 us
    ppermute x6, waiting for transfers between devices, exchanged(): lax.ppermute(value, axis, [(source, source ^ flip) for source in range(co...  4.77 us
    ppermute x2, waiting for transfers between devices, passed_back(): lax.ppermute(value, axis, [(source, source - 1) for source in range(1, co...  3.81 us
    pallas_call x1, Pallas kernels, one_beam(): pl.pallas_call(functools.partial(last_sums_kernel, outer, inner - 1, scal...  3.44 us
    pallas_call x1, Pallas kernels, one_beam(): pl.pallas_call(functools.partial(first_sums_kernel, outer), out_shape=sum...  3.34 us
    ppermute x2, starting transfers between devices, passed_back(): lax.ppermute(value, axis, [(source, source - 1) for source in range(1, co...  2.57 us
    pallas_call x1, Pallas kernels, one_beam(): pl.pallas_call(boxcar_kernel, out_shape=jax.ShapeDtypeStruct((padded, fil...  2.07 us
  transfers between devices with their start and end apart: 8, of which 6 were waited for; matrix products, arithmetic and copies ran while one was open for 0% of the time, Pallas kernels for 26%

profile of v3, /device:TPU:0, one launch (start us, length us, event | category | flops | bytes accessed | tf_op | source)
XLA Modules:
  0.0 39.5 jit_solution(3750299390098116606)
XLA Ops:
  0.0 1.3 %collective-permute-start = (bf16[1024,256]{1,0:T(8,128)(2,1)}, bf16[1024,256]{1,0:T(8,128)(2,1)S(1)}, u32[]{:S(2)}, u32[]{:S(2)}) collective-permute-start(bf16[1024,256]{1,0:T(8,128)(2,1)} %bitcast.7), channel_id=1, source_target_pairs={{1,0},{3,2},{5,4},{7,6},{9,8},{11,10},{13,12},{15,14},{17,16},{19,... | collective-permute-start | bytes 1572872 | tf_op jit(solution)/shard_map/ppermute | solution.py:24
  1.3 0.0 copy-start.3
  1.3 0.7 %copy-done.3 = s32[1024]{0:T(1024)S(1)} copy-done((s32[1024]{0:T(1024)S(1)}, s32[1024]{0:T(1024)}, u32[]{:S(2)}) %copy-start.3) | copy-done | bytes 4120
  2.0 2.0 %collective-permute-done.halo_ref = bf16[1024,256]{1,0:T(8,128)(2,1)S(1)} collective-permute-done((bf16[1024,256]{1,0:T(8,128)(2,1)}, bf16[1024,256]{1,0:T(8,128)(2,1)S(1)}, u32[]{:S(2)}, u32[]{:S(2)}) %collective-permute-start) | collective-permute-done | bytes 524320 | tf_op jit(solution)/shard_map/ppermute | solution.py:24
  4.0 0.0 copy-start.1
  4.0 1.0 %copy-done.1 = bf16[1,1024,256]{2,1,0:T(8,128)(2,1)S(1)} copy-done((bf16[1,1024,256]{2,1,0:T(8,128)(2,1)S(1)}, bf16[1,1024,256]{2,1,0:T(8,128)(2,1)}, u32[]{:S(2)}) %copy-start.1) | copy-done | bytes 524312
  5.0 0.0 copy-start
  5.1 0.7 %shard_map.46.refs_0_ = bf16[64,384]{1,0:T(8,128)(2,1)S(1)} custom-call(s32[1,1024]{1,0:T(1,128)S(1)} %bitcast.9, bf16[1024,256]{1,0:T(8,128)(2,1)S(1)} %bitcast.8, bf16[1024,256]{1,0:T(8,128)(2,1)S(1)} %collective-permute-done.halo_ref), custom_call_target="tpu_custom_call" | custom-call | tf_op jit(solution)/shard_map/pallas_call | solution.py:172
  5.7 5.1 %collective-permute-start.3 = (bf16[64,384]{1,0:T(8,128)(2,1)S(1)}, bf16[64,384]{1,0:T(8,128)(2,1)S(1)}, u32[]{:S(2)}, u32[]{:S(2)}) collective-permute-start(bf16[64,384]{1,0:T(8,128)(2,1)S(1)} %shard_map.46.refs_0_), channel_id=1, source_target_pairs={{0,24},{2,26},{4,28},{6,30},{8,16},{10,18},{12,20},{14,22},{16,8},... | collective-permute-start | bytes 147464 | tf_op jit(solution)/shard_map/ppermute | solution.py:29
  10.8 0.0 collective-permute-start.2
  10.8 0.6 %collective-permute-start.1 = (bf16[64,384]{1,0:T(8,128)(2,1)S(1)}, bf16[64,384]{1,0:T(8,128)(2,1)S(1)}, u32[]{:S(2)}, u32[]{:S(2)}) collective-permute-start(bf16[64,384]{1,0:T(8,128)(2,1)S(1)} %shard_map.46.refs_0_), channel_id=1, source_target_pairs={{0,8},{2,10},{4,12},{6,14},{8,0},{10,2},{12,4},{14,6},{16,24},{18,... | collective-permute-start | bytes 147464 | tf_op jit(solution)/shard_map/ppermute | solution.py:29
  11.5 0.1 pad_add_fusion.place_ref
  11.5 0.0 copy-done
  11.5 0.1 shard_map.48.lags_ref
  11.7 1.3 %collective-permute-done.3.refs_3_ = bf16[64,384]{1,0:T(8,128)(2,1)S(1)} collective-permute-done((bf16[64,384]{1,0:T(8,128)(2,1)S(1)}, bf16[64,384]{1,0:T(8,128)(2,1)S(1)}, u32[]{:S(2)}, u32[]{:S(2)}) %collective-permute-start.3) | collective-permute-done | bytes 49184 | tf_op jit(solution)/shard_map/ppermute | solution.py:29
  13.0 2.8 %collective-permute-done.2.refs_2_ = bf16[64,384]{1,0:T(8,128)(2,1)S(1)} collective-permute-done((bf16[64,384]{1,0:T(8,128)(2,1)S(1)}, bf16[64,384]{1,0:T(8,128)(2,1)S(1)}, u32[]{:S(2)}, u32[]{:S(2)}) %collective-permute-start.2) | collective-permute-done | bytes 49184 | tf_op jit(solution)/shard_map/ppermute | solution.py:29
  15.8 0.0 collective-permute-done.1.refs_1_
  15.8 0.7 %shard_map.47.turned_ref = bf16[352,256]{1,0:T(8,128)(2,1)S(1)} custom-call(s32[2]{0:T(128)S(1)} %pad_add_fusion.place_ref, bf16[64,384]{1,0:T(8,128)(2,1)S(1)} %shard_map.46.refs_0_, bf16[64,384]{1,0:T(8,128)(2,1)S(1)} %collective-permute-done.1.refs_1_, bf16[64,384]{1,0:T(8,128)(2,1)S(1)} %collective-permute-done.2.refs_2_, ...), custom_call_target="tpu_custom_call" | custom-call | tf_op jit(solution)/shard_map/pallas_call | solution.py:187
  16.5 1.6 %collective-permute-start.6 = (bf16[352,256]{1,0:T(8,128)(2,1)S(1)}, bf16[352,256]{1,0:T(8,128)(2,1)S(1)}, u32[]{:S(2)}, u32[]{:S(2)}) collective-permute-start(bf16[352,256]{1,0:T(8,128)(2,1)S(1)} %shard_map.47.turned_ref), channel_id=1, source_target_pairs={{0,2},{2,0},{4,6},{6,4},{8,10},{10,8},{12,14},{14,12},{16,18},{18,... | collective-permute-start | bytes 540680 | tf_op jit(solution)/shard_map/ppermute | solution.py:29
  18.1 1.5 %collective-permute-start.5 = (bf16[352,256]{1,0:T(8,128)(2,1)S(1)}, bf16[352,256]{1,0:T(8,128)(2,1)S(1)}, u32[]{:S(2)}, u32[]{:S(2)}) collective-permute-start(bf16[352,256]{1,0:T(8,128)(2,1)S(1)} %shard_map.47.turned_ref), channel_id=1, source_target_pairs={{0,4},{2,6},{4,0},{6,2},{8,12},{10,14},{12,8},{14,10},{16,20},{18,... | collective-permute-start | bytes 540680 | tf_op jit(solution)/shard_map/ppermute | solution.py:29
  19.6 0.5 %collective-permute-start.4 = (bf16[352,256]{1,0:T(8,128)(2,1)S(1)}, bf16[352,256]{1,0:T(8,128)(2,1)S(1)}, u32[]{:S(2)}, u32[]{:S(2)}) collective-permute-start(bf16[352,256]{1,0:T(8,128)(2,1)S(1)} %shard_map.47.turned_ref), channel_id=1, source_target_pairs={{0,6},{2,4},{4,2},{6,0},{8,14},{10,12},{12,10},{14,8},{16,22},{18,... | collective-permute-start | bytes 540680 | tf_op jit(solution)/shard_map/ppermute | solution.py:29
  20.1 3.3 %shard_map.49.before_ref = f32[256,128]{1,0:T(8,128)S(1)} custom-call(s32[2]{0:T(128)S(1)} %pad_add_fusion.place_ref, bf16[352,256]{1,0:T(8,128)(2,1)S(1)} %shard_map.47.turned_ref, bf16[1024,128]{1,0:T(8,128)(2,1)S(1)} %shard_map.48.lags_ref), custom_call_target="tpu_custom_call" | custom-call | flops 2237661184 | bytes 1048576 | tf_op jit(solution)/shard_map/pallas_call | solution.py:205
  23.4 0.4 collective-permute-done.6.turned_ref
  23.8 3.4 %shard_map.50.before_ref = f32[256,128]{1,0:T(8,128)S(1)} custom-call(s32[2]{0:T(128)S(1)} %pad_add_fusion.place_ref, bf16[352,256]{1,0:T(8,128)(2,1)S(1)} %collective-permute-done.6.turned_ref, bf16[1024,128]{1,0:T(8,128)(2,1)S(1)} %shard_map.48.lags_ref, f32[256,128]{1,0:T(8,128)S(1)} %shard_map.49.before_ref), custom_call_target="tpu_custom_call" | custom-call | flops 2237661184 | bytes 1048576 | tf_op jit(solution)/shard_map/pallas_call | solution.py:213
  27.2 0.3 collective-permute-done.5.turned_ref
  27.4 3.4 %shard_map.51.before_ref = f32[256,128]{1,0:T(8,128)S(1)} custom-call(s32[2]{0:T(128)S(1)} %pad_add_fusion.place_ref, bf16[352,256]{1,0:T(8,128)(2,1)S(1)} %collective-permute-done.5.turned_ref, bf16[1024,128]{1,0:T(8,128)(2,1)S(1)} %shard_map.48.lags_ref, f32[256,128]{1,0:T(8,128)S(1)} %shard_map.50.before_ref), custom_call_target="tpu_custom_call" | custom-call | flops 2237661184 | bytes 1048576 | tf_op jit(solution)/shard_map/pallas_call | solution.py:213
  30.8 0.0 collective-permute-done.4.turned_ref
  30.8 3.4 %shard_map.52 = (bf16[128,256]{1,0:T(8,128)(2,1)S(1)}, bf16[128,128]{1,0:T(8,128)(2,1)S(1)}) custom-call(s32[2]{0:T(128)S(1)} %pad_add_fusion.place_ref, bf16[352,256]{1,0:T(8,128)(2,1)S(1)} %collective-permute-done.4.turned_ref, bf16[1024,128]{1,0:T(8,128)(2,1)S(1)} %shard_map.48.lags_ref, f32[256,128]{1,0:T(8,128)S(1)} %shard_map.51.before_ref), custom_call_target="tpu_custom_call" | custom-call | flops 2237661184 | bytes 1048576 | tf_op jit(solution)/shard_map/pallas_call | solution.py:220
  34.3 0.0 copy-start.2
  34.3 1.3 %collective-permute-start.7 = (bf16[128,128]{1,0:T(8,128)(2,1)S(1)}, bf16[128,128]{1,0:T(8,128)(2,1)S(1)}, u32[]{:S(2)}, u32[]{:S(2)}) collective-permute-start(bf16[128,128]{1,0:T(8,128)(2,1)S(1)} %get-tuple-element.8), channel_id=1, source_target_pairs={{1,0},{3,2},{5,4},{7,6},{9,8},{11,10},{13,12},{15,14},{17,16},{19,... | collective-permute-start | bytes 98312 | tf_op jit(solution)/shard_map/ppermute | solution.py:24
  35.6 1.8 %collective-permute-done.7.later_ref = bf16[128,128]{1,0:T(8,128)(2,1)S(1)} collective-permute-done((bf16[128,128]{1,0:T(8,128)(2,1)S(1)}, bf16[128,128]{1,0:T(8,128)(2,1)S(1)}, u32[]{:S(2)}, u32[]{:S(2)}) %collective-permute-start.7) | collective-permute-done | bytes 32800 | tf_op jit(solution)/shard_map/ppermute | solution.py:24
  37.4 0.0 copy-done.2
  37.4 2.1 %shard_map.53 = f32[128,8,256]{2,1,0:T(8,128)} custom-call(s32[8]{0:T(128)S(1)} %copy-done.2, bf16[128,256]{1,0:T(8,128)(2,1)S(1)} %get-tuple-element.7.main_ref, bf16[128,128]{1,0:T(8,128)(2,1)S(1)} %collective-permute-done.7.later_ref), custom_call_target="tpu_custom_call" | custom-call | tf_op jit(solution)/shard_map/pallas_call | solution.py:231
  (1 shorter events, 0.0 us)
Async XLA Ops:
  0.0 4.0 %collective-permute-start = (bf16[1024,256]{1,0:T(8,128)(2,1)}, bf16[1024,256]{1,0:T(8,128)(2,1)S(1)}, u32[]{:S(2)}, u32[]{:S(2)}) collective-permute-start(bf16[1024,256]{1,0:T(8,128)(2,1)} %bitcast.7), channel_id=1, source_target_pairs={{1,0},{3,2},{5,4},{7,6},{9,8},{11,10},{13,12},{15,14},{17,16},{19,... | collective-permute-start | bytes 1572872 | tf_op jit(solution)/shard_map/ppermute | solution.py:24
  1.3 0.7 %copy-start.3 = (s32[1024]{0:T(1024)S(1)}, s32[1024]{0:T(1024)}, u32[]{:S(2)}) copy-start(s32[1024]{0:T(1024)} %param.5) | copy-start | bytes 12292
  4.0 1.0 %copy-start.1 = (bf16[1,1024,256]{2,1,0:T(8,128)(2,1)S(1)}, bf16[1,1024,256]{2,1,0:T(8,128)(2,1)}, u32[]{:S(2)}) copy-start(bf16[1,1024,256]{2,1,0:T(8,128)(2,1)} %param.4) | copy-start | bytes 1572868
  5.0 6.5 %copy-start = (s32[128,1024]{1,0:T(8,128)S(1)}, s32[128,1024]{1,0:T(8,128)}, u32[]{:S(2)}) copy-start(s32[128,1024]{1,0:T(8,128)} %offsets_ref.1) | copy-start | bytes 1572868
  5.7 7.3 %collective-permute-start.3 = (bf16[64,384]{1,0:T(8,128)(2,1)S(1)}, bf16[64,384]{1,0:T(8,128)(2,1)S(1)}, u32[]{:S(2)}, u32[]{:S(2)}) collective-permute-start(bf16[64,384]{1,0:T(8,128)(2,1)S(1)} %shard_map.46.refs_0_), channel_id=1, source_target_pairs={{0,24},{2,26},{4,28},{6,30},{8,16},{10,18},{12,20},{14,22},{16,8},... | collective-permute-start | bytes 147464 | tf_op jit(solution)/shard_map/ppermute | solution.py:29
  10.8 5.0 %collective-permute-start.2 = (bf16[64,384]{1,0:T(8,128)(2,1)S(1)}, bf16[64,384]{1,0:T(8,128)(2,1)S(1)}, u32[]{:S(2)}, u32[]{:S(2)}) collective-permute-start(bf16[64,384]{1,0:T(8,128)(2,1)S(1)} %shard_map.46.refs_0_), channel_id=1, source_target_pairs={{0,16},{2,18},{4,20},{6,22},{8,24},{10,26},{12,28},{14,30},{16,0},... | collective-permute-start | bytes 147464 | tf_op jit(solution)/shard_map/ppermute | solution.py:29
  10.8 5.0 %collective-permute-start.1 = (bf16[64,384]{1,0:T(8,128)(2,1)S(1)}, bf16[64,384]{1,0:T(8,128)(2,1)S(1)}, u32[]{:S(2)}, u32[]{:S(2)}) collective-permute-start(bf16[64,384]{1,0:T(8,128)(2,1)S(1)} %shard_map.46.refs_0_), channel_id=1, source_target_pairs={{0,8},{2,10},{4,12},{6,14},{8,0},{10,2},{12,4},{14,6},{16,24},{18,... | collective-permute-start | bytes 147464 | tf_op jit(solution)/shard_map/ppermute | solution.py:29
  16.5 7.3 %collective-permute-start.6 = (bf16[352,256]{1,0:T(8,128)(2,1)S(1)}, bf16[352,256]{1,0:T(8,128)(2,1)S(1)}, u32[]{:S(2)}, u32[]{:S(2)}) collective-permute-start(bf16[352,256]{1,0:T(8,128)(2,1)S(1)} %shard_map.47.turned_ref), channel_id=1, source_target_pairs={{0,2},{2,0},{4,6},{6,4},{8,10},{10,8},{12,14},{14,12},{16,18},{18,... | collective-permute-start | bytes 540680 | tf_op jit(solution)/shard_map/ppermute | solution.py:29
  18.1 9.4 %collective-permute-start.5 = (bf16[352,256]{1,0:T(8,128)(2,1)S(1)}, bf16[352,256]{1,0:T(8,128)(2,1)S(1)}, u32[]{:S(2)}, u32[]{:S(2)}) collective-permute-start(bf16[352,256]{1,0:T(8,128)(2,1)S(1)} %shard_map.47.turned_ref), channel_id=1, source_target_pairs={{0,4},{2,6},{4,0},{6,2},{8,12},{10,14},{12,8},{14,10},{16,20},{18,... | collective-permute-start | bytes 540680 | tf_op jit(solution)/shard_map/ppermute | solution.py:29
  19.6 11.2 %collective-permute-start.4 = (bf16[352,256]{1,0:T(8,128)(2,1)S(1)}, bf16[352,256]{1,0:T(8,128)(2,1)S(1)}, u32[]{:S(2)}, u32[]{:S(2)}) collective-permute-start(bf16[352,256]{1,0:T(8,128)(2,1)S(1)} %shard_map.47.turned_ref), channel_id=1, source_target_pairs={{0,6},{2,4},{4,2},{6,0},{8,14},{10,12},{12,10},{14,8},{16,22},{18,... | collective-permute-start | bytes 540680 | tf_op jit(solution)/shard_map/ppermute | solution.py:29
  34.3 3.1 %copy-start.2 = (s32[8]{0:T(128)S(1)}, s32[8]{0:T(128)}, u32[]{:S(2)}) copy-start(s32[8]{0:T(128)} %widths_ref.1) | copy-start | bytes 100
  34.3 3.1 %collective-permute-start.7 = (bf16[128,128]{1,0:T(8,128)(2,1)S(1)}, bf16[128,128]{1,0:T(8,128)(2,1)S(1)}, u32[]{:S(2)}, u32[]{:S(2)}) collective-permute-start(bf16[128,128]{1,0:T(8,128)(2,1)S(1)} %get-tuple-element.8), channel_id=1, source_target_pairs={{1,0},{3,2},{5,4},{7,6},{9,8},{11,10},{13,12},{15,14},{17,16},{19,... | collective-permute-start | bytes 98312 | tf_op jit(solution)/shard_map/ppermute | solution.py:24

commit v4 on v0

v4 whole, which is shorter than its diff:
```python
import functools
import math

import jax
import jax.numpy as jnp
from jax import lax
from jax.experimental import pallas as pl
from jax.experimental.pallas import tpu as pltpu
from jax.sharding import PartitionSpec as P

WMAX = 128
DCH = 16
OMAX = 96
LANES = 128
STEP = 16
GROUPS = OMAX // STEP
REACH = OMAX + DCH
VMEM = pl.BlockSpec(memory_space=pltpu.VMEM)
SMEM = pl.BlockSpec(memory_space=pltpu.SMEM)
HBM = pl.BlockSpec(memory_space=pltpu.HBM)
ANY = pl.BlockSpec(memory_space=pl.ANY)


def passed_back(value, axis):
    count = lax.axis_size(axis)
    return lax.ppermute(value, axis, [(source, source - 1) for source in range(1, count)])


def exchanged(value, axis, flip):
    count = lax.axis_size(axis)
    return lax.ppermute(value, axis, [(source, source ^ flip) for source in range(count)])


def series_kernel(per_sub, packed, delays_ref, data_ref, series_ref, held, sems):
    chans, length = data_ref.shape
    block = min(chans, 256)
    subs = block // per_sub
    wide = length + LANES
    copies = []
    for at in range(chans // block):
        here = pl.ds(at * block, block)
        copies.append(pltpu.make_async_copy(data_ref.at[here, :], held.at[here, :], sems.at[at]))
        copies[-1].start()
    rows = lax.broadcasted_iota(jnp.int32, (DCH * subs, block), 0)
    owner = lax.broadcasted_iota(jnp.int32, (1, block), 1) // per_sub
    blank = jnp.zeros((subs, LANES), jnp.float32)
    parts = []
    for at in range(chans // block):
        here = pl.ds(at * block, block)
        member = jnp.where(rows == delays_ref[:, here] * subs + owner, 1.0, 0.0).astype(jnp.bfloat16)
        copies[at].wait()
        picked = jnp.dot(member, held[here, :], preferred_element_type=jnp.float32)
        total = None
        for delay in range(DCH):
            late = jnp.concatenate([picked[delay * subs : (delay + 1) * subs, :], blank], axis=1)
            late = pltpu.roll(late, DCH - delay, 1)
            total = late if total is None else total + late
        parts.append(total)
    total = jnp.concatenate(parts, axis=0)
    if packed:
        half = series_ref.shape[0]
        both = jnp.concatenate([total, pltpu.roll(total, wide - half, 1)], axis=0)
        for first in range(0, half, LANES):
            count = min(LANES, half - first)
            tile = both[:, first : first + LANES].T
            series_ref[pl.ds(first, count), :] = tile[:count].astype(jnp.bfloat16)
    else:
        series_ref[...] = total.astype(jnp.bfloat16)


def join_packed_kernel(outer, *refs):
    blocks, joined_ref = refs[:outer], refs[-1]
    half = blocks[0].shape[0]
    rest = joined_ref.shape[0] - half
    lane = lax.broadcasted_iota(jnp.int32, (half, LANES), 1)
    for at in range(outer // 2):
        left = blocks[2 * at][...].astype(jnp.float32)
        right = blocks[2 * at + 1][...].astype(jnp.float32)
        lanes = pl.ds(at * LANES, LANES)
        early = jnp.where(lane < LANES // 2, left, pltpu.roll(right, LANES // 2, 1))
        late = jnp.where(lane < LANES // 2, pltpu.roll(left, LANES // 2, 1), right)
        joined_ref[pl.ds(0, half), lanes] = early.astype(jnp.bfloat16)
        joined_ref[pl.ds(half, rest), lanes] = late[:rest].astype(jnp.bfloat16)


def join_kernel(outer, *refs):
    blocks, joined_ref = refs[:outer], refs[-1]
    subs = blocks[0].shape[0]
    rows = joined_ref.shape[0]
    several = LANES // subs
    for at in range(outer // several):
        for first in range(0, rows, LANES):
            count = min(LANES, rows - first)
            tile = jnp.concatenate(
                [
                    blocks[at * several + slot][:, pl.ds(first, LANES)].astype(jnp.float32)
                    for slot in range(several)
                ],
                axis=0,
            ).T
            joined_ref[pl.ds(first, count), pl.ds(at * LANES, LANES)] = tile[:count].astype(jnp.bfloat16)


def offsets_kernel(offsets_ref, group_ref, lag_ref, held, sems):
    copies = []
    for at in range(offsets_ref.shape[1] // LANES):
        here = pl.ds(at * LANES, LANES)
        copies.append(pltpu.make_async_copy(offsets_ref.at[:, here], held.at[at], sems.at[at]))
        copies[-1].start()
    for at, copy in enumerate(copies):
        here = pl.ds(at * LANES, LANES)
        copy.wait()
        offset = held[at].astype(jnp.float32).T
        group = jnp.zeros_like(offset)
        for edge in range(1, GROUPS):
            group = group + jnp.where(offset >= float(STEP * edge), 1.0, 0.0)
        group_ref[here, :] = group.astype(jnp.bfloat16)
        lag_ref[here, :] = (offset - float(STEP) * group).astype(jnp.bfloat16)


def one_where(table, value):
    one = jnp.bfloat16(1)
    return jnp.maximum(one - jnp.abs(table - jnp.bfloat16(value)), jnp.bfloat16(0))


def choices_kernel(outer, inner, flip, me_ref, group_ref, lag_ref, chosen_ref):
    trials = lag_ref.shape[1]
    subs = lag_ref.shape[0] // (outer * inner)
    nsub = outer * subs
    row = me_ref[0] // inner
    column = (me_ref[0] % inner) ^ flip
    for slot in range(outer):
        start = pl.multiple_of(((row ^ slot) * inner + column) * subs, subs)
        groups = group_ref[pl.ds(start, subs), :]
        lags = lag_ref[pl.ds(start, subs), :]
        in_group = [one_where(groups, group) for group in range(GROUPS)]
        for lag in range(STEP + 1):
            at_lag = one_where(lags, lag)
            for group in range(GROUPS - 2 if lag == STEP else 0, GROUPS):
                place = (group // 2 * STEP + lag) * nsub + slot * subs
                chosen_ref[pl.ds(place, subs), pl.ds(group % 2 * trials, trials)] = at_lag * in_group[group]


def sums_kernel(given, joined_ref, chosen_ref, *refs):
    before_ref, sums_ref, *early_ref = refs[:-2] if given else (None, *refs[:-2])
    moving, shifted = refs[-2:]
    span, nsub = joined_ref.shape
    trials = chosen_ref.shape[1] // 2
    rows = span + STEP
    blank = jnp.zeros((STEP, nsub), jnp.float32)
    moving[pl.ds(0, STEP), :] = blank
    moving[pl.ds(STEP, span), :] = joined_ref[...].astype(jnp.float32)
    moving[pl.ds(STEP + span, STEP), :] = blank
    for lag in range(STEP + 1):
        shifted[:, pl.ds(lag * nsub, nsub)] = moving[pl.ds(lag, rows), :].astype(jnp.bfloat16)
    if before_ref is None:
        sums_ref[...] = jnp.zeros_like(sums_ref)
    else:
        sums_ref[...] = before_ref[...]
    for pair in range(GROUPS // 2):
        depth = (STEP + (pair == GROUPS // 2 - 1)) * nsub
        both = jnp.dot(
            shifted[:, pl.ds(0, depth)],
            chosen_ref[pl.ds(pair * STEP * nsub, depth), :],
            preferred_element_type=jnp.float32,
        )
        for odd in range(2):
            first = STEP * (GROUPS - 1 - 2 * pair - odd)
            sums_ref[pl.ds(first, rows), :] += both[:, odd * trials : (odd + 1) * trials]
    for ref in early_ref:
        ref[...] = sums_ref[pl.ds(0, ref.shape[0]), :]


def bands_kernel(widths_ref, bands_ref):
    shape = (bands_ref.shape[0], LANES)
    lag = lax.broadcasted_iota(jnp.int32, shape, 0) - lax.broadcasted_iota(jnp.int32, shape, 1)
    for at in range(widths_ref.shape[0]):
        band = jnp.where((lag >= 0) & (lag < widths_ref[at]), 1.0, 0.0)
        bands_ref[:, pl.ds(at * LANES, LANES)] = band.astype(jnp.bfloat16)


def boxcars_kernel(scale, widths_ref, bands_ref, sums_ref, later_ref, out_ref, values, mixed, tiles, sems):
    trials = sums_ref.shape[1]
    length = sums_ref.shape[0] - REACH
    filters = widths_ref.shape[0]
    whole = length - REACH
    total = jnp.concatenate(
        [
            sums_ref[pl.ds(REACH, whole), :],
            sums_ref[pl.ds(length, REACH), :] + later_ref[pl.ds(0, REACH), :],
            later_ref[pl.ds(REACH, WMAX), :],
        ],
        axis=0,
    )
    for first in range(0, length + WMAX, LANES):
        tile = (total[first : first + LANES] * scale).T
        values[:, pl.ds(first, LANES)] = tile.astype(jnp.bfloat16)
    share = trials // sems.shape[1]
    copies = []
    for part in range(length // LANES):
        lanes = pl.ds(part * LANES, LANES)
        for at in range(filters):
            sums = jnp.dot(
                values[:, pl.ds(part * LANES, LANES + WMAX)],
                bands_ref[:, pl.ds(at * LANES, LANES)],
                preferred_element_type=jnp.float32,
            )
            root = jnp.sqrt(jnp.full((1, LANES), widths_ref[at], jnp.int32).astype(jnp.float32))
            mixed[part, pl.ds(at, trials, stride=filters), :] = sums / root
        tiles[part] = mixed[part].reshape(trials, filters, LANES)
        for piece in range(sems.shape[1]):
            some = pl.ds(piece * share, share)
            copies.append(
                pltpu.make_async_copy(
                    tiles.at[part, some], out_ref.at[some, :, lanes], sems.at[part, piece]
                )
            )
            copies[-1].start()
    for copy in copies:
        copy.wait()


def call(kernel, out_shape, in_specs, args, scratch=(), flops=0, **options):
    several = isinstance(out_shape, list)
    options.setdefault("out_specs", [VMEM] * len(out_shape) if several else VMEM)
    return pl.pallas_call(
        kernel,
        out_shape=out_shape,
        in_specs=in_specs,
        scratch_shapes=list(scratch),
        compiler_params=pltpu.CompilerParams(vmem_limit_bytes=12 << 20),
        cost_estimate=pl.CostEstimate(flops=flops, bytes_accessed=1 << 20, transcendentals=0),
        **options,
    )(*args)


def one_beam(own, delays, choices, bands, widths, groups, outer, per_sub, scale):
    chans, length = own.shape
    sub_dev = chans // per_sub
    inner = groups // outer
    padded = choices[0].shape[1] // 2
    filters = widths.shape[0]
    span = length + DCH
    packed = 2 * sub_dev == LANES
    series_shape = (-(-span // 32) * 16, LANES) if packed else (sub_dev, length + LANES)
    steps = max(1, chans // 256)
    series = call(
        functools.partial(series_kernel, per_sub, packed),
        jax.ShapeDtypeStruct(series_shape, jnp.bfloat16),
        [VMEM, HBM],
        (delays[None, :], pltpu.with_memory_space_constraint(own, pltpu.HBM)),
        [pltpu.VMEM((chans, length), jnp.bfloat16), pltpu.SemaphoreType.DMA((steps,))],
    )
    line = [series] + [exchanged(series, "sub", flip * inner) for flip in range(1, outer)]
    nsub = outer * sub_dev
    tables = (*choices, bands)
    joined = call(
        functools.partial(join_packed_kernel if packed else join_kernel, outer),
        jax.ShapeDtypeStruct((span, nsub), jnp.bfloat16),
        [VMEM] * outer + [ANY] * len(tables),
        (*line, *tables),
    )
    blocks = [joined] + [exchanged(joined, "sub", flip) for flip in range(1, inner)]
    scratch = [
        pltpu.VMEM((span + 2 * STEP, nsub), jnp.float32),
        pltpu.VMEM((span + STEP, (STEP + 1) * nsub), jnp.bfloat16),
    ]
    flops = 2 * (span + STEP) * nsub * padded * (OMAX + 2)
    sums_shape = jax.ShapeDtypeStruct((length + REACH, padded), jnp.float32)
    early_shape = jax.ShapeDtypeStruct((REACH + WMAX, padded), jnp.float32)
    sums = []
    for flip in range(inner):
        sums = call(
            functools.partial(sums_kernel, flip > 0),
            [sums_shape, early_shape] if flip == inner - 1 else [sums_shape],
            [VMEM] * (2 + len(sums)),
            (blocks[flip], choices[flip], *sums),
            scratch,
            flops,
        )
    sums, early = sums
    later = passed_back(early, "tm")
    parts = length // LANES
    pieces = 4
    return call(
        functools.partial(boxcars_kernel, scale),
        jax.ShapeDtypeStruct((padded, filters, length), jnp.float32),
        [SMEM, VMEM, VMEM, VMEM],
        (widths, bands, sums, later),
        [
            pltpu.VMEM((padded, length + WMAX), jnp.bfloat16),
            pltpu.VMEM((parts, padded * filters, LANES), jnp.float32),
            pltpu.VMEM((parts, padded, filters, LANES), jnp.float32),
            pltpu.SemaphoreType.DMA((parts, pieces)),
        ],
        out_specs=HBM,
    )


def per_device(data, delays, offsets, widths):
    beams, chans, length = data.shape
    trials, nsub = offsets.shape
    groups = lax.axis_size("sub")
    outer = 1 << (groups.bit_length() // 2)
    outer = outer if groups % (outer * outer) == 0 else outer // 2
    inner = groups // outer
    per_sub = chans // (nsub // groups)
    scale = 1.0 / math.sqrt(chans * groups)
    padded = max(trials, LANES)
    offset_table = jnp.pad(offsets, ((0, padded - trials), (0, 0))) if padded > trials else offsets
    me = lax.axis_index("sub").astype(jnp.int32).reshape(1)
    split_shape = jax.ShapeDtypeStruct((nsub, padded), jnp.bfloat16)
    columns = nsub // LANES
    split = call(
        offsets_kernel,
        [split_shape, split_shape],
        [HBM],
        (pltpu.with_memory_space_constraint(offset_table, pltpu.HBM),),
        [pltpu.VMEM((columns, padded, LANES), jnp.int32), pltpu.SemaphoreType.DMA((columns,))],
    )
    rows = (GROUPS // 2 * STEP + 1) * (nsub // inner)
    choices = [
        call(
            functools.partial(choices_kernel, outer, inner, flip),
            jax.ShapeDtypeStruct((rows, 2 * padded), jnp.bfloat16),
            [SMEM, VMEM, VMEM],
            (me, *split),
        )
        for flip in range(inner)
    ]
    bands = call(
        bands_kernel,
        jax.ShapeDtypeStruct((LANES + WMAX, widths.shape[0] * LANES), jnp.bfloat16),
        [SMEM],
        (widths,),
    )
    outs = [
        one_beam(data[beam], delays, choices, bands, widths, groups, outer, per_sub, scale)[:trials, None]
        for beam in range(beams)
    ]
    return outs[0] if beams == 1 else jnp.concatenate(outs, axis=1)


def solution(mesh):
    placed = (P(None, "sub", "tm"), P("sub"), P("sub", None), P())
    return jax.shard_map(
        per_device,
        mesh=mesh,
        in_specs=placed,
        out_specs=P("sub", None, None, "tm"),
        check_vma=False,
    )
```

time: 174 us -> 35.6 us (0.20)
  waiting for transfers between devices: 84.1 us -> 3.85 us
  matrix products: 29.1 us -> 0 us
  local copies, waits for them, and re-layouts: 29.3 us -> 0.69 us
  Pallas kernels: 0 us -> 20.1 us
  between operations: 13.7 us -> 0.16 us
  loops' own time: 5.17 us -> 0 us
    reduce_scatter x1 -> x0, waiting for transfers between devices: 82.3 us -> none  [per_device(): lax.psum_scatter(blocks.reshape(lax.axis_size('sub') * dm_dev, beams, out...]
    dot_general x25 -> x0, matrix products: 29.1 us -> none  [the longest x8 21.3 us: project(): jnp.einsum('msk,bskt->mbt', onehot, hankel, preferred_element_type=jnp.fl...]
    pallas_call x0 -> x13, Pallas kernels: none -> 20.1 us  [call(): pl.pallas_call(kernel, out_shape=out_shape, in_specs=in_specs, scratch_sh...]
    dynamic_slice x16 -> x0, local copies, waits for them, and re-layouts: 12 us -> none  [the longest x8 6.8 us: one_block(): lag_rows = lax.dynamic_slice_in_dim(table, block_index * block, block, 0)]
    unnamed x102 -> x4, local copies, waits for them, and re-layouts: 10.9 us -> 0.69 us
    all_to_all x1 -> x0, starting transfers between devices: 8.36 us -> none  [per_device(): lax.all_to_all(offsets, 'sub', split_axis=1, concat_axis=0, tiled=True)]
    ppermute x2 -> x7, starting transfers between devices: 2.58 us -> 10.5 us  [the longest x6 9.24 us: exchanged(): lax.ppermute(value, axis, [(source, source ^ flip) for source in range(co...]
    another operation x1 -> x0, loops' own time: 5.17 us -> none  [per_device(): lax.map(one_block, jnp.arange(lax.axis_size('sub') * dm_dev // block, dty...]
  transfers between devices with their start and end apart: 4 -> 7, of which waited for: 2 -> 3; matrix products, arithmetic and copies ran while one was open for 11% -> 0% of each run, Pallas kernels for 0% -> 38%
where the time goes in v4:
time: 35.6 us; the launch traced here: 35.4 us
  Pallas kernels  20.1 us (56%)
  starting transfers between devices  10.5 us (29%)
  waiting for transfers between devices  3.85 us (11%)
  local copies, waits for them, and re-layouts  0.69 us (2%)
    pallas_call x13, Pallas kernels, call(): pl.pallas_call(kernel, out_shape=out_shape, in_specs=in_specs, scratch_sh...  20.1 us
    ppermute x6, starting transfers between devices, exchanged(): lax.ppermute(value, axis, [(source, source ^ flip) for source in range(co...  9.24 us
    ppermute x1, waiting for transfers between devices, passed_back(): lax.ppermute(value, axis, [(source, source - 1) for source in range(1, co...  1.93 us
    ppermute x6, waiting for transfers between devices, exchanged(): lax.ppermute(value, axis, [(source, source ^ flip) for source in range(co...  1.92 us
    ppermute x1, starting transfers between devices, passed_back(): lax.ppermute(value, axis, [(source, source - 1) for source in range(1, co...  1.29 us
  transfers between devices with their start and end apart: 7, of which 3 were waited for; matrix products, arithmetic and copies ran while one was open for 0% of the time, Pallas kernels for 38%

profile of v4, /device:TPU:0, one launch (start us, length us, event | category | flops | bytes accessed | tf_op | source)
XLA Modules:
  0.0 35.4 jit_solution(12219363781140787261)
XLA Ops:
  0.0 0.0 copy-start
  0.0 0.7 %copy-done = s32[1024]{0:T(1024)S(1)} copy-done((s32[1024]{0:T(1024)S(1)}, s32[1024]{0:T(1024)}, u32[]{:S(2)}) %copy-start) | copy-done | bytes 4120
  0.7 2.3 %shard_map.47.refs_0_ = bf16[144,128]{1,0:T(8,128)(2,1)S(1)} custom-call(s32[1,1024]{1,0:T(1,128)S(1)} %bitcast.6, bf16[1024,256]{1,0:T(8,128)(2,1)} %bitcast.7), custom_call_target="tpu_custom_call" | custom-call | bytes 1048576 | tf_op jit(solution)/shard_map/pallas_call | solution.py:226
  3.0 3.1 %collective-permute-start = (bf16[144,128]{1,0:T(8,128)(2,1)S(1)}, bf16[144,128]{1,0:T(8,128)(2,1)S(1)}, u32[]{:S(2)}, u32[]{:S(2)}) collective-permute-start(bf16[144,128]{1,0:T(8,128)(2,1)S(1)} %shard_map.47.refs_0_), channel_id=1, source_target_pairs={{0,8},{2,10},{4,12},{6,14},{8,0},{10,2},{12,4},{14,6},{16,24},{18,... | collective-permute-start | bytes 110600 | tf_op jit(solution)/shard_map/ppermute | solution.py:31
  6.1 2.6 %collective-permute-start.1 = (bf16[144,128]{1,0:T(8,128)(2,1)S(1)}, bf16[144,128]{1,0:T(8,128)(2,1)S(1)}, u32[]{:S(2)}, u32[]{:S(2)}) collective-permute-start(bf16[144,128]{1,0:T(8,128)(2,1)S(1)} %shard_map.47.refs_0_), channel_id=1, source_target_pairs={{0,16},{2,18},{4,20},{6,22},{8,24},{10,26},{12,28},{14,30},{16,0},... | collective-permute-start | bytes 110600 | tf_op jit(solution)/shard_map/ppermute | solution.py:31
  8.7 0.0 collective-permute-start.2
  8.7 1.8 %shard_map.48 = (bf16[1024,128]{1,0:T(8,128)(2,1)S(1)}, bf16[1024,128]{1,0:T(8,128)(2,1)S(1)}) custom-call(s32[128,1024]{1,0:T(8,128)} %offsets_ref.1), custom_call_target="tpu_custom_call" | custom-call | bytes 1048576 | tf_op jit(solution)/shard_map/pallas_call | solution.py:226
  10.5 1.2 %shard_map.49.refs_4_.chosen_ref = bf16[12544,256]{1,0:T(8,128)(2,1)S(1)} custom-call(s32[1]{0:T(128)} %bitcast.2.me_ref, bf16[1024,128]{1,0:T(8,128)(2,1)S(1)} %get-tuple-element.9.group_ref, bf16[1024,128]{1,0:T(8,128)(2,1)S(1)} %get-tuple-element.10.lag_ref), custom_call_target="tpu_custom_call" | custom-call | bytes 1048576 | tf_op jit(solution)/shard_map/pallas_call | solution.py:226
  11.7 1.2 %shard_map.50.refs_5_.chosen_ref = bf16[12544,256]{1,0:T(8,128)(2,1)S(1)} custom-call(s32[1]{0:T(128)} %bitcast.2.me_ref, bf16[1024,128]{1,0:T(8,128)(2,1)S(1)} %get-tuple-element.9.group_ref, bf16[1024,128]{1,0:T(8,128)(2,1)S(1)} %get-tuple-element.10.lag_ref), custom_call_target="tpu_custom_call" | custom-call | bytes 1048576 | tf_op jit(solution)/shard_map/pallas_call | solution.py:226
  12.9 0.0 copy-start.1
  12.9 1.2 %shard_map.51.refs_6_.chosen_ref = bf16[12544,256]{1,0:T(8,128)(2,1)S(1)} custom-call(s32[1]{0:T(128)} %bitcast.2.me_ref, bf16[1024,128]{1,0:T(8,128)(2,1)S(1)} %get-tuple-element.9.group_ref, bf16[1024,128]{1,0:T(8,128)(2,1)S(1)} %get-tuple-element.10.lag_ref), custom_call_target="tpu_custom_call" | custom-call | bytes 1048576 | tf_op jit(solution)/shard_map/pallas_call | solution.py:226
  14.1 1.2 %shard_map.52.refs_7_.chosen_ref = bf16[12544,256]{1,0:T(8,128)(2,1)S(1)} custom-call(s32[1]{0:T(128)} %bitcast.2.me_ref, bf16[1024,128]{1,0:T(8,128)(2,1)S(1)} %get-tuple-element.9.group_ref, bf16[1024,128]{1,0:T(8,128)(2,1)S(1)} %get-tuple-element.10.lag_ref), custom_call_target="tpu_custom_call" | custom-call | bytes 1048576 | tf_op jit(solution)/shard_map/pallas_call | solution.py:226
  15.3 0.0 copy-done.1
  15.3 0.7 %shard_map.46.refs_8_.bands_ref = bf16[256,1024]{1,0:T(8,128)(2,1)S(1)} custom-call(s32[8]{0:T(128)S(1)} %copy-done.1), custom_call_target="tpu_custom_call" | custom-call | bytes 1048576 | tf_op jit(solution)/shard_map/pallas_call | solution.py:226
  16.0 0.0 collective-permute-done.refs_1_
  16.0 0.0 collective-permute-done.1.refs_2_
  16.0 0.0 collective-permute-done.2.refs_3_
  16.0 0.1 shard_map.53.joined_ref
  16.1 1.8 %collective-permute-start.5 = (bf16[272,256]{1,0:T(8,128)(2,1)S(1)}, bf16[272,256]{1,0:T(8,128)(2,1)S(1)}, u32[]{:S(2)}, u32[]{:S(2)}) collective-permute-start(bf16[272,256]{1,0:T(8,128)(2,1)S(1)} %shard_map.53.joined_ref), channel_id=1, source_target_pairs={{0,2},{2,0},{4,6},{6,4},{8,10},{10,8},{12,14},{14,12},{16,18},{18,... | collective-permute-start | bytes 417800 | tf_op jit(solution)/shard_map/ppermute | solution.py:31
  17.9 1.5 %collective-permute-start.4 = (bf16[272,256]{1,0:T(8,128)(2,1)S(1)}, bf16[272,256]{1,0:T(8,128)(2,1)S(1)}, u32[]{:S(2)}, u32[]{:S(2)}) collective-permute-start(bf16[272,256]{1,0:T(8,128)(2,1)S(1)} %shard_map.53.joined_ref), channel_id=1, source_target_pairs={{0,4},{2,6},{4,0},{6,2},{8,12},{10,14},{12,8},{14,10},{16,20},{18,... | collective-permute-start | bytes 417800 | tf_op jit(solution)/shard_map/ppermute | solution.py:31
  19.4 0.3 collective-permute-start.3
  19.7 2.2 %shard_map.54.refs_0_ = f32[368,128]{1,0:T(8,128)S(1)} custom-call(bf16[272,256]{1,0:T(8,128)(2,1)S(1)} %shard_map.53.joined_ref, bf16[12544,256]{1,0:T(8,128)(2,1)S(1)} %shard_map.49.refs_4_.chosen_ref), custom_call_target="tpu_custom_call" | custom-call | flops 1849688064 | bytes 1048576 | tf_op jit(solution)/shard_map/pallas_call | solution.py:226
  21.8 0.2 collective-permute-done.5.joined_ref
  22.1 2.1 %shard_map.55.refs_0_ = f32[368,128]{1,0:T(8,128)S(1)} custom-call(bf16[272,256]{1,0:T(8,128)(2,1)S(1)} %collective-permute-done.5.joined_ref, bf16[12544,256]{1,0:T(8,128)(2,1)S(1)} %shard_map.50.refs_5_.chosen_ref, f32[368,128]{1,0:T(8,128)S(1)} %shard_map.54.refs_0_), custom_call_target="tpu_custom_call" | custom-call | flops 1849688064 | bytes 1048576 | tf_op jit(solution)/shard_map/pallas_call | solution.py:226
  24.2 1.7 %collective-permute-done.4.joined_ref = bf16[272,256]{1,0:T(8,128)(2,1)S(1)} collective-permute-done((bf16[272,256]{1,0:T(8,128)(2,1)S(1)}, bf16[272,256]{1,0:T(8,128)(2,1)S(1)}, u32[]{:S(2)}, u32[]{:S(2)}) %collective-permute-start.4) | collective-permute-done | bytes 139296 | tf_op jit(solution)/shard_map/ppermute | solution.py:31
  25.9 2.1 %shard_map.56.refs_0_ = f32[368,128]{1,0:T(8,128)S(1)} custom-call(bf16[272,256]{1,0:T(8,128)(2,1)S(1)} %collective-permute-done.4.joined_ref, bf16[12544,256]{1,0:T(8,128)(2,1)S(1)} %shard_map.51.refs_6_.chosen_ref, f32[368,128]{1,0:T(8,128)S(1)} %shard_map.55.refs_0_), custom_call_target="tpu_custom_call" | custom-call | flops 1849688064 | bytes 1048576 | tf_op jit(solution)/shard_map/pallas_call | solution.py:226
  28.0 0.0 collective-permute-done.3.joined_ref
  28.0 2.1 %shard_map.57 = (f32[368,128]{1,0:T(8,128)S(1)}, f32[240,128]{1,0:T(8,128)S(1)}) custom-call(bf16[272,256]{1,0:T(8,128)(2,1)S(1)} %collective-permute-done.3.joined_ref, bf16[12544,256]{1,0:T(8,128)(2,1)S(1)} %shard_map.52.refs_7_.chosen_ref, f32[368,128]{1,0:T(8,128)S(1)} %shard_map.56.refs_0_), custom_call_target="tpu_custom_call" | custom-call | flops 1849688064 | bytes 1048576 | tf_op jit(solution)/shard_map/pallas_call | solution.py:226
  30.1 1.3 %collective-permute-start.6 = (f32[240,128]{1,0:T(8,128)S(1)}, f32[240,128]{1,0:T(8,128)S(1)}, u32[]{:S(2)}, u32[]{:S(2)}) collective-permute-start(f32[240,128]{1,0:T(8,128)S(1)} %get-tuple-element.12), channel_id=1, source_target_pairs={{1,0},{3,2},{5,4},{7,6},{9,8},{11,10},{13,12},{15,14},{17,16},{19,... | collective-permute-start | bytes 368648 | tf_op jit(solution)/shard_map/ppermute | solution.py:26
  31.4 1.9 %collective-permute-done.6.later_ref = f32[240,128]{1,0:T(8,128)S(1)} collective-permute-done((f32[240,128]{1,0:T(8,128)S(1)}, f32[240,128]{1,0:T(8,128)S(1)}, u32[]{:S(2)}, u32[]{:S(2)}) %collective-permute-start.6) | collective-permute-done | bytes 122912 | tf_op jit(solution)/shard_map/ppermute | solution.py:26
  33.4 2.0 %shard_map.58 = f32[128,8,256]{2,1,0:T(8,128)} custom-call(s32[8]{0:T(128)S(1)} %copy-done.1, bf16[256,1024]{1,0:T(8,128)(2,1)S(1)} %shard_map.46.refs_8_.bands_ref, f32[368,128]{1,0:T(8,128)S(1)} %get-tuple-element.11.sums_ref, f32[240,128]{1,0:T(8,128)S(1)} %collective-permute-done.6.later_ref), custom_call_target="tpu_custom_call" | custom-call | bytes 1048576 | tf_op jit(solution)/shard_map/pallas_call | solution.py:226
Async XLA Ops:
  0.0 0.7 %copy-start = (s32[1024]{0:T(1024)S(1)}, s32[1024]{0:T(1024)}, u32[]{:S(2)}) copy-start(s32[1024]{0:T(1024)} %param.5) | copy-start | bytes 12292
  3.0 13.0 %collective-permute-start = (bf16[144,128]{1,0:T(8,128)(2,1)S(1)}, bf16[144,128]{1,0:T(8,128)(2,1)S(1)}, u32[]{:S(2)}, u32[]{:S(2)}) collective-permute-start(bf16[144,128]{1,0:T(8,128)(2,1)S(1)} %shard_map.47.refs_0_), channel_id=1, source_target_pairs={{0,8},{2,10},{4,12},{6,14},{8,0},{10,2},{12,4},{14,6},{16,24},{18,... | collective-permute-start | bytes 110600 | tf_op jit(solution)/shard_map/ppermute | solution.py:31
  6.1 9.9 %collective-permute-start.1 = (bf16[144,128]{1,0:T(8,128)(2,1)S(1)}, bf16[144,128]{1,0:T(8,128)(2,1)S(1)}, u32[]{:S(2)}, u32[]{:S(2)}) collective-permute-start(bf16[144,128]{1,0:T(8,128)(2,1)S(1)} %shard_map.47.refs_0_), channel_id=1, source_target_pairs={{0,16},{2,18},{4,20},{6,22},{8,24},{10,26},{12,28},{14,30},{16,0},... | collective-permute-start | bytes 110600 | tf_op jit(solution)/shard_map/ppermute | solution.py:31
  8.7 7.3 %collective-permute-start.2 = (bf16[144,128]{1,0:T(8,128)(2,1)S(1)}, bf16[144,128]{1,0:T(8,128)(2,1)S(1)}, u32[]{:S(2)}, u32[]{:S(2)}) collective-permute-start(bf16[144,128]{1,0:T(8,128)(2,1)S(1)} %shard_map.47.refs_0_), channel_id=1, source_target_pairs={{0,24},{2,26},{4,28},{6,30},{8,16},{10,18},{12,20},{14,22},{16,8},... | collective-permute-start | bytes 110600 | tf_op jit(solution)/shard_map/ppermute | solution.py:31
  12.9 2.4 %copy-start.1 = (s32[8]{0:T(128)S(1)}, s32[8]{0:T(128)}, u32[]{:S(2)}) copy-start(s32[8]{0:T(128)} %widths_ref.3) | copy-start | bytes 100
  16.1 6.0 %collective-permute-start.5 = (bf16[272,256]{1,0:T(8,128)(2,1)S(1)}, bf16[272,256]{1,0:T(8,128)(2,1)S(1)}, u32[]{:S(2)}, u32[]{:S(2)}) collective-permute-start(bf16[272,256]{1,0:T(8,128)(2,1)S(1)} %shard_map.53.joined_ref), channel_id=1, source_target_pairs={{0,2},{2,0},{4,6},{6,4},{8,10},{10,8},{12,14},{14,12},{16,18},{18,... | collective-permute-start | bytes 417800 | tf_op jit(solution)/shard_map/ppermute | solution.py:31
  17.9 8.0 %collective-permute-start.4 = (bf16[272,256]{1,0:T(8,128)(2,1)S(1)}, bf16[272,256]{1,0:T(8,128)(2,1)S(1)}, u32[]{:S(2)}, u32[]{:S(2)}) collective-permute-start(bf16[272,256]{1,0:T(8,128)(2,1)S(1)} %shard_map.53.joined_ref), channel_id=1, source_target_pairs={{0,4},{2,6},{4,0},{6,2},{8,12},{10,14},{12,8},{14,10},{16,20},{18,... | collective-permute-start | bytes 417800 | tf_op jit(solution)/shard_map/ppermute | solution.py:31
  19.4 8.6 %collective-permute-start.3 = (bf16[272,256]{1,0:T(8,128)(2,1)S(1)}, bf16[272,256]{1,0:T(8,128)(2,1)S(1)}, u32[]{:S(2)}, u32[]{:S(2)}) collective-permute-start(bf16[272,256]{1,0:T(8,128)(2,1)S(1)} %shard_map.53.joined_ref), channel_id=1, source_target_pairs={{0,6},{2,4},{4,2},{6,0},{8,14},{10,12},{12,10},{14,8},{16,22},{18,... | collective-permute-start | bytes 417800 | tf_op jit(solution)/shard_map/ppermute | solution.py:31
  30.1 3.2 %collective-permute-start.6 = (f32[240,128]{1,0:T(8,128)S(1)}, f32[240,128]{1,0:T(8,128)S(1)}, u32[]{:S(2)}, u32[]{:S(2)}) collective-permute-start(f32[240,128]{1,0:T(8,128)S(1)} %get-tuple-element.12), channel_id=1, source_target_pairs={{1,0},{3,2},{5,4},{7,6},{9,8},{11,10},{13,12},{15,14},{17,16},{19,... | collective-permute-start | bytes 368648 | tf_op jit(solution)/shard_map/ppermute | solution.py:26

commit v5 on v4

--- a/solution.py
+++ b/solution.py
@@ -31,25 +31,38 @@
     return lax.ppermute(value, axis, [(source, source ^ flip) for source in range(count)])
 
 
-def series_kernel(per_sub, packed, delays_ref, data_ref, series_ref, held, sems):
+def series_kernel(
+    per_sub, packed, delays_ref, data_ref, offsets_ref, series_ref, fetched_ref, delays, held, delays_sem, sems
+):
     chans, length = data_ref.shape
     block = min(chans, 256)
     subs = block // per_sub
     wide = length + LANES
+    first_copy = pltpu.make_async_copy(delays_ref, delays, delays_sem)
+    first_copy.start()
     copies = []
-    for at in range(chans // block):
-        here = pl.ds(at * block, block)
-        copies.append(pltpu.make_async_copy(data_ref.at[here, :], held.at[here, :], sems.at[at]))
-        copies[-1].start()
+    steps = sems.shape[0] // 2
+    for source, target, base in ((data_ref, held, 0), (offsets_ref, fetched_ref, steps)):
+        share = source.shape[0] // steps
+        for at in range(steps):
+            here = pl.ds(at * share, share)
+            copies.append(
+                pltpu.make_async_copy(source.at[here, :], target.at[here, :], sems.at[base + at])
+            )
+            copies[-1].start()
     rows = lax.broadcasted_iota(jnp.int32, (DCH * subs, block), 0)
     owner = lax.broadcasted_iota(jnp.int32, (1, block), 1) // per_sub
     blank = jnp.zeros((subs, LANES), jnp.float32)
+    first_copy.wait()
+    members = [
+        jnp.where(rows == delays[:, at * block : (at + 1) * block] * subs + owner, 1.0, 0.0).astype(jnp.bfloat16)
+        for at in range(chans // block)
+    ]
+    for copy in copies[:steps]:
+        copy.wait()
     parts = []
-    for at in range(chans // block):
-        here = pl.ds(at * block, block)
-        member = jnp.where(rows == delays_ref[:, here] * subs + owner, 1.0, 0.0).astype(jnp.bfloat16)
-        copies[at].wait()
-        picked = jnp.dot(member, held[here, :], preferred_element_type=jnp.float32)
+    for at, member in enumerate(members):
+        picked = jnp.dot(member, held[pl.ds(at * block, block), :], preferred_element_type=jnp.float32)
         total = None
         for delay in range(DCH):
             late = jnp.concatenate([picked[delay * subs : (delay + 1) * subs, :], blank], axis=1)
@@ -66,6 +79,8 @@
             series_ref[pl.ds(first, count), :] = tile[:count].astype(jnp.bfloat16)
     else:
         series_ref[...] = total.astype(jnp.bfloat16)
+    for copy in copies[steps:]:
+        copy.wait()
 
 
 def join_packed_kernel(outer, *refs):
@@ -101,19 +116,11 @@
             joined_ref[pl.ds(first, count), pl.ds(at * LANES, LANES)] = tile[:count].astype(jnp.bfloat16)
 
 
-def offsets_kernel(offsets_ref, group_ref, lag_ref, held, sems):
-    copies = []
+def offsets_kernel(offsets_ref, group_ref, lag_ref):
     for at in range(offsets_ref.shape[1] // LANES):
         here = pl.ds(at * LANES, LANES)
-        copies.append(pltpu.make_async_copy(offsets_ref.at[:, here], held.at[at], sems.at[at]))
-        copies[-1].start()
-    for at, copy in enumerate(copies):
-        here = pl.ds(at * LANES, LANES)
-        copy.wait()
-        offset = held[at].astype(jnp.float32).T
-        group = jnp.zeros_like(offset)
-        for edge in range(1, GROUPS):
-            group = group + jnp.where(offset >= float(STEP * edge), 1.0, 0.0)
+        offset = offsets_ref[:, here].astype(jnp.float32).T
+        group = jnp.minimum(jnp.floor(offset * (1.0 / STEP)), float(GROUPS - 1))
         group_ref[here, :] = group.astype(jnp.bfloat16)
         lag_ref[here, :] = (offset - float(STEP) * group).astype(jnp.bfloat16)
 
@@ -123,30 +130,23 @@
     return jnp.maximum(one - jnp.abs(table - jnp.bfloat16(value)), jnp.bfloat16(0))
 
 
-def choices_kernel(outer, inner, flip, me_ref, group_ref, lag_ref, chosen_ref):
+def sums_kernel(given, outer, inner, flip, me_ref, joined_ref, group_ref, lag_ref, *refs):
+    before_ref, sums_ref, *early_ref = refs[:-4] if given else (None, *refs[:-4])
+    moving, shifted, in_group, at_lag = refs[-4:]
+    span, nsub = joined_ref.shape
     trials = lag_ref.shape[1]
-    subs = lag_ref.shape[0] // (outer * inner)
-    nsub = outer * subs
+    rows = span + STEP
+    subs = nsub // outer
     row = me_ref[0] // inner
     column = (me_ref[0] % inner) ^ flip
     for slot in range(outer):
         start = pl.multiple_of(((row ^ slot) * inner + column) * subs, subs)
         groups = group_ref[pl.ds(start, subs), :]
         lags = lag_ref[pl.ds(start, subs), :]
-        in_group = [one_where(groups, group) for group in range(GROUPS)]
+        for group in range(GROUPS):
+            in_group[pl.ds(group * nsub + slot * subs, subs), :] = one_where(groups, group)
         for lag in range(STEP + 1):
-            at_lag = one_where(lags, lag)
-            for group in range(GROUPS - 2 if lag == STEP else 0, GROUPS):
-                place = (group // 2 * STEP + lag) * nsub + slot * subs
-                chosen_ref[pl.ds(place, subs), pl.ds(group % 2 * trials, trials)] = at_lag * in_group[group]
-
-
-def sums_kernel(given, joined_ref, chosen_ref, *refs):
-    before_ref, sums_ref, *early_ref = refs[:-2] if given else (None, *refs[:-2])
-    moving, shifted = refs[-2:]
-    span, nsub = joined_ref.shape
-    trials = chosen_ref.shape[1] // 2
-    rows = span + STEP
+            at_lag[pl.ds(lag * nsub + slot * subs, subs), :] = one_where(lags, lag)
     blank = jnp.zeros((STEP, nsub), jnp.float32)
     moving[pl.ds(0, STEP), :] = blank
     moving[pl.ds(STEP, span), :] = joined_ref[...].astype(jnp.float32)
@@ -158,12 +158,21 @@
     else:
         sums_ref[...] = before_ref[...]
     for pair in range(GROUPS // 2):
-        depth = (STEP + (pair == GROUPS // 2 - 1)) * nsub
-        both = jnp.dot(
-            shifted[:, pl.ds(0, depth)],
-            chosen_ref[pl.ds(pair * STEP * nsub, depth), :],
-            preferred_element_type=jnp.float32,
+        lags = STEP + (pair == GROUPS // 2 - 1)
+        chosen = jnp.concatenate(
+            [
+                jnp.concatenate(
+                    [
+                        at_lag[pl.ds(lag * nsub, nsub), :] * in_group[pl.ds((2 * pair + odd) * nsub, nsub), :]
+                        for odd in range(2)
+                    ],
+                    axis=1,
+                )
+                for lag in range(lags)
+            ],
+            axis=0,
         )
+        both = jnp.dot(shifted[:, pl.ds(0, lags * nsub)], chosen, preferred_element_type=jnp.float32)
         for odd in range(2):
             first = STEP * (GROUPS - 1 - 2 * pair - odd)
             sums_ref[pl.ds(first, rows), :] += both[:, odd * trials : (odd + 1) * trials]
@@ -171,7 +180,8 @@
         ref[...] = sums_ref[pl.ds(0, ref.shape[0]), :]
 
 
-def bands_kernel(widths_ref, bands_ref):
+def bands_kernel(widths_ref, early_ref, bands_ref):
+    del early_ref
     shape = (bands_ref.shape[0], LANES)
     lag = lax.broadcasted_iota(jnp.int32, shape, 0) - lax.broadcasted_iota(jnp.int32, shape, 1)
     for at in range(widths_ref.shape[0]):
@@ -234,36 +244,47 @@
     )(*args)
 
 
-def one_beam(own, delays, choices, bands, widths, groups, outer, per_sub, scale):
+def one_beam(own, delays, offsets, me, widths, groups, outer, per_sub, scale):
     chans, length = own.shape
+    padded, all_subs = offsets.shape
     sub_dev = chans // per_sub
     inner = groups // outer
-    padded = choices[0].shape[1] // 2
     filters = widths.shape[0]
     span = length + DCH
     packed = 2 * sub_dev == LANES
     series_shape = (-(-span // 32) * 16, LANES) if packed else (sub_dev, length + LANES)
-    steps = max(1, chans // 256)
-    series = call(
+    steps = 4
+    series, fetched = call(
         functools.partial(series_kernel, per_sub, packed),
-        jax.ShapeDtypeStruct(series_shape, jnp.bfloat16),
-        [VMEM, HBM],
-        (delays[None, :], pltpu.with_memory_space_constraint(own, pltpu.HBM)),
-        [pltpu.VMEM((chans, length), jnp.bfloat16), pltpu.SemaphoreType.DMA((steps,))],
+        [
+            jax.ShapeDtypeStruct(series_shape, jnp.bfloat16),
+            jax.ShapeDtypeStruct((padded, all_subs), jnp.int32),
+        ],
+        [HBM, HBM, HBM],
+        tuple(pltpu.with_memory_space_constraint(x, pltpu.HBM) for x in (delays[None, :], own, offsets)),
+        [
+            pltpu.VMEM((1, chans), jnp.int32),
+            pltpu.VMEM((chans, length), jnp.bfloat16),
+            pltpu.SemaphoreType.DMA,
+            pltpu.SemaphoreType.DMA((2 * steps,)),
+        ],
     )
     line = [series] + [exchanged(series, "sub", flip * inner) for flip in range(1, outer)]
+    split_shape = jax.ShapeDtypeStruct((all_subs, padded), jnp.bfloat16)
+    split = call(offsets_kernel, [split_shape, split_shape], [VMEM], (fetched,))
     nsub = outer * sub_dev
-    tables = (*choices, bands)
     joined = call(
         functools.partial(join_packed_kernel if packed else join_kernel, outer),
         jax.ShapeDtypeStruct((span, nsub), jnp.bfloat16),
-        [VMEM] * outer + [ANY] * len(tables),
-        (*line, *tables),
+        [VMEM] * outer + [ANY] * len(split),
+        (*line, *split),
     )
     blocks = [joined] + [exchanged(joined, "sub", flip) for flip in range(1, inner)]
     scratch = [
         pltpu.VMEM((span + 2 * STEP, nsub), jnp.float32),
         pltpu.VMEM((span + STEP, (STEP + 1) * nsub), jnp.bfloat16),
+        pltpu.VMEM((GROUPS * nsub, padded), jnp.bfloat16),
+        pltpu.VMEM(((STEP + 1) * nsub, padded), jnp.bfloat16),
     ]
     flops = 2 * (span + STEP) * nsub * padded * (OMAX + 2)
     sums_shape = jax.ShapeDtypeStruct((length + REACH, padded), jnp.float32)
@@ -271,15 +292,21 @@
     sums = []
     for flip in range(inner):
         sums = call(
-            functools.partial(sums_kernel, flip > 0),
+            functools.partial(sums_kernel, flip > 0, outer, inner, flip),
             [sums_shape, early_shape] if flip == inner - 1 else [sums_shape],
-            [VMEM] * (2 + len(sums)),
-            (blocks[flip], choices[flip], *sums),
+            [SMEM] + [VMEM] * (3 + len(sums)),
+            (me, blocks[flip], *split, *sums),
             scratch,
             flops,
         )
     sums, early = sums
     later = passed_back(early, "tm")
+    bands = call(
+        bands_kernel,
+        jax.ShapeDtypeStruct((LANES + WMAX, filters * LANES), jnp.bfloat16),
+        [SMEM, ANY],
+        (widths, early),
+    )
     parts = length // LANES
     pieces = 4
     return call(
@@ -303,39 +330,13 @@
     groups = lax.axis_size("sub")
     outer = 1 << (groups.bit_length() // 2)
     outer = outer if groups % (outer * outer) == 0 else outer // 2
-    inner = groups // outer
     per_sub = chans // (nsub // groups)
     scale = 1.0 / math.sqrt(chans * groups)
     padded = max(trials, LANES)
-    offset_table = jnp.pad(offsets, ((0, padded - trials), (0, 0))) if padded > trials else offsets
+    table = jnp.pad(offsets, ((0, padded - trials), (0, 0))) if padded > trials else offsets
     me = lax.axis_index("sub").astype(jnp.int32).reshape(1)
-    split_shape = jax.ShapeDtypeStruct((nsub, padded), jnp.bfloat16)
-    columns = nsub // LANES
-    split = call(
-        offsets_kernel,
-        [split_shape, split_shape],
-        [HBM],
-        (pltpu.with_memory_space_constraint(offset_table, pltpu.HBM),),
-        [pltpu.VMEM((columns, padded, LANES), jnp.int32), pltpu.SemaphoreType.DMA((columns,))],
-    )
-    rows = (GROUPS // 2 * STEP + 1) * (nsub // inner)
-    choices = [
-        call(
-            functools.partial(choices_kernel, outer, inner, flip),
-            jax.ShapeDtypeStruct((rows, 2 * padded), jnp.bfloat16),
-            [SMEM, VMEM, VMEM],
-            (me, *split),
-        )
-        for flip in range(inner)
-    ]
-    bands = call(
-        bands_kernel,
-        jax.ShapeDtypeStruct((LANES + WMAX, widths.shape[0] * LANES), jnp.bfloat16),
-        [SMEM],
-        (widths,),
-    )
     outs = [
-        one_beam(data[beam], delays, choices, bands, widths, groups, outer, per_sub, scale)[:trials, None]
+        one_beam(data[beam], delays, table, me, widths, groups, outer, per_sub, scale)[:trials, None]
         for beam in range(beams)
     ]
     return outs[0] if beams == 1 else jnp.concatenate(outs, axis=1)

time: 35.6 us -> 33.3 us (0.935)
  Pallas kernels: 20.1 us -> 17.2 us
  waiting for transfers between devices: 3.85 us -> 5.23 us
  local copies, waits for them, and re-layouts: 0.69 us -> 0.01 us
    pallas_call x13 -> x9, Pallas kernels: 20.1 us -> 17.2 us  [call(): pl.pallas_call(kernel, out_shape=out_shape, in_specs=in_specs, scratch_sh...]
    ppermute x6, waiting for transfers between devices: 1.92 us -> 4.01 us  [exchanged(): lax.ppermute(value, axis, [(source, source ^ flip) for source in range(co...]
    ppermute x1, waiting for transfers between devices: 1.93 us -> 1.21 us  [passed_back(): lax.ppermute(value, axis, [(source, source - 1) for source in range(1, co...]
    unnamed x4 -> x2, local copies, waits for them, and re-layouts: 0.69 us -> 0.01 us
  transfers between devices with their start and end apart: 7 -> 7, of which waited for: 3 -> 3; matrix products, arithmetic and copies ran while one was open for 0% -> 0% of each run, Pallas kernels for 38% -> 30%
where the time goes in v5:
time: 33.3 us; the launch traced here: 33.1 us
  Pallas kernels  17.2 us (52%)
  starting transfers between devices  10.6 us (32%)
  waiting for transfers between devices  5.23 us (16%)
    pallas_call x9, Pallas kernels, call(): pl.pallas_call(kernel, out_shape=out_shape, in_specs=in_specs, scratch_sh...  17.2 us
    ppermute x6, starting transfers between devices, exchanged(): lax.ppermute(value, axis, [(source, source ^ flip) for source in range(co...  9.31 us
    ppermute x6, waiting for transfers between devices, exchanged(): lax.ppermute(value, axis, [(source, source ^ flip) for source in range(co...  4.01 us
    ppermute x1, starting transfers between devices, passed_back(): lax.ppermute(value, axis, [(source, source - 1) for source in range(1, co...  1.29 us
    ppermute x1, waiting for transfers between devices, passed_back(): lax.ppermute(value, axis, [(source, source - 1) for source in range(1, co...  1.21 us
  transfers between devices with their start and end apart: 7, of which 3 were waited for; matrix products, arithmetic and copies ran while one was open for 0% of the time, Pallas kernels for 30%

profile of v5, /device:TPU:0, one launch (start us, length us, event | category | flops | bytes accessed | tf_op | source)
XLA Modules:
  0.0 33.1 jit_solution(12142672531408247184)
XLA Ops:
  0.0 1.9 %shard_map.46 = (bf16[144,128]{1,0:T(8,128)(2,1)S(1)}, s32[128,1024]{1,0:T(8,128)S(1)}) custom-call(s32[1,1024]{1,0:T(1,128)} %bitcast.7, bf16[1024,256]{1,0:T(8,128)(2,1)} %bitcast.6, s32[128,1024]{1,0:T(8,128)} %offsets_ref.1), custom_call_target="tpu_custom_call" | custom-call | bytes 1048576 | tf_op jit(solution)/shard_map/pallas_call | solution.py:236
  1.9 5.1 %collective-permute-start.2 = (bf16[144,128]{1,0:T(8,128)(2,1)S(1)}, bf16[144,128]{1,0:T(8,128)(2,1)S(1)}, u32[]{:S(2)}, u32[]{:S(2)}) collective-permute-start(bf16[144,128]{1,0:T(8,128)(2,1)S(1)} %get-tuple-element.11.refs_0_), channel_id=1, source_target_pairs={{0,24},{2,26},{4,28},{6,30},{8,16},{10,18},{12,20},{14,22},{16,8},... | collective-permute-start | bytes 110600 | tf_op jit(solution)/shard_map/ppermute | solution.py:31
  7.0 0.0 collective-permute-start.1
  7.1 0.6 %collective-permute-start = (bf16[144,128]{1,0:T(8,128)(2,1)S(1)}, bf16[144,128]{1,0:T(8,128)(2,1)S(1)}, u32[]{:S(2)}, u32[]{:S(2)}) collective-permute-start(bf16[144,128]{1,0:T(8,128)(2,1)S(1)} %get-tuple-element.11.refs_0_), channel_id=1, source_target_pairs={{0,8},{2,10},{4,12},{6,14},{8,0},{10,2},{12,4},{14,6},{16,24},{18,... | collective-permute-start | bytes 110600 | tf_op jit(solution)/shard_map/ppermute | solution.py:31
  7.7 0.2 shard_map.47
  7.9 1.1 %collective-permute-done.2.refs_3_ = bf16[144,128]{1,0:T(8,128)(2,1)S(1)} collective-permute-done((bf16[144,128]{1,0:T(8,128)(2,1)S(1)}, bf16[144,128]{1,0:T(8,128)(2,1)S(1)}, u32[]{:S(2)}, u32[]{:S(2)}) %collective-permute-start.2) | collective-permute-done | bytes 36896 | tf_op jit(solution)/shard_map/ppermute | solution.py:31
  9.0 2.9 %collective-permute-done.1.refs_2_ = bf16[144,128]{1,0:T(8,128)(2,1)S(1)} collective-permute-done((bf16[144,128]{1,0:T(8,128)(2,1)S(1)}, bf16[144,128]{1,0:T(8,128)(2,1)S(1)}, u32[]{:S(2)}, u32[]{:S(2)}) %collective-permute-start.1) | collective-permute-done | bytes 36896 | tf_op jit(solution)/shard_map/ppermute | solution.py:31
  11.9 0.0 collective-permute-done.refs_1_
  11.9 0.1 shard_map.48.joined_ref
  12.0 1.6 %collective-permute-start.5 = (bf16[272,256]{1,0:T(8,128)(2,1)S(1)}, bf16[272,256]{1,0:T(8,128)(2,1)S(1)}, u32[]{:S(2)}, u32[]{:S(2)}) collective-permute-start(bf16[272,256]{1,0:T(8,128)(2,1)S(1)} %shard_map.48.joined_ref), channel_id=1, source_target_pairs={{0,2},{2,0},{4,6},{6,4},{8,10},{10,8},{12,14},{14,12},{16,18},{18,... | collective-permute-start | bytes 417800 | tf_op jit(solution)/shard_map/ppermute | solution.py:31
  13.6 1.5 %collective-permute-start.4 = (bf16[272,256]{1,0:T(8,128)(2,1)S(1)}, bf16[272,256]{1,0:T(8,128)(2,1)S(1)}, u32[]{:S(2)}, u32[]{:S(2)}) collective-permute-start(bf16[272,256]{1,0:T(8,128)(2,1)S(1)} %shard_map.48.joined_ref), channel_id=1, source_target_pairs={{0,4},{2,6},{4,0},{6,2},{8,12},{10,14},{12,8},{14,10},{16,20},{18,... | collective-permute-start | bytes 417800 | tf_op jit(solution)/shard_map/ppermute | solution.py:31
  15.1 0.5 %collective-permute-start.3 = (bf16[272,256]{1,0:T(8,128)(2,1)S(1)}, bf16[272,256]{1,0:T(8,128)(2,1)S(1)}, u32[]{:S(2)}, u32[]{:S(2)}) collective-permute-start(bf16[272,256]{1,0:T(8,128)(2,1)S(1)} %shard_map.48.joined_ref), channel_id=1, source_target_pairs={{0,6},{2,4},{4,2},{6,0},{8,14},{10,12},{12,10},{14,8},{16,22},{18,... | collective-permute-start | bytes 417800 | tf_op jit(solution)/shard_map/ppermute | solution.py:31
  15.6 3.1 %shard_map.49.refs_0_ = f32[368,128]{1,0:T(8,128)S(1)} custom-call(s32[1]{0:T(128)} %bitcast.me_ref, bf16[272,256]{1,0:T(8,128)(2,1)S(1)} %shard_map.48.joined_ref, bf16[1024,128]{1,0:T(8,128)(2,1)S(1)} %get-tuple-element.13.refs_4_.group_ref, bf16[1024,128]{1,0:T(8,128)(2,1)S(1)} %get-tuple-element.14.refs_5_.lag_ref), custom_call_target="tpu_custom_call" | custom-call | flops 1849688064 | bytes 1048576 | tf_op jit(solution)/shard_map/pallas_call | solution.py:236
  18.6 0.0 collective-permute-done.5.joined_ref
  18.6 3.1 %shard_map.50.refs_0_ = f32[368,128]{1,0:T(8,128)S(1)} custom-call(s32[1]{0:T(128)} %bitcast.me_ref, bf16[272,256]{1,0:T(8,128)(2,1)S(1)} %collective-permute-done.5.joined_ref, bf16[1024,128]{1,0:T(8,128)(2,1)S(1)} %get-tuple-element.13.refs_4_.group_ref, bf16[1024,128]{1,0:T(8,128)(2,1)S(1)} %get-tuple-element.14.refs_5_.lag_ref, ...), custom_call_target="tpu_custom_call" | custom-call | flops 1849688064 | bytes 1048576 | tf_op jit(solution)/shard_map/pallas_call | solution.py:236
  21.7 0.0 collective-permute-done.4.joined_ref
  21.7 3.1 %shard_map.51.refs_0_ = f32[368,128]{1,0:T(8,128)S(1)} custom-call(s32[1]{0:T(128)} %bitcast.me_ref, bf16[272,256]{1,0:T(8,128)(2,1)S(1)} %collective-permute-done.4.joined_ref, bf16[1024,128]{1,0:T(8,128)(2,1)S(1)} %get-tuple-element.13.refs_4_.group_ref, bf16[1024,128]{1,0:T(8,128)(2,1)S(1)} %get-tuple-element.14.refs_5_.lag_ref, ...), custom_call_target="tpu_custom_call" | custom-call | flops 1849688064 | bytes 1048576 | tf_op jit(solution)/shard_map/pallas_call | solution.py:236
  24.8 0.0 collective-permute-done.3.joined_ref
  24.8 3.1 %shard_map.52 = (f32[368,128]{1,0:T(8,128)S(1)}, f32[240,128]{1,0:T(8,128)S(1)}) custom-call(s32[1]{0:T(128)} %bitcast.me_ref, bf16[272,256]{1,0:T(8,128)(2,1)S(1)} %collective-permute-done.3.joined_ref, bf16[1024,128]{1,0:T(8,128)(2,1)S(1)} %get-tuple-element.13.refs_4_.group_ref, bf16[1024,128]{1,0:T(8,128)(2,1)S(1)} %get-tuple-element.14.refs_5_.lag_ref, ...), custom_call_target="tpu_custom_call" | custom-call | flops 1849688064 | bytes 1048576 | tf_op jit(solution)/shard_map/pallas_call | solution.py:236
  27.9 0.0 copy-start
  27.9 1.3 %collective-permute-start.6 = (f32[240,128]{1,0:T(8,128)S(1)}, f32[240,128]{1,0:T(8,128)S(1)}, u32[]{:S(2)}, u32[]{:S(2)}) collective-permute-start(f32[240,128]{1,0:T(8,128)S(1)} %get-tuple-element.15.early_ref), channel_id=1, source_target_pairs={{1,0},{3,2},{5,4},{7,6},{9,8},{11,10},{13,12},{15,14},{17,16},{19,... | collective-permute-start | bytes 368648 | tf_op jit(solution)/shard_map/ppermute | solution.py:26
  29.2 0.0 copy-done
  29.2 0.7 %shard_map.53.bands_ref = bf16[256,1024]{1,0:T(8,128)(2,1)S(1)} custom-call(s32[8]{0:T(128)S(1)} %copy-done, f32[240,128]{1,0:T(8,128)S(1)} %get-tuple-element.15.early_ref), custom_call_target="tpu_custom_call" | custom-call | bytes 1048576 | tf_op jit(solution)/shard_map/pallas_call | solution.py:236
  29.9 1.2 %collective-permute-done.6.later_ref = f32[240,128]{1,0:T(8,128)S(1)} collective-permute-done((f32[240,128]{1,0:T(8,128)S(1)}, f32[240,128]{1,0:T(8,128)S(1)}, u32[]{:S(2)}, u32[]{:S(2)}) %collective-permute-start.6) | collective-permute-done | bytes 122912 | tf_op jit(solution)/shard_map/ppermute | solution.py:26
  31.1 2.0 %shard_map.54 = f32[128,8,256]{2,1,0:T(8,128)} custom-call(s32[8]{0:T(128)S(1)} %copy-done, bf16[256,1024]{1,0:T(8,128)(2,1)S(1)} %shard_map.53.bands_ref, f32[368,128]{1,0:T(8,128)S(1)} %get-tuple-element.16.sums_ref, f32[240,128]{1,0:T(8,128)S(1)} %collective-permute-done.6.later_ref), custom_call_target="tpu_custom_call" | custom-call | bytes 1048576 | tf_op jit(solution)/shard_map/pallas_call | solution.py:236
Async XLA Ops:
  1.9 7.1 %collective-permute-start.2 = (bf16[144,128]{1,0:T(8,128)(2,1)S(1)}, bf16[144,128]{1,0:T(8,128)(2,1)S(1)}, u32[]{:S(2)}, u32[]{:S(2)}) collective-permute-start(bf16[144,128]{1,0:T(8,128)(2,1)S(1)} %get-tuple-element.11.refs_0_), channel_id=1, source_target_pairs={{0,24},{2,26},{4,28},{6,30},{8,16},{10,18},{12,20},{14,22},{16,8},... | collective-permute-start | bytes 110600 | tf_op jit(solution)/shard_map/ppermute | solution.py:31
  7.0 4.9 %collective-permute-start.1 = (bf16[144,128]{1,0:T(8,128)(2,1)S(1)}, bf16[144,128]{1,0:T(8,128)(2,1)S(1)}, u32[]{:S(2)}, u32[]{:S(2)}) collective-permute-start(bf16[144,128]{1,0:T(8,128)(2,1)S(1)} %get-tuple-element.11.refs_0_), channel_id=1, source_target_pairs={{0,16},{2,18},{4,20},{6,22},{8,24},{10,26},{12,28},{14,30},{16,0},... | collective-permute-start | bytes 110600 | tf_op jit(solution)/shard_map/ppermute | solution.py:31
  7.1 4.9 %collective-permute-start = (bf16[144,128]{1,0:T(8,128)(2,1)S(1)}, bf16[144,128]{1,0:T(8,128)(2,1)S(1)}, u32[]{:S(2)}, u32[]{:S(2)}) collective-permute-start(bf16[144,128]{1,0:T(8,128)(2,1)S(1)} %get-tuple-element.11.refs_0_), channel_id=1, source_target_pairs={{0,8},{2,10},{4,12},{6,14},{8,0},{10,2},{12,4},{14,6},{16,24},{18,... | collective-permute-start | bytes 110600 | tf_op jit(solution)/shard_map/ppermute | solution.py:31
  12.0 6.6 %collective-permute-start.5 = (bf16[272,256]{1,0:T(8,128)(2,1)S(1)}, bf16[272,256]{1,0:T(8,128)(2,1)S(1)}, u32[]{:S(2)}, u32[]{:S(2)}) collective-permute-start(bf16[272,256]{1,0:T(8,128)(2,1)S(1)} %shard_map.48.joined_ref), channel_id=1, source_target_pairs={{0,2},{2,0},{4,6},{6,4},{8,10},{10,8},{12,14},{14,12},{16,18},{18,... | collective-permute-start | bytes 417800 | tf_op jit(solution)/shard_map/ppermute | solution.py:31
  13.6 8.1 %collective-permute-start.4 = (bf16[272,256]{1,0:T(8,128)(2,1)S(1)}, bf16[272,256]{1,0:T(8,128)(2,1)S(1)}, u32[]{:S(2)}, u32[]{:S(2)}) collective-permute-start(bf16[272,256]{1,0:T(8,128)(2,1)S(1)} %shard_map.48.joined_ref), channel_id=1, source_target_pairs={{0,4},{2,6},{4,0},{6,2},{8,12},{10,14},{12,8},{14,10},{16,20},{18,... | collective-permute-start | bytes 417800 | tf_op jit(solution)/shard_map/ppermute | solution.py:31
  15.1 9.7 %collective-permute-start.3 = (bf16[272,256]{1,0:T(8,128)(2,1)S(1)}, bf16[272,256]{1,0:T(8,128)(2,1)S(1)}, u32[]{:S(2)}, u32[]{:S(2)}) collective-permute-start(bf16[272,256]{1,0:T(8,128)(2,1)S(1)} %shard_map.48.joined_ref), channel_id=1, source_target_pairs={{0,6},{2,4},{4,2},{6,0},{8,14},{10,12},{12,10},{14,8},{16,22},{18,... | collective-permute-start | bytes 417800 | tf_op jit(solution)/shard_map/ppermute | solution.py:31
  27.9 1.3 %copy-start = (s32[8]{0:T(128)S(1)}, s32[8]{0:T(128)}, u32[]{:S(2)}) copy-start(s32[8]{0:T(128)} %widths_ref.3) | copy-start | bytes 100
  27.9 3.2 %collective-permute-start.6 = (f32[240,128]{1,0:T(8,128)S(1)}, f32[240,128]{1,0:T(8,128)S(1)}, u32[]{:S(2)}, u32[]{:S(2)}) collective-permute-start(f32[240,128]{1,0:T(8,128)S(1)} %get-tuple-element.15.early_ref), channel_id=1, source_target_pairs={{1,0},{3,2},{5,4},{7,6},{9,8},{11,10},{13,12},{15,14},{17,16},{19,... | collective-permute-start | bytes 368648 | tf_op jit(solution)/shard_map/ppermute | solution.py:26

commit v6 on v5

--- a/solution.py
+++ b/solution.py
@@ -130,23 +130,34 @@
     return jnp.maximum(one - jnp.abs(table - jnp.bfloat16(value)), jnp.bfloat16(0))
 
 
-def sums_kernel(given, outer, inner, flip, me_ref, joined_ref, group_ref, lag_ref, *refs):
-    before_ref, sums_ref, *early_ref = refs[:-4] if given else (None, *refs[:-4])
-    moving, shifted, in_group, at_lag = refs[-4:]
+def store_choices(slot, outer, inner, flip, me_ref, group_ref, lag_ref, chosen_ref):
+    trials = lag_ref.shape[1]
+    subs = lag_ref.shape[0] // (outer * inner)
+    nsub = outer * subs
+    row = me_ref[0] // inner
+    column = (me_ref[0] % inner) ^ flip
+    start = pl.multiple_of(((row ^ slot) * inner + column) * subs, subs)
+    groups = group_ref[pl.ds(start, subs), :]
+    lags = lag_ref[pl.ds(start, subs), :]
+    in_group = [one_where(groups, group) for group in range(GROUPS)]
+    for lag in range(STEP + 1):
+        at_lag = one_where(lags, lag)
+        for group in range(GROUPS - 2 if lag == STEP else 0, GROUPS):
+            place = (group // 2 * STEP + lag) * nsub + slot * subs
+            chosen_ref[pl.ds(place, subs), pl.ds(group % 2 * trials, trials)] = at_lag * in_group[group]
+
+
+def choices_kernel(outer, inner, me_ref, group_ref, lag_ref, chosen_ref):
+    for slot in range(outer):
+        store_choices(slot, outer, inner, 0, me_ref, group_ref, lag_ref, chosen_ref)
+
+
+def sums_kernel(given, then, outer, inner, me_ref, joined_ref, group_ref, lag_ref, chosen_ref, *refs):
+    before_ref, sums_ref, other_ref = refs[:-2] if given else (None, *refs[:-2])
+    moving, shifted = refs[-2:]
     span, nsub = joined_ref.shape
     trials = lag_ref.shape[1]
     rows = span + STEP
-    subs = nsub // outer
-    row = me_ref[0] // inner
-    column = (me_ref[0] % inner) ^ flip
-    for slot in range(outer):
-        start = pl.multiple_of(((row ^ slot) * inner + column) * subs, subs)
-        groups = group_ref[pl.ds(start, subs), :]
-        lags = lag_ref[pl.ds(start, subs), :]
-        for group in range(GROUPS):
-            in_group[pl.ds(group * nsub + slot * subs, subs), :] = one_where(groups, group)
-        for lag in range(STEP + 1):
-            at_lag[pl.ds(lag * nsub + slot * subs, subs), :] = one_where(lags, lag)
     blank = jnp.zeros((STEP, nsub), jnp.float32)
     moving[pl.ds(0, STEP), :] = blank
     moving[pl.ds(STEP, span), :] = joined_ref[...].astype(jnp.float32)
@@ -157,27 +168,22 @@
         sums_ref[...] = jnp.zeros_like(sums_ref)
     else:
         sums_ref[...] = before_ref[...]
-    for pair in range(GROUPS // 2):
-        lags = STEP + (pair == GROUPS // 2 - 1)
-        chosen = jnp.concatenate(
-            [
-                jnp.concatenate(
-                    [
-                        at_lag[pl.ds(lag * nsub, nsub), :] * in_group[pl.ds((2 * pair + odd) * nsub, nsub), :]
-                        for odd in range(2)
-                    ],
-                    axis=1,
-                )
-                for lag in range(lags)
-            ],
-            axis=0,
+    pairs = GROUPS // 2
+    for pair in range(pairs):
+        if then < inner:
+            for slot in range(outer * pair // pairs, outer * (pair + 1) // pairs):
+                store_choices(slot, outer, inner, then, me_ref, group_ref, lag_ref, other_ref)
+        depth = (STEP + (pair == pairs - 1)) * nsub
+        both = jnp.dot(
+            shifted[:, pl.ds(0, depth)],
+            chosen_ref[pl.ds(pair * STEP * nsub, depth), :],
+            preferred_element_type=jnp.float32,
         )
-        both = jnp.dot(shifted[:, pl.ds(0, lags * nsub)], chosen, preferred_element_type=jnp.float32)
         for odd in range(2):
             first = STEP * (GROUPS - 1 - 2 * pair - odd)
             sums_ref[pl.ds(first, rows), :] += both[:, odd * trials : (odd + 1) * trials]
-    for ref in early_ref:
-        ref[...] = sums_ref[pl.ds(0, ref.shape[0]), :]
+    if then == inner:
+        other_ref[...] = sums_ref[pl.ds(0, other_ref.shape[0]), :]
 
 
 def bands_kernel(widths_ref, early_ref, bands_ref):
@@ -206,6 +212,8 @@
         tile = (total[first : first + LANES] * scale).T
         values[:, pl.ds(first, LANES)] = tile.astype(jnp.bfloat16)
     share = trials // sems.shape[1]
+    widths = [jnp.full((1, LANES), widths_ref[at], jnp.int32).astype(jnp.float32) for at in range(filters)]
+    shares = [1.0 / jnp.sqrt(width) for width in widths]
     copies = []
     for part in range(length // LANES):
         lanes = pl.ds(part * LANES, LANES)
@@ -215,8 +223,7 @@
                 bands_ref[:, pl.ds(at * LANES, LANES)],
                 preferred_element_type=jnp.float32,
             )
-            root = jnp.sqrt(jnp.full((1, LANES), widths_ref[at], jnp.int32).astype(jnp.float32))
-            mixed[part, pl.ds(at, trials, stride=filters), :] = sums / root
+            mixed[part, pl.ds(at, trials, stride=filters), :] = sums * shares[at]
         tiles[part] = mixed[part].reshape(trials, filters, LANES)
         for piece in range(sems.shape[1]):
             some = pl.ds(piece * share, share)
@@ -273,33 +280,36 @@
     split_shape = jax.ShapeDtypeStruct((all_subs, padded), jnp.bfloat16)
     split = call(offsets_kernel, [split_shape, split_shape], [VMEM], (fetched,))
     nsub = outer * sub_dev
+    chosen_shape = jax.ShapeDtypeStruct(((GROUPS // 2 * STEP + 1) * nsub, 2 * padded), jnp.bfloat16)
+    chosen = call(
+        functools.partial(choices_kernel, outer, inner), chosen_shape, [SMEM, VMEM, VMEM], (me, *split)
+    )
     joined = call(
         functools.partial(join_packed_kernel if packed else join_kernel, outer),
         jax.ShapeDtypeStruct((span, nsub), jnp.bfloat16),
-        [VMEM] * outer + [ANY] * len(split),
-        (*line, *split),
+        [VMEM] * outer + [ANY],
+        (*line, chosen),
     )
     blocks = [joined] + [exchanged(joined, "sub", flip) for flip in range(1, inner)]
     scratch = [
         pltpu.VMEM((span + 2 * STEP, nsub), jnp.float32),
         pltpu.VMEM((span + STEP, (STEP + 1) * nsub), jnp.bfloat16),
-        pltpu.VMEM((GROUPS * nsub, padded), jnp.bfloat16),
-        pltpu.VMEM(((STEP + 1) * nsub, padded), jnp.bfloat16),
     ]
     flops = 2 * (span + STEP) * nsub * padded * (OMAX + 2)
     sums_shape = jax.ShapeDtypeStruct((length + REACH, padded), jnp.float32)
     early_shape = jax.ShapeDtypeStruct((REACH + WMAX, padded), jnp.float32)
-    sums = []
+    before = ()
     for flip in range(inner):
-        sums = call(
-            functools.partial(sums_kernel, flip > 0, outer, inner, flip),
-            [sums_shape, early_shape] if flip == inner - 1 else [sums_shape],
-            [SMEM] + [VMEM] * (3 + len(sums)),
-            (me, blocks[flip], *split, *sums),
+        sums, chosen = call(
+            functools.partial(sums_kernel, flip > 0, flip + 1, outer, inner),
+            [sums_shape, early_shape if flip == inner - 1 else chosen_shape],
+            [SMEM] + [VMEM] * (4 + len(before)),
+            (me, blocks[flip], *split, chosen, *before),
             scratch,
             flops,
         )
-    sums, early = sums
+        before = (sums,)
+    early = chosen
     later = passed_back(early, "tm")
     bands = call(
         bands_kernel,

time: 33.3 us -> 34.5 us (1.036)
  Pallas kernels: 17.2 us -> 18.1 us
    pallas_call x9 -> x10, Pallas kernels: 17.2 us -> 18.1 us  [call(): pl.pallas_call(kernel, out_shape=out_shape, in_specs=in_specs, scratch_sh...]
  transfers between devices with their start and end apart: 7 -> 7, of which waited for: 3 -> 3; matrix products, arithmetic and copies ran while one was open for 0% -> 0% of each run, Pallas kernels for 30% -> 35%
where the time goes in v6:
time: 34.5 us; the launch traced here: 34.3 us
  Pallas kernels  18.1 us (52%)
  starting transfers between devices  10.5 us (30%)
  waiting for transfers between devices  5.56 us (16%)
    pallas_call x10, Pallas kernels, call(): pl.pallas_call(kernel, out_shape=out_shape, in_specs=in_specs, scratch_sh...  18.1 us
    ppermute x6, starting transfers between devices, exchanged(): lax.ppermute(value, axis, [(source, source ^ flip) for source in range(co...  9.23 us
    ppermute x6, waiting for transfers between devices, exchanged(): lax.ppermute(value, axis, [(source, source ^ flip) for source in range(co...  4.35 us
    ppermute x1, starting transfers between devices, passed_back(): lax.ppermute(value, axis, [(source, source - 1) for source in range(1, co...  1.29 us
    ppermute x1, waiting for transfers between devices, passed_back(): lax.ppermute(value, axis, [(source, source - 1) for source in range(1, co...  1.21 us
  transfers between devices with their start and end apart: 7, of which 3 were waited for; matrix products, arithmetic and copies ran while one was open for 0% of the time, Pallas kernels for 35%

profile of v6, /device:TPU:0, one launch (start us, length us, event | category | flops | bytes accessed | tf_op | source)
XLA Modules:
  0.0 34.3 jit_solution(3238643785321590712)
XLA Ops:
  0.0 1.9 %shard_map.46 = (bf16[144,128]{1,0:T(8,128)(2,1)S(1)}, s32[128,1024]{1,0:T(8,128)S(1)}) custom-call(s32[1,1024]{1,0:T(1,128)} %bitcast.7, bf16[1024,256]{1,0:T(8,128)(2,1)} %bitcast.6, s32[128,1024]{1,0:T(8,128)} %offsets_ref.1), custom_call_target="tpu_custom_call" | custom-call | bytes 1048576 | tf_op jit(solution)/shard_map/pallas_call | solution.py:243
  1.9 3.1 %collective-permute-start = (bf16[144,128]{1,0:T(8,128)(2,1)S(1)}, bf16[144,128]{1,0:T(8,128)(2,1)S(1)}, u32[]{:S(2)}, u32[]{:S(2)}) collective-permute-start(bf16[144,128]{1,0:T(8,128)(2,1)S(1)} %get-tuple-element.17.refs_0_), channel_id=1, source_target_pairs={{0,8},{2,10},{4,12},{6,14},{8,0},{10,2},{12,4},{14,6},{16,24},{18,... | collective-permute-start | bytes 110600 | tf_op jit(solution)/shard_map/ppermute | solution.py:31
  5.0 2.6 %collective-permute-start.1 = (bf16[144,128]{1,0:T(8,128)(2,1)S(1)}, bf16[144,128]{1,0:T(8,128)(2,1)S(1)}, u32[]{:S(2)}, u32[]{:S(2)}) collective-permute-start(bf16[144,128]{1,0:T(8,128)(2,1)S(1)} %get-tuple-element.17.refs_0_), channel_id=1, source_target_pairs={{0,16},{2,18},{4,20},{6,22},{8,24},{10,26},{12,28},{14,30},{16,0},... | collective-permute-start | bytes 110600 | tf_op jit(solution)/shard_map/ppermute | solution.py:31
  7.6 0.0 collective-permute-start.2
  7.6 0.2 shard_map.47
  7.8 1.2 %shard_map.48.refs_4_.chosen_ref = bf16[12544,256]{1,0:T(8,128)(2,1)S(1)} custom-call(s32[1]{0:T(128)} %bitcast.me_ref, bf16[1024,128]{1,0:T(8,128)(2,1)S(1)} %get-tuple-element.19.group_ref, bf16[1024,128]{1,0:T(8,128)(2,1)S(1)} %get-tuple-element.20.lag_ref), custom_call_target="tpu_custom_call" | custom-call | bytes 1048576 | tf_op jit(solution)/shard_map/pallas_call | solution.py:243
  9.0 0.0 collective-permute-done.refs_1_
  9.0 1.5 %collective-permute-done.1.refs_2_ = bf16[144,128]{1,0:T(8,128)(2,1)S(1)} collective-permute-done((bf16[144,128]{1,0:T(8,128)(2,1)S(1)}, bf16[144,128]{1,0:T(8,128)(2,1)S(1)}, u32[]{:S(2)}, u32[]{:S(2)}) %collective-permute-start.1) | collective-permute-done | bytes 36896 | tf_op jit(solution)/shard_map/ppermute | solution.py:31
  10.6 2.8 %collective-permute-done.2.refs_3_ = bf16[144,128]{1,0:T(8,128)(2,1)S(1)} collective-permute-done((bf16[144,128]{1,0:T(8,128)(2,1)S(1)}, bf16[144,128]{1,0:T(8,128)(2,1)S(1)}, u32[]{:S(2)}, u32[]{:S(2)}) %collective-permute-start.2) | collective-permute-done | bytes 36896 | tf_op jit(solution)/shard_map/ppermute | solution.py:31
  13.4 0.1 shard_map.49.joined_ref
  13.5 1.6 %collective-permute-start.5 = (bf16[272,256]{1,0:T(8,128)(2,1)S(1)}, bf16[272,256]{1,0:T(8,128)(2,1)S(1)}, u32[]{:S(2)}, u32[]{:S(2)}) collective-permute-start(bf16[272,256]{1,0:T(8,128)(2,1)S(1)} %shard_map.49.joined_ref), channel_id=1, source_target_pairs={{0,2},{2,0},{4,6},{6,4},{8,10},{10,8},{12,14},{14,12},{16,18},{18,... | collective-permute-start | bytes 417800 | tf_op jit(solution)/shard_map/ppermute | solution.py:31
  15.0 1.5 %collective-permute-start.4 = (bf16[272,256]{1,0:T(8,128)(2,1)S(1)}, bf16[272,256]{1,0:T(8,128)(2,1)S(1)}, u32[]{:S(2)}, u32[]{:S(2)}) collective-permute-start(bf16[272,256]{1,0:T(8,128)(2,1)S(1)} %shard_map.49.joined_ref), channel_id=1, source_target_pairs={{0,4},{2,6},{4,0},{6,2},{8,12},{10,14},{12,8},{14,10},{16,20},{18,... | collective-permute-start | bytes 417800 | tf_op jit(solution)/shard_map/ppermute | solution.py:31
  16.6 0.5 %collective-permute-start.3 = (bf16[272,256]{1,0:T(8,128)(2,1)S(1)}, bf16[272,256]{1,0:T(8,128)(2,1)S(1)}, u32[]{:S(2)}, u32[]{:S(2)}) collective-permute-start(bf16[272,256]{1,0:T(8,128)(2,1)S(1)} %shard_map.49.joined_ref), channel_id=1, source_target_pairs={{0,6},{2,4},{4,2},{6,0},{8,14},{10,12},{12,10},{14,8},{16,22},{18,... | collective-permute-start | bytes 417800 | tf_op jit(solution)/shard_map/ppermute | solution.py:31
  17.0 3.3 %shard_map.50 = (f32[368,128]{1,0:T(8,128)S(1)}, bf16[12544,256]{1,0:T(8,128)(2,1)S(1)}) custom-call(s32[1]{0:T(128)} %bitcast.me_ref, bf16[272,256]{1,0:T(8,128)(2,1)S(1)} %shard_map.49.joined_ref, bf16[1024,128]{1,0:T(8,128)(2,1)S(1)} %get-tuple-element.19.group_ref, bf16[1024,128]{1,0:T(8,128)(2,1)S(1)} %get-tuple-element.20.lag_ref, ...), custom_call_target="tpu_custom_call" | custom-call | flops 1849688064 | bytes 1048576 | tf_op jit(solution)/shard_map/pallas_call | solution.py:243
  20.3 0.0 collective-permute-done.5.joined_ref
  20.3 3.3 %shard_map.51 = (f32[368,128]{1,0:T(8,128)S(1)}, bf16[12544,256]{1,0:T(8,128)(2,1)S(1)}) custom-call(s32[1]{0:T(128)} %bitcast.me_ref, bf16[272,256]{1,0:T(8,128)(2,1)S(1)} %collective-permute-done.5.joined_ref, bf16[1024,128]{1,0:T(8,128)(2,1)S(1)} %get-tuple-element.19.group_ref, bf16[1024,128]{1,0:T(8,128)(2,1)S(1)} %get-tuple-element.20.lag_ref, ...), custom_call_target="tpu_custom_call" | custom-call | flops 1849688064 | bytes 1048576 | tf_op jit(solution)/shard_map/pallas_call | solution.py:243
  23.6 0.0 collective-permute-done.4.joined_ref
  23.6 0.0 copy-start
  23.7 3.3 %shard_map.52 = (f32[368,128]{1,0:T(8,128)S(1)}, bf16[12544,256]{1,0:T(8,128)(2,1)S(1)}) custom-call(s32[1]{0:T(128)} %bitcast.me_ref, bf16[272,256]{1,0:T(8,128)(2,1)S(1)} %collective-permute-done.4.joined_ref, bf16[1024,128]{1,0:T(8,128)(2,1)S(1)} %get-tuple-element.19.group_ref, bf16[1024,128]{1,0:T(8,128)(2,1)S(1)} %get-tuple-element.20.lag_ref, ...), custom_call_target="tpu_custom_call" | custom-call | flops 1849688064 | bytes 1048576 | tf_op jit(solution)/shard_map/pallas_call | solution.py:243
  26.9 0.0 collective-permute-done.3.joined_ref
  26.9 2.1 %shard_map.53 = (f32[368,128]{1,0:T(8,128)S(1)}, f32[240,128]{1,0:T(8,128)S(1)}) custom-call(s32[1]{0:T(128)} %bitcast.me_ref, bf16[272,256]{1,0:T(8,128)(2,1)S(1)} %collective-permute-done.3.joined_ref, bf16[1024,128]{1,0:T(8,128)(2,1)S(1)} %get-tuple-element.19.group_ref, bf16[1024,128]{1,0:T(8,128)(2,1)S(1)} %get-tuple-element.20.lag_ref, ...), custom_call_target="tpu_custom_call" | custom-call | flops 1849688064 | bytes 1048576 | tf_op jit(solution)/shard_map/pallas_call | solution.py:243
  29.1 1.3 %collective-permute-start.6 = (f32[240,128]{1,0:T(8,128)S(1)}, f32[240,128]{1,0:T(8,128)S(1)}, u32[]{:S(2)}, u32[]{:S(2)}) collective-permute-start(f32[240,128]{1,0:T(8,128)S(1)} %get-tuple-element.27.early_ref), channel_id=1, source_target_pairs={{1,0},{3,2},{5,4},{7,6},{9,8},{11,10},{13,12},{15,14},{17,16},{19,... | collective-permute-start | bytes 368648 | tf_op jit(solution)/shard_map/ppermute | solution.py:26
  30.4 0.0 copy-done
  30.4 0.7 %shard_map.54.bands_ref = bf16[256,1024]{1,0:T(8,128)(2,1)S(1)} custom-call(s32[8]{0:T(128)S(1)} %copy-done, f32[240,128]{1,0:T(8,128)S(1)} %get-tuple-element.27.early_ref), custom_call_target="tpu_custom_call" | custom-call | bytes 1048576 | tf_op jit(solution)/shard_map/pallas_call | solution.py:243
  31.1 1.2 %collective-permute-done.6.later_ref = f32[240,128]{1,0:T(8,128)S(1)} collective-permute-done((f32[240,128]{1,0:T(8,128)S(1)}, f32[240,128]{1,0:T(8,128)S(1)}, u32[]{:S(2)}, u32[]{:S(2)}) %collective-permute-start.6) | collective-permute-done | bytes 122912 | tf_op jit(solution)/shard_map/ppermute | solution.py:26
  32.3 2.0 %shard_map.55 = f32[128,8,256]{2,1,0:T(8,128)} custom-call(s32[8]{0:T(128)S(1)} %copy-done, bf16[256,1024]{1,0:T(8,128)(2,1)S(1)} %shard_map.54.bands_ref, f32[368,128]{1,0:T(8,128)S(1)} %get-tuple-element.28.sums_ref, f32[240,128]{1,0:T(8,128)S(1)} %collective-permute-done.6.later_ref), custom_call_target="tpu_custom_call" | custom-call | bytes 1048576 | tf_op jit(solution)/shard_map/pallas_call | solution.py:243
Async XLA Ops:
  1.9 7.1 %collective-permute-start = (bf16[144,128]{1,0:T(8,128)(2,1)S(1)}, bf16[144,128]{1,0:T(8,128)(2,1)S(1)}, u32[]{:S(2)}, u32[]{:S(2)}) collective-permute-start(bf16[144,128]{1,0:T(8,128)(2,1)S(1)} %get-tuple-element.17.refs_0_), channel_id=1, source_target_pairs={{0,8},{2,10},{4,12},{6,14},{8,0},{10,2},{12,4},{14,6},{16,24},{18,... | collective-permute-start | bytes 110600 | tf_op jit(solution)/shard_map/ppermute | solution.py:31
  5.0 5.5 %collective-permute-start.1 = (bf16[144,128]{1,0:T(8,128)(2,1)S(1)}, bf16[144,128]{1,0:T(8,128)(2,1)S(1)}, u32[]{:S(2)}, u32[]{:S(2)}) collective-permute-start(bf16[144,128]{1,0:T(8,128)(2,1)S(1)} %get-tuple-element.17.refs_0_), channel_id=1, source_target_pairs={{0,16},{2,18},{4,20},{6,22},{8,24},{10,26},{12,28},{14,30},{16,0},... | collective-permute-start | bytes 110600 | tf_op jit(solution)/shard_map/ppermute | solution.py:31
  7.6 5.8 %collective-permute-start.2 = (bf16[144,128]{1,0:T(8,128)(2,1)S(1)}, bf16[144,128]{1,0:T(8,128)(2,1)S(1)}, u32[]{:S(2)}, u32[]{:S(2)}) collective-permute-start(bf16[144,128]{1,0:T(8,128)(2,1)S(1)} %get-tuple-element.17.refs_0_), channel_id=1, source_target_pairs={{0,24},{2,26},{4,28},{6,30},{8,16},{10,18},{12,20},{14,22},{16,8},... | collective-permute-start | bytes 110600 | tf_op jit(solution)/shard_map/ppermute | solution.py:31
  13.5 6.8 %collective-permute-start.5 = (bf16[272,256]{1,0:T(8,128)(2,1)S(1)}, bf16[272,256]{1,0:T(8,128)(2,1)S(1)}, u32[]{:S(2)}, u32[]{:S(2)}) collective-permute-start(bf16[272,256]{1,0:T(8,128)(2,1)S(1)} %shard_map.49.joined_ref), channel_id=1, source_target_pairs={{0,2},{2,0},{4,6},{6,4},{8,10},{10,8},{12,14},{14,12},{16,18},{18,... | collective-permute-start | bytes 417800 | tf_op jit(solution)/shard_map/ppermute | solution.py:31
  15.0 8.6 %collective-permute-start.4 = (bf16[272,256]{1,0:T(8,128)(2,1)S(1)}, bf16[272,256]{1,0:T(8,128)(2,1)S(1)}, u32[]{:S(2)}, u32[]{:S(2)}) collective-permute-start(bf16[272,256]{1,0:T(8,128)(2,1)S(1)} %shard_map.49.joined_ref), channel_id=1, source_target_pairs={{0,4},{2,6},{4,0},{6,2},{8,12},{10,14},{12,8},{14,10},{16,20},{18,... | collective-permute-start | bytes 417800 | tf_op jit(solution)/shard_map/ppermute | solution.py:31
  16.6 10.4 %collective-permute-start.3 = (bf16[272,256]{1,0:T(8,128)(2,1)S(1)}, bf16[272,256]{1,0:T(8,128)(2,1)S(1)}, u32[]{:S(2)}, u32[]{:S(2)}) collective-permute-start(bf16[272,256]{1,0:T(8,128)(2,1)S(1)} %shard_map.49.joined_ref), channel_id=1, source_target_pairs={{0,6},{2,4},{4,2},{6,0},{8,14},{10,12},{12,10},{14,8},{16,22},{18,... | collective-permute-start | bytes 417800 | tf_op jit(solution)/shard_map/ppermute | solution.py:31
  23.6 6.7 %copy-start = (s32[8]{0:T(128)S(1)}, s32[8]{0:T(128)}, u32[]{:S(2)}) copy-start(s32[8]{0:T(128)} %widths_ref.3) | copy-start | bytes 100
  29.1 3.2 %collective-permute-start.6 = (f32[240,128]{1,0:T(8,128)S(1)}, f32[240,128]{1,0:T(8,128)S(1)}, u32[]{:S(2)}, u32[]{:S(2)}) collective-permute-start(f32[240,128]{1,0:T(8,128)S(1)} %get-tuple-element.27.early_ref), channel_id=1, source_target_pairs={{1,0},{3,2},{5,4},{7,6},{9,8},{11,10},{13,12},{15,14},{17,16},{19,... | collective-permute-start | bytes 368648 | tf_op jit(solution)/shard_map/ppermute | solution.py:26

commit v7 on v6

--- a/solution.py
+++ b/solution.py
@@ -131,7 +131,6 @@
 
 
 def store_choices(slot, outer, inner, flip, me_ref, group_ref, lag_ref, chosen_ref):
-    trials = lag_ref.shape[1]
     subs = lag_ref.shape[0] // (outer * inner)
     nsub = outer * subs
     row = me_ref[0] // inner
@@ -144,7 +143,7 @@
         at_lag = one_where(lags, lag)
         for group in range(GROUPS - 2 if lag == STEP else 0, GROUPS):
             place = (group // 2 * STEP + lag) * nsub + slot * subs
-            chosen_ref[pl.ds(place, subs), pl.ds(group % 2 * trials, trials)] = at_lag * in_group[group]
+            chosen_ref[group % 2, pl.ds(place, subs), :] = at_lag * in_group[group]
 
 
 def choices_kernel(outer, inner, me_ref, group_ref, lag_ref, chosen_ref):
@@ -174,9 +173,10 @@
             for slot in range(outer * pair // pairs, outer * (pair + 1) // pairs):
                 store_choices(slot, outer, inner, then, me_ref, group_ref, lag_ref, other_ref)
         depth = (STEP + (pair == pairs - 1)) * nsub
+        weights = [chosen_ref[odd, pl.ds(pair * STEP * nsub, depth), :] for odd in range(2)]
         both = jnp.dot(
             shifted[:, pl.ds(0, depth)],
-            chosen_ref[pl.ds(pair * STEP * nsub, depth), :],
+            jnp.concatenate(weights, axis=1),
             preferred_element_type=jnp.float32,
         )
         for odd in range(2):
@@ -280,7 +280,7 @@
     split_shape = jax.ShapeDtypeStruct((all_subs, padded), jnp.bfloat16)
     split = call(offsets_kernel, [split_shape, split_shape], [VMEM], (fetched,))
     nsub = outer * sub_dev
-    chosen_shape = jax.ShapeDtypeStruct(((GROUPS // 2 * STEP + 1) * nsub, 2 * padded), jnp.bfloat16)
+    chosen_shape = jax.ShapeDtypeStruct((2, (GROUPS // 2 * STEP + 1) * nsub, padded), jnp.bfloat16)
     chosen = call(
         functools.partial(choices_kernel, outer, inner), chosen_shape, [SMEM, VMEM, VMEM], (me, *split)
     )

time: 34.5 us -> 34.1 us (0.988)
  Pallas kernels: 18.1 us -> 17.6 us
    pallas_call x10, Pallas kernels: 18.1 us -> 17.6 us  [call(): pl.pallas_call(kernel, out_shape=out_shape, in_specs=in_specs, scratch_sh...]
  transfers between devices with their start and end apart: 7 -> 7, of which waited for: 3 -> 3; matrix products, arithmetic and copies ran while one was open for 0% -> 0% of each run, Pallas kernels for 35% -> 34%
where the time goes in v7:
time: 34.1 us; the launch traced here: 33.9 us
  Pallas kernels  17.6 us (52%)
  starting transfers between devices  10.5 us (31%)
  waiting for transfers between devices  5.65 us (17%)
    pallas_call x10, Pallas kernels, call(): pl.pallas_call(kernel, out_shape=out_shape, in_specs=in_specs, scratch_sh...  17.6 us
    ppermute x6, starting transfers between devices, exchanged(): lax.ppermute(value, axis, [(source, source ^ flip) for source in range(co...  9.23 us
    ppermute x6, waiting for transfers between devices, exchanged(): lax.ppermute(value, axis, [(source, source ^ flip) for source in range(co...  4.44 us
    ppermute x1, starting transfers between devices, passed_back(): lax.ppermute(value, axis, [(source, source - 1) for source in range(1, co...  1.29 us
    ppermute x1, waiting for transfers between devices, passed_back(): lax.ppermute(value, axis, [(source, source - 1) for source in range(1, co...  1.21 us
  transfers between devices with their start and end apart: 7, of which 3 were waited for; matrix products, arithmetic and copies ran while one was open for 0% of the time, Pallas kernels for 34%

profile of v7, /device:TPU:0, one launch (start us, length us, event | category | flops | bytes accessed | tf_op | source)
XLA Modules:
  0.0 33.9 jit_solution(5170735576352214025)
XLA Ops:
  0.0 1.9 %shard_map.46 = (bf16[144,128]{1,0:T(8,128)(2,1)S(1)}, s32[128,1024]{1,0:T(8,128)S(1)}) custom-call(s32[1,1024]{1,0:T(1,128)} %bitcast.7, bf16[1024,256]{1,0:T(8,128)(2,1)} %bitcast.6, s32[128,1024]{1,0:T(8,128)} %offsets_ref.1), custom_call_target="tpu_custom_call" | custom-call | bytes 1048576 | tf_op jit(solution)/shard_map/pallas_call | solution.py:243
  1.9 3.1 %collective-permute-start = (bf16[144,128]{1,0:T(8,128)(2,1)S(1)}, bf16[144,128]{1,0:T(8,128)(2,1)S(1)}, u32[]{:S(2)}, u32[]{:S(2)}) collective-permute-start(bf16[144,128]{1,0:T(8,128)(2,1)S(1)} %get-tuple-element.17.refs_0_), channel_id=1, source_target_pairs={{0,8},{2,10},{4,12},{6,14},{8,0},{10,2},{12,4},{14,6},{16,24},{18,... | collective-permute-start | bytes 110600 | tf_op jit(solution)/shard_map/ppermute | solution.py:31
  5.0 2.6 %collective-permute-start.1 = (bf16[144,128]{1,0:T(8,128)(2,1)S(1)}, bf16[144,128]{1,0:T(8,128)(2,1)S(1)}, u32[]{:S(2)}, u32[]{:S(2)}) collective-permute-start(bf16[144,128]{1,0:T(8,128)(2,1)S(1)} %get-tuple-element.17.refs_0_), channel_id=1, source_target_pairs={{0,16},{2,18},{4,20},{6,22},{8,24},{10,26},{12,28},{14,30},{16,0},... | collective-permute-start | bytes 110600 | tf_op jit(solution)/shard_map/ppermute | solution.py:31
  7.6 0.0 collective-permute-start.2
  7.6 0.2 shard_map.47
  7.8 1.1 %shard_map.48.refs_4_.chosen_ref = bf16[2,12544,128]{2,1,0:T(8,128)(2,1)S(1)} custom-call(s32[1]{0:T(128)} %bitcast.me_ref, bf16[1024,128]{1,0:T(8,128)(2,1)S(1)} %get-tuple-element.19.group_ref, bf16[1024,128]{1,0:T(8,128)(2,1)S(1)} %get-tuple-element.20.lag_ref), custom_call_target="tpu_custom_call" | custom-call | bytes 1048576 | tf_op jit(solution)/shard_map/pallas_call | solution.py:243
  8.9 0.0 collective-permute-done.refs_1_
  8.9 1.6 %collective-permute-done.1.refs_2_ = bf16[144,128]{1,0:T(8,128)(2,1)S(1)} collective-permute-done((bf16[144,128]{1,0:T(8,128)(2,1)S(1)}, bf16[144,128]{1,0:T(8,128)(2,1)S(1)}, u32[]{:S(2)}, u32[]{:S(2)}) %collective-permute-start.1) | collective-permute-done | bytes 36896 | tf_op jit(solution)/shard_map/ppermute | solution.py:31
  10.6 2.8 %collective-permute-done.2.refs_3_ = bf16[144,128]{1,0:T(8,128)(2,1)S(1)} collective-permute-done((bf16[144,128]{1,0:T(8,128)(2,1)S(1)}, bf16[144,128]{1,0:T(8,128)(2,1)S(1)}, u32[]{:S(2)}, u32[]{:S(2)}) %collective-permute-start.2) | collective-permute-done | bytes 36896 | tf_op jit(solution)/shard_map/ppermute | solution.py:31
  13.4 0.1 shard_map.49.joined_ref
  13.5 1.6 %collective-permute-start.5 = (bf16[272,256]{1,0:T(8,128)(2,1)S(1)}, bf16[272,256]{1,0:T(8,128)(2,1)S(1)}, u32[]{:S(2)}, u32[]{:S(2)}) collective-permute-start(bf16[272,256]{1,0:T(8,128)(2,1)S(1)} %shard_map.49.joined_ref), channel_id=1, source_target_pairs={{0,2},{2,0},{4,6},{6,4},{8,10},{10,8},{12,14},{14,12},{16,18},{18,... | collective-permute-start | bytes 417800 | tf_op jit(solution)/shard_map/ppermute | solution.py:31
  15.0 1.5 %collective-permute-start.4 = (bf16[272,256]{1,0:T(8,128)(2,1)S(1)}, bf16[272,256]{1,0:T(8,128)(2,1)S(1)}, u32[]{:S(2)}, u32[]{:S(2)}) collective-permute-start(bf16[272,256]{1,0:T(8,128)(2,1)S(1)} %shard_map.49.joined_ref), channel_id=1, source_target_pairs={{0,4},{2,6},{4,0},{6,2},{8,12},{10,14},{12,8},{14,10},{16,20},{18,... | collective-permute-start | bytes 417800 | tf_op jit(solution)/shard_map/ppermute | solution.py:31
  16.6 0.5 %collective-permute-start.3 = (bf16[272,256]{1,0:T(8,128)(2,1)S(1)}, bf16[272,256]{1,0:T(8,128)(2,1)S(1)}, u32[]{:S(2)}, u32[]{:S(2)}) collective-permute-start(bf16[272,256]{1,0:T(8,128)(2,1)S(1)} %shard_map.49.joined_ref), channel_id=1, source_target_pairs={{0,6},{2,4},{4,2},{6,0},{8,14},{10,12},{12,10},{14,8},{16,22},{18,... | collective-permute-start | bytes 417800 | tf_op jit(solution)/shard_map/ppermute | solution.py:31
  17.0 3.1 %shard_map.50 = (f32[368,128]{1,0:T(8,128)S(1)}, bf16[2,12544,128]{2,1,0:T(8,128)(2,1)S(1)}) custom-call(s32[1]{0:T(128)} %bitcast.me_ref, bf16[272,256]{1,0:T(8,128)(2,1)S(1)} %shard_map.49.joined_ref, bf16[1024,128]{1,0:T(8,128)(2,1)S(1)} %get-tuple-element.19.group_ref, bf16[1024,128]{1,0:T(8,128)(2,1)S(1)} %get-tuple-element.20.lag_ref, ...), custom_call_target="tpu_custom_call" | custom-call | flops 1849688064 | bytes 1048576 | tf_op jit(solution)/shard_map/pallas_call | solution.py:243
  20.2 0.0 collective-permute-done.5.joined_ref
  20.2 3.2 %shard_map.51 = (f32[368,128]{1,0:T(8,128)S(1)}, bf16[2,12544,128]{2,1,0:T(8,128)(2,1)S(1)}) custom-call(s32[1]{0:T(128)} %bitcast.me_ref, bf16[272,256]{1,0:T(8,128)(2,1)S(1)} %collective-permute-done.5.joined_ref, bf16[1024,128]{1,0:T(8,128)(2,1)S(1)} %get-tuple-element.19.group_ref, bf16[1024,128]{1,0:T(8,128)(2,1)S(1)} %get-tuple-element.20.lag_ref, ...), custom_call_target="tpu_custom_call" | custom-call | flops 1849688064 | bytes 1048576 | tf_op jit(solution)/shard_map/pallas_call | solution.py:243
  23.4 0.0 collective-permute-done.4.joined_ref
  23.4 0.0 copy-start
  23.4 3.2 %shard_map.52 = (f32[368,128]{1,0:T(8,128)S(1)}, bf16[2,12544,128]{2,1,0:T(8,128)(2,1)S(1)}) custom-call(s32[1]{0:T(128)} %bitcast.me_ref, bf16[272,256]{1,0:T(8,128)(2,1)S(1)} %collective-permute-done.4.joined_ref, bf16[1024,128]{1,0:T(8,128)(2,1)S(1)} %get-tuple-element.19.group_ref, bf16[1024,128]{1,0:T(8,128)(2,1)S(1)} %get-tuple-element.20.lag_ref, ...), custom_call_target="tpu_custom_call" | custom-call | flops 1849688064 | bytes 1048576 | tf_op jit(solution)/shard_map/pallas_call | solution.py:243
  26.6 0.0 collective-permute-done.3.joined_ref
  26.6 2.1 %shard_map.53 = (f32[368,128]{1,0:T(8,128)S(1)}, f32[240,128]{1,0:T(8,128)S(1)}) custom-call(s32[1]{0:T(128)} %bitcast.me_ref, bf16[272,256]{1,0:T(8,128)(2,1)S(1)} %collective-permute-done.3.joined_ref, bf16[1024,128]{1,0:T(8,128)(2,1)S(1)} %get-tuple-element.19.group_ref, bf16[1024,128]{1,0:T(8,128)(2,1)S(1)} %get-tuple-element.20.lag_ref, ...), custom_call_target="tpu_custom_call" | custom-call | flops 1849688064 | bytes 1048576 | tf_op jit(solution)/shard_map/pallas_call | solution.py:243
  28.7 1.3 %collective-permute-start.6 = (f32[240,128]{1,0:T(8,128)S(1)}, f32[240,128]{1,0:T(8,128)S(1)}, u32[]{:S(2)}, u32[]{:S(2)}) collective-permute-start(f32[240,128]{1,0:T(8,128)S(1)} %get-tuple-element.27.early_ref), channel_id=1, source_target_pairs={{1,0},{3,2},{5,4},{7,6},{9,8},{11,10},{13,12},{15,14},{17,16},{19,... | collective-permute-start | bytes 368648 | tf_op jit(solution)/shard_map/ppermute | solution.py:26
  30.0 0.0 copy-done
  30.0 0.7 %shard_map.54.bands_ref = bf16[256,1024]{1,0:T(8,128)(2,1)S(1)} custom-call(s32[8]{0:T(128)S(1)} %copy-done, f32[240,128]{1,0:T(8,128)S(1)} %get-tuple-element.27.early_ref), custom_call_target="tpu_custom_call" | custom-call | bytes 1048576 | tf_op jit(solution)/shard_map/pallas_call | solution.py:243
  30.7 1.2 %collective-permute-done.6.later_ref = f32[240,128]{1,0:T(8,128)S(1)} collective-permute-done((f32[240,128]{1,0:T(8,128)S(1)}, f32[240,128]{1,0:T(8,128)S(1)}, u32[]{:S(2)}, u32[]{:S(2)}) %collective-permute-start.6) | collective-permute-done | bytes 122912 | tf_op jit(solution)/shard_map/ppermute | solution.py:26
  31.9 2.0 %shard_map.55 = f32[128,8,256]{2,1,0:T(8,128)} custom-call(s32[8]{0:T(128)S(1)} %copy-done, bf16[256,1024]{1,0:T(8,128)(2,1)S(1)} %shard_map.54.bands_ref, f32[368,128]{1,0:T(8,128)S(1)} %get-tuple-element.28.sums_ref, f32[240,128]{1,0:T(8,128)S(1)} %collective-permute-done.6.later_ref), custom_call_target="tpu_custom_call" | custom-call | bytes 1048576 | tf_op jit(solution)/shard_map/pallas_call | solution.py:243
Async XLA Ops:
  1.9 7.0 %collective-permute-start = (bf16[144,128]{1,0:T(8,128)(2,1)S(1)}, bf16[144,128]{1,0:T(8,128)(2,1)S(1)}, u32[]{:S(2)}, u32[]{:S(2)}) collective-permute-start(bf16[144,128]{1,0:T(8,128)(2,1)S(1)} %get-tuple-element.17.refs_0_), channel_id=1, source_target_pairs={{0,8},{2,10},{4,12},{6,14},{8,0},{10,2},{12,4},{14,6},{16,24},{18,... | collective-permute-start | bytes 110600 | tf_op jit(solution)/shard_map/ppermute | solution.py:31
  5.0 5.5 %collective-permute-start.1 = (bf16[144,128]{1,0:T(8,128)(2,1)S(1)}, bf16[144,128]{1,0:T(8,128)(2,1)S(1)}, u32[]{:S(2)}, u32[]{:S(2)}) collective-permute-start(bf16[144,128]{1,0:T(8,128)(2,1)S(1)} %get-tuple-element.17.refs_0_), channel_id=1, source_target_pairs={{0,16},{2,18},{4,20},{6,22},{8,24},{10,26},{12,28},{14,30},{16,0},... | collective-permute-start | bytes 110600 | tf_op jit(solution)/shard_map/ppermute | solution.py:31
  7.6 5.8 %collective-permute-start.2 = (bf16[144,128]{1,0:T(8,128)(2,1)S(1)}, bf16[144,128]{1,0:T(8,128)(2,1)S(1)}, u32[]{:S(2)}, u32[]{:S(2)}) collective-permute-start(bf16[144,128]{1,0:T(8,128)(2,1)S(1)} %get-tuple-element.17.refs_0_), channel_id=1, source_target_pairs={{0,24},{2,26},{4,28},{6,30},{8,16},{10,18},{12,20},{14,22},{16,8},... | collective-permute-start | bytes 110600 | tf_op jit(solution)/shard_map/ppermute | solution.py:31
  13.5 6.7 %collective-permute-start.5 = (bf16[272,256]{1,0:T(8,128)(2,1)S(1)}, bf16[272,256]{1,0:T(8,128)(2,1)S(1)}, u32[]{:S(2)}, u32[]{:S(2)}) collective-permute-start(bf16[272,256]{1,0:T(8,128)(2,1)S(1)} %shard_map.49.joined_ref), channel_id=1, source_target_pairs={{0,2},{2,0},{4,6},{6,4},{8,10},{10,8},{12,14},{14,12},{16,18},{18,... | collective-permute-start | bytes 417800 | tf_op jit(solution)/shard_map/ppermute | solution.py:31
  15.0 8.3 %collective-permute-start.4 = (bf16[272,256]{1,0:T(8,128)(2,1)S(1)}, bf16[272,256]{1,0:T(8,128)(2,1)S(1)}, u32[]{:S(2)}, u32[]{:S(2)}) collective-permute-start(bf16[272,256]{1,0:T(8,128)(2,1)S(1)} %shard_map.49.joined_ref), channel_id=1, source_target_pairs={{0,4},{2,6},{4,0},{6,2},{8,12},{10,14},{12,8},{14,10},{16,20},{18,... | collective-permute-start | bytes 417800 | tf_op jit(solution)/shard_map/ppermute | solution.py:31
  16.6 10.0 %collective-permute-start.3 = (bf16[272,256]{1,0:T(8,128)(2,1)S(1)}, bf16[272,256]{1,0:T(8,128)(2,1)S(1)}, u32[]{:S(2)}, u32[]{:S(2)}) collective-permute-start(bf16[272,256]{1,0:T(8,128)(2,1)S(1)} %shard_map.49.joined_ref), channel_id=1, source_target_pairs={{0,6},{2,4},{4,2},{6,0},{8,14},{10,12},{12,10},{14,8},{16,22},{18,... | collective-permute-start | bytes 417800 | tf_op jit(solution)/shard_map/ppermute | solution.py:31
  23.4 6.6 %copy-start = (s32[8]{0:T(128)S(1)}, s32[8]{0:T(128)}, u32[]{:S(2)}) copy-start(s32[8]{0:T(128)} %widths_ref.3) | copy-start | bytes 100
  28.7 3.2 %collective-permute-start.6 = (f32[240,128]{1,0:T(8,128)S(1)}, f32[240,128]{1,0:T(8,128)S(1)}, u32[]{:S(2)}, u32[]{:S(2)}) collective-permute-start(f32[240,128]{1,0:T(8,128)S(1)} %get-tuple-element.27.early_ref), channel_id=1, source_target_pairs={{1,0},{3,2},{5,4},{7,6},{9,8},{11,10},{13,12},{15,14},{17,16},{19,... | collective-permute-start | bytes 368648 | tf_op jit(solution)/shard_map/ppermute | solution.py:26

commit v8 on v7

--- a/solution.py
+++ b/solution.py
@@ -121,41 +121,37 @@
         here = pl.ds(at * LANES, LANES)
         offset = offsets_ref[:, here].astype(jnp.float32).T
         group = jnp.minimum(jnp.floor(offset * (1.0 / STEP)), float(GROUPS - 1))
-        group_ref[here, :] = group.astype(jnp.bfloat16)
-        lag_ref[here, :] = (offset - float(STEP) * group).astype(jnp.bfloat16)
-
-
-def one_where(table, value):
-    one = jnp.bfloat16(1)
-    return jnp.maximum(one - jnp.abs(table - jnp.bfloat16(value)), jnp.bfloat16(0))
-
-
-def store_choices(slot, outer, inner, flip, me_ref, group_ref, lag_ref, chosen_ref):
+        group_ref[here, :] = group
+        lag_ref[here, :] = offset - float(STEP) * group
+
+
+def choices_kernel(outer, inner, flip, me_ref, group_ref, lag_ref, *refs):
+    chosen_ref = refs[-1]
     subs = lag_ref.shape[0] // (outer * inner)
     nsub = outer * subs
     row = me_ref[0] // inner
     column = (me_ref[0] % inner) ^ flip
-    start = pl.multiple_of(((row ^ slot) * inner + column) * subs, subs)
-    groups = group_ref[pl.ds(start, subs), :]
-    lags = lag_ref[pl.ds(start, subs), :]
-    in_group = [one_where(groups, group) for group in range(GROUPS)]
-    for lag in range(STEP + 1):
-        at_lag = one_where(lags, lag)
-        for group in range(GROUPS - 2 if lag == STEP else 0, GROUPS):
-            place = (group // 2 * STEP + lag) * nsub + slot * subs
-            chosen_ref[group % 2, pl.ds(place, subs), :] = at_lag * in_group[group]
-
-
-def choices_kernel(outer, inner, me_ref, group_ref, lag_ref, chosen_ref):
     for slot in range(outer):
-        store_choices(slot, outer, inner, 0, me_ref, group_ref, lag_ref, chosen_ref)
-
-
-def sums_kernel(given, then, outer, inner, me_ref, joined_ref, group_ref, lag_ref, chosen_ref, *refs):
-    before_ref, sums_ref, other_ref = refs[:-2] if given else (None, *refs[:-2])
+        start = pl.multiple_of(((row ^ slot) * inner + column) * subs, subs)
+        for first in range(0, subs, 16):
+            here = pl.ds(pl.multiple_of(start + first, 16), 16)
+            groups = group_ref[here, :]
+            lags = lag_ref[here, :]
+            in_group = [jnp.where(groups == float(group), 1.0, 0.0) for group in range(GROUPS)]
+            for lag in range(STEP + 1):
+                at_lag = jnp.where(lags == float(lag), 1.0, 0.0)
+                for group in range(GROUPS - 2 if lag == STEP else 0, GROUPS):
+                    place = (group // 2 * STEP + lag) * nsub + slot * subs + first
+                    chosen_ref[group % 2, pl.ds(place, 16), :] = (at_lag * in_group[group]).astype(
+                        jnp.bfloat16
+                    )
+
+
+def sums_kernel(given, joined_ref, chosen_ref, *refs):
+    before_ref, sums_ref, *early_ref = refs[:-2] if given else (None, *refs[:-2])
     moving, shifted = refs[-2:]
     span, nsub = joined_ref.shape
-    trials = lag_ref.shape[1]
+    trials = chosen_ref.shape[2]
     rows = span + STEP
     blank = jnp.zeros((STEP, nsub), jnp.float32)
     moving[pl.ds(0, STEP), :] = blank
@@ -169,9 +165,6 @@
         sums_ref[...] = before_ref[...]
     pairs = GROUPS // 2
     for pair in range(pairs):
-        if then < inner:
-            for slot in range(outer * pair // pairs, outer * (pair + 1) // pairs):
-                store_choices(slot, outer, inner, then, me_ref, group_ref, lag_ref, other_ref)
         depth = (STEP + (pair == pairs - 1)) * nsub
         weights = [chosen_ref[odd, pl.ds(pair * STEP * nsub, depth), :] for odd in range(2)]
         both = jnp.dot(
@@ -182,8 +175,8 @@
         for odd in range(2):
             first = STEP * (GROUPS - 1 - 2 * pair - odd)
             sums_ref[pl.ds(first, rows), :] += both[:, odd * trials : (odd + 1) * trials]
-    if then == inner:
-        other_ref[...] = sums_ref[pl.ds(0, other_ref.shape[0]), :]
+    for ref in early_ref:
+        ref[...] = sums_ref[pl.ds(0, ref.shape[0]), :]
 
 
 def bands_kernel(widths_ref, early_ref, bands_ref):
@@ -277,19 +270,27 @@
         ],
     )
     line = [series] + [exchanged(series, "sub", flip * inner) for flip in range(1, outer)]
-    split_shape = jax.ShapeDtypeStruct((all_subs, padded), jnp.bfloat16)
+    split_shape = jax.ShapeDtypeStruct((all_subs, padded), jnp.float32)
     split = call(offsets_kernel, [split_shape, split_shape], [VMEM], (fetched,))
     nsub = outer * sub_dev
     chosen_shape = jax.ShapeDtypeStruct((2, (GROUPS // 2 * STEP + 1) * nsub, padded), jnp.bfloat16)
-    chosen = call(
-        functools.partial(choices_kernel, outer, inner), chosen_shape, [SMEM, VMEM, VMEM], (me, *split)
-    )
+
+    def choices_of(flip, *after):
+        return call(
+            functools.partial(choices_kernel, outer, inner, flip),
+            chosen_shape,
+            [SMEM, VMEM, VMEM] + [ANY] * len(after),
+            (me, *split, *after),
+        )
+
+    soon = [choices_of(flip) for flip in range(inner - 1)]
     joined = call(
         functools.partial(join_packed_kernel if packed else join_kernel, outer),
         jax.ShapeDtypeStruct((span, nsub), jnp.bfloat16),
-        [VMEM] * outer + [ANY],
-        (*line, chosen),
-    )
+        [VMEM] * outer + [ANY] * len(soon),
+        (*line, *soon),
+    )
+    choices = soon + [choices_of(inner - 1, joined)]
     blocks = [joined] + [exchanged(joined, "sub", flip) for flip in range(1, inner)]
     scratch = [
         pltpu.VMEM((span + 2 * STEP, nsub), jnp.float32),
@@ -298,18 +299,17 @@
     flops = 2 * (span + STEP) * nsub * padded * (OMAX + 2)
     sums_shape = jax.ShapeDtypeStruct((length + REACH, padded), jnp.float32)
     early_shape = jax.ShapeDtypeStruct((REACH + WMAX, padded), jnp.float32)
-    before = ()
+    sums = []
     for flip in range(inner):
-        sums, chosen = call(
-            functools.partial(sums_kernel, flip > 0, flip + 1, outer, inner),
-            [sums_shape, early_shape if flip == inner - 1 else chosen_shape],
-            [SMEM] + [VMEM] * (4 + len(before)),
-            (me, blocks[flip], *split, chosen, *before),
+        sums = call(
+            functools.partial(sums_kernel, flip > 0),
+            [sums_shape, early_shape] if flip == inner - 1 else [sums_shape],
+            [VMEM] * (2 + len(sums)),
+            (blocks[flip], choices[flip], *sums),
             scratch,
             flops,
         )
-        before = (sums,)
-    early = chosen
+    sums, early = sums
     later = passed_back(early, "tm")
     bands = call(
         bands_kernel,

time: 34.1 us -> 30.9 us (0.906)
  waiting for transfers between devices: 5.65 us -> 2.49 us
    ppermute x6, waiting for transfers between devices: 4.44 us -> 1.28 us  [exchanged(): lax.ppermute(value, axis, [(source, source ^ flip) for source in range(co...]
    pallas_call x10 -> x13, Pallas kernels: 17.6 us -> 17.5 us  [call(): pl.pallas_call(kernel, out_shape=out_shape, in_specs=in_specs, scratch_sh...]
  transfers between devices with their start and end apart: 7 -> 7, of which waited for: 3 -> 3; matrix products, arithmetic and copies ran while one was open for 0% -> 0% of each run, Pallas kernels for 34% -> 37%
where the time goes in v8:
time: 30.9 us; the launch traced here: 30.7 us
  Pallas kernels  17.5 us (57%)
  starting transfers between devices  10.6 us (34%)
  waiting for transfers between devices  2.49 us (8%)
    pallas_call x13, Pallas kernels, call(): pl.pallas_call(kernel, out_shape=out_shape, in_specs=in_specs, scratch_sh...  17.5 us
    ppermute x6, starting transfers between devices, exchanged(): lax.ppermute(value, axis, [(source, source ^ flip) for source in range(co...  9.31 us
    ppermute x1, starting transfers between devices, passed_back(): lax.ppermute(value, axis, [(source, source - 1) for source in range(1, co...  1.29 us
    ppermute x6, waiting for transfers between devices, exchanged(): lax.ppermute(value, axis, [(source, source ^ flip) for source in range(co...  1.28 us
    ppermute x1, waiting for transfers between devices, passed_back(): lax.ppermute(value, axis, [(source, source - 1) for source in range(1, co...  1.21 us
  transfers between devices with their start and end apart: 7, of which 3 were waited for; matrix products, arithmetic and copies ran while one was open for 0% of the time, Pallas kernels for 37%

profile of v8, /device:TPU:0, one launch (start us, length us, event | category | flops | bytes accessed | tf_op | source)
XLA Modules:
  0.0 30.7 jit_solution(2257976638695845884)
XLA Ops:
  0.0 1.9 %shard_map.46 = (bf16[144,128]{1,0:T(8,128)(2,1)S(1)}, s32[128,1024]{1,0:T(8,128)S(1)}) custom-call(s32[1,1024]{1,0:T(1,128)} %bitcast.7, bf16[1024,256]{1,0:T(8,128)(2,1)} %bitcast.6, s32[128,1024]{1,0:T(8,128)} %offsets_ref.1), custom_call_target="tpu_custom_call" | custom-call | bytes 1048576 | tf_op jit(solution)/shard_map/pallas_call | solution.py:236
  1.9 5.1 %collective-permute-start.2 = (bf16[144,128]{1,0:T(8,128)(2,1)S(1)}, bf16[144,128]{1,0:T(8,128)(2,1)S(1)}, u32[]{:S(2)}, u32[]{:S(2)}) collective-permute-start(bf16[144,128]{1,0:T(8,128)(2,1)S(1)} %get-tuple-element.11.refs_0_), channel_id=1, source_target_pairs={{0,24},{2,26},{4,28},{6,30},{8,16},{10,18},{12,20},{14,22},{16,8},... | collective-permute-start | bytes 110600 | tf_op jit(solution)/shard_map/ppermute | solution.py:31
  7.0 0.0 collective-permute-start.1
  7.1 0.6 %collective-permute-start = (bf16[144,128]{1,0:T(8,128)(2,1)S(1)}, bf16[144,128]{1,0:T(8,128)(2,1)S(1)}, u32[]{:S(2)}, u32[]{:S(2)}) collective-permute-start(bf16[144,128]{1,0:T(8,128)(2,1)S(1)} %get-tuple-element.11.refs_0_), channel_id=1, source_target_pairs={{0,8},{2,10},{4,12},{6,14},{8,0},{10,2},{12,4},{14,6},{16,24},{18,... | collective-permute-start | bytes 110600 | tf_op jit(solution)/shard_map/ppermute | solution.py:31
  7.7 0.2 shard_map.47
  7.9 1.0 %shard_map.50.refs_6_.chosen_ref = bf16[2,12544,128]{2,1,0:T(8,128)(2,1)S(1)} custom-call(s32[1]{0:T(128)} %bitcast.2.me_ref, f32[1024,128]{1,0:T(8,128)S(1)} %get-tuple-element.13.group_ref, f32[1024,128]{1,0:T(8,128)S(1)} %get-tuple-element.14.lag_ref), custom_call_target="tpu_custom_call" | custom-call | bytes 1048576 | tf_op jit(solution)/shard_map/pallas_call | solution.py:236
  8.9 1.0 %shard_map.49.refs_5_.chosen_ref = bf16[2,12544,128]{2,1,0:T(8,128)(2,1)S(1)} custom-call(s32[1]{0:T(128)} %bitcast.2.me_ref, f32[1024,128]{1,0:T(8,128)S(1)} %get-tuple-element.13.group_ref, f32[1024,128]{1,0:T(8,128)S(1)} %get-tuple-element.14.lag_ref), custom_call_target="tpu_custom_call" | custom-call | bytes 1048576 | tf_op jit(solution)/shard_map/pallas_call | solution.py:236
  9.9 1.0 %shard_map.48.refs_4_.chosen_ref = bf16[2,12544,128]{2,1,0:T(8,128)(2,1)S(1)} custom-call(s32[1]{0:T(128)} %bitcast.2.me_ref, f32[1024,128]{1,0:T(8,128)S(1)} %get-tuple-element.13.group_ref, f32[1024,128]{1,0:T(8,128)S(1)} %get-tuple-element.14.lag_ref), custom_call_target="tpu_custom_call" | custom-call | bytes 1048576 | tf_op jit(solution)/shard_map/pallas_call | solution.py:236
  10.9 0.0 collective-permute-done.2.refs_3_
  11.0 0.9 %collective-permute-done.1.refs_2_ = bf16[144,128]{1,0:T(8,128)(2,1)S(1)} collective-permute-done((bf16[144,128]{1,0:T(8,128)(2,1)S(1)}, bf16[144,128]{1,0:T(8,128)(2,1)S(1)}, u32[]{:S(2)}, u32[]{:S(2)}) %collective-permute-start.1) | collective-permute-done | bytes 36896 | tf_op jit(solution)/shard_map/ppermute | solution.py:31
  11.9 0.0 collective-permute-done.refs_1_
  11.9 0.1 shard_map.51.refs_0_.joined_ref
  12.0 1.6 %collective-permute-start.5 = (bf16[272,256]{1,0:T(8,128)(2,1)S(1)}, bf16[272,256]{1,0:T(8,128)(2,1)S(1)}, u32[]{:S(2)}, u32[]{:S(2)}) collective-permute-start(bf16[272,256]{1,0:T(8,128)(2,1)S(1)} %shard_map.51.refs_0_.joined_ref), channel_id=1, source_target_pairs={{0,2},{2,0},{4,6},{6,4},{8,10},{10,8},{12,14},{14,12},{16,18},{18,... | collective-permute-start | bytes 417800 | tf_op jit(solution)/shard_map/ppermute | solution.py:31
  13.6 1.5 %collective-permute-start.4 = (bf16[272,256]{1,0:T(8,128)(2,1)S(1)}, bf16[272,256]{1,0:T(8,128)(2,1)S(1)}, u32[]{:S(2)}, u32[]{:S(2)}) collective-permute-start(bf16[272,256]{1,0:T(8,128)(2,1)S(1)} %shard_map.51.refs_0_.joined_ref), channel_id=1, source_target_pairs={{0,4},{2,6},{4,0},{6,2},{8,12},{10,14},{12,8},{14,10},{16,20},{18,... | collective-permute-start | bytes 417800 | tf_op jit(solution)/shard_map/ppermute | solution.py:31
  15.1 0.5 %collective-permute-start.3 = (bf16[272,256]{1,0:T(8,128)(2,1)S(1)}, bf16[272,256]{1,0:T(8,128)(2,1)S(1)}, u32[]{:S(2)}, u32[]{:S(2)}) collective-permute-start(bf16[272,256]{1,0:T(8,128)(2,1)S(1)} %shard_map.51.refs_0_.joined_ref), channel_id=1, source_target_pairs={{0,6},{2,4},{4,2},{6,0},{8,14},{10,12},{12,10},{14,8},{16,22},{18,... | collective-permute-start | bytes 417800 | tf_op jit(solution)/shard_map/ppermute | solution.py:31
  15.6 1.0 %shard_map.52.chosen_ref = bf16[2,12544,128]{2,1,0:T(8,128)(2,1)S(1)} custom-call(s32[1]{0:T(128)} %bitcast.2.me_ref, f32[1024,128]{1,0:T(8,128)S(1)} %get-tuple-element.13.group_ref, f32[1024,128]{1,0:T(8,128)S(1)} %get-tuple-element.14.lag_ref, bf16[272,256]{1,0:T(8,128)(2,1)S(1)} %shard_map.51.refs_0_.joined_ref), custom_call_target="tpu_custom_call" | custom-call | bytes 1048576 | tf_op jit(solution)/shard_map/pallas_call | solution.py:236
  16.6 2.1 %shard_map.53.refs_0_ = f32[368,128]{1,0:T(8,128)S(1)} custom-call(bf16[272,256]{1,0:T(8,128)(2,1)S(1)} %shard_map.51.refs_0_.joined_ref, bf16[2,12544,128]{2,1,0:T(8,128)(2,1)S(1)} %shard_map.48.refs_4_.chosen_ref), custom_call_target="tpu_custom_call" | custom-call | flops 1849688064 | bytes 1048576 | tf_op jit(solution)/shard_map/pallas_call | solution.py:236
  18.7 0.0 collective-permute-done.5.joined_ref
  18.7 2.1 %shard_map.54.refs_0_ = f32[368,128]{1,0:T(8,128)S(1)} custom-call(bf16[272,256]{1,0:T(8,128)(2,1)S(1)} %collective-permute-done.5.joined_ref, bf16[2,12544,128]{2,1,0:T(8,128)(2,1)S(1)} %shard_map.49.refs_5_.chosen_ref, f32[368,128]{1,0:T(8,128)S(1)} %shard_map.53.refs_0_), custom_call_target="tpu_custom_call" | custom-call | flops 1849688064 | bytes 1048576 | tf_op jit(solution)/shard_map/pallas_call | solution.py:236
  20.9 0.0 copy-start
  20.9 0.3 %collective-permute-done.4.joined_ref = bf16[272,256]{1,0:T(8,128)(2,1)S(1)} collective-permute-done((bf16[272,256]{1,0:T(8,128)(2,1)S(1)}, bf16[272,256]{1,0:T(8,128)(2,1)S(1)}, u32[]{:S(2)}, u32[]{:S(2)}) %collective-permute-start.4) | collective-permute-done | bytes 139296 | tf_op jit(solution)/shard_map/ppermute | solution.py:31
  21.2 2.1 %shard_map.55.refs_0_ = f32[368,128]{1,0:T(8,128)S(1)} custom-call(bf16[272,256]{1,0:T(8,128)(2,1)S(1)} %collective-permute-done.4.joined_ref, bf16[2,12544,128]{2,1,0:T(8,128)(2,1)S(1)} %shard_map.50.refs_6_.chosen_ref, f32[368,128]{1,0:T(8,128)S(1)} %shard_map.54.refs_0_), custom_call_target="tpu_custom_call" | custom-call | flops 1849688064 | bytes 1048576 | tf_op jit(solution)/shard_map/pallas_call | solution.py:236
  23.3 0.0 collective-permute-done.3.joined_ref
  23.3 2.1 %shard_map.56 = (f32[368,128]{1,0:T(8,128)S(1)}, f32[240,128]{1,0:T(8,128)S(1)}) custom-call(bf16[272,256]{1,0:T(8,128)(2,1)S(1)} %collective-permute-done.3.joined_ref, bf16[2,12544,128]{2,1,0:T(8,128)(2,1)S(1)} %shard_map.52.chosen_ref, f32[368,128]{1,0:T(8,128)S(1)} %shard_map.55.refs_0_), custom_call_target="tpu_custom_call" | custom-call | flops 1849688064 | bytes 1048576 | tf_op jit(solution)/shard_map/pallas_call | solution.py:236
  25.5 1.3 %collective-permute-start.6 = (f32[240,128]{1,0:T(8,128)S(1)}, f32[240,128]{1,0:T(8,128)S(1)}, u32[]{:S(2)}, u32[]{:S(2)}) collective-permute-start(f32[240,128]{1,0:T(8,128)S(1)} %get-tuple-element.15.early_ref), channel_id=1, source_target_pairs={{1,0},{3,2},{5,4},{7,6},{9,8},{11,10},{13,12},{15,14},{17,16},{19,... | collective-permute-start | bytes 368648 | tf_op jit(solution)/shard_map/ppermute | solution.py:26
  26.8 0.0 copy-done
  26.8 0.7 %shard_map.57.bands_ref = bf16[256,1024]{1,0:T(8,128)(2,1)S(1)} custom-call(s32[8]{0:T(128)S(1)} %copy-done, f32[240,128]{1,0:T(8,128)S(1)} %get-tuple-element.15.early_ref), custom_call_target="tpu_custom_call" | custom-call | bytes 1048576 | tf_op jit(solution)/shard_map/pallas_call | solution.py:236
  27.5 1.2 %collective-permute-done.6.later_ref = f32[240,128]{1,0:T(8,128)S(1)} collective-permute-done((f32[240,128]{1,0:T(8,128)S(1)}, f32[240,128]{1,0:T(8,128)S(1)}, u32[]{:S(2)}, u32[]{:S(2)}) %collective-permute-start.6) | collective-permute-done | bytes 122912 | tf_op jit(solution)/shard_map/ppermute | solution.py:26
  28.7 2.0 %shard_map.58 = f32[128,8,256]{2,1,0:T(8,128)} custom-call(s32[8]{0:T(128)S(1)} %copy-done, bf16[256,1024]{1,0:T(8,128)(2,1)S(1)} %shard_map.57.bands_ref, f32[368,128]{1,0:T(8,128)S(1)} %get-tuple-element.16.sums_ref, f32[240,128]{1,0:T(8,128)S(1)} %collective-permute-done.6.later_ref), custom_call_target="tpu_custom_call" | custom-call | bytes 1048576 | tf_op jit(solution)/shard_map/pallas_call | solution.py:236
Async XLA Ops:
  1.9 9.0 %collective-permute-start.2 = (bf16[144,128]{1,0:T(8,128)(2,1)S(1)}, bf16[144,128]{1,0:T(8,128)(2,1)S(1)}, u32[]{:S(2)}, u32[]{:S(2)}) collective-permute-start(bf16[144,128]{1,0:T(8,128)(2,1)S(1)} %get-tuple-element.11.refs_0_), channel_id=1, source_target_pairs={{0,24},{2,26},{4,28},{6,30},{8,16},{10,18},{12,20},{14,22},{16,8},... | collective-permute-start | bytes 110600 | tf_op jit(solution)/shard_map/ppermute | solution.py:31
  7.0 4.9 %collective-permute-start.1 = (bf16[144,128]{1,0:T(8,128)(2,1)S(1)}, bf16[144,128]{1,0:T(8,128)(2,1)S(1)}, u32[]{:S(2)}, u32[]{:S(2)}) collective-permute-start(bf16[144,128]{1,0:T(8,128)(2,1)S(1)} %get-tuple-element.11.refs_0_), channel_id=1, source_target_pairs={{0,16},{2,18},{4,20},{6,22},{8,24},{10,26},{12,28},{14,30},{16,0},... | collective-permute-start | bytes 110600 | tf_op jit(solution)/shard_map/ppermute | solution.py:31
  7.1 4.9 %collective-permute-start = (bf16[144,128]{1,0:T(8,128)(2,1)S(1)}, bf16[144,128]{1,0:T(8,128)(2,1)S(1)}, u32[]{:S(2)}, u32[]{:S(2)}) collective-permute-start(bf16[144,128]{1,0:T(8,128)(2,1)S(1)} %get-tuple-element.11.refs_0_), channel_id=1, source_target_pairs={{0,8},{2,10},{4,12},{6,14},{8,0},{10,2},{12,4},{14,6},{16,24},{18,... | collective-permute-start | bytes 110600 | tf_op jit(solution)/shard_map/ppermute | solution.py:31
  12.0 6.7 %collective-permute-start.5 = (bf16[272,256]{1,0:T(8,128)(2,1)S(1)}, bf16[272,256]{1,0:T(8,128)(2,1)S(1)}, u32[]{:S(2)}, u32[]{:S(2)}) collective-permute-start(bf16[272,256]{1,0:T(8,128)(2,1)S(1)} %shard_map.51.refs_0_.joined_ref), channel_id=1, source_target_pairs={{0,2},{2,0},{4,6},{6,4},{8,10},{10,8},{12,14},{14,12},{16,18},{18,... | collective-permute-start | bytes 417800 | tf_op jit(solution)/shard_map/ppermute | solution.py:31
  13.6 7.6 %collective-permute-start.4 = (bf16[272,256]{1,0:T(8,128)(2,1)S(1)}, bf16[272,256]{1,0:T(8,128)(2,1)S(1)}, u32[]{:S(2)}, u32[]{:S(2)}) collective-permute-start(bf16[272,256]{1,0:T(8,128)(2,1)S(1)} %shard_map.51.refs_0_.joined_ref), channel_id=1, source_target_pairs={{0,4},{2,6},{4,0},{6,2},{8,12},{10,14},{12,8},{14,10},{16,20},{18,... | collective-permute-start | bytes 417800 | tf_op jit(solution)/shard_map/ppermute | solution.py:31
  15.1 8.2 %collective-permute-start.3 = (bf16[272,256]{1,0:T(8,128)(2,1)S(1)}, bf16[272,256]{1,0:T(8,128)(2,1)S(1)}, u32[]{:S(2)}, u32[]{:S(2)}) collective-permute-start(bf16[272,256]{1,0:T(8,128)(2,1)S(1)} %shard_map.51.refs_0_.joined_ref), channel_id=1, source_target_pairs={{0,6},{2,4},{4,2},{6,0},{8,14},{10,12},{12,10},{14,8},{16,22},{18,... | collective-permute-start | bytes 417800 | tf_op jit(solution)/shard_map/ppermute | solution.py:31
  20.9 5.9 %copy-start = (s32[8]{0:T(128)S(1)}, s32[8]{0:T(128)}, u32[]{:S(2)}) copy-start(s32[8]{0:T(128)} %widths_ref.3) | copy-start | bytes 100
  25.5 3.2 %collective-permute-start.6 = (f32[240,128]{1,0:T(8,128)S(1)}, f32[240,128]{1,0:T(8,128)S(1)}, u32[]{:S(2)}, u32[]{:S(2)}) collective-permute-start(f32[240,128]{1,0:T(8,128)S(1)} %get-tuple-element.15.early_ref), channel_id=1, source_target_pairs={{1,0},{3,2},{5,4},{7,6},{9,8},{11,10},{13,12},{15,14},{17,16},{19,... | collective-permute-start | bytes 368648 | tf_op jit(solution)/shard_map/ppermute | solution.py:26

commit v9 on v8

--- a/solution.py
+++ b/solution.py
@@ -116,27 +116,25 @@
             joined_ref[pl.ds(first, count), pl.ds(at * LANES, LANES)] = tile[:count].astype(jnp.bfloat16)
 
 
-def offsets_kernel(offsets_ref, group_ref, lag_ref):
+def offsets_kernel(offsets_ref, table_ref):
     for at in range(offsets_ref.shape[1] // LANES):
         here = pl.ds(at * LANES, LANES)
-        offset = offsets_ref[:, here].astype(jnp.float32).T
-        group = jnp.minimum(jnp.floor(offset * (1.0 / STEP)), float(GROUPS - 1))
-        group_ref[here, :] = group
-        lag_ref[here, :] = offset - float(STEP) * group
-
-
-def choices_kernel(outer, inner, flip, me_ref, group_ref, lag_ref, *refs):
-    chosen_ref = refs[-1]
-    subs = lag_ref.shape[0] // (outer * inner)
+        table_ref[here, :] = offsets_ref[:, here].astype(jnp.float32).T
+
+
+def slot_start(slot, flip, outer, inner, subs, me):
+    return pl.multiple_of((((me // inner) ^ slot) * inner + ((me % inner) ^ flip)) * subs, subs)
+
+
+def choices_kernel(outer, inner, me_ref, table_ref, chosen_ref):
+    subs = table_ref.shape[0] // (outer * inner)
     nsub = outer * subs
-    row = me_ref[0] // inner
-    column = (me_ref[0] % inner) ^ flip
     for slot in range(outer):
-        start = pl.multiple_of(((row ^ slot) * inner + column) * subs, subs)
+        start = slot_start(slot, 0, outer, inner, subs, me_ref[0])
         for first in range(0, subs, 16):
-            here = pl.ds(pl.multiple_of(start + first, 16), 16)
-            groups = group_ref[here, :]
-            lags = lag_ref[here, :]
+            offset = table_ref[pl.ds(pl.multiple_of(start + first, 16), 16), :]
+            groups = jnp.minimum(jnp.floor(offset * (1.0 / STEP)), float(GROUPS - 1))
+            lags = offset - float(STEP) * groups
             in_group = [jnp.where(groups == float(group), 1.0, 0.0) for group in range(GROUPS)]
             for lag in range(STEP + 1):
                 at_lag = jnp.where(lags == float(lag), 1.0, 0.0)
@@ -147,36 +145,76 @@
                     )
 
 
-def sums_kernel(given, joined_ref, chosen_ref, *refs):
-    before_ref, sums_ref, *early_ref = refs[:-2] if given else (None, *refs[:-2])
-    moving, shifted = refs[-2:]
+def shift_series(joined_ref, moving, shifted):
     span, nsub = joined_ref.shape
-    trials = chosen_ref.shape[2]
-    rows = span + STEP
     blank = jnp.zeros((STEP, nsub), jnp.float32)
     moving[pl.ds(0, STEP), :] = blank
     moving[pl.ds(STEP, span), :] = joined_ref[...].astype(jnp.float32)
     moving[pl.ds(STEP + span, STEP), :] = blank
     for lag in range(STEP + 1):
-        shifted[:, pl.ds(lag * nsub, nsub)] = moving[pl.ds(lag, rows), :].astype(jnp.bfloat16)
-    if before_ref is None:
-        sums_ref[...] = jnp.zeros_like(sums_ref)
-    else:
-        sums_ref[...] = before_ref[...]
-    pairs = GROUPS // 2
-    for pair in range(pairs):
-        depth = (STEP + (pair == pairs - 1)) * nsub
+        shifted[:, pl.ds(lag * nsub, nsub)] = moving[pl.ds(lag, span + STEP), :].astype(jnp.bfloat16)
+
+
+def add_pair(total, pair, both):
+    rows, trials = both.shape[0], both.shape[1] // 2
+    for odd in range(2):
+        first = STEP * (GROUPS - 1 - 2 * pair - odd)
+        total[pl.ds(first, rows), :] += both[:, odd * trials : (odd + 1) * trials]
+
+
+def first_sums_kernel(joined_ref, chosen_ref, sums_ref, moving, shifted):
+    nsub = joined_ref.shape[1]
+    shift_series(joined_ref, moving, shifted)
+    sums_ref[...] = jnp.zeros_like(sums_ref)
+    for pair in range(GROUPS // 2):
+        depth = (STEP + (pair == GROUPS // 2 - 1)) * nsub
         weights = [chosen_ref[odd, pl.ds(pair * STEP * nsub, depth), :] for odd in range(2)]
+        add_pair(
+            sums_ref,
+            pair,
+            jnp.dot(
+                shifted[:, pl.ds(0, depth)],
+                jnp.concatenate(weights, axis=1),
+                preferred_element_type=jnp.float32,
+            ),
+        )
+
+
+def more_sums_kernel(outer, inner, flip, me_ref, joined_ref, table_ref, before_ref, sums_ref, *refs):
+    *early_ref, moving, shifted, total, table = refs[: -(GROUPS // 2)]
+    weights = refs[-(GROUPS // 2) :]
+    nsub = joined_ref.shape[1]
+    subs = nsub // outer
+    trials = table_ref.shape[1]
+    for slot in range(outer):
+        start = slot_start(slot, flip, outer, inner, subs, me_ref[0])
+        table[pl.ds(slot * subs, subs), :] = table_ref[pl.ds(start, subs), :]
+    total[...] = before_ref[...]
+    shift_series(joined_ref, moving, shifted)
+
+    def make(pair):
+        for first in range(0, nsub, 16):
+            offset = table[pl.ds(first, 16), :]
+            for lag in range(weights[pair].shape[0] // nsub):
+                for odd in range(2):
+                    wanted = float(STEP * (2 * pair + odd) + lag) if lag < STEP or odd else -1.0
+                    weights[pair][pl.ds(lag * nsub + first, 16), pl.ds(odd * trials, trials)] = jnp.where(
+                        offset == wanted, 1.0, 0.0
+                    ).astype(jnp.bfloat16)
+
+    make(0)
+    for pair in range(GROUPS // 2):
+        if pair + 1 < GROUPS // 2:
+            make(pair + 1)
         both = jnp.dot(
-            shifted[:, pl.ds(0, depth)],
-            jnp.concatenate(weights, axis=1),
+            shifted[:, pl.ds(0, weights[pair].shape[0])],
+            weights[pair][...],
             preferred_element_type=jnp.float32,
         )
-        for odd in range(2):
-            first = STEP * (GROUPS - 1 - 2 * pair - odd)
-            sums_ref[pl.ds(first, rows), :] += both[:, odd * trials : (odd + 1) * trials]
+        add_pair(total, pair, both)
+    sums_ref[...] = total[...]
     for ref in early_ref:
-        ref[...] = sums_ref[pl.ds(0, ref.shape[0]), :]
+        ref[...] = total[pl.ds(0, ref.shape[0]), :]
 
 
 def bands_kernel(widths_ref, early_ref, bands_ref):
@@ -238,7 +276,7 @@
         out_shape=out_shape,
         in_specs=in_specs,
         scratch_shapes=list(scratch),
-        compiler_params=pltpu.CompilerParams(vmem_limit_bytes=12 << 20),
+        compiler_params=pltpu.CompilerParams(vmem_limit_bytes=16 << 20),
         cost_estimate=pl.CostEstimate(flops=flops, bytes_accessed=1 << 20, transcendentals=0),
         **options,
     )(*args)
@@ -270,27 +308,20 @@
         ],
     )
     line = [series] + [exchanged(series, "sub", flip * inner) for flip in range(1, outer)]
-    split_shape = jax.ShapeDtypeStruct((all_subs, padded), jnp.float32)
-    split = call(offsets_kernel, [split_shape, split_shape], [VMEM], (fetched,))
     nsub = outer * sub_dev
-    chosen_shape = jax.ShapeDtypeStruct((2, (GROUPS // 2 * STEP + 1) * nsub, padded), jnp.bfloat16)
-
-    def choices_of(flip, *after):
-        return call(
-            functools.partial(choices_kernel, outer, inner, flip),
-            chosen_shape,
-            [SMEM, VMEM, VMEM] + [ANY] * len(after),
-            (me, *split, *after),
-        )
-
-    soon = [choices_of(flip) for flip in range(inner - 1)]
+    table = call(offsets_kernel, jax.ShapeDtypeStruct((all_subs, padded), jnp.float32), [VMEM], (fetched,))
+    chosen = call(
+        functools.partial(choices_kernel, outer, inner),
+        jax.ShapeDtypeStruct((2, (GROUPS // 2 * STEP + 1) * nsub, padded), jnp.bfloat16),
+        [SMEM, VMEM],
+        (me, table),
+    )
     joined = call(
         functools.partial(join_packed_kernel if packed else join_kernel, outer),
         jax.ShapeDtypeStruct((span, nsub), jnp.bfloat16),
-        [VMEM] * outer + [ANY] * len(soon),
-        (*line, *soon),
-    )
-    choices = soon + [choices_of(inner - 1, joined)]
+        [VMEM] * outer + [ANY],
+        (*line, chosen),
+    )
     blocks = [joined] + [exchanged(joined, "sub", flip) for flip in range(1, inner)]
     scratch = [
         pltpu.VMEM((span + 2 * STEP, nsub), jnp.float32),
@@ -299,17 +330,25 @@
     flops = 2 * (span + STEP) * nsub * padded * (OMAX + 2)
     sums_shape = jax.ShapeDtypeStruct((length + REACH, padded), jnp.float32)
     early_shape = jax.ShapeDtypeStruct((REACH + WMAX, padded), jnp.float32)
-    sums = []
-    for flip in range(inner):
-        sums = call(
-            functools.partial(sums_kernel, flip > 0),
+    sums = call(first_sums_kernel, sums_shape, [VMEM, VMEM], (joined, chosen), scratch, flops)
+    for flip in range(1, inner):
+        sums, *early = call(
+            functools.partial(more_sums_kernel, outer, inner, flip),
             [sums_shape, early_shape] if flip == inner - 1 else [sums_shape],
-            [VMEM] * (2 + len(sums)),
-            (blocks[flip], choices[flip], *sums),
-            scratch,
+            [SMEM, VMEM, VMEM, VMEM],
+            (me, blocks[flip], table, sums),
+            [
+                *scratch,
+                pltpu.VMEM((length + REACH, padded), jnp.float32),
+                pltpu.VMEM((nsub, padded), jnp.float32),
+                *(
+                    pltpu.VMEM(((STEP + (pair == GROUPS // 2 - 1)) * nsub, 2 * padded), jnp.bfloat16)
+                    for pair in range(GROUPS // 2)
+                ),
+            ],
             flops,
         )
-    sums, early = sums
+    early = early[0]
     later = passed_back(early, "tm")
     bands = call(
         bands_kernel,

time: 30.9 us -> 32.8 us (1.061)
  waiting for transfers between devices: 2.49 us -> 5.02 us
  Pallas kernels: 17.5 us -> 16.9 us
    ppermute x6, waiting for transfers between devices: 1.28 us -> 3.81 us  [exchanged(): lax.ppermute(value, axis, [(source, source ^ flip) for source in range(co...]
    pallas_call x13 -> x10, Pallas kernels: 17.5 us -> 16.9 us  [call(): pl.pallas_call(kernel, out_shape=out_shape, in_specs=in_specs, scratch_sh...]
  transfers between devices with their start and end apart: 7 -> 7, of which waited for: 3 -> 4; matrix products, arithmetic and copies ran while one was open for 0% -> 0% of each run, Pallas kernels for 37% -> 30%
where the time goes in v9:
time: 32.8 us; the launch traced here: 32.6 us
  Pallas kernels  16.9 us (52%)
  starting transfers between devices  10.6 us (32%)
  waiting for transfers between devices  5.02 us (15%)
    pallas_call x10, Pallas kernels, call(): pl.pallas_call(kernel, out_shape=out_shape, in_specs=in_specs, scratch_sh...  16.9 us
    ppermute x6, starting transfers between devices, exchanged(): lax.ppermute(value, axis, [(source, source ^ flip) for source in range(co...  9.31 us
    ppermute x6, waiting for transfers between devices, exchanged(): lax.ppermute(value, axis, [(source, source ^ flip) for source in range(co...  3.81 us
    ppermute x1, starting transfers between devices, passed_back(): lax.ppermute(value, axis, [(source, source - 1) for source in range(1, co...  1.29 us
    ppermute x1, waiting for transfers between devices, passed_back(): lax.ppermute(value, axis, [(source, source - 1) for source in range(1, co...  1.21 us
  transfers between devices with their start and end apart: 7, of which 4 were waited for; matrix products, arithmetic and copies ran while one was open for 0% of the time, Pallas kernels for 30%

profile of v9, /device:TPU:0, one launch (start us, length us, event | category | flops | bytes accessed | tf_op | source)
XLA Modules:
  0.0 32.6 jit_solution(14197121570875831952)
XLA Ops:
  0.0 1.9 %shard_map.46 = (bf16[144,128]{1,0:T(8,128)(2,1)S(1)}, s32[128,1024]{1,0:T(8,128)S(1)}) custom-call(s32[1,1024]{1,0:T(1,128)} %bitcast.7, bf16[1024,256]{1,0:T(8,128)(2,1)} %bitcast.6, s32[128,1024]{1,0:T(8,128)} %offsets_ref.1), custom_call_target="tpu_custom_call" | custom-call | bytes 1048576 | tf_op jit(solution)/shard_map/pallas_call | solution.py:274
  1.9 5.1 %collective-permute-start.2 = (bf16[144,128]{1,0:T(8,128)(2,1)S(1)}, bf16[144,128]{1,0:T(8,128)(2,1)S(1)}, u32[]{:S(2)}, u32[]{:S(2)}) collective-permute-start(bf16[144,128]{1,0:T(8,128)(2,1)S(1)} %get-tuple-element.9.refs_0_), channel_id=1, source_target_pairs={{0,24},{2,26},{4,28},{6,30},{8,16},{10,18},{12,20},{14,22},{16,8},... | collective-permute-start | bytes 110600 | tf_op jit(solution)/shard_map/ppermute | solution.py:31
  7.0 0.0 collective-permute-start.1
  7.1 0.6 %collective-permute-start = (bf16[144,128]{1,0:T(8,128)(2,1)S(1)}, bf16[144,128]{1,0:T(8,128)(2,1)S(1)}, u32[]{:S(2)}, u32[]{:S(2)}) collective-permute-start(bf16[144,128]{1,0:T(8,128)(2,1)S(1)} %get-tuple-element.9.refs_0_), channel_id=1, source_target_pairs={{0,8},{2,10},{4,12},{6,14},{8,0},{10,2},{12,4},{14,6},{16,24},{18,... | collective-permute-start | bytes 110600 | tf_op jit(solution)/shard_map/ppermute | solution.py:31
  7.7 0.2 shard_map.47.table_ref
  7.9 1.0 %shard_map.48.refs_4_.chosen_ref = bf16[2,12544,128]{2,1,0:T(8,128)(2,1)S(1)} custom-call(s32[1]{0:T(128)} %bitcast.me_ref, f32[1024,128]{1,0:T(8,128)S(1)} %shard_map.47.table_ref), custom_call_target="tpu_custom_call" | custom-call | bytes 1048576 | tf_op jit(solution)/shard_map/pallas_call | solution.py:274
  8.9 0.1 collective-permute-done.2.refs_3_
  9.0 2.9 %collective-permute-done.1.refs_2_ = bf16[144,128]{1,0:T(8,128)(2,1)S(1)} collective-permute-done((bf16[144,128]{1,0:T(8,128)(2,1)S(1)}, bf16[144,128]{1,0:T(8,128)(2,1)S(1)}, u32[]{:S(2)}, u32[]{:S(2)}) %collective-permute-start.1) | collective-permute-done | bytes 36896 | tf_op jit(solution)/shard_map/ppermute | solution.py:31
  11.9 0.0 collective-permute-done.refs_1_
  11.9 0.1 shard_map.49.joined_ref
  12.0 1.6 %collective-permute-start.5 = (bf16[272,256]{1,0:T(8,128)(2,1)S(1)}, bf16[272,256]{1,0:T(8,128)(2,1)S(1)}, u32[]{:S(2)}, u32[]{:S(2)}) collective-permute-start(bf16[272,256]{1,0:T(8,128)(2,1)S(1)} %shard_map.49.joined_ref), channel_id=1, source_target_pairs={{0,2},{2,0},{4,6},{6,4},{8,10},{10,8},{12,14},{14,12},{16,18},{18,... | collective-permute-start | bytes 417800 | tf_op jit(solution)/shard_map/ppermute | solution.py:31
  13.6 1.5 %collective-permute-start.4 = (bf16[272,256]{1,0:T(8,128)(2,1)S(1)}, bf16[272,256]{1,0:T(8,128)(2,1)S(1)}, u32[]{:S(2)}, u32[]{:S(2)}) collective-permute-start(bf16[272,256]{1,0:T(8,128)(2,1)S(1)} %shard_map.49.joined_ref), channel_id=1, source_target_pairs={{0,4},{2,6},{4,0},{6,2},{8,12},{10,14},{12,8},{14,10},{16,20},{18,... | collective-permute-start | bytes 417800 | tf_op jit(solution)/shard_map/ppermute | solution.py:31
  15.1 0.5 %collective-permute-start.3 = (bf16[272,256]{1,0:T(8,128)(2,1)S(1)}, bf16[272,256]{1,0:T(8,128)(2,1)S(1)}, u32[]{:S(2)}, u32[]{:S(2)}) collective-permute-start(bf16[272,256]{1,0:T(8,128)(2,1)S(1)} %shard_map.49.joined_ref), channel_id=1, source_target_pairs={{0,6},{2,4},{4,2},{6,0},{8,14},{10,12},{12,10},{14,8},{16,22},{18,... | collective-permute-start | bytes 417800 | tf_op jit(solution)/shard_map/ppermute | solution.py:31
  15.6 2.1 %shard_map.50.before_ref = f32[368,128]{1,0:T(8,128)S(1)} custom-call(bf16[272,256]{1,0:T(8,128)(2,1)S(1)} %shard_map.49.joined_ref, bf16[2,12544,128]{2,1,0:T(8,128)(2,1)S(1)} %shard_map.48.refs_4_.chosen_ref), custom_call_target="tpu_custom_call" | custom-call | flops 1849688064 | bytes 1048576 | tf_op jit(solution)/shard_map/pallas_call | solution.py:274
  17.6 0.8 %collective-permute-done.5.joined_ref = bf16[272,256]{1,0:T(8,128)(2,1)S(1)} collective-permute-done((bf16[272,256]{1,0:T(8,128)(2,1)S(1)}, bf16[272,256]{1,0:T(8,128)(2,1)S(1)}, u32[]{:S(2)}, u32[]{:S(2)}) %collective-permute-start.5) | collective-permute-done | bytes 139296 | tf_op jit(solution)/shard_map/ppermute | solution.py:31
  18.5 3.0 %shard_map.51.before_ref = f32[368,128]{1,0:T(8,128)S(1)} custom-call(s32[1]{0:T(128)} %bitcast.me_ref, bf16[272,256]{1,0:T(8,128)(2,1)S(1)} %collective-permute-done.5.joined_ref, f32[1024,128]{1,0:T(8,128)S(1)} %shard_map.47.table_ref, f32[368,128]{1,0:T(8,128)S(1)} %shard_map.50.before_ref), custom_call_target="tpu_custom_call" | custom-call | flops 1849688064 | bytes 1048576 | tf_op jit(solution)/shard_map/pallas_call | solution.py:274
  21.4 0.0 copy-start
  21.4 0.0 collective-permute-done.4.joined_ref
  21.4 3.0 %shard_map.52.before_ref = f32[368,128]{1,0:T(8,128)S(1)} custom-call(s32[1]{0:T(128)} %bitcast.me_ref, bf16[272,256]{1,0:T(8,128)(2,1)S(1)} %collective-permute-done.4.joined_ref, f32[1024,128]{1,0:T(8,128)S(1)} %shard_map.47.table_ref, f32[368,128]{1,0:T(8,128)S(1)} %shard_map.51.before_ref), custom_call_target="tpu_custom_call" | custom-call | flops 1849688064 | bytes 1048576 | tf_op jit(solution)/shard_map/pallas_call | solution.py:274
  24.4 0.0 collective-permute-done.3.joined_ref
  24.4 3.0 %shard_map.53 = (f32[368,128]{1,0:T(8,128)S(1)}, f32[240,128]{1,0:T(8,128)S(1)}) custom-call(s32[1]{0:T(128)} %bitcast.me_ref, bf16[272,256]{1,0:T(8,128)(2,1)S(1)} %collective-permute-done.3.joined_ref, f32[1024,128]{1,0:T(8,128)S(1)} %shard_map.47.table_ref, f32[368,128]{1,0:T(8,128)S(1)} %shard_map.52.before_ref), custom_call_target="tpu_custom_call" | custom-call | flops 1849688064 | bytes 1048576 | tf_op jit(solution)/shard_map/pallas_call | solution.py:274
  27.4 1.3 %collective-permute-start.6 = (f32[240,128]{1,0:T(8,128)S(1)}, f32[240,128]{1,0:T(8,128)S(1)}, u32[]{:S(2)}, u32[]{:S(2)}) collective-permute-start(f32[240,128]{1,0:T(8,128)S(1)} %get-tuple-element.11.early_ref), channel_id=1, source_target_pairs={{1,0},{3,2},{5,4},{7,6},{9,8},{11,10},{13,12},{15,14},{17,16},{19,... | collective-permute-start | bytes 368648 | tf_op jit(solution)/shard_map/ppermute | solution.py:26
  28.7 0.0 copy-done
  28.7 0.7 %shard_map.54.bands_ref = bf16[256,1024]{1,0:T(8,128)(2,1)S(1)} custom-call(s32[8]{0:T(128)S(1)} %copy-done, f32[240,128]{1,0:T(8,128)S(1)} %get-tuple-element.11.early_ref), custom_call_target="tpu_custom_call" | custom-call | bytes 1048576 | tf_op jit(solution)/shard_map/pallas_call | solution.py:274
  29.4 1.2 %collective-permute-done.6.later_ref = f32[240,128]{1,0:T(8,128)S(1)} collective-permute-done((f32[240,128]{1,0:T(8,128)S(1)}, f32[240,128]{1,0:T(8,128)S(1)}, u32[]{:S(2)}, u32[]{:S(2)}) %collective-permute-start.6) | collective-permute-done | bytes 122912 | tf_op jit(solution)/shard_map/ppermute | solution.py:26
  30.6 2.0 %shard_map.55 = f32[128,8,256]{2,1,0:T(8,128)} custom-call(s32[8]{0:T(128)S(1)} %copy-done, bf16[256,1024]{1,0:T(8,128)(2,1)S(1)} %shard_map.54.bands_ref, f32[368,128]{1,0:T(8,128)S(1)} %get-tuple-element.12.sums_ref, f32[240,128]{1,0:T(8,128)S(1)} %collective-permute-done.6.later_ref), custom_call_target="tpu_custom_call" | custom-call | bytes 1048576 | tf_op jit(solution)/shard_map/pallas_call | solution.py:274
Async XLA Ops:
  1.9 7.1 %collective-permute-start.2 = (bf16[144,128]{1,0:T(8,128)(2,1)S(1)}, bf16[144,128]{1,0:T(8,128)(2,1)S(1)}, u32[]{:S(2)}, u32[]{:S(2)}) collective-permute-start(bf16[144,128]{1,0:T(8,128)(2,1)S(1)} %get-tuple-element.9.refs_0_), channel_id=1, source_target_pairs={{0,24},{2,26},{4,28},{6,30},{8,16},{10,18},{12,20},{14,22},{16,8},... | collective-permute-start | bytes 110600 | tf_op jit(solution)/shard_map/ppermute | solution.py:31
  7.0 4.9 %collective-permute-start.1 = (bf16[144,128]{1,0:T(8,128)(2,1)S(1)}, bf16[144,128]{1,0:T(8,128)(2,1)S(1)}, u32[]{:S(2)}, u32[]{:S(2)}) collective-permute-start(bf16[144,128]{1,0:T(8,128)(2,1)S(1)} %get-tuple-element.9.refs_0_), channel_id=1, source_target_pairs={{0,16},{2,18},{4,20},{6,22},{8,24},{10,26},{12,28},{14,30},{16,0},... | collective-permute-start | bytes 110600 | tf_op jit(solution)/shard_map/ppermute | solution.py:31
  7.1 4.9 %collective-permute-start = (bf16[144,128]{1,0:T(8,128)(2,1)S(1)}, bf16[144,128]{1,0:T(8,128)(2,1)S(1)}, u32[]{:S(2)}, u32[]{:S(2)}) collective-permute-start(bf16[144,128]{1,0:T(8,128)(2,1)S(1)} %get-tuple-element.9.refs_0_), channel_id=1, source_target_pairs={{0,8},{2,10},{4,12},{6,14},{8,0},{10,2},{12,4},{14,6},{16,24},{18,... | collective-permute-start | bytes 110600 | tf_op jit(solution)/shard_map/ppermute | solution.py:31
  12.0 6.4 %collective-permute-start.5 = (bf16[272,256]{1,0:T(8,128)(2,1)S(1)}, bf16[272,256]{1,0:T(8,128)(2,1)S(1)}, u32[]{:S(2)}, u32[]{:S(2)}) collective-permute-start(bf16[272,256]{1,0:T(8,128)(2,1)S(1)} %shard_map.49.joined_ref), channel_id=1, source_target_pairs={{0,2},{2,0},{4,6},{6,4},{8,10},{10,8},{12,14},{14,12},{16,18},{18,... | collective-permute-start | bytes 417800 | tf_op jit(solution)/shard_map/ppermute | solution.py:31
  13.6 7.9 %collective-permute-start.4 = (bf16[272,256]{1,0:T(8,128)(2,1)S(1)}, bf16[272,256]{1,0:T(8,128)(2,1)S(1)}, u32[]{:S(2)}, u32[]{:S(2)}) collective-permute-start(bf16[272,256]{1,0:T(8,128)(2,1)S(1)} %shard_map.49.joined_ref), channel_id=1, source_target_pairs={{0,4},{2,6},{4,0},{6,2},{8,12},{10,14},{12,8},{14,10},{16,20},{18,... | collective-permute-start | bytes 417800 | tf_op jit(solution)/shard_map/ppermute | solution.py:31
  15.1 9.3 %collective-permute-start.3 = (bf16[272,256]{1,0:T(8,128)(2,1)S(1)}, bf16[272,256]{1,0:T(8,128)(2,1)S(1)}, u32[]{:S(2)}, u32[]{:S(2)}) collective-permute-start(bf16[272,256]{1,0:T(8,128)(2,1)S(1)} %shard_map.49.joined_ref), channel_id=1, source_target_pairs={{0,6},{2,4},{4,2},{6,0},{8,14},{10,12},{12,10},{14,8},{16,22},{18,... | collective-permute-start | bytes 417800 | tf_op jit(solution)/shard_map/ppermute | solution.py:31
  21.4 7.3 %copy-start = (s32[8]{0:T(128)S(1)}, s32[8]{0:T(128)}, u32[]{:S(2)}) copy-start(s32[8]{0:T(128)} %widths_ref.3) | copy-start | bytes 100
  27.4 3.2 %collective-permute-start.6 = (f32[240,128]{1,0:T(8,128)S(1)}, f32[240,128]{1,0:T(8,128)S(1)}, u32[]{:S(2)}, u32[]{:S(2)}) collective-permute-start(f32[240,128]{1,0:T(8,128)S(1)} %get-tuple-element.11.early_ref), channel_id=1, source_target_pairs={{1,0},{3,2},{5,4},{7,6},{9,8},{11,10},{13,12},{15,14},{17,16},{19,... | collective-permute-start | bytes 368648 | tf_op jit(solution)/shard_map/ppermute | solution.py:26

commit v10 on v9

--- a/solution.py
+++ b/solution.py
@@ -181,40 +181,37 @@
 
 
 def more_sums_kernel(outer, inner, flip, me_ref, joined_ref, table_ref, before_ref, sums_ref, *refs):
-    *early_ref, moving, shifted, total, table = refs[: -(GROUPS // 2)]
-    weights = refs[-(GROUPS // 2) :]
+    pairs = GROUPS // 2
+    *early_ref, moving, shifted, table = refs[:-pairs]
+    totals = refs[-pairs:]
     nsub = joined_ref.shape[1]
     subs = nsub // outer
-    trials = table_ref.shape[1]
     for slot in range(outer):
         start = slot_start(slot, flip, outer, inner, subs, me_ref[0])
         table[pl.ds(slot * subs, subs), :] = table_ref[pl.ds(start, subs), :]
-    total[...] = before_ref[...]
     shift_series(joined_ref, moving, shifted)
-
-    def make(pair):
-        for first in range(0, nsub, 16):
-            offset = table[pl.ds(first, 16), :]
-            for lag in range(weights[pair].shape[0] // nsub):
-                for odd in range(2):
-                    wanted = float(STEP * (2 * pair + odd) + lag) if lag < STEP or odd else -1.0
-                    weights[pair][pl.ds(lag * nsub + first, 16), pl.ds(odd * trials, trials)] = jnp.where(
-                        offset == wanted, 1.0, 0.0
-                    ).astype(jnp.bfloat16)
-
-    make(0)
-    for pair in range(GROUPS // 2):
-        if pair + 1 < GROUPS // 2:
-            make(pair + 1)
-        both = jnp.dot(
-            shifted[:, pl.ds(0, weights[pair].shape[0])],
-            weights[pair][...],
-            preferred_element_type=jnp.float32,
-        )
-        add_pair(total, pair, both)
-    sums_ref[...] = total[...]
+    for lag in range(STEP + 1):
+        for pair in range(pairs - 1 if lag == STEP else 0, pairs):
+            weights = [
+                jnp.where(table[...] == float(STEP * (2 * pair + odd) + lag), 1.0, 0.0).astype(jnp.bfloat16)
+                if lag < STEP or odd
+                else jnp.zeros(table.shape, jnp.bfloat16)
+                for odd in range(2)
+            ]
+            both = jnp.dot(
+                shifted[:, pl.ds(lag * nsub, nsub)],
+                jnp.concatenate(weights, axis=1),
+                preferred_element_type=jnp.float32,
+            )
+            if lag:
+                totals[pair][...] += both
+            else:
+                totals[pair][...] = both
+    sums_ref[...] = before_ref[...]
+    for pair in range(pairs):
+        add_pair(sums_ref, pair, totals[pair][...])
     for ref in early_ref:
-        ref[...] = total[pl.ds(0, ref.shape[0]), :]
+        ref[...] = sums_ref[pl.ds(0, ref.shape[0]), :]
 
 
 def bands_kernel(widths_ref, early_ref, bands_ref):
@@ -339,12 +336,8 @@
             (me, blocks[flip], table, sums),
             [
                 *scratch,
-                pltpu.VMEM((length + REACH, padded), jnp.float32),
                 pltpu.VMEM((nsub, padded), jnp.float32),
-                *(
-                    pltpu.VMEM(((STEP + (pair == GROUPS // 2 - 1)) * nsub, 2 * padded), jnp.bfloat16)
-                    for pair in range(GROUPS // 2)
-                ),
+                *[pltpu.VMEM((span + STEP, 2 * padded), jnp.float32)] * (GROUPS // 2),
             ],
             flops,
         )

time: 32.8 us -> 30.8 us (0.939)
  Pallas kernels: 16.9 us -> 14.2 us
  waiting for transfers between devices: 5.02 us -> 5.64 us
    pallas_call x10, Pallas kernels: 16.9 us -> 14.2 us  [call(): pl.pallas_call(kernel, out_shape=out_shape, in_specs=in_specs, scratch_sh...]
    ppermute x6, waiting for transfers between devices: 3.81 us -> 4.43 us  [exchanged(): lax.ppermute(value, axis, [(source, source ^ flip) for source in range(co...]
  transfers between devices with their start and end apart: 7 -> 7, of which waited for: 4 -> 5; matrix products, arithmetic and copies ran while one was open for 0% -> 0% of each run, Pallas kernels for 30% -> 27%
where the time goes in v10:
time: 30.8 us; the launch traced here: 30.6 us
  Pallas kernels  14.2 us (46%)
  starting transfers between devices  10.6 us (34%)
  waiting for transfers between devices  5.64 us (18%)
    pallas_call x10, Pallas kernels, call(): pl.pallas_call(kernel, out_shape=out_shape, in_specs=in_specs, scratch_sh...  14.2 us
    ppermute x6, starting transfers between devices, exchanged(): lax.ppermute(value, axis, [(source, source ^ flip) for source in range(co...  9.31 us
    ppermute x6, waiting for transfers between devices, exchanged(): lax.ppermute(value, axis, [(source, source ^ flip) for source in range(co...  4.43 us
    ppermute x1, starting transfers between devices, passed_back(): lax.ppermute(value, axis, [(source, source - 1) for source in range(1, co...  1.29 us
    ppermute x1, waiting for transfers between devices, passed_back(): lax.ppermute(value, axis, [(source, source - 1) for source in range(1, co...  1.21 us
  transfers between devices with their start and end apart: 7, of which 5 were waited for; matrix products, arithmetic and copies ran while one was open for 0% of the time, Pallas kernels for 27%

profile of v10, /device:TPU:0, one launch (start us, length us, event | category | flops | bytes accessed | tf_op | source)
XLA Modules:
  0.0 30.6 jit_solution(12116113120502688520)
XLA Ops:
  0.0 1.9 %shard_map.46 = (bf16[144,128]{1,0:T(8,128)(2,1)S(1)}, s32[128,1024]{1,0:T(8,128)S(1)}) custom-call(s32[1,1024]{1,0:T(1,128)} %bitcast.7, bf16[1024,256]{1,0:T(8,128)(2,1)} %bitcast.6, s32[128,1024]{1,0:T(8,128)} %offsets_ref.1), custom_call_target="tpu_custom_call" | custom-call | bytes 1048576 | tf_op jit(solution)/shard_map/pallas_call | solution.py:271
  1.9 5.1 %collective-permute-start.2 = (bf16[144,128]{1,0:T(8,128)(2,1)S(1)}, bf16[144,128]{1,0:T(8,128)(2,1)S(1)}, u32[]{:S(2)}, u32[]{:S(2)}) collective-permute-start(bf16[144,128]{1,0:T(8,128)(2,1)S(1)} %get-tuple-element.9.refs_0_), channel_id=1, source_target_pairs={{0,24},{2,26},{4,28},{6,30},{8,16},{10,18},{12,20},{14,22},{16,8},... | collective-permute-start | bytes 110600 | tf_op jit(solution)/shard_map/ppermute | solution.py:31
  7.0 0.0 collective-permute-start.1
  7.1 0.6 %collective-permute-start = (bf16[144,128]{1,0:T(8,128)(2,1)S(1)}, bf16[144,128]{1,0:T(8,128)(2,1)S(1)}, u32[]{:S(2)}, u32[]{:S(2)}) collective-permute-start(bf16[144,128]{1,0:T(8,128)(2,1)S(1)} %get-tuple-element.9.refs_0_), channel_id=1, source_target_pairs={{0,8},{2,10},{4,12},{6,14},{8,0},{10,2},{12,4},{14,6},{16,24},{18,... | collective-permute-start | bytes 110600 | tf_op jit(solution)/shard_map/ppermute | solution.py:31
  7.7 0.2 shard_map.47.table_ref
  7.9 1.0 %shard_map.48.refs_4_.chosen_ref = bf16[2,12544,128]{2,1,0:T(8,128)(2,1)S(1)} custom-call(s32[1]{0:T(128)} %bitcast.me_ref, f32[1024,128]{1,0:T(8,128)S(1)} %shard_map.47.table_ref), custom_call_target="tpu_custom_call" | custom-call | bytes 1048576 | tf_op jit(solution)/shard_map/pallas_call | solution.py:271
  8.9 0.1 collective-permute-done.2.refs_3_
  9.0 2.9 %collective-permute-done.1.refs_2_ = bf16[144,128]{1,0:T(8,128)(2,1)S(1)} collective-permute-done((bf16[144,128]{1,0:T(8,128)(2,1)S(1)}, bf16[144,128]{1,0:T(8,128)(2,1)S(1)}, u32[]{:S(2)}, u32[]{:S(2)}) %collective-permute-start.1) | collective-permute-done | bytes 36896 | tf_op jit(solution)/shard_map/ppermute | solution.py:31
  11.9 0.0 collective-permute-done.refs_1_
  11.9 0.1 shard_map.49.joined_ref
  12.0 1.6 %collective-permute-start.5 = (bf16[272,256]{1,0:T(8,128)(2,1)S(1)}, bf16[272,256]{1,0:T(8,128)(2,1)S(1)}, u32[]{:S(2)}, u32[]{:S(2)}) collective-permute-start(bf16[272,256]{1,0:T(8,128)(2,1)S(1)} %shard_map.49.joined_ref), channel_id=1, source_target_pairs={{0,2},{2,0},{4,6},{6,4},{8,10},{10,8},{12,14},{14,12},{16,18},{18,... | collective-permute-start | bytes 417800 | tf_op jit(solution)/shard_map/ppermute | solution.py:31
  13.6 1.5 %collective-permute-start.4 = (bf16[272,256]{1,0:T(8,128)(2,1)S(1)}, bf16[272,256]{1,0:T(8,128)(2,1)S(1)}, u32[]{:S(2)}, u32[]{:S(2)}) collective-permute-start(bf16[272,256]{1,0:T(8,128)(2,1)S(1)} %shard_map.49.joined_ref), channel_id=1, source_target_pairs={{0,4},{2,6},{4,0},{6,2},{8,12},{10,14},{12,8},{14,10},{16,20},{18,... | collective-permute-start | bytes 417800 | tf_op jit(solution)/shard_map/ppermute | solution.py:31
  15.1 0.5 %collective-permute-start.3 = (bf16[272,256]{1,0:T(8,128)(2,1)S(1)}, bf16[272,256]{1,0:T(8,128)(2,1)S(1)}, u32[]{:S(2)}, u32[]{:S(2)}) collective-permute-start(bf16[272,256]{1,0:T(8,128)(2,1)S(1)} %shard_map.49.joined_ref), channel_id=1, source_target_pairs={{0,6},{2,4},{4,2},{6,0},{8,14},{10,12},{12,10},{14,8},{16,22},{18,... | collective-permute-start | bytes 417800 | tf_op jit(solution)/shard_map/ppermute | solution.py:31
  15.6 2.1 %shard_map.50.before_ref = f32[368,128]{1,0:T(8,128)S(1)} custom-call(bf16[272,256]{1,0:T(8,128)(2,1)S(1)} %shard_map.49.joined_ref, bf16[2,12544,128]{2,1,0:T(8,128)(2,1)S(1)} %shard_map.48.refs_4_.chosen_ref), custom_call_target="tpu_custom_call" | custom-call | flops 1849688064 | bytes 1048576 | tf_op jit(solution)/shard_map/pallas_call | solution.py:271
  17.6 0.8 %collective-permute-done.5.joined_ref = bf16[272,256]{1,0:T(8,128)(2,1)S(1)} collective-permute-done((bf16[272,256]{1,0:T(8,128)(2,1)S(1)}, bf16[272,256]{1,0:T(8,128)(2,1)S(1)}, u32[]{:S(2)}, u32[]{:S(2)}) %collective-permute-start.5) | collective-permute-done | bytes 139296 | tf_op jit(solution)/shard_map/ppermute | solution.py:31
  18.5 2.1 %shard_map.51.before_ref = f32[368,128]{1,0:T(8,128)S(1)} custom-call(s32[1]{0:T(128)} %bitcast.me_ref, bf16[272,256]{1,0:T(8,128)(2,1)S(1)} %collective-permute-done.5.joined_ref, f32[1024,128]{1,0:T(8,128)S(1)} %shard_map.47.table_ref, f32[368,128]{1,0:T(8,128)S(1)} %shard_map.50.before_ref), custom_call_target="tpu_custom_call" | custom-call | flops 1849688064 | bytes 1048576 | tf_op jit(solution)/shard_map/pallas_call | solution.py:271
  20.6 0.0 copy-start
  20.6 0.6 %collective-permute-done.4.joined_ref = bf16[272,256]{1,0:T(8,128)(2,1)S(1)} collective-permute-done((bf16[272,256]{1,0:T(8,128)(2,1)S(1)}, bf16[272,256]{1,0:T(8,128)(2,1)S(1)}, u32[]{:S(2)}, u32[]{:S(2)}) %collective-permute-start.4) | collective-permute-done | bytes 139296 | tf_op jit(solution)/shard_map/ppermute | solution.py:31
  21.2 2.1 %shard_map.52.before_ref = f32[368,128]{1,0:T(8,128)S(1)} custom-call(s32[1]{0:T(128)} %bitcast.me_ref, bf16[272,256]{1,0:T(8,128)(2,1)S(1)} %collective-permute-done.4.joined_ref, f32[1024,128]{1,0:T(8,128)S(1)} %shard_map.47.table_ref, f32[368,128]{1,0:T(8,128)S(1)} %shard_map.51.before_ref), custom_call_target="tpu_custom_call" | custom-call | flops 1849688064 | bytes 1048576 | tf_op jit(solution)/shard_map/pallas_call | solution.py:271
  23.3 0.0 collective-permute-done.3.joined_ref
  23.3 2.1 %shard_map.53 = (f32[368,128]{1,0:T(8,128)S(1)}, f32[240,128]{1,0:T(8,128)S(1)}) custom-call(s32[1]{0:T(128)} %bitcast.me_ref, bf16[272,256]{1,0:T(8,128)(2,1)S(1)} %collective-permute-done.3.joined_ref, f32[1024,128]{1,0:T(8,128)S(1)} %shard_map.47.table_ref, f32[368,128]{1,0:T(8,128)S(1)} %shard_map.52.before_ref), custom_call_target="tpu_custom_call" | custom-call | flops 1849688064 | bytes 1048576 | tf_op jit(solution)/shard_map/pallas_call | solution.py:271
  25.4 1.3 %collective-permute-start.6 = (f32[240,128]{1,0:T(8,128)S(1)}, f32[240,128]{1,0:T(8,128)S(1)}, u32[]{:S(2)}, u32[]{:S(2)}) collective-permute-start(f32[240,128]{1,0:T(8,128)S(1)} %get-tuple-element.11.early_ref), channel_id=1, source_target_pairs={{1,0},{3,2},{5,4},{7,6},{9,8},{11,10},{13,12},{15,14},{17,16},{19,... | collective-permute-start | bytes 368648 | tf_op jit(solution)/shard_map/ppermute | solution.py:26
  26.7 0.0 copy-done
  26.7 0.7 %shard_map.54.bands_ref = bf16[256,1024]{1,0:T(8,128)(2,1)S(1)} custom-call(s32[8]{0:T(128)S(1)} %copy-done, f32[240,128]{1,0:T(8,128)S(1)} %get-tuple-element.11.early_ref), custom_call_target="tpu_custom_call" | custom-call | bytes 1048576 | tf_op jit(solution)/shard_map/pallas_call | solution.py:271
  27.4 1.2 %collective-permute-done.6.later_ref = f32[240,128]{1,0:T(8,128)S(1)} collective-permute-done((f32[240,128]{1,0:T(8,128)S(1)}, f32[240,128]{1,0:T(8,128)S(1)}, u32[]{:S(2)}, u32[]{:S(2)}) %collective-permute-start.6) | collective-permute-done | bytes 122912 | tf_op jit(solution)/shard_map/ppermute | solution.py:26
  28.6 2.0 %shard_map.55 = f32[128,8,256]{2,1,0:T(8,128)} custom-call(s32[8]{0:T(128)S(1)} %copy-done, bf16[256,1024]{1,0:T(8,128)(2,1)S(1)} %shard_map.54.bands_ref, f32[368,128]{1,0:T(8,128)S(1)} %get-tuple-element.12.sums_ref, f32[240,128]{1,0:T(8,128)S(1)} %collective-permute-done.6.later_ref), custom_call_target="tpu_custom_call" | custom-call | bytes 1048576 | tf_op jit(solution)/shard_map/pallas_call | solution.py:271
Async XLA Ops:
  1.9 7.1 %collective-permute-start.2 = (bf16[144,128]{1,0:T(8,128)(2,1)S(1)}, bf16[144,128]{1,0:T(8,128)(2,1)S(1)}, u32[]{:S(2)}, u32[]{:S(2)}) collective-permute-start(bf16[144,128]{1,0:T(8,128)(2,1)S(1)} %get-tuple-element.9.refs_0_), channel_id=1, source_target_pairs={{0,24},{2,26},{4,28},{6,30},{8,16},{10,18},{12,20},{14,22},{16,8},... | collective-permute-start | bytes 110600 | tf_op jit(solution)/shard_map/ppermute | solution.py:31
  7.0 4.9 %collective-permute-start.1 = (bf16[144,128]{1,0:T(8,128)(2,1)S(1)}, bf16[144,128]{1,0:T(8,128)(2,1)S(1)}, u32[]{:S(2)}, u32[]{:S(2)}) collective-permute-start(bf16[144,128]{1,0:T(8,128)(2,1)S(1)} %get-tuple-element.9.refs_0_), channel_id=1, source_target_pairs={{0,16},{2,18},{4,20},{6,22},{8,24},{10,26},{12,28},{14,30},{16,0},... | collective-permute-start | bytes 110600 | tf_op jit(solution)/shard_map/ppermute | solution.py:31
  7.1 4.9 %collective-permute-start = (bf16[144,128]{1,0:T(8,128)(2,1)S(1)}, bf16[144,128]{1,0:T(8,128)(2,1)S(1)}, u32[]{:S(2)}, u32[]{:S(2)}) collective-permute-start(bf16[144,128]{1,0:T(8,128)(2,1)S(1)} %get-tuple-element.9.refs_0_), channel_id=1, source_target_pairs={{0,8},{2,10},{4,12},{6,14},{8,0},{10,2},{12,4},{14,6},{16,24},{18,... | collective-permute-start | bytes 110600 | tf_op jit(solution)/shard_map/ppermute | solution.py:31
  12.0 6.4 %collective-permute-start.5 = (bf16[272,256]{1,0:T(8,128)(2,1)S(1)}, bf16[272,256]{1,0:T(8,128)(2,1)S(1)}, u32[]{:S(2)}, u32[]{:S(2)}) collective-permute-start(bf16[272,256]{1,0:T(8,128)(2,1)S(1)} %shard_map.49.joined_ref), channel_id=1, source_target_pairs={{0,2},{2,0},{4,6},{6,4},{8,10},{10,8},{12,14},{14,12},{16,18},{18,... | collective-permute-start | bytes 417800 | tf_op jit(solution)/shard_map/ppermute | solution.py:31
  13.6 7.6 %collective-permute-start.4 = (bf16[272,256]{1,0:T(8,128)(2,1)S(1)}, bf16[272,256]{1,0:T(8,128)(2,1)S(1)}, u32[]{:S(2)}, u32[]{:S(2)}) collective-permute-start(bf16[272,256]{1,0:T(8,128)(2,1)S(1)} %shard_map.49.joined_ref), channel_id=1, source_target_pairs={{0,4},{2,6},{4,0},{6,2},{8,12},{10,14},{12,8},{14,10},{16,20},{18,... | collective-permute-start | bytes 417800 | tf_op jit(solution)/shard_map/ppermute | solution.py:31
  15.1 8.2 %collective-permute-start.3 = (bf16[272,256]{1,0:T(8,128)(2,1)S(1)}, bf16[272,256]{1,0:T(8,128)(2,1)S(1)}, u32[]{:S(2)}, u32[]{:S(2)}) collective-permute-start(bf16[272,256]{1,0:T(8,128)(2,1)S(1)} %shard_map.49.joined_ref), channel_id=1, source_target_pairs={{0,6},{2,4},{4,2},{6,0},{8,14},{10,12},{12,10},{14,8},{16,22},{18,... | collective-permute-start | bytes 417800 | tf_op jit(solution)/shard_map/ppermute | solution.py:31
  20.6 6.1 %copy-start = (s32[8]{0:T(128)S(1)}, s32[8]{0:T(128)}, u32[]{:S(2)}) copy-start(s32[8]{0:T(128)} %widths_ref.3) | copy-start | bytes 100
  25.4 3.2 %collective-permute-start.6 = (f32[240,128]{1,0:T(8,128)S(1)}, f32[240,128]{1,0:T(8,128)S(1)}, u32[]{:S(2)}, u32[]{:S(2)}) collective-permute-start(f32[240,128]{1,0:T(8,128)S(1)} %get-tuple-element.11.early_ref), channel_id=1, source_target_pairs={{1,0},{3,2},{5,4},{7,6},{9,8},{11,10},{13,12},{15,14},{17,16},{19,... | collective-permute-start | bytes 368648 | tf_op jit(solution)/shard_map/ppermute | solution.py:26

commit v11 on v10

--- a/solution.py
+++ b/solution.py
@@ -58,10 +58,11 @@
         jnp.where(rows == delays[:, at * block : (at + 1) * block] * subs + owner, 1.0, 0.0).astype(jnp.bfloat16)
         for at in range(chans // block)
     ]
-    for copy in copies[:steps]:
-        copy.wait()
     parts = []
     for at, member in enumerate(members):
+        if at * 2 % steps == 0:
+            for copy in copies[at : at + steps // 2] if len(members) == steps else copies[:steps]:
+                copy.wait()
         picked = jnp.dot(member, held[pl.ds(at * block, block), :], preferred_element_type=jnp.float32)
         total = None
         for delay in range(DCH):
@@ -126,35 +127,6 @@
     return pl.multiple_of((((me // inner) ^ slot) * inner + ((me % inner) ^ flip)) * subs, subs)
 
 
-def choices_kernel(outer, inner, me_ref, table_ref, chosen_ref):
-    subs = table_ref.shape[0] // (outer * inner)
-    nsub = outer * subs
-    for slot in range(outer):
-        start = slot_start(slot, 0, outer, inner, subs, me_ref[0])
-        for first in range(0, subs, 16):
-            offset = table_ref[pl.ds(pl.multiple_of(start + first, 16), 16), :]
-            groups = jnp.minimum(jnp.floor(offset * (1.0 / STEP)), float(GROUPS - 1))
-            lags = offset - float(STEP) * groups
-            in_group = [jnp.where(groups == float(group), 1.0, 0.0) for group in range(GROUPS)]
-            for lag in range(STEP + 1):
-                at_lag = jnp.where(lags == float(lag), 1.0, 0.0)
-                for group in range(GROUPS - 2 if lag == STEP else 0, GROUPS):
-                    place = (group // 2 * STEP + lag) * nsub + slot * subs + first
-                    chosen_ref[group % 2, pl.ds(place, 16), :] = (at_lag * in_group[group]).astype(
-                        jnp.bfloat16
-                    )
-
-
-def shift_series(joined_ref, moving, shifted):
-    span, nsub = joined_ref.shape
-    blank = jnp.zeros((STEP, nsub), jnp.float32)
-    moving[pl.ds(0, STEP), :] = blank
-    moving[pl.ds(STEP, span), :] = joined_ref[...].astype(jnp.float32)
-    moving[pl.ds(STEP + span, STEP), :] = blank
-    for lag in range(STEP + 1):
-        shifted[:, pl.ds(lag * nsub, nsub)] = moving[pl.ds(lag, span + STEP), :].astype(jnp.bfloat16)
-
-
 def add_pair(total, pair, both):
     rows, trials = both.shape[0], both.shape[1] // 2
     for odd in range(2):
@@ -162,35 +134,28 @@
         total[pl.ds(first, rows), :] += both[:, odd * trials : (odd + 1) * trials]
 
 
-def first_sums_kernel(joined_ref, chosen_ref, sums_ref, moving, shifted):
-    nsub = joined_ref.shape[1]
-    shift_series(joined_ref, moving, shifted)
-    sums_ref[...] = jnp.zeros_like(sums_ref)
-    for pair in range(GROUPS // 2):
-        depth = (STEP + (pair == GROUPS // 2 - 1)) * nsub
-        weights = [chosen_ref[odd, pl.ds(pair * STEP * nsub, depth), :] for odd in range(2)]
-        add_pair(
-            sums_ref,
-            pair,
-            jnp.dot(
-                shifted[:, pl.ds(0, depth)],
-                jnp.concatenate(weights, axis=1),
-                preferred_element_type=jnp.float32,
-            ),
-        )
-
-
-def more_sums_kernel(outer, inner, flip, me_ref, joined_ref, table_ref, before_ref, sums_ref, *refs):
+def sums_kernel(given, outer, inner, flip, me_ref, joined_ref, table_ref, *refs):
     pairs = GROUPS // 2
-    *early_ref, moving, shifted, table = refs[:-pairs]
+    before_ref, sums_ref, *early_ref = refs[: -3 - pairs] if given else (None, *refs[: -3 - pairs])
+    moving, shifted, table = refs[-3 - pairs : -pairs]
     totals = refs[-pairs:]
-    nsub = joined_ref.shape[1]
+    span, nsub = joined_ref.shape
     subs = nsub // outer
     for slot in range(outer):
         start = slot_start(slot, flip, outer, inner, subs, me_ref[0])
         table[pl.ds(slot * subs, subs), :] = table_ref[pl.ds(start, subs), :]
-    shift_series(joined_ref, moving, shifted)
+    blank = jnp.zeros((STEP, nsub), jnp.float32)
+    moving[pl.ds(0, STEP), :] = blank
+    moving[pl.ds(STEP, span), :] = joined_ref[...].astype(jnp.float32)
+    moving[pl.ds(STEP + span, STEP), :] = blank
+
+    def shift(lag):
+        shifted[:, pl.ds(lag * nsub, nsub)] = moving[pl.ds(lag, span + STEP), :].astype(jnp.bfloat16)
+
+    shift(0)
     for lag in range(STEP + 1):
+        if lag < STEP:
+            shift(lag + 1)
         for pair in range(pairs - 1 if lag == STEP else 0, pairs):
             weights = [
                 jnp.where(table[...] == float(STEP * (2 * pair + odd) + lag), 1.0, 0.0).astype(jnp.bfloat16)
@@ -207,7 +172,10 @@
                 totals[pair][...] += both
             else:
                 totals[pair][...] = both
-    sums_ref[...] = before_ref[...]
+    if before_ref is None:
+        sums_ref[...] = jnp.zeros_like(sums_ref)
+    else:
+        sums_ref[...] = before_ref[...]
     for pair in range(pairs):
         add_pair(sums_ref, pair, totals[pair][...])
     for ref in early_ref:
@@ -223,7 +191,7 @@
         bands_ref[:, pl.ds(at * LANES, LANES)] = band.astype(jnp.bfloat16)
 
 
-def boxcars_kernel(scale, widths_ref, bands_ref, sums_ref, later_ref, out_ref, values, mixed, tiles, sems):
+def boxcars_kernel(scale, widths_ref, bands_ref, sums_ref, later_ref, out_ref, values, mixed, sems):
     trials = sums_ref.shape[1]
     length = sums_ref.shape[0] - REACH
     filters = widths_ref.shape[0]
@@ -239,27 +207,23 @@
     for first in range(0, length + WMAX, LANES):
         tile = (total[first : first + LANES] * scale).T
         values[:, pl.ds(first, LANES)] = tile.astype(jnp.bfloat16)
-    share = trials // sems.shape[1]
+    parts, pieces = sems.shape
+    share = trials // pieces
     widths = [jnp.full((1, LANES), widths_ref[at], jnp.int32).astype(jnp.float32) for at in range(filters)]
     shares = [1.0 / jnp.sqrt(width) for width in widths]
+    tiles = mixed.reshape(parts, trials, filters, LANES)
     copies = []
-    for part in range(length // LANES):
-        lanes = pl.ds(part * LANES, LANES)
-        for at in range(filters):
-            sums = jnp.dot(
-                values[:, pl.ds(part * LANES, LANES + WMAX)],
-                bands_ref[:, pl.ds(at * LANES, LANES)],
-                preferred_element_type=jnp.float32,
-            )
-            mixed[part, pl.ds(at, trials, stride=filters), :] = sums * shares[at]
-        tiles[part] = mixed[part].reshape(trials, filters, LANES)
-        for piece in range(sems.shape[1]):
-            some = pl.ds(piece * share, share)
-            copies.append(
-                pltpu.make_async_copy(
-                    tiles.at[part, some], out_ref.at[some, :, lanes], sems.at[part, piece]
+    for piece in range(pieces):
+        some = pl.ds(piece * share, share)
+        windows = [values[some, pl.ds(part * LANES, LANES + WMAX)] for part in range(parts)]
+        sums = jnp.dot(jnp.concatenate(windows, axis=0), bands_ref[...], preferred_element_type=jnp.float32)
+        for part in range(parts):
+            for at in range(filters):
+                mixed[part, pl.ds(piece * share * filters + at, share, stride=filters), :] = (
+                    sums[part * share : (part + 1) * share, at * LANES : (at + 1) * LANES] * shares[at]
                 )
-            )
+            target = out_ref.at[some, :, pl.ds(part * LANES, LANES)]
+            copies.append(pltpu.make_async_copy(tiles.at[part, some], target, sems.at[part, piece]))
             copies[-1].start()
     for copy in copies:
         copy.wait()
@@ -307,40 +271,33 @@
     line = [series] + [exchanged(series, "sub", flip * inner) for flip in range(1, outer)]
     nsub = outer * sub_dev
     table = call(offsets_kernel, jax.ShapeDtypeStruct((all_subs, padded), jnp.float32), [VMEM], (fetched,))
-    chosen = call(
-        functools.partial(choices_kernel, outer, inner),
-        jax.ShapeDtypeStruct((2, (GROUPS // 2 * STEP + 1) * nsub, padded), jnp.bfloat16),
-        [SMEM, VMEM],
-        (me, table),
-    )
     joined = call(
         functools.partial(join_packed_kernel if packed else join_kernel, outer),
         jax.ShapeDtypeStruct((span, nsub), jnp.bfloat16),
         [VMEM] * outer + [ANY],
-        (*line, chosen),
+        (*line, table),
     )
     blocks = [joined] + [exchanged(joined, "sub", flip) for flip in range(1, inner)]
     scratch = [
         pltpu.VMEM((span + 2 * STEP, nsub), jnp.float32),
         pltpu.VMEM((span + STEP, (STEP + 1) * nsub), jnp.bfloat16),
+        pltpu.VMEM((nsub, padded), jnp.float32),
+        *[pltpu.VMEM((span + STEP, 2 * padded), jnp.float32)] * (GROUPS // 2),
     ]
     flops = 2 * (span + STEP) * nsub * padded * (OMAX + 2)
     sums_shape = jax.ShapeDtypeStruct((length + REACH, padded), jnp.float32)
     early_shape = jax.ShapeDtypeStruct((REACH + WMAX, padded), jnp.float32)
-    sums = call(first_sums_kernel, sums_shape, [VMEM, VMEM], (joined, chosen), scratch, flops)
-    for flip in range(1, inner):
+    given = ()
+    for flip in range(inner):
         sums, *early = call(
-            functools.partial(more_sums_kernel, outer, inner, flip),
+            functools.partial(sums_kernel, flip > 0, outer, inner, flip),
             [sums_shape, early_shape] if flip == inner - 1 else [sums_shape],
-            [SMEM, VMEM, VMEM, VMEM],
-            (me, blocks[flip], table, sums),
-            [
-                *scratch,
-                pltpu.VMEM((nsub, padded), jnp.float32),
-                *[pltpu.VMEM((span + STEP, 2 * padded), jnp.float32)] * (GROUPS // 2),
-            ],
+            [SMEM] + [VMEM] * (2 + len(given)),
+            (me, blocks[flip], table, *given),
+            scratch,
             flops,
         )
+        given = (sums,)
     early = early[0]
     later = passed_back(early, "tm")
     bands = call(
@@ -350,7 +307,7 @@
         (widths, early),
     )
     parts = length // LANES
-    pieces = 4
+    pieces = 2
     return call(
         functools.partial(boxcars_kernel, scale),
         jax.ShapeDtypeStruct((padded, filters, length), jnp.float32),
@@ -359,7 +316,6 @@
         [
             pltpu.VMEM((padded, length + WMAX), jnp.bfloat16),
             pltpu.VMEM((parts, padded * filters, LANES), jnp.float32),
-            pltpu.VMEM((parts, padded, filters, LANES), jnp.float32),
             pltpu.SemaphoreType.DMA((parts, pieces)),
         ],
         out_specs=HBM,

time: 30.8 us -> 30.8 us (level)
  waiting for transfers between devices: 5.64 us -> 6.66 us
  Pallas kernels: 14.2 us -> 13.3 us
    ppermute x6, waiting for transfers between devices: 4.43 us -> 5.44 us  [exchanged(): lax.ppermute(value, axis, [(source, source ^ flip) for source in range(co...]
    pallas_call x10 -> x9, Pallas kernels: 14.2 us -> 13.3 us  [call(): pl.pallas_call(kernel, out_shape=out_shape, in_specs=in_specs, scratch_sh...]
  transfers between devices with their start and end apart: 7 -> 7, of which waited for: 5 -> 5; matrix products, arithmetic and copies ran while one was open for 0% -> 0% of each run, Pallas kernels for 27% -> 23%
where the time goes in v11:
time: 30.8 us; the launch traced here: 30.7 us
  Pallas kernels  13.3 us (43%)
  starting transfers between devices  10.6 us (34%)
  waiting for transfers between devices  6.66 us (22%)
    pallas_call x9, Pallas kernels, call(): pl.pallas_call(kernel, out_shape=out_shape, in_specs=in_specs, scratch_sh...  13.3 us
    ppermute x6, starting transfers between devices, exchanged(): lax.ppermute(value, axis, [(source, source ^ flip) for source in range(co...  9.31 us
    ppermute x6, waiting for transfers between devices, exchanged(): lax.ppermute(value, axis, [(source, source ^ flip) for source in range(co...  5.44 us
    ppermute x1, starting transfers between devices, passed_back(): lax.ppermute(value, axis, [(source, source - 1) for source in range(1, co...  1.29 us
    ppermute x1, waiting for transfers between devices, passed_back(): lax.ppermute(value, axis, [(source, source - 1) for source in range(1, co...  1.21 us
  transfers between devices with their start and end apart: 7, of which 5 were waited for; matrix products, arithmetic and copies ran while one was open for 0% of the time, Pallas kernels for 23%

profile of v11, /device:TPU:0, one launch (start us, length us, event | category | flops | bytes accessed | tf_op | source)
XLA Modules:
  0.0 30.7 jit_solution(14242523315699903531)
XLA Ops:
  0.0 2.2 %shard_map.46 = (bf16[144,128]{1,0:T(8,128)(2,1)S(1)}, s32[128,1024]{1,0:T(8,128)S(1)}) custom-call(s32[1,1024]{1,0:T(1,128)} %bitcast.7, bf16[1024,256]{1,0:T(8,128)(2,1)} %bitcast.6, s32[128,1024]{1,0:T(8,128)} %offsets_ref.1), custom_call_target="tpu_custom_call" | custom-call | bytes 1048576 | tf_op jit(solution)/shard_map/pallas_call | solution.py:235
  2.2 5.1 %collective-permute-start.2 = (bf16[144,128]{1,0:T(8,128)(2,1)S(1)}, bf16[144,128]{1,0:T(8,128)(2,1)S(1)}, u32[]{:S(2)}, u32[]{:S(2)}) collective-permute-start(bf16[144,128]{1,0:T(8,128)(2,1)S(1)} %get-tuple-element.9.refs_0_), channel_id=1, source_target_pairs={{0,24},{2,26},{4,28},{6,30},{8,16},{10,18},{12,20},{14,22},{16,8},... | collective-permute-start | bytes 110600 | tf_op jit(solution)/shard_map/ppermute | solution.py:31
  7.3 0.0 collective-permute-start.1
  7.3 0.6 %collective-permute-start = (bf16[144,128]{1,0:T(8,128)(2,1)S(1)}, bf16[144,128]{1,0:T(8,128)(2,1)S(1)}, u32[]{:S(2)}, u32[]{:S(2)}) collective-permute-start(bf16[144,128]{1,0:T(8,128)(2,1)S(1)} %get-tuple-element.9.refs_0_), channel_id=1, source_target_pairs={{0,8},{2,10},{4,12},{6,14},{8,0},{10,2},{12,4},{14,6},{16,24},{18,... | collective-permute-start | bytes 110600 | tf_op jit(solution)/shard_map/ppermute | solution.py:31
  7.9 0.2 shard_map.47.refs_4_.table_ref
  8.1 1.1 %collective-permute-done.2.refs_3_ = bf16[144,128]{1,0:T(8,128)(2,1)S(1)} collective-permute-done((bf16[144,128]{1,0:T(8,128)(2,1)S(1)}, bf16[144,128]{1,0:T(8,128)(2,1)S(1)}, u32[]{:S(2)}, u32[]{:S(2)}) %collective-permute-start.2) | collective-permute-done | bytes 36896 | tf_op jit(solution)/shard_map/ppermute | solution.py:31
  9.2 2.9 %collective-permute-done.1.refs_2_ = bf16[144,128]{1,0:T(8,128)(2,1)S(1)} collective-permute-done((bf16[144,128]{1,0:T(8,128)(2,1)S(1)}, bf16[144,128]{1,0:T(8,128)(2,1)S(1)}, u32[]{:S(2)}, u32[]{:S(2)}) %collective-permute-start.1) | collective-permute-done | bytes 36896 | tf_op jit(solution)/shard_map/ppermute | solution.py:31
  12.1 0.0 collective-permute-done.refs_1_
  12.1 0.1 shard_map.48.joined_ref
  12.2 1.6 %collective-permute-start.5 = (bf16[272,256]{1,0:T(8,128)(2,1)S(1)}, bf16[272,256]{1,0:T(8,128)(2,1)S(1)}, u32[]{:S(2)}, u32[]{:S(2)}) collective-permute-start(bf16[272,256]{1,0:T(8,128)(2,1)S(1)} %shard_map.48.joined_ref), channel_id=1, source_target_pairs={{0,2},{2,0},{4,6},{6,4},{8,10},{10,8},{12,14},{14,12},{16,18},{18,... | collective-permute-start | bytes 417800 | tf_op jit(solution)/shard_map/ppermute | solution.py:31
  13.8 1.5 %collective-permute-start.4 = (bf16[272,256]{1,0:T(8,128)(2,1)S(1)}, bf16[272,256]{1,0:T(8,128)(2,1)S(1)}, u32[]{:S(2)}, u32[]{:S(2)}) collective-permute-start(bf16[272,256]{1,0:T(8,128)(2,1)S(1)} %shard_map.48.joined_ref), channel_id=1, source_target_pairs={{0,4},{2,6},{4,0},{6,2},{8,12},{10,14},{12,8},{14,10},{16,20},{18,... | collective-permute-start | bytes 417800 | tf_op jit(solution)/shard_map/ppermute | solution.py:31
  15.3 0.5 %collective-permute-start.3 = (bf16[272,256]{1,0:T(8,128)(2,1)S(1)}, bf16[272,256]{1,0:T(8,128)(2,1)S(1)}, u32[]{:S(2)}, u32[]{:S(2)}) collective-permute-start(bf16[272,256]{1,0:T(8,128)(2,1)S(1)} %shard_map.48.joined_ref), channel_id=1, source_target_pairs={{0,6},{2,4},{4,2},{6,0},{8,14},{10,12},{12,10},{14,8},{16,22},{18,... | collective-permute-start | bytes 417800 | tf_op jit(solution)/shard_map/ppermute | solution.py:31
  15.8 2.1 %shard_map.49.refs_0_ = f32[368,128]{1,0:T(8,128)S(1)} custom-call(s32[1]{0:T(128)} %bitcast.me_ref, bf16[272,256]{1,0:T(8,128)(2,1)S(1)} %shard_map.48.joined_ref, f32[1024,128]{1,0:T(8,128)S(1)} %shard_map.47.refs_4_.table_ref), custom_call_target="tpu_custom_call" | custom-call | flops 1849688064 | bytes 1048576 | tf_op jit(solution)/shard_map/pallas_call | solution.py:235
  17.9 0.8 %collective-permute-done.5.joined_ref = bf16[272,256]{1,0:T(8,128)(2,1)S(1)} collective-permute-done((bf16[272,256]{1,0:T(8,128)(2,1)S(1)}, bf16[272,256]{1,0:T(8,128)(2,1)S(1)}, u32[]{:S(2)}, u32[]{:S(2)}) %collective-permute-start.5) | collective-permute-done | bytes 139296 | tf_op jit(solution)/shard_map/ppermute | solution.py:31
  18.7 2.1 %shard_map.50.refs_0_ = f32[368,128]{1,0:T(8,128)S(1)} custom-call(s32[1]{0:T(128)} %bitcast.me_ref, bf16[272,256]{1,0:T(8,128)(2,1)S(1)} %collective-permute-done.5.joined_ref, f32[1024,128]{1,0:T(8,128)S(1)} %shard_map.47.refs_4_.table_ref, f32[368,128]{1,0:T(8,128)S(1)} %shard_map.49.refs_0_), custom_call_target="tpu_custom_call" | custom-call | flops 1849688064 | bytes 1048576 | tf_op jit(solution)/shard_map/pallas_call | solution.py:235
  20.8 0.6 %collective-permute-done.4.joined_ref = bf16[272,256]{1,0:T(8,128)(2,1)S(1)} collective-permute-done((bf16[272,256]{1,0:T(8,128)(2,1)S(1)}, bf16[272,256]{1,0:T(8,128)(2,1)S(1)}, u32[]{:S(2)}, u32[]{:S(2)}) %collective-permute-start.4) | collective-permute-done | bytes 139296 | tf_op jit(solution)/shard_map/ppermute | solution.py:31
  21.4 2.1 %shard_map.51.refs_0_ = f32[368,128]{1,0:T(8,128)S(1)} custom-call(s32[1]{0:T(128)} %bitcast.me_ref, bf16[272,256]{1,0:T(8,128)(2,1)S(1)} %collective-permute-done.4.joined_ref, f32[1024,128]{1,0:T(8,128)S(1)} %shard_map.47.refs_4_.table_ref, f32[368,128]{1,0:T(8,128)S(1)} %shard_map.50.refs_0_), custom_call_target="tpu_custom_call" | custom-call | flops 1849688064 | bytes 1048576 | tf_op jit(solution)/shard_map/pallas_call | solution.py:235
  23.5 0.0 collective-permute-done.3.joined_ref
  23.5 2.1 %shard_map.52 = (f32[368,128]{1,0:T(8,128)S(1)}, f32[240,128]{1,0:T(8,128)S(1)}) custom-call(s32[1]{0:T(128)} %bitcast.me_ref, bf16[272,256]{1,0:T(8,128)(2,1)S(1)} %collective-permute-done.3.joined_ref, f32[1024,128]{1,0:T(8,128)S(1)} %shard_map.47.refs_4_.table_ref, f32[368,128]{1,0:T(8,128)S(1)} %shard_map.51.refs_0_), custom_call_target="tpu_custom_call" | custom-call | flops 1849688064 | bytes 1048576 | tf_op jit(solution)/shard_map/pallas_call | solution.py:235
  25.6 0.0 copy-start
  25.6 1.3 %collective-permute-start.6 = (f32[240,128]{1,0:T(8,128)S(1)}, f32[240,128]{1,0:T(8,128)S(1)}, u32[]{:S(2)}, u32[]{:S(2)}) collective-permute-start(f32[240,128]{1,0:T(8,128)S(1)} %get-tuple-element.11.early_ref), channel_id=1, source_target_pairs={{1,0},{3,2},{5,4},{7,6},{9,8},{11,10},{13,12},{15,14},{17,16},{19,... | collective-permute-start | bytes 368648 | tf_op jit(solution)/shard_map/ppermute | solution.py:26
  26.9 0.0 copy-done
  26.9 0.7 %shard_map.53.bands_ref = bf16[256,1024]{1,0:T(8,128)(2,1)S(1)} custom-call(s32[8]{0:T(128)S(1)} %copy-done, f32[240,128]{1,0:T(8,128)S(1)} %get-tuple-element.11.early_ref), custom_call_target="tpu_custom_call" | custom-call | bytes 1048576 | tf_op jit(solution)/shard_map/pallas_call | solution.py:235
  27.6 1.2 %collective-permute-done.6.later_ref = f32[240,128]{1,0:T(8,128)S(1)} collective-permute-done((f32[240,128]{1,0:T(8,128)S(1)}, f32[240,128]{1,0:T(8,128)S(1)}, u32[]{:S(2)}, u32[]{:S(2)}) %collective-permute-start.6) | collective-permute-done | bytes 122912 | tf_op jit(solution)/shard_map/ppermute | solution.py:26
  28.8 1.8 %shard_map.54 = f32[128,8,256]{2,1,0:T(8,128)} custom-call(s32[8]{0:T(128)S(1)} %copy-done, bf16[256,1024]{1,0:T(8,128)(2,1)S(1)} %shard_map.53.bands_ref, f32[368,128]{1,0:T(8,128)S(1)} %get-tuple-element.12.sums_ref, f32[240,128]{1,0:T(8,128)S(1)} %collective-permute-done.6.later_ref), custom_call_target="tpu_custom_call" | custom-call | bytes 1048576 | tf_op jit(solution)/shard_map/pallas_call | solution.py:235
Async XLA Ops:
  2.2 7.0 %collective-permute-start.2 = (bf16[144,128]{1,0:T(8,128)(2,1)S(1)}, bf16[144,128]{1,0:T(8,128)(2,1)S(1)}, u32[]{:S(2)}, u32[]{:S(2)}) collective-permute-start(bf16[144,128]{1,0:T(8,128)(2,1)S(1)} %get-tuple-element.9.refs_0_), channel_id=1, source_target_pairs={{0,24},{2,26},{4,28},{6,30},{8,16},{10,18},{12,20},{14,22},{16,8},... | collective-permute-start | bytes 110600 | tf_op jit(solution)/shard_map/ppermute | solution.py:31
  7.3 4.9 %collective-permute-start.1 = (bf16[144,128]{1,0:T(8,128)(2,1)S(1)}, bf16[144,128]{1,0:T(8,128)(2,1)S(1)}, u32[]{:S(2)}, u32[]{:S(2)}) collective-permute-start(bf16[144,128]{1,0:T(8,128)(2,1)S(1)} %get-tuple-element.9.refs_0_), channel_id=1, source_target_pairs={{0,16},{2,18},{4,20},{6,22},{8,24},{10,26},{12,28},{14,30},{16,0},... | collective-permute-start | bytes 110600 | tf_op jit(solution)/shard_map/ppermute | solution.py:31
  7.3 4.9 %collective-permute-start = (bf16[144,128]{1,0:T(8,128)(2,1)S(1)}, bf16[144,128]{1,0:T(8,128)(2,1)S(1)}, u32[]{:S(2)}, u32[]{:S(2)}) collective-permute-start(bf16[144,128]{1,0:T(8,128)(2,1)S(1)} %get-tuple-element.9.refs_0_), channel_id=1, source_target_pairs={{0,8},{2,10},{4,12},{6,14},{8,0},{10,2},{12,4},{14,6},{16,24},{18,... | collective-permute-start | bytes 110600 | tf_op jit(solution)/shard_map/ppermute | solution.py:31
  12.2 6.4 %collective-permute-start.5 = (bf16[272,256]{1,0:T(8,128)(2,1)S(1)}, bf16[272,256]{1,0:T(8,128)(2,1)S(1)}, u32[]{:S(2)}, u32[]{:S(2)}) collective-permute-start(bf16[272,256]{1,0:T(8,128)(2,1)S(1)} %shard_map.48.joined_ref), channel_id=1, source_target_pairs={{0,2},{2,0},{4,6},{6,4},{8,10},{10,8},{12,14},{14,12},{16,18},{18,... | collective-permute-start | bytes 417800 | tf_op jit(solution)/shard_map/ppermute | solution.py:31
  13.8 7.6 %collective-permute-start.4 = (bf16[272,256]{1,0:T(8,128)(2,1)S(1)}, bf16[272,256]{1,0:T(8,128)(2,1)S(1)}, u32[]{:S(2)}, u32[]{:S(2)}) collective-permute-start(bf16[272,256]{1,0:T(8,128)(2,1)S(1)} %shard_map.48.joined_ref), channel_id=1, source_target_pairs={{0,4},{2,6},{4,0},{6,2},{8,12},{10,14},{12,8},{14,10},{16,20},{18,... | collective-permute-start | bytes 417800 | tf_op jit(solution)/shard_map/ppermute | solution.py:31
  15.3 8.2 %collective-permute-start.3 = (bf16[272,256]{1,0:T(8,128)(2,1)S(1)}, bf16[272,256]{1,0:T(8,128)(2,1)S(1)}, u32[]{:S(2)}, u32[]{:S(2)}) collective-permute-start(bf16[272,256]{1,0:T(8,128)(2,1)S(1)} %shard_map.48.joined_ref), channel_id=1, source_target_pairs={{0,6},{2,4},{4,2},{6,0},{8,14},{10,12},{12,10},{14,8},{16,22},{18,... | collective-permute-start | bytes 417800 | tf_op jit(solution)/shard_map/ppermute | solution.py:31
  25.6 1.3 %copy-start = (s32[8]{0:T(128)S(1)}, s32[8]{0:T(128)}, u32[]{:S(2)}) copy-start(s32[8]{0:T(128)} %widths_ref.3) | copy-start | bytes 100
  25.6 3.2 %collective-permute-start.6 = (f32[240,128]{1,0:T(8,128)S(1)}, f32[240,128]{1,0:T(8,128)S(1)}, u32[]{:S(2)}, u32[]{:S(2)}) collective-permute-start(f32[240,128]{1,0:T(8,128)S(1)} %get-tuple-element.11.early_ref), channel_id=1, source_target_pairs={{1,0},{3,2},{5,4},{7,6},{9,8},{11,10},{13,12},{15,14},{17,16},{19,... | collective-permute-start | bytes 368648 | tf_op jit(solution)/shard_map/ppermute | solution.py:26

commit v12 on v11

--- a/solution.py
+++ b/solution.py
@@ -14,6 +14,7 @@
 LANES = 128
 STEP = 16
 GROUPS = OMAX // STEP
+TOGETHER = 2
 REACH = OMAX + DCH
 VMEM = pl.BlockSpec(memory_space=pltpu.VMEM)
 SMEM = pl.BlockSpec(memory_space=pltpu.SMEM)
@@ -58,11 +59,10 @@
         jnp.where(rows == delays[:, at * block : (at + 1) * block] * subs + owner, 1.0, 0.0).astype(jnp.bfloat16)
         for at in range(chans // block)
     ]
+    for copy in copies[:steps]:
+        copy.wait()
     parts = []
     for at, member in enumerate(members):
-        if at * 2 % steps == 0:
-            for copy in copies[at : at + steps // 2] if len(members) == steps else copies[:steps]:
-                copy.wait()
         picked = jnp.dot(member, held[pl.ds(at * block, block), :], preferred_element_type=jnp.float32)
         total = None
         for delay in range(DCH):
@@ -152,23 +152,28 @@
     def shift(lag):
         shifted[:, pl.ds(lag * nsub, nsub)] = moving[pl.ds(lag, span + STEP), :].astype(jnp.bfloat16)
 
-    shift(0)
-    for lag in range(STEP + 1):
-        if lag < STEP:
-            shift(lag + 1)
-        for pair in range(pairs - 1 if lag == STEP else 0, pairs):
-            weights = [
-                jnp.where(table[...] == float(STEP * (2 * pair + odd) + lag), 1.0, 0.0).astype(jnp.bfloat16)
-                if lag < STEP or odd
-                else jnp.zeros(table.shape, jnp.bfloat16)
-                for odd in range(2)
-            ]
+    def tile(lag, pair):
+        halves = [
+            jnp.where(table[...] == float(STEP * (2 * pair + odd) + lag), 1.0, 0.0).astype(jnp.bfloat16)
+            if lag < STEP or odd
+            else jnp.zeros(table.shape, jnp.bfloat16)
+            for odd in range(2)
+        ]
+        return jnp.concatenate(halves, axis=1)
+
+    for lag in range(TOGETHER):
+        shift(lag)
+    for first in range(0, STEP + 1, TOGETHER):
+        lags = range(first, min(first + TOGETHER, STEP + 1))
+        for lag in range(first + TOGETHER, min(first + 2 * TOGETHER, STEP + 1)):
+            shift(lag)
+        for pair in range(pairs - 1 if first == STEP else 0, pairs):
             both = jnp.dot(
-                shifted[:, pl.ds(lag * nsub, nsub)],
-                jnp.concatenate(weights, axis=1),
+                shifted[:, pl.ds(first * nsub, len(lags) * nsub)],
+                jnp.concatenate([tile(lag, pair) for lag in lags], axis=0),
                 preferred_element_type=jnp.float32,
             )
-            if lag:
+            if first:
                 totals[pair][...] += both
             else:
                 totals[pair][...] = both
@@ -288,10 +293,10 @@
     sums_shape = jax.ShapeDtypeStruct((length + REACH, padded), jnp.float32)
     early_shape = jax.ShapeDtypeStruct((REACH + WMAX, padded), jnp.float32)
     given = ()
-    for flip in range(inner):
+    for flip in (0, *range(inner - 1, 0, -1)):
         sums, *early = call(
             functools.partial(sums_kernel, flip > 0, outer, inner, flip),
-            [sums_shape, early_shape] if flip == inner - 1 else [sums_shape],
+            [sums_shape, early_shape] if flip == 1 else [sums_shape],
             [SMEM] + [VMEM] * (2 + len(given)),
             (me, blocks[flip], table, *given),
             scratch,

time: 30.8 us -> 31.1 us (level)
  waiting for transfers between devices: 6.66 us -> 7.08 us
    ppermute x6, waiting for transfers between devices: 5.44 us -> 5.87 us  [exchanged(): lax.ppermute(value, axis, [(source, source ^ flip) for source in range(co...]
  transfers between devices with their start and end apart: 7 -> 7, of which waited for: 5 -> 4; matrix products, arithmetic and copies ran while one was open for 0% -> 0% of each run, Pallas kernels for 23% -> 23%
where the time goes in v12:
time: 31.1 us; the launch traced here: 31 us
  Pallas kernels  13.2 us (42%)
  starting transfers between devices  10.6 us (34%)
  waiting for transfers between devices  7.08 us (23%)
    pallas_call x9, Pallas kernels, call(): pl.pallas_call(kernel, out_shape=out_shape, in_specs=in_specs, scratch_sh...  13.2 us
    ppermute x6, starting transfers between devices, exchanged(): lax.ppermute(value, axis, [(source, source ^ flip) for source in range(co...  9.31 us
    ppermute x6, waiting for transfers between devices, exchanged(): lax.ppermute(value, axis, [(source, source ^ flip) for source in range(co...  5.87 us
    ppermute x1, starting transfers between devices, passed_back(): lax.ppermute(value, axis, [(source, source - 1) for source in range(1, co...  1.29 us
    ppermute x1, waiting for transfers between devices, passed_back(): lax.ppermute(value, axis, [(source, source - 1) for source in range(1, co...  1.21 us
  transfers between devices with their start and end apart: 7, of which 4 were waited for; matrix products, arithmetic and copies ran while one was open for 0% of the time, Pallas kernels for 23%

profile of v12, /device:TPU:0, one launch (start us, length us, event | category | flops | bytes accessed | tf_op | source)
XLA Modules:
  0.0 31.0 jit_solution(17015646223802091835)
XLA Ops:
  0.0 1.9 %shard_map.46 = (bf16[144,128]{1,0:T(8,128)(2,1)S(1)}, s32[128,1024]{1,0:T(8,128)S(1)}) custom-call(s32[1,1024]{1,0:T(1,128)} %bitcast.7, bf16[1024,256]{1,0:T(8,128)(2,1)} %bitcast.6, s32[128,1024]{1,0:T(8,128)} %offsets_ref.1), custom_call_target="tpu_custom_call" | custom-call | bytes 1048576 | tf_op jit(solution)/shard_map/pallas_call | solution.py:240
  1.9 5.1 %collective-permute-start.2 = (bf16[144,128]{1,0:T(8,128)(2,1)S(1)}, bf16[144,128]{1,0:T(8,128)(2,1)S(1)}, u32[]{:S(2)}, u32[]{:S(2)}) collective-permute-start(bf16[144,128]{1,0:T(8,128)(2,1)S(1)} %get-tuple-element.9.refs_0_), channel_id=1, source_target_pairs={{0,24},{2,26},{4,28},{6,30},{8,16},{10,18},{12,20},{14,22},{16,8},... | collective-permute-start | bytes 110600 | tf_op jit(solution)/shard_map/ppermute | solution.py:32
  7.0 0.0 collective-permute-start.1
  7.1 0.6 %collective-permute-start = (bf16[144,128]{1,0:T(8,128)(2,1)S(1)}, bf16[144,128]{1,0:T(8,128)(2,1)S(1)}, u32[]{:S(2)}, u32[]{:S(2)}) collective-permute-start(bf16[144,128]{1,0:T(8,128)(2,1)S(1)} %get-tuple-element.9.refs_0_), channel_id=1, source_target_pairs={{0,8},{2,10},{4,12},{6,14},{8,0},{10,2},{12,4},{14,6},{16,24},{18,... | collective-permute-start | bytes 110600 | tf_op jit(solution)/shard_map/ppermute | solution.py:32
  7.7 0.2 shard_map.47.refs_4_.table_ref
  7.9 1.1 %collective-permute-done.2.refs_3_ = bf16[144,128]{1,0:T(8,128)(2,1)S(1)} collective-permute-done((bf16[144,128]{1,0:T(8,128)(2,1)S(1)}, bf16[144,128]{1,0:T(8,128)(2,1)S(1)}, u32[]{:S(2)}, u32[]{:S(2)}) %collective-permute-start.2) | collective-permute-done | bytes 36896 | tf_op jit(solution)/shard_map/ppermute | solution.py:32
  9.0 2.9 %collective-permute-done.1.refs_2_ = bf16[144,128]{1,0:T(8,128)(2,1)S(1)} collective-permute-done((bf16[144,128]{1,0:T(8,128)(2,1)S(1)}, bf16[144,128]{1,0:T(8,128)(2,1)S(1)}, u32[]{:S(2)}, u32[]{:S(2)}) %collective-permute-start.1) | collective-permute-done | bytes 36896 | tf_op jit(solution)/shard_map/ppermute | solution.py:32
  11.9 0.0 collective-permute-done.refs_1_
  11.9 0.1 shard_map.48.joined_ref
  12.0 2.5 %collective-permute-start.5 = (bf16[272,256]{1,0:T(8,128)(2,1)S(1)}, bf16[272,256]{1,0:T(8,128)(2,1)S(1)}, u32[]{:S(2)}, u32[]{:S(2)}) collective-permute-start(bf16[272,256]{1,0:T(8,128)(2,1)S(1)} %shard_map.48.joined_ref), channel_id=1, source_target_pairs={{0,6},{2,4},{4,2},{6,0},{8,14},{10,12},{12,10},{14,8},{16,22},{18,... | collective-permute-start | bytes 417800 | tf_op jit(solution)/shard_map/ppermute | solution.py:32
  14.5 0.5 %collective-permute-start.4 = (bf16[272,256]{1,0:T(8,128)(2,1)S(1)}, bf16[272,256]{1,0:T(8,128)(2,1)S(1)}, u32[]{:S(2)}, u32[]{:S(2)}) collective-permute-start(bf16[272,256]{1,0:T(8,128)(2,1)S(1)} %shard_map.48.joined_ref), channel_id=1, source_target_pairs={{0,4},{2,6},{4,0},{6,2},{8,12},{10,14},{12,8},{14,10},{16,20},{18,... | collective-permute-start | bytes 417800 | tf_op jit(solution)/shard_map/ppermute | solution.py:32
  15.0 0.5 %collective-permute-start.3 = (bf16[272,256]{1,0:T(8,128)(2,1)S(1)}, bf16[272,256]{1,0:T(8,128)(2,1)S(1)}, u32[]{:S(2)}, u32[]{:S(2)}) collective-permute-start(bf16[272,256]{1,0:T(8,128)(2,1)S(1)} %shard_map.48.joined_ref), channel_id=1, source_target_pairs={{0,2},{2,0},{4,6},{6,4},{8,10},{10,8},{12,14},{14,12},{16,18},{18,... | collective-permute-start | bytes 417800 | tf_op jit(solution)/shard_map/ppermute | solution.py:32
  15.6 2.1 %shard_map.49.refs_0_ = f32[368,128]{1,0:T(8,128)S(1)} custom-call(s32[1]{0:T(128)} %bitcast.me_ref, bf16[272,256]{1,0:T(8,128)(2,1)S(1)} %shard_map.48.joined_ref, f32[1024,128]{1,0:T(8,128)S(1)} %shard_map.47.refs_4_.table_ref), custom_call_target="tpu_custom_call" | custom-call | flops 1849688064 | bytes 1048576 | tf_op jit(solution)/shard_map/pallas_call | solution.py:240
  17.7 1.8 %collective-permute-done.5.joined_ref = bf16[272,256]{1,0:T(8,128)(2,1)S(1)} collective-permute-done((bf16[272,256]{1,0:T(8,128)(2,1)S(1)}, bf16[272,256]{1,0:T(8,128)(2,1)S(1)}, u32[]{:S(2)}, u32[]{:S(2)}) %collective-permute-start.5) | collective-permute-done | bytes 139296 | tf_op jit(solution)/shard_map/ppermute | solution.py:32
  19.5 2.1 %shard_map.50.refs_0_ = f32[368,128]{1,0:T(8,128)S(1)} custom-call(s32[1]{0:T(128)} %bitcast.me_ref, bf16[272,256]{1,0:T(8,128)(2,1)S(1)} %collective-permute-done.5.joined_ref, f32[1024,128]{1,0:T(8,128)S(1)} %shard_map.47.refs_4_.table_ref, f32[368,128]{1,0:T(8,128)S(1)} %shard_map.49.refs_0_), custom_call_target="tpu_custom_call" | custom-call | flops 1849688064 | bytes 1048576 | tf_op jit(solution)/shard_map/pallas_call | solution.py:240
  21.6 0.0 collective-permute-done.4.joined_ref
  21.7 2.1 %shard_map.51.refs_0_ = f32[368,128]{1,0:T(8,128)S(1)} custom-call(s32[1]{0:T(128)} %bitcast.me_ref, bf16[272,256]{1,0:T(8,128)(2,1)S(1)} %collective-permute-done.4.joined_ref, f32[1024,128]{1,0:T(8,128)S(1)} %shard_map.47.refs_4_.table_ref, f32[368,128]{1,0:T(8,128)S(1)} %shard_map.50.refs_0_), custom_call_target="tpu_custom_call" | custom-call | flops 1849688064 | bytes 1048576 | tf_op jit(solution)/shard_map/pallas_call | solution.py:240
  23.8 0.0 collective-permute-done.3.joined_ref
  23.8 2.1 %shard_map.52 = (f32[368,128]{1,0:T(8,128)S(1)}, f32[240,128]{1,0:T(8,128)S(1)}) custom-call(s32[1]{0:T(128)} %bitcast.me_ref, bf16[272,256]{1,0:T(8,128)(2,1)S(1)} %collective-permute-done.3.joined_ref, f32[1024,128]{1,0:T(8,128)S(1)} %shard_map.47.refs_4_.table_ref, f32[368,128]{1,0:T(8,128)S(1)} %shard_map.51.refs_0_), custom_call_target="tpu_custom_call" | custom-call | flops 1849688064 | bytes 1048576 | tf_op jit(solution)/shard_map/pallas_call | solution.py:240
  25.9 0.0 copy-start
  25.9 1.3 %collective-permute-start.6 = (f32[240,128]{1,0:T(8,128)S(1)}, f32[240,128]{1,0:T(8,128)S(1)}, u32[]{:S(2)}, u32[]{:S(2)}) collective-permute-start(f32[240,128]{1,0:T(8,128)S(1)} %get-tuple-element.11.early_ref), channel_id=1, source_target_pairs={{1,0},{3,2},{5,4},{7,6},{9,8},{11,10},{13,12},{15,14},{17,16},{19,... | collective-permute-start | bytes 368648 | tf_op jit(solution)/shard_map/ppermute | solution.py:27
  27.2 0.0 copy-done
  27.2 0.7 %shard_map.53.bands_ref = bf16[256,1024]{1,0:T(8,128)(2,1)S(1)} custom-call(s32[8]{0:T(128)S(1)} %copy-done, f32[240,128]{1,0:T(8,128)S(1)} %get-tuple-element.11.early_ref), custom_call_target="tpu_custom_call" | custom-call | bytes 1048576 | tf_op jit(solution)/shard_map/pallas_call | solution.py:240
  27.9 1.2 %collective-permute-done.6.later_ref = f32[240,128]{1,0:T(8,128)S(1)} collective-permute-done((f32[240,128]{1,0:T(8,128)S(1)}, f32[240,128]{1,0:T(8,128)S(1)}, u32[]{:S(2)}, u32[]{:S(2)}) %collective-permute-start.6) | collective-permute-done | bytes 122912 | tf_op jit(solution)/shard_map/ppermute | solution.py:27
  29.2 1.8 %shard_map.54 = f32[128,8,256]{2,1,0:T(8,128)} custom-call(s32[8]{0:T(128)S(1)} %copy-done, bf16[256,1024]{1,0:T(8,128)(2,1)S(1)} %shard_map.53.bands_ref, f32[368,128]{1,0:T(8,128)S(1)} %get-tuple-element.12.sums_ref, f32[240,128]{1,0:T(8,128)S(1)} %collective-permute-done.6.later_ref), custom_call_target="tpu_custom_call" | custom-call | bytes 1048576 | tf_op jit(solution)/shard_map/pallas_call | solution.py:240
Async XLA Ops:
  1.9 7.1 %collective-permute-start.2 = (bf16[144,128]{1,0:T(8,128)(2,1)S(1)}, bf16[144,128]{1,0:T(8,128)(2,1)S(1)}, u32[]{:S(2)}, u32[]{:S(2)}) collective-permute-start(bf16[144,128]{1,0:T(8,128)(2,1)S(1)} %get-tuple-element.9.refs_0_), channel_id=1, source_target_pairs={{0,24},{2,26},{4,28},{6,30},{8,16},{10,18},{12,20},{14,22},{16,8},... | collective-permute-start | bytes 110600 | tf_op jit(solution)/shard_map/ppermute | solution.py:32
  7.0 4.9 %collective-permute-start.1 = (bf16[144,128]{1,0:T(8,128)(2,1)S(1)}, bf16[144,128]{1,0:T(8,128)(2,1)S(1)}, u32[]{:S(2)}, u32[]{:S(2)}) collective-permute-start(bf16[144,128]{1,0:T(8,128)(2,1)S(1)} %get-tuple-element.9.refs_0_), channel_id=1, source_target_pairs={{0,16},{2,18},{4,20},{6,22},{8,24},{10,26},{12,28},{14,30},{16,0},... | collective-permute-start | bytes 110600 | tf_op jit(solution)/shard_map/ppermute | solution.py:32
  7.1 4.9 %collective-permute-start = (bf16[144,128]{1,0:T(8,128)(2,1)S(1)}, bf16[144,128]{1,0:T(8,128)(2,1)S(1)}, u32[]{:S(2)}, u32[]{:S(2)}) collective-permute-start(bf16[144,128]{1,0:T(8,128)(2,1)S(1)} %get-tuple-element.9.refs_0_), channel_id=1, source_target_pairs={{0,8},{2,10},{4,12},{6,14},{8,0},{10,2},{12,4},{14,6},{16,24},{18,... | collective-permute-start | bytes 110600 | tf_op jit(solution)/shard_map/ppermute | solution.py:32
  12.0 7.5 %collective-permute-start.5 = (bf16[272,256]{1,0:T(8,128)(2,1)S(1)}, bf16[272,256]{1,0:T(8,128)(2,1)S(1)}, u32[]{:S(2)}, u32[]{:S(2)}) collective-permute-start(bf16[272,256]{1,0:T(8,128)(2,1)S(1)} %shard_map.48.joined_ref), channel_id=1, source_target_pairs={{0,6},{2,4},{4,2},{6,0},{8,14},{10,12},{12,10},{14,8},{16,22},{18,... | collective-permute-start | bytes 417800 | tf_op jit(solution)/shard_map/ppermute | solution.py:32
  14.5 7.1 %collective-permute-start.4 = (bf16[272,256]{1,0:T(8,128)(2,1)S(1)}, bf16[272,256]{1,0:T(8,128)(2,1)S(1)}, u32[]{:S(2)}, u32[]{:S(2)}) collective-permute-start(bf16[272,256]{1,0:T(8,128)(2,1)S(1)} %shard_map.48.joined_ref), channel_id=1, source_target_pairs={{0,4},{2,6},{4,0},{6,2},{8,12},{10,14},{12,8},{14,10},{16,20},{18,... | collective-permute-start | bytes 417800 | tf_op jit(solution)/shard_map/ppermute | solution.py:32
  15.0 8.7 %collective-permute-start.3 = (bf16[272,256]{1,0:T(8,128)(2,1)S(1)}, bf16[272,256]{1,0:T(8,128)(2,1)S(1)}, u32[]{:S(2)}, u32[]{:S(2)}) collective-permute-start(bf16[272,256]{1,0:T(8,128)(2,1)S(1)} %shard_map.48.joined_ref), channel_id=1, source_target_pairs={{0,2},{2,0},{4,6},{6,4},{8,10},{10,8},{12,14},{14,12},{16,18},{18,... | collective-permute-start | bytes 417800 | tf_op jit(solution)/shard_map/ppermute | solution.py:32
  25.9 1.3 %copy-start = (s32[8]{0:T(128)S(1)}, s32[8]{0:T(128)}, u32[]{:S(2)}) copy-start(s32[8]{0:T(128)} %widths_ref.3) | copy-start | bytes 100
  25.9 3.2 %collective-permute-start.6 = (f32[240,128]{1,0:T(8,128)S(1)}, f32[240,128]{1,0:T(8,128)S(1)}, u32[]{:S(2)}, u32[]{:S(2)}) collective-permute-start(f32[240,128]{1,0:T(8,128)S(1)} %get-tuple-element.11.early_ref), channel_id=1, source_target_pairs={{1,0},{3,2},{5,4},{7,6},{9,8},{11,10},{13,12},{15,14},{17,16},{19,... | collective-permute-start | bytes 368648 | tf_op jit(solution)/shard_map/ppermute | solution.py:27

commit v13 on v11

--- a/solution.py
+++ b/solution.py
@@ -14,6 +14,7 @@
 LANES = 128
 STEP = 16
 GROUPS = OMAX // STEP
+TOGETHER = 1
 REACH = OMAX + DCH
 VMEM = pl.BlockSpec(memory_space=pltpu.VMEM)
 SMEM = pl.BlockSpec(memory_space=pltpu.SMEM)
@@ -58,11 +59,10 @@
         jnp.where(rows == delays[:, at * block : (at + 1) * block] * subs + owner, 1.0, 0.0).astype(jnp.bfloat16)
         for at in range(chans // block)
     ]
+    for copy in copies[:steps]:
+        copy.wait()
     parts = []
     for at, member in enumerate(members):
-        if at * 2 % steps == 0:
-            for copy in copies[at : at + steps // 2] if len(members) == steps else copies[:steps]:
-                copy.wait()
         picked = jnp.dot(member, held[pl.ds(at * block, block), :], preferred_element_type=jnp.float32)
         total = None
         for delay in range(DCH):
@@ -134,56 +134,67 @@
         total[pl.ds(first, rows), :] += both[:, odd * trials : (odd + 1) * trials]
 
 
-def sums_kernel(given, outer, inner, flip, me_ref, joined_ref, table_ref, *refs):
+def sums_kernel(given, here, outer, inner, flip, me_ref, joined_ref, table_ref, *refs):
     pairs = GROUPS // 2
     before_ref, sums_ref, *early_ref = refs[: -3 - pairs] if given else (None, *refs[: -3 - pairs])
     moving, shifted, table = refs[-3 - pairs : -pairs]
     totals = refs[-pairs:]
-    span, nsub = joined_ref.shape
-    subs = nsub // outer
-    for slot in range(outer):
-        start = slot_start(slot, flip, outer, inner, subs, me_ref[0])
-        table[pl.ds(slot * subs, subs), :] = table_ref[pl.ds(start, subs), :]
-    blank = jnp.zeros((STEP, nsub), jnp.float32)
-    moving[pl.ds(0, STEP), :] = blank
-    moving[pl.ds(STEP, span), :] = joined_ref[...].astype(jnp.float32)
-    moving[pl.ds(STEP + span, STEP), :] = blank
-
-    def shift(lag):
-        shifted[:, pl.ds(lag * nsub, nsub)] = moving[pl.ds(lag, span + STEP), :].astype(jnp.bfloat16)
-
-    shift(0)
-    for lag in range(STEP + 1):
-        if lag < STEP:
-            shift(lag + 1)
-        for pair in range(pairs - 1 if lag == STEP else 0, pairs):
-            weights = [
+    if before_ref is None:
+        sums_ref[...] = jnp.zeros_like(sums_ref)
+    else:
+        sums_ref[...] = before_ref[...]
+
+    def add_block():
+        span, nsub = joined_ref.shape
+        subs = nsub // outer
+        for slot in range(outer):
+            start = slot_start(slot, flip, outer, inner, subs, me_ref[0])
+            table[pl.ds(slot * subs, subs), :] = table_ref[pl.ds(start, subs), :]
+        blank = jnp.zeros((STEP, nsub), jnp.float32)
+        moving[pl.ds(0, STEP), :] = blank
+        moving[pl.ds(STEP, span), :] = joined_ref[...].astype(jnp.float32)
+        moving[pl.ds(STEP + span, STEP), :] = blank
+
+        def shift(lag):
+            shifted[:, pl.ds(lag * nsub, nsub)] = moving[pl.ds(lag, span + STEP), :].astype(jnp.bfloat16)
+
+        def tile(lag, pair):
+            halves = [
                 jnp.where(table[...] == float(STEP * (2 * pair + odd) + lag), 1.0, 0.0).astype(jnp.bfloat16)
                 if lag < STEP or odd
                 else jnp.zeros(table.shape, jnp.bfloat16)
                 for odd in range(2)
             ]
-            both = jnp.dot(
-                shifted[:, pl.ds(lag * nsub, nsub)],
-                jnp.concatenate(weights, axis=1),
-                preferred_element_type=jnp.float32,
-            )
-            if lag:
-                totals[pair][...] += both
-            else:
-                totals[pair][...] = both
-    if before_ref is None:
-        sums_ref[...] = jnp.zeros_like(sums_ref)
+            return jnp.concatenate(halves, axis=1)
+
+        for lag in range(TOGETHER):
+            shift(lag)
+        for first in range(0, STEP + 1, TOGETHER):
+            lags = range(first, min(first + TOGETHER, STEP + 1))
+            for lag in range(first + TOGETHER, min(first + 2 * TOGETHER, STEP + 1)):
+                shift(lag)
+            for pair in range(pairs - 1 if first == STEP else 0, pairs):
+                both = jnp.dot(
+                    shifted[:, pl.ds(first * nsub, len(lags) * nsub)],
+                    jnp.concatenate([tile(lag, pair) for lag in lags], axis=0),
+                    preferred_element_type=jnp.float32,
+                )
+                if first:
+                    totals[pair][...] += both
+                else:
+                    totals[pair][...] = both
+        for pair in range(pairs):
+            add_pair(sums_ref, pair, totals[pair][...])
+
+    if here is None:
+        add_block()
     else:
-        sums_ref[...] = before_ref[...]
-    for pair in range(pairs):
-        add_pair(sums_ref, pair, totals[pair][...])
+        pl.when(here(me_ref[1]))(add_block)
     for ref in early_ref:
         ref[...] = sums_ref[pl.ds(0, ref.shape[0]), :]
 
 
-def bands_kernel(widths_ref, early_ref, bands_ref):
-    del early_ref
+def bands_kernel(widths_ref, bands_ref):
     shape = (bands_ref.shape[0], LANES)
     lag = lax.broadcasted_iota(jnp.int32, shape, 0) - lax.broadcasted_iota(jnp.int32, shape, 1)
     for at in range(widths_ref.shape[0]):
@@ -271,11 +282,17 @@
     line = [series] + [exchanged(series, "sub", flip * inner) for flip in range(1, outer)]
     nsub = outer * sub_dev
     table = call(offsets_kernel, jax.ShapeDtypeStruct((all_subs, padded), jnp.float32), [VMEM], (fetched,))
+    bands = call(
+        bands_kernel,
+        jax.ShapeDtypeStruct((LANES + WMAX, filters * LANES), jnp.bfloat16),
+        [SMEM],
+        (widths,),
+    )
     joined = call(
         functools.partial(join_packed_kernel if packed else join_kernel, outer),
         jax.ShapeDtypeStruct((span, nsub), jnp.bfloat16),
-        [VMEM] * outer + [ANY],
-        (*line, table),
+        [VMEM] * outer + [ANY] * 2,
+        (*line, table, bands),
     )
     blocks = [joined] + [exchanged(joined, "sub", flip) for flip in range(1, inner)]
     scratch = [
@@ -287,25 +304,21 @@
     flops = 2 * (span + STEP) * nsub * padded * (OMAX + 2)
     sums_shape = jax.ShapeDtypeStruct((length + REACH, padded), jnp.float32)
     early_shape = jax.ShapeDtypeStruct((REACH + WMAX, padded), jnp.float32)
+    steps = [(flip, None) for flip in range(inner - 1)]
+    steps += [(inner - 1, lambda tm: tm > 0), (inner - 1, lambda tm: tm == 0)]
     given = ()
-    for flip in range(inner):
-        sums, *early = call(
-            functools.partial(sums_kernel, flip > 0, outer, inner, flip),
-            [sums_shape, early_shape] if flip == inner - 1 else [sums_shape],
+    for at, (flip, here) in enumerate(steps):
+        sums, *rest = call(
+            functools.partial(sums_kernel, at > 0, here, outer, inner, flip),
+            [sums_shape, early_shape] if at == inner - 1 else [sums_shape],
             [SMEM] + [VMEM] * (2 + len(given)),
             (me, blocks[flip], table, *given),
             scratch,
             flops,
         )
         given = (sums,)
-    early = early[0]
-    later = passed_back(early, "tm")
-    bands = call(
-        bands_kernel,
-        jax.ShapeDtypeStruct((LANES + WMAX, filters * LANES), jnp.bfloat16),
-        [SMEM, ANY],
-        (widths, early),
-    )
+        if rest:
+            later = passed_back(rest[0], "tm")
     parts = length // LANES
     pieces = 2
     return call(
@@ -332,7 +345,7 @@
     scale = 1.0 / math.sqrt(chans * groups)
     padded = max(trials, LANES)
     table = jnp.pad(offsets, ((0, padded - trials), (0, 0))) if padded > trials else offsets
-    me = lax.axis_index("sub").astype(jnp.int32).reshape(1)
+    me = jnp.stack([lax.axis_index("sub"), lax.axis_index("tm")]).astype(jnp.int32)
     outs = [
         one_beam(data[beam], delays, table, me, widths, groups, outer, per_sub, scale)[:trials, None]
         for beam in range(beams)

time: 30.8 us -> 30.4 us (0.987)
  waiting for transfers between devices: 6.66 us -> 3.01 us
  Pallas kernels: 13.3 us -> 15.8 us
  local copies, waits for them, and re-layouts: 0.01 us -> 0.58 us
    pallas_call x9 -> x10, Pallas kernels: 13.3 us -> 15.8 us  [call(): pl.pallas_call(kernel, out_shape=out_shape, in_specs=in_specs, scratch_sh...]
    ppermute x6, waiting for transfers between devices: 5.44 us -> 3.01 us  [exchanged(): lax.ppermute(value, axis, [(source, source ^ flip) for source in range(co...]
    ppermute x1, waiting for transfers between devices: 1.21 us -> 0.01 us  [passed_back(): lax.ppermute(value, axis, [(source, source - 1) for source in range(1, co...]
    unnamed x2, local copies, waits for them, and re-layouts: 0.01 us -> 0.58 us
  transfers between devices with their start and end apart: 7 -> 7, of which waited for: 5 -> 3; matrix products, arithmetic and copies ran while one was open for 0% -> 0% of each run, Pallas kernels for 23% -> 38%
where the time goes in v13:
time: 30.4 us; the launch traced here: 30.2 us
  Pallas kernels  15.8 us (52%)
  starting transfers between devices  10.6 us (35%)
  waiting for transfers between devices  3.01 us (10%)
  local copies, waits for them, and re-layouts  0.58 us (2%)
    pallas_call x10, Pallas kernels, call(): pl.pallas_call(kernel, out_shape=out_shape, in_specs=in_specs, scratch_sh...  15.8 us
    ppermute x6, starting transfers between devices, exchanged(): lax.ppermute(value, axis, [(source, source ^ flip) for source in range(co...  9.31 us
    ppermute x6, waiting for transfers between devices, exchanged(): lax.ppermute(value, axis, [(source, source ^ flip) for source in range(co...  3.01 us
    ppermute x1, starting transfers between devices, passed_back(): lax.ppermute(value, axis, [(source, source - 1) for source in range(1, co...  1.29 us
  transfers between devices with their start and end apart: 7, of which 3 were waited for; matrix products, arithmetic and copies ran while one was open for 0% of the time, Pallas kernels for 38%

profile of v13, /device:TPU:0, one launch (start us, length us, event | category | flops | bytes accessed | tf_op | source)
XLA Modules:
  0.0 30.2 jit_solution(5573411305077173551)
XLA Ops:
  0.0 1.9 %shard_map.47 = (bf16[144,128]{1,0:T(8,128)(2,1)S(1)}, s32[128,1024]{1,0:T(8,128)S(1)}) custom-call(s32[1,1024]{1,0:T(1,128)} %bitcast.8, bf16[1024,256]{1,0:T(8,128)(2,1)} %bitcast.7, s32[128,1024]{1,0:T(8,128)} %offsets_ref.1), custom_call_target="tpu_custom_call" | custom-call | bytes 1048576 | tf_op jit(solution)/shard_map/pallas_call | solution.py:246
  1.9 5.1 %collective-permute-start.2 = (bf16[144,128]{1,0:T(8,128)(2,1)S(1)}, bf16[144,128]{1,0:T(8,128)(2,1)S(1)}, u32[]{:S(2)}, u32[]{:S(2)}) collective-permute-start(bf16[144,128]{1,0:T(8,128)(2,1)S(1)} %get-tuple-element.9.refs_0_), channel_id=1, source_target_pairs={{0,24},{2,26},{4,28},{6,30},{8,16},{10,18},{12,20},{14,22},{16,8},... | collective-permute-start | bytes 110600 | tf_op jit(solution)/shard_map/ppermute | solution.py:32
  7.0 0.0 collective-permute-start.1
  7.1 0.6 %collective-permute-start = (bf16[144,128]{1,0:T(8,128)(2,1)S(1)}, bf16[144,128]{1,0:T(8,128)(2,1)S(1)}, u32[]{:S(2)}, u32[]{:S(2)}) collective-permute-start(bf16[144,128]{1,0:T(8,128)(2,1)S(1)} %get-tuple-element.9.refs_0_), channel_id=1, source_target_pairs={{0,8},{2,10},{4,12},{6,14},{8,0},{10,2},{12,4},{14,6},{16,24},{18,... | collective-permute-start | bytes 110600 | tf_op jit(solution)/shard_map/ppermute | solution.py:32
  7.7 0.0 copy-start
  7.7 0.1 pad_add_fusion.me_ref
  7.8 0.6 %copy-done = s32[8]{0:T(128)S(1)} copy-done((s32[8]{0:T(128)S(1)}, s32[8]{0:T(128)}, u32[]{:S(2)}) %copy-start) | copy-done | bytes 56
  8.3 0.7 %shard_map.46.refs_5_.bands_ref = bf16[256,1024]{1,0:T(8,128)(2,1)S(1)} custom-call(s32[8]{0:T(128)S(1)} %copy-done), custom_call_target="tpu_custom_call" | custom-call | bytes 1048576 | tf_op jit(solution)/shard_map/pallas_call | solution.py:246
  9.1 0.2 shard_map.48.refs_4_.table_ref
  9.2 0.0 collective-permute-done.2.refs_3_
  9.3 2.6 %collective-permute-done.1.refs_2_ = bf16[144,128]{1,0:T(8,128)(2,1)S(1)} collective-permute-done((bf16[144,128]{1,0:T(8,128)(2,1)S(1)}, bf16[144,128]{1,0:T(8,128)(2,1)S(1)}, u32[]{:S(2)}, u32[]{:S(2)}) %collective-permute-start.1) | collective-permute-done | bytes 36896 | tf_op jit(solution)/shard_map/ppermute | solution.py:32
  11.9 0.0 collective-permute-done.refs_1_
  11.9 0.1 shard_map.49.joined_ref
  12.0 1.6 %collective-permute-start.5 = (bf16[272,256]{1,0:T(8,128)(2,1)S(1)}, bf16[272,256]{1,0:T(8,128)(2,1)S(1)}, u32[]{:S(2)}, u32[]{:S(2)}) collective-permute-start(bf16[272,256]{1,0:T(8,128)(2,1)S(1)} %shard_map.49.joined_ref), channel_id=1, source_target_pairs={{0,2},{2,0},{4,6},{6,4},{8,10},{10,8},{12,14},{14,12},{16,18},{18,... | collective-permute-start | bytes 417800 | tf_op jit(solution)/shard_map/ppermute | solution.py:32
  13.6 1.5 %collective-permute-start.4 = (bf16[272,256]{1,0:T(8,128)(2,1)S(1)}, bf16[272,256]{1,0:T(8,128)(2,1)S(1)}, u32[]{:S(2)}, u32[]{:S(2)}) collective-permute-start(bf16[272,256]{1,0:T(8,128)(2,1)S(1)} %shard_map.49.joined_ref), channel_id=1, source_target_pairs={{0,4},{2,6},{4,0},{6,2},{8,12},{10,14},{12,8},{14,10},{16,20},{18,... | collective-permute-start | bytes 417800 | tf_op jit(solution)/shard_map/ppermute | solution.py:32
  15.1 0.5 %collective-permute-start.3 = (bf16[272,256]{1,0:T(8,128)(2,1)S(1)}, bf16[272,256]{1,0:T(8,128)(2,1)S(1)}, u32[]{:S(2)}, u32[]{:S(2)}) collective-permute-start(bf16[272,256]{1,0:T(8,128)(2,1)S(1)} %shard_map.49.joined_ref), channel_id=1, source_target_pairs={{0,6},{2,4},{4,2},{6,0},{8,14},{10,12},{12,10},{14,8},{16,22},{18,... | collective-permute-start | bytes 417800 | tf_op jit(solution)/shard_map/ppermute | solution.py:32
  15.6 2.6 %shard_map.50.refs_0_ = f32[368,128]{1,0:T(8,128)S(1)} custom-call(s32[2]{0:T(128)S(1)} %pad_add_fusion.me_ref, bf16[272,256]{1,0:T(8,128)(2,1)S(1)} %shard_map.49.joined_ref, f32[1024,128]{1,0:T(8,128)S(1)} %shard_map.48.refs_4_.table_ref), custom_call_target="tpu_custom_call" | custom-call | flops 1849688064 | bytes 1048576 | tf_op jit(solution)/shard_map/pallas_call | solution.py:246
  18.2 0.3 collective-permute-done.5.joined_ref
  18.5 2.6 %shard_map.51.refs_0_ = f32[368,128]{1,0:T(8,128)S(1)} custom-call(s32[2]{0:T(128)S(1)} %pad_add_fusion.me_ref, bf16[272,256]{1,0:T(8,128)(2,1)S(1)} %collective-permute-done.5.joined_ref, f32[1024,128]{1,0:T(8,128)S(1)} %shard_map.48.refs_4_.table_ref, f32[368,128]{1,0:T(8,128)S(1)} %shard_map.50.refs_0_), custom_call_target="tpu_custom_call" | custom-call | flops 1849688064 | bytes 1048576 | tf_op jit(solution)/shard_map/pallas_call | solution.py:246
  21.1 0.1 collective-permute-done.4.joined_ref
  21.2 2.6 %shard_map.52.refs_0_ = f32[368,128]{1,0:T(8,128)S(1)} custom-call(s32[2]{0:T(128)S(1)} %pad_add_fusion.me_ref, bf16[272,256]{1,0:T(8,128)(2,1)S(1)} %collective-permute-done.4.joined_ref, f32[1024,128]{1,0:T(8,128)S(1)} %shard_map.48.refs_4_.table_ref, f32[368,128]{1,0:T(8,128)S(1)} %shard_map.51.refs_0_), custom_call_target="tpu_custom_call" | custom-call | flops 1849688064 | bytes 1048576 | tf_op jit(solution)/shard_map/pallas_call | solution.py:246
  23.8 0.0 collective-permute-done.3.joined_ref
  23.8 0.6 %shard_map.53 = (f32[368,128]{1,0:T(8,128)S(1)}, f32[240,128]{1,0:T(8,128)S(1)}) custom-call(s32[2]{0:T(128)S(1)} %pad_add_fusion.me_ref, bf16[272,256]{1,0:T(8,128)(2,1)S(1)} %collective-permute-done.3.joined_ref, f32[1024,128]{1,0:T(8,128)S(1)} %shard_map.48.refs_4_.table_ref, f32[368,128]{1,0:T(8,128)S(1)} %shard_map.52.refs_0_), custom_call_target="tpu_custom_call" | custom-call | flops 1849688064 | bytes 1048576 | tf_op jit(solution)/shard_map/pallas_call | solution.py:246
  24.4 1.3 %collective-permute-start.6 = (f32[240,128]{1,0:T(8,128)S(1)}, f32[240,128]{1,0:T(8,128)S(1)}, u32[]{:S(2)}, u32[]{:S(2)}) collective-permute-start(f32[240,128]{1,0:T(8,128)S(1)} %get-tuple-element.12), channel_id=1, source_target_pairs={{1,0},{3,2},{5,4},{7,6},{9,8},{11,10},{13,12},{15,14},{17,16},{19,... | collective-permute-start | bytes 368648 | tf_op jit(solution)/shard_map/ppermute | solution.py:27
  25.7 2.6 %shard_map.54.sums_ref = f32[368,128]{1,0:T(8,128)S(1)} custom-call(s32[2]{0:T(128)S(1)} %pad_add_fusion.me_ref, bf16[272,256]{1,0:T(8,128)(2,1)S(1)} %collective-permute-done.3.joined_ref, f32[1024,128]{1,0:T(8,128)S(1)} %shard_map.48.refs_4_.table_ref, f32[368,128]{1,0:T(8,128)S(1)} %get-tuple-element.11.refs_0_), custom_call_target="tpu_custom_call" | custom-call | flops 1849688064 | bytes 1048576 | tf_op jit(solution)/shard_map/pallas_call | solution.py:246
  28.4 0.0 collective-permute-done.6.later_ref
  28.4 1.8 %shard_map.55 = f32[128,8,256]{2,1,0:T(8,128)} custom-call(s32[8]{0:T(128)S(1)} %copy-done, bf16[256,1024]{1,0:T(8,128)(2,1)S(1)} %shard_map.46.refs_5_.bands_ref, f32[368,128]{1,0:T(8,128)S(1)} %shard_map.54.sums_ref, f32[240,128]{1,0:T(8,128)S(1)} %collective-permute-done.6.later_ref), custom_call_target="tpu_custom_call" | custom-call | bytes 1048576 | tf_op jit(solution)/shard_map/pallas_call | solution.py:246
Async XLA Ops:
  1.9 7.3 %collective-permute-start.2 = (bf16[144,128]{1,0:T(8,128)(2,1)S(1)}, bf16[144,128]{1,0:T(8,128)(2,1)S(1)}, u32[]{:S(2)}, u32[]{:S(2)}) collective-permute-start(bf16[144,128]{1,0:T(8,128)(2,1)S(1)} %get-tuple-element.9.refs_0_), channel_id=1, source_target_pairs={{0,24},{2,26},{4,28},{6,30},{8,16},{10,18},{12,20},{14,22},{16,8},... | collective-permute-start | bytes 110600 | tf_op jit(solution)/shard_map/ppermute | solution.py:32
  7.0 4.9 %collective-permute-start.1 = (bf16[144,128]{1,0:T(8,128)(2,1)S(1)}, bf16[144,128]{1,0:T(8,128)(2,1)S(1)}, u32[]{:S(2)}, u32[]{:S(2)}) collective-permute-start(bf16[144,128]{1,0:T(8,128)(2,1)S(1)} %get-tuple-element.9.refs_0_), channel_id=1, source_target_pairs={{0,16},{2,18},{4,20},{6,22},{8,24},{10,26},{12,28},{14,30},{16,0},... | collective-permute-start | bytes 110600 | tf_op jit(solution)/shard_map/ppermute | solution.py:32
  7.1 4.9 %collective-permute-start = (bf16[144,128]{1,0:T(8,128)(2,1)S(1)}, bf16[144,128]{1,0:T(8,128)(2,1)S(1)}, u32[]{:S(2)}, u32[]{:S(2)}) collective-permute-start(bf16[144,128]{1,0:T(8,128)(2,1)S(1)} %get-tuple-element.9.refs_0_), channel_id=1, source_target_pairs={{0,8},{2,10},{4,12},{6,14},{8,0},{10,2},{12,4},{14,6},{16,24},{18,... | collective-permute-start | bytes 110600 | tf_op jit(solution)/shard_map/ppermute | solution.py:32
  7.7 0.7 %copy-start = (s32[8]{0:T(128)S(1)}, s32[8]{0:T(128)}, u32[]{:S(2)}) copy-start(s32[8]{0:T(128)} %widths_ref.3) | copy-start | bytes 100
  12.0 6.4 %collective-permute-start.5 = (bf16[272,256]{1,0:T(8,128)(2,1)S(1)}, bf16[272,256]{1,0:T(8,128)(2,1)S(1)}, u32[]{:S(2)}, u32[]{:S(2)}) collective-permute-start(bf16[272,256]{1,0:T(8,128)(2,1)S(1)} %shard_map.49.joined_ref), channel_id=1, source_target_pairs={{0,2},{2,0},{4,6},{6,4},{8,10},{10,8},{12,14},{14,12},{16,18},{18,... | collective-permute-start | bytes 417800 | tf_op jit(solution)/shard_map/ppermute | solution.py:32
  13.6 7.6 %collective-permute-start.4 = (bf16[272,256]{1,0:T(8,128)(2,1)S(1)}, bf16[272,256]{1,0:T(8,128)(2,1)S(1)}, u32[]{:S(2)}, u32[]{:S(2)}) collective-permute-start(bf16[272,256]{1,0:T(8,128)(2,1)S(1)} %shard_map.49.joined_ref), channel_id=1, source_target_pairs={{0,4},{2,6},{4,0},{6,2},{8,12},{10,14},{12,8},{14,10},{16,20},{18,... | collective-permute-start | bytes 417800 | tf_op jit(solution)/shard_map/ppermute | solution.py:32
  15.1 8.7 %collective-permute-start.3 = (bf16[272,256]{1,0:T(8,128)(2,1)S(1)}, bf16[272,256]{1,0:T(8,128)(2,1)S(1)}, u32[]{:S(2)}, u32[]{:S(2)}) collective-permute-start(bf16[272,256]{1,0:T(8,128)(2,1)S(1)} %shard_map.49.joined_ref), channel_id=1, source_target_pairs={{0,6},{2,4},{4,2},{6,0},{8,14},{10,12},{12,10},{14,8},{16,22},{18,... | collective-permute-start | bytes 417800 | tf_op jit(solution)/shard_map/ppermute | solution.py:32
  24.4 3.9 %collective-permute-start.6 = (f32[240,128]{1,0:T(8,128)S(1)}, f32[240,128]{1,0:T(8,128)S(1)}, u32[]{:S(2)}, u32[]{:S(2)}) collective-permute-start(f32[240,128]{1,0:T(8,128)S(1)} %get-tuple-element.12), channel_id=1, source_target_pairs={{1,0},{3,2},{5,4},{7,6},{9,8},{11,10},{13,12},{15,14},{17,16},{19,... | collective-permute-start | bytes 368648 | tf_op jit(solution)/shard_map/ppermute | solution.py:27

commit v14 on v13

--- a/solution.py
+++ b/solution.py
@@ -134,7 +134,7 @@
         total[pl.ds(first, rows), :] += both[:, odd * trials : (odd + 1) * trials]
 
 
-def sums_kernel(given, here, outer, inner, flip, me_ref, joined_ref, table_ref, *refs):
+def sums_kernel(given, here, outer, inner, flip, me_ref, tm_ref, joined_ref, table_ref, *refs):
     pairs = GROUPS // 2
     before_ref, sums_ref, *early_ref = refs[: -3 - pairs] if given else (None, *refs[: -3 - pairs])
     moving, shifted, table = refs[-3 - pairs : -pairs]
@@ -189,7 +189,7 @@
     if here is None:
         add_block()
     else:
-        pl.when(here(me_ref[1]))(add_block)
+        pl.when(here(tm_ref[0]))(add_block)
     for ref in early_ref:
         ref[...] = sums_ref[pl.ds(0, ref.shape[0]), :]
 
@@ -311,8 +311,8 @@
         sums, *rest = call(
             functools.partial(sums_kernel, at > 0, here, outer, inner, flip),
             [sums_shape, early_shape] if at == inner - 1 else [sums_shape],
-            [SMEM] + [VMEM] * (2 + len(given)),
-            (me, blocks[flip], table, *given),
+            [SMEM] * 2 + [VMEM] * (2 + len(given)),
+            (*me, blocks[flip], table, *given),
             scratch,
             flops,
         )
@@ -345,7 +345,7 @@
     scale = 1.0 / math.sqrt(chans * groups)
     padded = max(trials, LANES)
     table = jnp.pad(offsets, ((0, padded - trials), (0, 0))) if padded > trials else offsets
-    me = jnp.stack([lax.axis_index("sub"), lax.axis_index("tm")]).astype(jnp.int32)
+    me = [lax.axis_index(axis).astype(jnp.int32).reshape(1) for axis in ("sub", "tm")]
     outs = [
         one_beam(data[beam], delays, table, me, widths, groups, outer, per_sub, scale)[:trials, None]
         for beam in range(beams)

time: 30.4 us -> 28.7 us (0.944)
  Pallas kernels: 15.8 us -> 13.1 us
  waiting for transfers between devices: 3.01 us -> 4.09 us
    pallas_call x10, Pallas kernels: 15.8 us -> 13.1 us  [call(): pl.pallas_call(kernel, out_shape=out_shape, in_specs=in_specs, scratch_sh...]
    ppermute x6, waiting for transfers between devices: 3.01 us -> 4.09 us  [exchanged(): lax.ppermute(value, axis, [(source, source ^ flip) for source in range(co...]
  transfers between devices with their start and end apart: 7 -> 7, of which waited for: 3 -> 3; matrix products, arithmetic and copies ran while one was open for 0% -> 0% of each run, Pallas kernels for 38% -> 32%
where the time goes in v14:
time: 28.7 us; the launch traced here: 28.6 us
  Pallas kernels  13.1 us (46%)
  starting transfers between devices  10.6 us (37%)
  waiting for transfers between devices  4.09 us (14%)
  local copies, waits for them, and re-layouts  0.65 us (2%)
    pallas_call x10, Pallas kernels, call(): pl.pallas_call(kernel, out_shape=out_shape, in_specs=in_specs, scratch_sh...  13.1 us
    ppermute x6, starting transfers between devices, exchanged(): lax.ppermute(value, axis, [(source, source ^ flip) for source in range(co...  9.31 us
    ppermute x6, waiting for transfers between devices, exchanged(): lax.ppermute(value, axis, [(source, source ^ flip) for source in range(co...  4.09 us
    ppermute x1, starting transfers between devices, passed_back(): lax.ppermute(value, axis, [(source, source - 1) for source in range(1, co...  1.29 us
    unnamed x2, local copies, waits for them, and re-layouts  0.65 us
  transfers between devices with their start and end apart: 7, of which 3 were waited for; matrix products, arithmetic and copies ran while one was open for 0% of the time, Pallas kernels for 32%

profile of v14, /device:TPU:0, one launch (start us, length us, event | category | flops | bytes accessed | tf_op | source)
XLA Modules:
  0.0 28.6 jit_solution(15027847776900388293)
XLA Ops:
  0.0 1.9 %shard_map.47 = (bf16[144,128]{1,0:T(8,128)(2,1)S(1)}, s32[128,1024]{1,0:T(8,128)S(1)}) custom-call(s32[1,1024]{1,0:T(1,128)} %bitcast.8, bf16[1024,256]{1,0:T(8,128)(2,1)} %bitcast.7, s32[128,1024]{1,0:T(8,128)} %offsets_ref.1), custom_call_target="tpu_custom_call" | custom-call | bytes 1048576 | tf_op jit(solution)/shard_map/pallas_call | solution.py:246
  1.9 5.1 %collective-permute-start.2 = (bf16[144,128]{1,0:T(8,128)(2,1)S(1)}, bf16[144,128]{1,0:T(8,128)(2,1)S(1)}, u32[]{:S(2)}, u32[]{:S(2)}) collective-permute-start(bf16[144,128]{1,0:T(8,128)(2,1)S(1)} %get-tuple-element.9.refs_0_), channel_id=1, source_target_pairs={{0,24},{2,26},{4,28},{6,30},{8,16},{10,18},{12,20},{14,22},{16,8},... | collective-permute-start | bytes 110600 | tf_op jit(solution)/shard_map/ppermute | solution.py:32
  7.0 0.0 collective-permute-start.1
  7.1 0.6 %collective-permute-start = (bf16[144,128]{1,0:T(8,128)(2,1)S(1)}, bf16[144,128]{1,0:T(8,128)(2,1)S(1)}, u32[]{:S(2)}, u32[]{:S(2)}) collective-permute-start(bf16[144,128]{1,0:T(8,128)(2,1)S(1)} %get-tuple-element.9.refs_0_), channel_id=1, source_target_pairs={{0,8},{2,10},{4,12},{6,14},{8,0},{10,2},{12,4},{14,6},{16,24},{18,... | collective-permute-start | bytes 110600 | tf_op jit(solution)/shard_map/ppermute | solution.py:32
  7.7 0.0 copy-start
  7.7 0.7 %copy-done = s32[8]{0:T(128)S(1)} copy-done((s32[8]{0:T(128)S(1)}, s32[8]{0:T(128)}, u32[]{:S(2)}) %copy-start) | copy-done | bytes 56
  8.3 0.7 %shard_map.46.refs_5_.bands_ref = bf16[256,1024]{1,0:T(8,128)(2,1)S(1)} custom-call(s32[8]{0:T(128)S(1)} %copy-done), custom_call_target="tpu_custom_call" | custom-call | bytes 1048576 | tf_op jit(solution)/shard_map/pallas_call | solution.py:246
  9.1 0.2 shard_map.48.refs_4_.table_ref
  9.2 0.0 collective-permute-done.2.refs_3_
  9.3 2.6 %collective-permute-done.1.refs_2_ = bf16[144,128]{1,0:T(8,128)(2,1)S(1)} collective-permute-done((bf16[144,128]{1,0:T(8,128)(2,1)S(1)}, bf16[144,128]{1,0:T(8,128)(2,1)S(1)}, u32[]{:S(2)}, u32[]{:S(2)}) %collective-permute-start.1) | collective-permute-done | bytes 36896 | tf_op jit(solution)/shard_map/ppermute | solution.py:32
  11.9 0.0 collective-permute-done.refs_1_
  11.9 0.1 shard_map.49.joined_ref
  12.0 1.6 %collective-permute-start.5 = (bf16[272,256]{1,0:T(8,128)(2,1)S(1)}, bf16[272,256]{1,0:T(8,128)(2,1)S(1)}, u32[]{:S(2)}, u32[]{:S(2)}) collective-permute-start(bf16[272,256]{1,0:T(8,128)(2,1)S(1)} %shard_map.49.joined_ref), channel_id=1, source_target_pairs={{0,2},{2,0},{4,6},{6,4},{8,10},{10,8},{12,14},{14,12},{16,18},{18,... | collective-permute-start | bytes 417800 | tf_op jit(solution)/shard_map/ppermute | solution.py:32
  13.6 1.5 %collective-permute-start.4 = (bf16[272,256]{1,0:T(8,128)(2,1)S(1)}, bf16[272,256]{1,0:T(8,128)(2,1)S(1)}, u32[]{:S(2)}, u32[]{:S(2)}) collective-permute-start(bf16[272,256]{1,0:T(8,128)(2,1)S(1)} %shard_map.49.joined_ref), channel_id=1, source_target_pairs={{0,4},{2,6},{4,0},{6,2},{8,12},{10,14},{12,8},{14,10},{16,20},{18,... | collective-permute-start | bytes 417800 | tf_op jit(solution)/shard_map/ppermute | solution.py:32
  15.1 0.5 %collective-permute-start.3 = (bf16[272,256]{1,0:T(8,128)(2,1)S(1)}, bf16[272,256]{1,0:T(8,128)(2,1)S(1)}, u32[]{:S(2)}, u32[]{:S(2)}) collective-permute-start(bf16[272,256]{1,0:T(8,128)(2,1)S(1)} %shard_map.49.joined_ref), channel_id=1, source_target_pairs={{0,6},{2,4},{4,2},{6,0},{8,14},{10,12},{12,10},{14,8},{16,22},{18,... | collective-permute-start | bytes 417800 | tf_op jit(solution)/shard_map/ppermute | solution.py:32
  15.6 2.1 %shard_map.50.refs_0_ = f32[368,128]{1,0:T(8,128)S(1)} custom-call(s32[1]{0:T(128)} %bitcast.me_ref, s32[1]{0:T(128)} %bitcast.1.tm_ref, bf16[272,256]{1,0:T(8,128)(2,1)S(1)} %shard_map.49.joined_ref, f32[1024,128]{1,0:T(8,128)S(1)} %shard_map.48.refs_4_.table_ref), custom_call_target="tpu_custom_call" | custom-call | flops 1849688064 | bytes 1048576 | tf_op jit(solution)/shard_map/pallas_call | solution.py:246
  17.7 0.8 %collective-permute-done.5.joined_ref = bf16[272,256]{1,0:T(8,128)(2,1)S(1)} collective-permute-done((bf16[272,256]{1,0:T(8,128)(2,1)S(1)}, bf16[272,256]{1,0:T(8,128)(2,1)S(1)}, u32[]{:S(2)}, u32[]{:S(2)}) %collective-permute-start.5) | collective-permute-done | bytes 139296 | tf_op jit(solution)/shard_map/ppermute | solution.py:32
  18.5 2.1 %shard_map.51.refs_0_ = f32[368,128]{1,0:T(8,128)S(1)} custom-call(s32[1]{0:T(128)} %bitcast.me_ref, s32[1]{0:T(128)} %bitcast.1.tm_ref, bf16[272,256]{1,0:T(8,128)(2,1)S(1)} %collective-permute-done.5.joined_ref, f32[1024,128]{1,0:T(8,128)S(1)} %shard_map.48.refs_4_.table_ref, f32[368,128]{1,0:T(8,128)S(1)} %shard_map.50.refs_0_), custom_call_target="tpu_custom_call" | custom-call | flops 1849688064 | bytes 1048576 | tf_op jit(solution)/shard_map/pallas_call | solution.py:246
  20.6 0.6 %collective-permute-done.4.joined_ref = bf16[272,256]{1,0:T(8,128)(2,1)S(1)} collective-permute-done((bf16[272,256]{1,0:T(8,128)(2,1)S(1)}, bf16[272,256]{1,0:T(8,128)(2,1)S(1)}, u32[]{:S(2)}, u32[]{:S(2)}) %collective-permute-start.4) | collective-permute-done | bytes 139296 | tf_op jit(solution)/shard_map/ppermute | solution.py:32
  21.2 2.1 %shard_map.52.refs_0_ = f32[368,128]{1,0:T(8,128)S(1)} custom-call(s32[1]{0:T(128)} %bitcast.me_ref, s32[1]{0:T(128)} %bitcast.1.tm_ref, bf16[272,256]{1,0:T(8,128)(2,1)S(1)} %collective-permute-done.4.joined_ref, f32[1024,128]{1,0:T(8,128)S(1)} %shard_map.48.refs_4_.table_ref, f32[368,128]{1,0:T(8,128)S(1)} %shard_map.51.refs_0_), custom_call_target="tpu_custom_call" | custom-call | flops 1849688064 | bytes 1048576 | tf_op jit(solution)/shard_map/pallas_call | solution.py:246
  23.3 0.0 collective-permute-done.3.joined_ref
  23.3 1.3 %collective-permute-start.6 = (f32[240,128]{1,0:T(8,128)S(1)}, f32[240,128]{1,0:T(8,128)S(1)}, u32[]{:S(2)}, u32[]{:S(2)}) collective-permute-start(f32[240,128]{1,0:T(8,128)S(1)} %get-tuple-element.12), channel_id=1, source_target_pairs={{1,0},{3,2},{5,4},{7,6},{9,8},{11,10},{13,12},{15,14},{17,16},{19,... | collective-permute-start | bytes 368648 | tf_op jit(solution)/shard_map/ppermute | solution.py:27
  24.6 2.1 %shard_map.54.sums_ref = f32[368,128]{1,0:T(8,128)S(1)} custom-call(s32[1]{0:T(128)} %bitcast.me_ref, s32[1]{0:T(128)} %bitcast.1.tm_ref, bf16[272,256]{1,0:T(8,128)(2,1)S(1)} %collective-permute-done.3.joined_ref, f32[1024,128]{1,0:T(8,128)S(1)} %shard_map.48.refs_4_.table_ref, f32[368,128]{1,0:T(8,128)S(1)} %get-tuple-element.11.refs_0_), custom_call_target="tpu_custom_call" | custom-call | flops 1849688064 | bytes 1048576 | tf_op jit(solution)/shard_map/pallas_call | solution.py:246
  26.7 0.0 collective-permute-done.6.later_ref
  26.7 1.8 %shard_map.55 = f32[128,8,256]{2,1,0:T(8,128)} custom-call(s32[8]{0:T(128)S(1)} %copy-done, bf16[256,1024]{1,0:T(8,128)(2,1)S(1)} %shard_map.46.refs_5_.bands_ref, f32[368,128]{1,0:T(8,128)S(1)} %shard_map.54.sums_ref, f32[240,128]{1,0:T(8,128)S(1)} %collective-permute-done.6.later_ref), custom_call_target="tpu_custom_call" | custom-call | bytes 1048576 | tf_op jit(solution)/shard_map/pallas_call | solution.py:246
  (1 shorter events, 0.0 us)
Async XLA Ops:
  1.9 7.3 %collective-permute-start.2 = (bf16[144,128]{1,0:T(8,128)(2,1)S(1)}, bf16[144,128]{1,0:T(8,128)(2,1)S(1)}, u32[]{:S(2)}, u32[]{:S(2)}) collective-permute-start(bf16[144,128]{1,0:T(8,128)(2,1)S(1)} %get-tuple-element.9.refs_0_), channel_id=1, source_target_pairs={{0,24},{2,26},{4,28},{6,30},{8,16},{10,18},{12,20},{14,22},{16,8},... | collective-permute-start | bytes 110600 | tf_op jit(solution)/shard_map/ppermute | solution.py:32
  7.0 4.9 %collective-permute-start.1 = (bf16[144,128]{1,0:T(8,128)(2,1)S(1)}, bf16[144,128]{1,0:T(8,128)(2,1)S(1)}, u32[]{:S(2)}, u32[]{:S(2)}) collective-permute-start(bf16[144,128]{1,0:T(8,128)(2,1)S(1)} %get-tuple-element.9.refs_0_), channel_id=1, source_target_pairs={{0,16},{2,18},{4,20},{6,22},{8,24},{10,26},{12,28},{14,30},{16,0},... | collective-permute-start | bytes 110600 | tf_op jit(solution)/shard_map/ppermute | solution.py:32
  7.1 4.9 %collective-permute-start = (bf16[144,128]{1,0:T(8,128)(2,1)S(1)}, bf16[144,128]{1,0:T(8,128)(2,1)S(1)}, u32[]{:S(2)}, u32[]{:S(2)}) collective-permute-start(bf16[144,128]{1,0:T(8,128)(2,1)S(1)} %get-tuple-element.9.refs_0_), channel_id=1, source_target_pairs={{0,8},{2,10},{4,12},{6,14},{8,0},{10,2},{12,4},{14,6},{16,24},{18,... | collective-permute-start | bytes 110600 | tf_op jit(solution)/shard_map/ppermute | solution.py:32
  7.7 0.7 %copy-start = (s32[8]{0:T(128)S(1)}, s32[8]{0:T(128)}, u32[]{:S(2)}) copy-start(s32[8]{0:T(128)} %widths_ref.3) | copy-start | bytes 100
  12.0 6.4 %collective-permute-start.5 = (bf16[272,256]{1,0:T(8,128)(2,1)S(1)}, bf16[272,256]{1,0:T(8,128)(2,1)S(1)}, u32[]{:S(2)}, u32[]{:S(2)}) collective-permute-start(bf16[272,256]{1,0:T(8,128)(2,1)S(1)} %shard_map.49.joined_ref), channel_id=1, source_target_pairs={{0,2},{2,0},{4,6},{6,4},{8,10},{10,8},{12,14},{14,12},{16,18},{18,... | collective-permute-start | bytes 417800 | tf_op jit(solution)/shard_map/ppermute | solution.py:32
  13.6 7.6 %collective-permute-start.4 = (bf16[272,256]{1,0:T(8,128)(2,1)S(1)}, bf16[272,256]{1,0:T(8,128)(2,1)S(1)}, u32[]{:S(2)}, u32[]{:S(2)}) collective-permute-start(bf16[272,256]{1,0:T(8,128)(2,1)S(1)} %shard_map.49.joined_ref), channel_id=1, source_target_pairs={{0,4},{2,6},{4,0},{6,2},{8,12},{10,14},{12,8},{14,10},{16,20},{18,... | collective-permute-start | bytes 417800 | tf_op jit(solution)/shard_map/ppermute | solution.py:32
  15.1 8.2 %collective-permute-start.3 = (bf16[272,256]{1,0:T(8,128)(2,1)S(1)}, bf16[272,256]{1,0:T(8,128)(2,1)S(1)}, u32[]{:S(2)}, u32[]{:S(2)}) collective-permute-start(bf16[272,256]{1,0:T(8,128)(2,1)S(1)} %shard_map.49.joined_ref), channel_id=1, source_target_pairs={{0,6},{2,4},{4,2},{6,0},{8,14},{10,12},{12,10},{14,8},{16,22},{18,... | collective-permute-start | bytes 417800 | tf_op jit(solution)/shard_map/ppermute | solution.py:32
  23.3 3.4 %collective-permute-start.6 = (f32[240,128]{1,0:T(8,128)S(1)}, f32[240,128]{1,0:T(8,128)S(1)}, u32[]{:S(2)}, u32[]{:S(2)}) collective-permute-start(f32[240,128]{1,0:T(8,128)S(1)} %get-tuple-element.12), channel_id=1, source_target_pairs={{1,0},{3,2},{5,4},{7,6},{9,8},{11,10},{13,12},{15,14},{17,16},{19,... | collective-permute-start | bytes 368648 | tf_op jit(solution)/shard_map/ppermute | solution.py:27

commit v15 on v14

--- a/solution.py
+++ b/solution.py
@@ -194,18 +194,20 @@
         ref[...] = sums_ref[pl.ds(0, ref.shape[0]), :]
 
 
-def bands_kernel(widths_ref, bands_ref):
+def bands_kernel(widths_ref, bands_ref, shares_ref):
     shape = (bands_ref.shape[0], LANES)
     lag = lax.broadcasted_iota(jnp.int32, shape, 0) - lax.broadcasted_iota(jnp.int32, shape, 1)
     for at in range(widths_ref.shape[0]):
         band = jnp.where((lag >= 0) & (lag < widths_ref[at]), 1.0, 0.0)
         bands_ref[:, pl.ds(at * LANES, LANES)] = band.astype(jnp.bfloat16)
-
-
-def boxcars_kernel(scale, widths_ref, bands_ref, sums_ref, later_ref, out_ref, values, mixed, sems):
+        width = jnp.full((1, LANES), widths_ref[at], jnp.int32).astype(jnp.float32)
+        shares_ref[pl.ds(at, 1), :] = 1.0 / jnp.sqrt(width)
+
+
+def boxcars_kernel(scale, shares_ref, bands_ref, sums_ref, later_ref, out_ref, values, mixed, sems):
     trials = sums_ref.shape[1]
     length = sums_ref.shape[0] - REACH
-    filters = widths_ref.shape[0]
+    filters = shares_ref.shape[0]
     whole = length - REACH
     total = jnp.concatenate(
         [
@@ -220,8 +222,7 @@
         values[:, pl.ds(first, LANES)] = tile.astype(jnp.bfloat16)
     parts, pieces = sems.shape
     share = trials // pieces
-    widths = [jnp.full((1, LANES), widths_ref[at], jnp.int32).astype(jnp.float32) for at in range(filters)]
-    shares = [1.0 / jnp.sqrt(width) for width in widths]
+    shares = [shares_ref[pl.ds(at, 1), :] for at in range(filters)]
     tiles = mixed.reshape(parts, trials, filters, LANES)
     copies = []
     for piece in range(pieces):
@@ -282,9 +283,12 @@
     line = [series] + [exchanged(series, "sub", flip * inner) for flip in range(1, outer)]
     nsub = outer * sub_dev
     table = call(offsets_kernel, jax.ShapeDtypeStruct((all_subs, padded), jnp.float32), [VMEM], (fetched,))
-    bands = call(
+    bands, shares = call(
         bands_kernel,
-        jax.ShapeDtypeStruct((LANES + WMAX, filters * LANES), jnp.bfloat16),
+        [
+            jax.ShapeDtypeStruct((LANES + WMAX, filters * LANES), jnp.bfloat16),
+            jax.ShapeDtypeStruct((filters, LANES), jnp.float32),
+        ],
         [SMEM],
         (widths,),
     )
@@ -324,8 +328,8 @@
     return call(
         functools.partial(boxcars_kernel, scale),
         jax.ShapeDtypeStruct((padded, filters, length), jnp.float32),
-        [SMEM, VMEM, VMEM, VMEM],
-        (widths, bands, sums, later),
+        [VMEM] * 4,
+        (shares, bands, sums, later),
         [
             pltpu.VMEM((padded, length + WMAX), jnp.bfloat16),
             pltpu.VMEM((parts, padded * filters, LANES), jnp.float32),

time: 28.7 us -> 28.2 us (0.983)
  Pallas kernels: 13.1 us -> 12.6 us
    pallas_call x10, Pallas kernels: 13.1 us -> 12.6 us  [call(): pl.pallas_call(kernel, out_shape=out_shape, in_specs=in_specs, scratch_sh...]
  transfers between devices with their start and end apart: 7 -> 7, of which waited for: 3 -> 3; matrix products, arithmetic and copies ran while one was open for 0% -> 0% of each run, Pallas kernels for 32% -> 33%
where the time goes in v15:
time: 28.2 us; the launch traced here: 28 us
  Pallas kernels  12.6 us (45%)
  starting transfers between devices  10.6 us (38%)
  waiting for transfers between devices  4.07 us (14%)
  local copies, waits for them, and re-layouts  0.65 us (2%)
    pallas_call x10, Pallas kernels, call(): pl.pallas_call(kernel, out_shape=out_shape, in_specs=in_specs, scratch_sh...  12.6 us
    ppermute x6, starting transfers between devices, exchanged(): lax.ppermute(value, axis, [(source, source ^ flip) for source in range(co...  9.31 us
    ppermute x6, waiting for transfers between devices, exchanged(): lax.ppermute(value, axis, [(source, source ^ flip) for source in range(co...  4.07 us
    ppermute x1, starting transfers between devices, passed_back(): lax.ppermute(value, axis, [(source, source - 1) for source in range(1, co...  1.29 us
    unnamed x2, local copies, waits for them, and re-layouts  0.65 us
  transfers between devices with their start and end apart: 7, of which 3 were waited for; matrix products, arithmetic and copies ran while one was open for 0% of the time, Pallas kernels for 33%

profile of v15, /device:TPU:0, one launch (start us, length us, event | category | flops | bytes accessed | tf_op | source)
XLA Modules:
  0.0 28.0 jit_solution(8654370210841598644)
XLA Ops:
  0.0 1.9 %shard_map.47 = (bf16[144,128]{1,0:T(8,128)(2,1)S(1)}, s32[128,1024]{1,0:T(8,128)S(1)}) custom-call(s32[1,1024]{1,0:T(1,128)} %bitcast.8, bf16[1024,256]{1,0:T(8,128)(2,1)} %bitcast.7, s32[128,1024]{1,0:T(8,128)} %offsets_ref.1), custom_call_target="tpu_custom_call" | custom-call | bytes 1048576 | tf_op jit(solution)/shard_map/pallas_call | solution.py:247
  1.9 5.1 %collective-permute-start.2 = (bf16[144,128]{1,0:T(8,128)(2,1)S(1)}, bf16[144,128]{1,0:T(8,128)(2,1)S(1)}, u32[]{:S(2)}, u32[]{:S(2)}) collective-permute-start(bf16[144,128]{1,0:T(8,128)(2,1)S(1)} %get-tuple-element.13.refs_0_), channel_id=1, source_target_pairs={{0,24},{2,26},{4,28},{6,30},{8,16},{10,18},{12,20},{14,22},{16,8},... | collective-permute-start | bytes 110600 | tf_op jit(solution)/shard_map/ppermute | solution.py:32
  7.0 0.0 collective-permute-start.1
  7.1 0.6 %collective-permute-start = (bf16[144,128]{1,0:T(8,128)(2,1)S(1)}, bf16[144,128]{1,0:T(8,128)(2,1)S(1)}, u32[]{:S(2)}, u32[]{:S(2)}) collective-permute-start(bf16[144,128]{1,0:T(8,128)(2,1)S(1)} %get-tuple-element.13.refs_0_), channel_id=1, source_target_pairs={{0,8},{2,10},{4,12},{6,14},{8,0},{10,2},{12,4},{14,6},{16,24},{18,... | collective-permute-start | bytes 110600 | tf_op jit(solution)/shard_map/ppermute | solution.py:32
  7.7 0.0 copy-start
  7.7 0.7 %copy-done = s32[8]{0:T(128)S(1)} copy-done((s32[8]{0:T(128)S(1)}, s32[8]{0:T(128)}, u32[]{:S(2)}) %copy-start) | copy-done | bytes 56
  8.3 0.7 %shard_map.46 = (bf16[256,1024]{1,0:T(8,128)(2,1)S(1)}, f32[8,128]{1,0:T(8,128)S(1)}) custom-call(s32[8]{0:T(128)S(1)} %copy-done), custom_call_target="tpu_custom_call" | custom-call | bytes 1048576 | tf_op jit(solution)/shard_map/pallas_call | solution.py:247
  9.1 0.2 shard_map.48.refs_4_.table_ref
  9.3 0.0 collective-permute-done.2.refs_3_
  9.3 2.6 %collective-permute-done.1.refs_2_ = bf16[144,128]{1,0:T(8,128)(2,1)S(1)} collective-permute-done((bf16[144,128]{1,0:T(8,128)(2,1)S(1)}, bf16[144,128]{1,0:T(8,128)(2,1)S(1)}, u32[]{:S(2)}, u32[]{:S(2)}) %collective-permute-start.1) | collective-permute-done | bytes 36896 | tf_op jit(solution)/shard_map/ppermute | solution.py:32
  11.9 0.0 collective-permute-done.refs_1_
  11.9 0.1 shard_map.49.joined_ref
  12.0 1.6 %collective-permute-start.5 = (bf16[272,256]{1,0:T(8,128)(2,1)S(1)}, bf16[272,256]{1,0:T(8,128)(2,1)S(1)}, u32[]{:S(2)}, u32[]{:S(2)}) collective-permute-start(bf16[272,256]{1,0:T(8,128)(2,1)S(1)} %shard_map.49.joined_ref), channel_id=1, source_target_pairs={{0,2},{2,0},{4,6},{6,4},{8,10},{10,8},{12,14},{14,12},{16,18},{18,... | collective-permute-start | bytes 417800 | tf_op jit(solution)/shard_map/ppermute | solution.py:32
  13.6 1.5 %collective-permute-start.4 = (bf16[272,256]{1,0:T(8,128)(2,1)S(1)}, bf16[272,256]{1,0:T(8,128)(2,1)S(1)}, u32[]{:S(2)}, u32[]{:S(2)}) collective-permute-start(bf16[272,256]{1,0:T(8,128)(2,1)S(1)} %shard_map.49.joined_ref), channel_id=1, source_target_pairs={{0,4},{2,6},{4,0},{6,2},{8,12},{10,14},{12,8},{14,10},{16,20},{18,... | collective-permute-start | bytes 417800 | tf_op jit(solution)/shard_map/ppermute | solution.py:32
  15.1 0.5 %collective-permute-start.3 = (bf16[272,256]{1,0:T(8,128)(2,1)S(1)}, bf16[272,256]{1,0:T(8,128)(2,1)S(1)}, u32[]{:S(2)}, u32[]{:S(2)}) collective-permute-start(bf16[272,256]{1,0:T(8,128)(2,1)S(1)} %shard_map.49.joined_ref), channel_id=1, source_target_pairs={{0,6},{2,4},{4,2},{6,0},{8,14},{10,12},{12,10},{14,8},{16,22},{18,... | collective-permute-start | bytes 417800 | tf_op jit(solution)/shard_map/ppermute | solution.py:32
  15.6 2.1 %shard_map.50.refs_0_ = f32[368,128]{1,0:T(8,128)S(1)} custom-call(s32[1]{0:T(128)} %bitcast.me_ref, s32[1]{0:T(128)} %bitcast.1.tm_ref, bf16[272,256]{1,0:T(8,128)(2,1)S(1)} %shard_map.49.joined_ref, f32[1024,128]{1,0:T(8,128)S(1)} %shard_map.48.refs_4_.table_ref), custom_call_target="tpu_custom_call" | custom-call | flops 1849688064 | bytes 1048576 | tf_op jit(solution)/shard_map/pallas_call | solution.py:247
  17.7 0.8 %collective-permute-done.5.joined_ref = bf16[272,256]{1,0:T(8,128)(2,1)S(1)} collective-permute-done((bf16[272,256]{1,0:T(8,128)(2,1)S(1)}, bf16[272,256]{1,0:T(8,128)(2,1)S(1)}, u32[]{:S(2)}, u32[]{:S(2)}) %collective-permute-start.5) | collective-permute-done | bytes 139296 | tf_op jit(solution)/shard_map/ppermute | solution.py:32
  18.5 2.1 %shard_map.51.refs_0_ = f32[368,128]{1,0:T(8,128)S(1)} custom-call(s32[1]{0:T(128)} %bitcast.me_ref, s32[1]{0:T(128)} %bitcast.1.tm_ref, bf16[272,256]{1,0:T(8,128)(2,1)S(1)} %collective-permute-done.5.joined_ref, f32[1024,128]{1,0:T(8,128)S(1)} %shard_map.48.refs_4_.table_ref, f32[368,128]{1,0:T(8,128)S(1)} %shard_map.50.refs_0_), custom_call_target="tpu_custom_call" | custom-call | flops 1849688064 | bytes 1048576 | tf_op jit(solution)/shard_map/pallas_call | solution.py:247
  20.6 0.6 %collective-permute-done.4.joined_ref = bf16[272,256]{1,0:T(8,128)(2,1)S(1)} collective-permute-done((bf16[272,256]{1,0:T(8,128)(2,1)S(1)}, bf16[272,256]{1,0:T(8,128)(2,1)S(1)}, u32[]{:S(2)}, u32[]{:S(2)}) %collective-permute-start.4) | collective-permute-done | bytes 139296 | tf_op jit(solution)/shard_map/ppermute | solution.py:32
  21.2 2.1 %shard_map.52.refs_0_ = f32[368,128]{1,0:T(8,128)S(1)} custom-call(s32[1]{0:T(128)} %bitcast.me_ref, s32[1]{0:T(128)} %bitcast.1.tm_ref, bf16[272,256]{1,0:T(8,128)(2,1)S(1)} %collective-permute-done.4.joined_ref, f32[1024,128]{1,0:T(8,128)S(1)} %shard_map.48.refs_4_.table_ref, f32[368,128]{1,0:T(8,128)S(1)} %shard_map.51.refs_0_), custom_call_target="tpu_custom_call" | custom-call | flops 1849688064 | bytes 1048576 | tf_op jit(solution)/shard_map/pallas_call | solution.py:247
  23.3 0.0 collective-permute-done.3.joined_ref
  23.3 1.3 %collective-permute-start.6 = (f32[240,128]{1,0:T(8,128)S(1)}, f32[240,128]{1,0:T(8,128)S(1)}, u32[]{:S(2)}, u32[]{:S(2)}) collective-permute-start(f32[240,128]{1,0:T(8,128)S(1)} %get-tuple-element.16), channel_id=1, source_target_pairs={{1,0},{3,2},{5,4},{7,6},{9,8},{11,10},{13,12},{15,14},{17,16},{19,... | collective-permute-start | bytes 368648 | tf_op jit(solution)/shard_map/ppermute | solution.py:27
  24.6 2.1 %shard_map.54.sums_ref = f32[368,128]{1,0:T(8,128)S(1)} custom-call(s32[1]{0:T(128)} %bitcast.me_ref, s32[1]{0:T(128)} %bitcast.1.tm_ref, bf16[272,256]{1,0:T(8,128)(2,1)S(1)} %collective-permute-done.3.joined_ref, f32[1024,128]{1,0:T(8,128)S(1)} %shard_map.48.refs_4_.table_ref, f32[368,128]{1,0:T(8,128)S(1)} %get-tuple-element.15.refs_0_), custom_call_target="tpu_custom_call" | custom-call | flops 1849688064 | bytes 1048576 | tf_op jit(solution)/shard_map/pallas_call | solution.py:247
  26.7 0.0 collective-permute-done.6.later_ref
  26.8 1.3 %shard_map.55 = f32[128,8,256]{2,1,0:T(8,128)} custom-call(f32[8,128]{1,0:T(8,128)S(1)} %get-tuple-element.11.shares_ref, bf16[256,1024]{1,0:T(8,128)(2,1)S(1)} %get-tuple-element.12.refs_5_.bands_ref, f32[368,128]{1,0:T(8,128)S(1)} %shard_map.54.sums_ref, f32[240,128]{1,0:T(8,128)S(1)} %collective-permute-done.6.later_ref), custom_call_target="tpu_custom_call" | custom-call | bytes 1048576 | tf_op jit(solution)/shard_map/pallas_call | solution.py:247
  (1 shorter events, 0.0 us)
Async XLA Ops:
  1.9 7.3 %collective-permute-start.2 = (bf16[144,128]{1,0:T(8,128)(2,1)S(1)}, bf16[144,128]{1,0:T(8,128)(2,1)S(1)}, u32[]{:S(2)}, u32[]{:S(2)}) collective-permute-start(bf16[144,128]{1,0:T(8,128)(2,1)S(1)} %get-tuple-element.13.refs_0_), channel_id=1, source_target_pairs={{0,24},{2,26},{4,28},{6,30},{8,16},{10,18},{12,20},{14,22},{16,8},... | collective-permute-start | bytes 110600 | tf_op jit(solution)/shard_map/ppermute | solution.py:32
  7.0 4.9 %collective-permute-start.1 = (bf16[144,128]{1,0:T(8,128)(2,1)S(1)}, bf16[144,128]{1,0:T(8,128)(2,1)S(1)}, u32[]{:S(2)}, u32[]{:S(2)}) collective-permute-start(bf16[144,128]{1,0:T(8,128)(2,1)S(1)} %get-tuple-element.13.refs_0_), channel_id=1, source_target_pairs={{0,16},{2,18},{4,20},{6,22},{8,24},{10,26},{12,28},{14,30},{16,0},... | collective-permute-start | bytes 110600 | tf_op jit(solution)/shard_map/ppermute | solution.py:32
  7.1 4.9 %collective-permute-start = (bf16[144,128]{1,0:T(8,128)(2,1)S(1)}, bf16[144,128]{1,0:T(8,128)(2,1)S(1)}, u32[]{:S(2)}, u32[]{:S(2)}) collective-permute-start(bf16[144,128]{1,0:T(8,128)(2,1)S(1)} %get-tuple-element.13.refs_0_), channel_id=1, source_target_pairs={{0,8},{2,10},{4,12},{6,14},{8,0},{10,2},{12,4},{14,6},{16,24},{18,... | collective-permute-start | bytes 110600 | tf_op jit(solution)/shard_map/ppermute | solution.py:32
  7.7 0.7 %copy-start = (s32[8]{0:T(128)S(1)}, s32[8]{0:T(128)}, u32[]{:S(2)}) copy-start(s32[8]{0:T(128)} %widths_ref.1) | copy-start | bytes 100
  12.0 6.4 %collective-permute-start.5 = (bf16[272,256]{1,0:T(8,128)(2,1)S(1)}, bf16[272,256]{1,0:T(8,128)(2,1)S(1)}, u32[]{:S(2)}, u32[]{:S(2)}) collective-permute-start(bf16[272,256]{1,0:T(8,128)(2,1)S(1)} %shard_map.49.joined_ref), channel_id=1, source_target_pairs={{0,2},{2,0},{4,6},{6,4},{8,10},{10,8},{12,14},{14,12},{16,18},{18,... | collective-permute-start | bytes 417800 | tf_op jit(solution)/shard_map/ppermute | solution.py:32
  13.6 7.6 %collective-permute-start.4 = (bf16[272,256]{1,0:T(8,128)(2,1)S(1)}, bf16[272,256]{1,0:T(8,128)(2,1)S(1)}, u32[]{:S(2)}, u32[]{:S(2)}) collective-permute-start(bf16[272,256]{1,0:T(8,128)(2,1)S(1)} %shard_map.49.joined_ref), channel_id=1, source_target_pairs={{0,4},{2,6},{4,0},{6,2},{8,12},{10,14},{12,8},{14,10},{16,20},{18,... | collective-permute-start | bytes 417800 | tf_op jit(solution)/shard_map/ppermute | solution.py:32
  15.1 8.2 %collective-permute-start.3 = (bf16[272,256]{1,0:T(8,128)(2,1)S(1)}, bf16[272,256]{1,0:T(8,128)(2,1)S(1)}, u32[]{:S(2)}, u32[]{:S(2)}) collective-permute-start(bf16[272,256]{1,0:T(8,128)(2,1)S(1)} %shard_map.49.joined_ref), channel_id=1, source_target_pairs={{0,6},{2,4},{4,2},{6,0},{8,14},{10,12},{12,10},{14,8},{16,22},{18,... | collective-permute-start | bytes 417800 | tf_op jit(solution)/shard_map/ppermute | solution.py:32
  23.3 3.4 %collective-permute-start.6 = (f32[240,128]{1,0:T(8,128)S(1)}, f32[240,128]{1,0:T(8,128)S(1)}, u32[]{:S(2)}, u32[]{:S(2)}) collective-permute-start(f32[240,128]{1,0:T(8,128)S(1)} %get-tuple-element.16), channel_id=1, source_target_pairs={{1,0},{3,2},{5,4},{7,6},{9,8},{11,10},{13,12},{15,14},{17,16},{19,... | collective-permute-start | bytes 368648 | tf_op jit(solution)/shard_map/ppermute | solution.py:27

commit v16 on v15

--- a/solution.py
+++ b/solution.py
@@ -14,7 +14,7 @@
 LANES = 128
 STEP = 16
 GROUPS = OMAX // STEP
-TOGETHER = 1
+TOGETHER = 2
 REACH = OMAX + DCH
 VMEM = pl.BlockSpec(memory_space=pltpu.VMEM)
 SMEM = pl.BlockSpec(memory_space=pltpu.SMEM)
@@ -136,9 +136,8 @@
 
 def sums_kernel(given, here, outer, inner, flip, me_ref, tm_ref, joined_ref, table_ref, *refs):
     pairs = GROUPS // 2
-    before_ref, sums_ref, *early_ref = refs[: -3 - pairs] if given else (None, *refs[: -3 - pairs])
-    moving, shifted, table = refs[-3 - pairs : -pairs]
-    totals = refs[-pairs:]
+    before_ref, sums_ref, *early_ref = refs[:-3] if given else (None, *refs[:-3])
+    moving, shifted, table = refs[-3:]
     if before_ref is None:
         sums_ref[...] = jnp.zeros_like(sums_ref)
     else:
@@ -179,12 +178,7 @@
                     jnp.concatenate([tile(lag, pair) for lag in lags], axis=0),
                     preferred_element_type=jnp.float32,
                 )
-                if first:
-                    totals[pair][...] += both
-                else:
-                    totals[pair][...] = both
-        for pair in range(pairs):
-            add_pair(sums_ref, pair, totals[pair][...])
+                add_pair(sums_ref, pair, both)
 
     if here is None:
         add_block()
@@ -303,7 +297,6 @@
         pltpu.VMEM((span + 2 * STEP, nsub), jnp.float32),
         pltpu.VMEM((span + STEP, (STEP + 1) * nsub), jnp.bfloat16),
         pltpu.VMEM((nsub, padded), jnp.float32),
-        *[pltpu.VMEM((span + STEP, 2 * padded), jnp.float32)] * (GROUPS // 2),
     ]
     flops = 2 * (span + STEP) * nsub * padded * (OMAX + 2)
     sums_shape = jax.ShapeDtypeStruct((length + REACH, padded), jnp.float32)

time: 28.2 us -> 28.6 us (1.014)
  Pallas kernels: 12.6 us -> 13 us
    pallas_call x10, Pallas kernels: 12.6 us -> 13 us  [call(): pl.pallas_call(kernel, out_shape=out_shape, in_specs=in_specs, scratch_sh...]
  transfers between devices with their start and end apart: 7 -> 7, of which waited for: 3 -> 3; matrix products, arithmetic and copies ran while one was open for 0% -> 0% of each run, Pallas kernels for 33% -> 34%
where the time goes in v16:
time: 28.6 us; the launch traced here: 28.5 us
  Pallas kernels  13 us (45%)
  starting transfers between devices  10.6 us (37%)
  waiting for transfers between devices  3.97 us (14%)
  local copies, waits for them, and re-layouts  0.65 us (2%)
    pallas_call x10, Pallas kernels, call(): pl.pallas_call(kernel, out_shape=out_shape, in_specs=in_specs, scratch_sh...  13 us
    ppermute x6, starting transfers between devices, exchanged(): lax.ppermute(value, axis, [(source, source ^ flip) for source in range(co...  9.31 us
    ppermute x6, waiting for transfers between devices, exchanged(): lax.ppermute(value, axis, [(source, source ^ flip) for source in range(co...  3.97 us
    ppermute x1, starting transfers between devices, passed_back(): lax.ppermute(value, axis, [(source, source - 1) for source in range(1, co...  1.29 us
    unnamed x2, local copies, waits for them, and re-layouts  0.65 us
  transfers between devices with their start and end apart: 7, of which 3 were waited for; matrix products, arithmetic and copies ran while one was open for 0% of the time, Pallas kernels for 34%

profile of v16, /device:TPU:0, one launch (start us, length us, event | category | flops | bytes accessed | tf_op | source)
XLA Modules:
  0.0 28.5 jit_solution(1396899618184278481)
XLA Ops:
  0.0 1.9 %shard_map.47 = (bf16[144,128]{1,0:T(8,128)(2,1)S(1)}, s32[128,1024]{1,0:T(8,128)S(1)}) custom-call(s32[1,1024]{1,0:T(1,128)} %bitcast.8, bf16[1024,256]{1,0:T(8,128)(2,1)} %bitcast.7, s32[128,1024]{1,0:T(8,128)} %offsets_ref.1), custom_call_target="tpu_custom_call" | custom-call | bytes 1048576 | tf_op jit(solution)/shard_map/pallas_call | solution.py:241
  1.9 5.1 %collective-permute-start.2 = (bf16[144,128]{1,0:T(8,128)(2,1)S(1)}, bf16[144,128]{1,0:T(8,128)(2,1)S(1)}, u32[]{:S(2)}, u32[]{:S(2)}) collective-permute-start(bf16[144,128]{1,0:T(8,128)(2,1)S(1)} %get-tuple-element.13.refs_0_), channel_id=1, source_target_pairs={{0,24},{2,26},{4,28},{6,30},{8,16},{10,18},{12,20},{14,22},{16,8},... | collective-permute-start | bytes 110600 | tf_op jit(solution)/shard_map/ppermute | solution.py:32
  7.1 0.0 collective-permute-start.1
  7.1 0.6 %collective-permute-start = (bf16[144,128]{1,0:T(8,128)(2,1)S(1)}, bf16[144,128]{1,0:T(8,128)(2,1)S(1)}, u32[]{:S(2)}, u32[]{:S(2)}) collective-permute-start(bf16[144,128]{1,0:T(8,128)(2,1)S(1)} %get-tuple-element.13.refs_0_), channel_id=1, source_target_pairs={{0,8},{2,10},{4,12},{6,14},{8,0},{10,2},{12,4},{14,6},{16,24},{18,... | collective-permute-start | bytes 110600 | tf_op jit(solution)/shard_map/ppermute | solution.py:32
  7.7 0.0 copy-start
  7.7 0.7 %copy-done = s32[8]{0:T(128)S(1)} copy-done((s32[8]{0:T(128)S(1)}, s32[8]{0:T(128)}, u32[]{:S(2)}) %copy-start) | copy-done | bytes 56
  8.4 0.7 %shard_map.46 = (bf16[256,1024]{1,0:T(8,128)(2,1)S(1)}, f32[8,128]{1,0:T(8,128)S(1)}) custom-call(s32[8]{0:T(128)S(1)} %copy-done), custom_call_target="tpu_custom_call" | custom-call | bytes 1048576 | tf_op jit(solution)/shard_map/pallas_call | solution.py:241
  9.1 0.2 shard_map.48.refs_4_.table_ref
  9.3 0.0 collective-permute-done.2.refs_3_
  9.3 2.6 %collective-permute-done.1.refs_2_ = bf16[144,128]{1,0:T(8,128)(2,1)S(1)} collective-permute-done((bf16[144,128]{1,0:T(8,128)(2,1)S(1)}, bf16[144,128]{1,0:T(8,128)(2,1)S(1)}, u32[]{:S(2)}, u32[]{:S(2)}) %collective-permute-start.1) | collective-permute-done | bytes 36896 | tf_op jit(solution)/shard_map/ppermute | solution.py:32
  11.9 0.0 collective-permute-done.refs_1_
  11.9 0.1 shard_map.49.joined_ref
  12.0 1.6 %collective-permute-start.5 = (bf16[272,256]{1,0:T(8,128)(2,1)S(1)}, bf16[272,256]{1,0:T(8,128)(2,1)S(1)}, u32[]{:S(2)}, u32[]{:S(2)}) collective-permute-start(bf16[272,256]{1,0:T(8,128)(2,1)S(1)} %shard_map.49.joined_ref), channel_id=1, source_target_pairs={{0,2},{2,0},{4,6},{6,4},{8,10},{10,8},{12,14},{14,12},{16,18},{18,... | collective-permute-start | bytes 417800 | tf_op jit(solution)/shard_map/ppermute | solution.py:32
  13.6 1.5 %collective-permute-start.4 = (bf16[272,256]{1,0:T(8,128)(2,1)S(1)}, bf16[272,256]{1,0:T(8,128)(2,1)S(1)}, u32[]{:S(2)}, u32[]{:S(2)}) collective-permute-start(bf16[272,256]{1,0:T(8,128)(2,1)S(1)} %shard_map.49.joined_ref), channel_id=1, source_target_pairs={{0,4},{2,6},{4,0},{6,2},{8,12},{10,14},{12,8},{14,10},{16,20},{18,... | collective-permute-start | bytes 417800 | tf_op jit(solution)/shard_map/ppermute | solution.py:32
  15.1 0.5 %collective-permute-start.3 = (bf16[272,256]{1,0:T(8,128)(2,1)S(1)}, bf16[272,256]{1,0:T(8,128)(2,1)S(1)}, u32[]{:S(2)}, u32[]{:S(2)}) collective-permute-start(bf16[272,256]{1,0:T(8,128)(2,1)S(1)} %shard_map.49.joined_ref), channel_id=1, source_target_pairs={{0,6},{2,4},{4,2},{6,0},{8,14},{10,12},{12,10},{14,8},{16,22},{18,... | collective-permute-start | bytes 417800 | tf_op jit(solution)/shard_map/ppermute | solution.py:32
  15.6 2.1 %shard_map.50.refs_0_ = f32[368,128]{1,0:T(8,128)S(1)} custom-call(s32[1]{0:T(128)} %bitcast.me_ref, s32[1]{0:T(128)} %bitcast.1.tm_ref, bf16[272,256]{1,0:T(8,128)(2,1)S(1)} %shard_map.49.joined_ref, f32[1024,128]{1,0:T(8,128)S(1)} %shard_map.48.refs_4_.table_ref), custom_call_target="tpu_custom_call" | custom-call | flops 1849688064 | bytes 1048576 | tf_op jit(solution)/shard_map/pallas_call | solution.py:241
  17.7 0.7 %collective-permute-done.5.joined_ref = bf16[272,256]{1,0:T(8,128)(2,1)S(1)} collective-permute-done((bf16[272,256]{1,0:T(8,128)(2,1)S(1)}, bf16[272,256]{1,0:T(8,128)(2,1)S(1)}, u32[]{:S(2)}, u32[]{:S(2)}) %collective-permute-start.5) | collective-permute-done | bytes 139296 | tf_op jit(solution)/shard_map/ppermute | solution.py:32
  18.5 2.1 %shard_map.51.refs_0_ = f32[368,128]{1,0:T(8,128)S(1)} custom-call(s32[1]{0:T(128)} %bitcast.me_ref, s32[1]{0:T(128)} %bitcast.1.tm_ref, bf16[272,256]{1,0:T(8,128)(2,1)S(1)} %collective-permute-done.5.joined_ref, f32[1024,128]{1,0:T(8,128)S(1)} %shard_map.48.refs_4_.table_ref, f32[368,128]{1,0:T(8,128)S(1)} %shard_map.50.refs_0_), custom_call_target="tpu_custom_call" | custom-call | flops 1849688064 | bytes 1048576 | tf_op jit(solution)/shard_map/pallas_call | solution.py:241
  20.6 0.6 %collective-permute-done.4.joined_ref = bf16[272,256]{1,0:T(8,128)(2,1)S(1)} collective-permute-done((bf16[272,256]{1,0:T(8,128)(2,1)S(1)}, bf16[272,256]{1,0:T(8,128)(2,1)S(1)}, u32[]{:S(2)}, u32[]{:S(2)}) %collective-permute-start.4) | collective-permute-done | bytes 139296 | tf_op jit(solution)/shard_map/ppermute | solution.py:32
  21.2 2.1 %shard_map.52.refs_0_ = f32[368,128]{1,0:T(8,128)S(1)} custom-call(s32[1]{0:T(128)} %bitcast.me_ref, s32[1]{0:T(128)} %bitcast.1.tm_ref, bf16[272,256]{1,0:T(8,128)(2,1)S(1)} %collective-permute-done.4.joined_ref, f32[1024,128]{1,0:T(8,128)S(1)} %shard_map.48.refs_4_.table_ref, f32[368,128]{1,0:T(8,128)S(1)} %shard_map.51.refs_0_), custom_call_target="tpu_custom_call" | custom-call | flops 1849688064 | bytes 1048576 | tf_op jit(solution)/shard_map/pallas_call | solution.py:241
  23.3 0.0 collective-permute-done.3.joined_ref
  23.4 1.3 %collective-permute-start.6 = (f32[240,128]{1,0:T(8,128)S(1)}, f32[240,128]{1,0:T(8,128)S(1)}, u32[]{:S(2)}, u32[]{:S(2)}) collective-permute-start(f32[240,128]{1,0:T(8,128)S(1)} %get-tuple-element.16), channel_id=1, source_target_pairs={{1,0},{3,2},{5,4},{7,6},{9,8},{11,10},{13,12},{15,14},{17,16},{19,... | collective-permute-start | bytes 368648 | tf_op jit(solution)/shard_map/ppermute | solution.py:27
  24.7 2.3 %shard_map.54.sums_ref = f32[368,128]{1,0:T(8,128)S(1)} custom-call(s32[1]{0:T(128)} %bitcast.me_ref, s32[1]{0:T(128)} %bitcast.1.tm_ref, bf16[272,256]{1,0:T(8,128)(2,1)S(1)} %collective-permute-done.3.joined_ref, f32[1024,128]{1,0:T(8,128)S(1)} %shard_map.48.refs_4_.table_ref, f32[368,128]{1,0:T(8,128)S(1)} %get-tuple-element.15.refs_0_), custom_call_target="tpu_custom_call" | custom-call | flops 1849688064 | bytes 1048576 | tf_op jit(solution)/shard_map/pallas_call | solution.py:241
  27.0 0.0 collective-permute-done.6.later_ref
  27.0 1.3 %shard_map.55 = f32[128,8,256]{2,1,0:T(8,128)} custom-call(f32[8,128]{1,0:T(8,128)S(1)} %get-tuple-element.11.shares_ref, bf16[256,1024]{1,0:T(8,128)(2,1)S(1)} %get-tuple-element.12.refs_5_.bands_ref, f32[368,128]{1,0:T(8,128)S(1)} %shard_map.54.sums_ref, f32[240,128]{1,0:T(8,128)S(1)} %collective-permute-done.6.later_ref), custom_call_target="tpu_custom_call" | custom-call | bytes 1048576 | tf_op jit(solution)/shard_map/pallas_call | solution.py:241
  (1 shorter events, 0.0 us)
Async XLA Ops:
  1.9 7.3 %collective-permute-start.2 = (bf16[144,128]{1,0:T(8,128)(2,1)S(1)}, bf16[144,128]{1,0:T(8,128)(2,1)S(1)}, u32[]{:S(2)}, u32[]{:S(2)}) collective-permute-start(bf16[144,128]{1,0:T(8,128)(2,1)S(1)} %get-tuple-element.13.refs_0_), channel_id=1, source_target_pairs={{0,24},{2,26},{4,28},{6,30},{8,16},{10,18},{12,20},{14,22},{16,8},... | collective-permute-start | bytes 110600 | tf_op jit(solution)/shard_map/ppermute | solution.py:32
  7.1 4.9 %collective-permute-start.1 = (bf16[144,128]{1,0:T(8,128)(2,1)S(1)}, bf16[144,128]{1,0:T(8,128)(2,1)S(1)}, u32[]{:S(2)}, u32[]{:S(2)}) collective-permute-start(bf16[144,128]{1,0:T(8,128)(2,1)S(1)} %get-tuple-element.13.refs_0_), channel_id=1, source_target_pairs={{0,16},{2,18},{4,20},{6,22},{8,24},{10,26},{12,28},{14,30},{16,0},... | collective-permute-start | bytes 110600 | tf_op jit(solution)/shard_map/ppermute | solution.py:32
  7.1 4.9 %collective-permute-start = (bf16[144,128]{1,0:T(8,128)(2,1)S(1)}, bf16[144,128]{1,0:T(8,128)(2,1)S(1)}, u32[]{:S(2)}, u32[]{:S(2)}) collective-permute-start(bf16[144,128]{1,0:T(8,128)(2,1)S(1)} %get-tuple-element.13.refs_0_), channel_id=1, source_target_pairs={{0,8},{2,10},{4,12},{6,14},{8,0},{10,2},{12,4},{14,6},{16,24},{18,... | collective-permute-start | bytes 110600 | tf_op jit(solution)/shard_map/ppermute | solution.py:32
  7.7 0.7 %copy-start = (s32[8]{0:T(128)S(1)}, s32[8]{0:T(128)}, u32[]{:S(2)}) copy-start(s32[8]{0:T(128)} %widths_ref.1) | copy-start | bytes 100
  12.0 6.4 %collective-permute-start.5 = (bf16[272,256]{1,0:T(8,128)(2,1)S(1)}, bf16[272,256]{1,0:T(8,128)(2,1)S(1)}, u32[]{:S(2)}, u32[]{:S(2)}) collective-permute-start(bf16[272,256]{1,0:T(8,128)(2,1)S(1)} %shard_map.49.joined_ref), channel_id=1, source_target_pairs={{0,2},{2,0},{4,6},{6,4},{8,10},{10,8},{12,14},{14,12},{16,18},{18,... | collective-permute-start | bytes 417800 | tf_op jit(solution)/shard_map/ppermute | solution.py:32
  13.6 7.6 %collective-permute-start.4 = (bf16[272,256]{1,0:T(8,128)(2,1)S(1)}, bf16[272,256]{1,0:T(8,128)(2,1)S(1)}, u32[]{:S(2)}, u32[]{:S(2)}) collective-permute-start(bf16[272,256]{1,0:T(8,128)(2,1)S(1)} %shard_map.49.joined_ref), channel_id=1, source_target_pairs={{0,4},{2,6},{4,0},{6,2},{8,12},{10,14},{12,8},{14,10},{16,20},{18,... | collective-permute-start | bytes 417800 | tf_op jit(solution)/shard_map/ppermute | solution.py:32
  15.1 8.2 %collective-permute-start.3 = (bf16[272,256]{1,0:T(8,128)(2,1)S(1)}, bf16[272,256]{1,0:T(8,128)(2,1)S(1)}, u32[]{:S(2)}, u32[]{:S(2)}) collective-permute-start(bf16[272,256]{1,0:T(8,128)(2,1)S(1)} %shard_map.49.joined_ref), channel_id=1, source_target_pairs={{0,6},{2,4},{4,2},{6,0},{8,14},{10,12},{12,10},{14,8},{16,22},{18,... | collective-permute-start | bytes 417800 | tf_op jit(solution)/shard_map/ppermute | solution.py:32
  23.4 3.6 %collective-permute-start.6 = (f32[240,128]{1,0:T(8,128)S(1)}, f32[240,128]{1,0:T(8,128)S(1)}, u32[]{:S(2)}, u32[]{:S(2)}) collective-permute-start(f32[240,128]{1,0:T(8,128)S(1)} %get-tuple-element.16), channel_id=1, source_target_pairs={{1,0},{3,2},{5,4},{7,6},{9,8},{11,10},{13,12},{15,14},{17,16},{19,... | collective-permute-start | bytes 368648 | tf_op jit(solution)/shard_map/ppermute | solution.py:27

commit v17 on v15

--- a/solution.py
+++ b/solution.py
@@ -33,7 +33,7 @@
 
 
 def series_kernel(
-    per_sub, packed, delays_ref, data_ref, offsets_ref, series_ref, fetched_ref, delays, held, delays_sem, sems
+    per_sub, packed, delays_ref, data_ref, series_ref, delays, held, delays_sem, sems
 ):
     chans, length = data_ref.shape
     block = min(chans, 256)
@@ -42,15 +42,11 @@
     first_copy = pltpu.make_async_copy(delays_ref, delays, delays_sem)
     first_copy.start()
     copies = []
-    steps = sems.shape[0] // 2
-    for source, target, base in ((data_ref, held, 0), (offsets_ref, fetched_ref, steps)):
-        share = source.shape[0] // steps
-        for at in range(steps):
-            here = pl.ds(at * share, share)
-            copies.append(
-                pltpu.make_async_copy(source.at[here, :], target.at[here, :], sems.at[base + at])
-            )
-            copies[-1].start()
+    share = chans // sems.shape[0]
+    for at in range(sems.shape[0]):
+        here = pl.ds(at * share, share)
+        copies.append(pltpu.make_async_copy(data_ref.at[here, :], held.at[here, :], sems.at[at]))
+        copies[-1].start()
     rows = lax.broadcasted_iota(jnp.int32, (DCH * subs, block), 0)
     owner = lax.broadcasted_iota(jnp.int32, (1, block), 1) // per_sub
     blank = jnp.zeros((subs, LANES), jnp.float32)
@@ -59,7 +55,7 @@
         jnp.where(rows == delays[:, at * block : (at + 1) * block] * subs + owner, 1.0, 0.0).astype(jnp.bfloat16)
         for at in range(chans // block)
     ]
-    for copy in copies[:steps]:
+    for copy in copies:
         copy.wait()
     parts = []
     for at, member in enumerate(members):
@@ -80,8 +76,6 @@
             series_ref[pl.ds(first, count), :] = tile[:count].astype(jnp.bfloat16)
     else:
         series_ref[...] = total.astype(jnp.bfloat16)
-    for copy in copies[steps:]:
-        copy.wait()
 
 
 def join_packed_kernel(outer, *refs):
@@ -115,12 +109,6 @@
                 axis=0,
             ).T
             joined_ref[pl.ds(first, count), pl.ds(at * LANES, LANES)] = tile[:count].astype(jnp.bfloat16)
-
-
-def offsets_kernel(offsets_ref, table_ref):
-    for at in range(offsets_ref.shape[1] // LANES):
-        here = pl.ds(at * LANES, LANES)
-        table_ref[here, :] = offsets_ref[:, here].astype(jnp.float32).T
 
 
 def slot_start(slot, flip, outer, inner, subs, me):
@@ -194,14 +182,28 @@
         ref[...] = sums_ref[pl.ds(0, ref.shape[0]), :]
 
 
-def bands_kernel(widths_ref, bands_ref, shares_ref):
+def tables_kernel(widths_ref, offsets_ref, bands_ref, shares_ref, table_ref, widths, offsets, widths_sem, sems):
+    first_copy = pltpu.make_async_copy(widths_ref, widths, widths_sem)
+    first_copy.start()
+    share = offsets_ref.shape[0] // sems.shape[0]
+    copies = []
+    for at in range(sems.shape[0]):
+        here = pl.ds(at * share, share)
+        copies.append(pltpu.make_async_copy(offsets_ref.at[here, :], offsets.at[here, :], sems.at[at]))
+        copies[-1].start()
     shape = (bands_ref.shape[0], LANES)
     lag = lax.broadcasted_iota(jnp.int32, shape, 0) - lax.broadcasted_iota(jnp.int32, shape, 1)
+    first_copy.wait()
     for at in range(widths_ref.shape[0]):
-        band = jnp.where((lag >= 0) & (lag < widths_ref[at]), 1.0, 0.0)
+        band = jnp.where((lag >= 0) & (lag < widths[at]), 1.0, 0.0)
         bands_ref[:, pl.ds(at * LANES, LANES)] = band.astype(jnp.bfloat16)
-        width = jnp.full((1, LANES), widths_ref[at], jnp.int32).astype(jnp.float32)
+        width = jnp.full((1, LANES), widths[at], jnp.int32).astype(jnp.float32)
         shares_ref[pl.ds(at, 1), :] = 1.0 / jnp.sqrt(width)
+    for copy in copies:
+        copy.wait()
+    for at in range(offsets.shape[1] // LANES):
+        here = pl.ds(at * LANES, LANES)
+        table_ref[here, :] = offsets[:, here].astype(jnp.float32).T
 
 
 def boxcars_kernel(scale, shares_ref, bands_ref, sums_ref, later_ref, out_ref, values, mixed, sems):
@@ -265,32 +267,35 @@
     packed = 2 * sub_dev == LANES
     series_shape = (-(-span // 32) * 16, LANES) if packed else (sub_dev, length + LANES)
     steps = 4
-    series, fetched = call(
+    series = call(
         functools.partial(series_kernel, per_sub, packed),
-        [
-            jax.ShapeDtypeStruct(series_shape, jnp.bfloat16),
-            jax.ShapeDtypeStruct((padded, all_subs), jnp.int32),
-        ],
-        [HBM, HBM, HBM],
-        tuple(pltpu.with_memory_space_constraint(x, pltpu.HBM) for x in (delays[None, :], own, offsets)),
+        jax.ShapeDtypeStruct(series_shape, jnp.bfloat16),
+        [HBM, HBM],
+        tuple(pltpu.with_memory_space_constraint(x, pltpu.HBM) for x in (delays[None, :], own)),
         [
             pltpu.VMEM((1, chans), jnp.int32),
             pltpu.VMEM((chans, length), jnp.bfloat16),
             pltpu.SemaphoreType.DMA,
-            pltpu.SemaphoreType.DMA((2 * steps,)),
+            pltpu.SemaphoreType.DMA((steps,)),
         ],
     )
     line = [series] + [exchanged(series, "sub", flip * inner) for flip in range(1, outer)]
     nsub = outer * sub_dev
-    table = call(offsets_kernel, jax.ShapeDtypeStruct((all_subs, padded), jnp.float32), [VMEM], (fetched,))
-    bands, shares = call(
-        bands_kernel,
+    bands, shares, table = call(
+        tables_kernel,
         [
             jax.ShapeDtypeStruct((LANES + WMAX, filters * LANES), jnp.bfloat16),
             jax.ShapeDtypeStruct((filters, LANES), jnp.float32),
-        ],
-        [SMEM],
-        (widths,),
+            jax.ShapeDtypeStruct((all_subs, padded), jnp.float32),
+        ],
+        [HBM, HBM],
+        tuple(pltpu.with_memory_space_constraint(x, pltpu.HBM) for x in (widths, offsets)),
+        [
+            pltpu.SMEM((filters,), jnp.int32),
+            pltpu.VMEM((padded, all_subs), jnp.int32),
+            pltpu.SemaphoreType.DMA,
+            pltpu.SemaphoreType.DMA((steps,)),
+        ],
     )
     joined = call(
         functools.partial(join_packed_kernel if packed else join_kernel, outer),

time: 28.2 us -> 28.1 us (level)
  local copies, waits for them, and re-layouts: 0.65 us -> 0 us
  Pallas kernels: 12.6 us -> 12.9 us
    unnamed x2 -> x0, local copies, waits for them, and re-layouts: 0.65 us -> none
    pallas_call x10 -> x9, Pallas kernels: 12.6 us -> 12.9 us  [call(): pl.pallas_call(kernel, out_shape=out_shape, in_specs=in_specs, scratch_sh...]
  transfers between devices with their start and end apart: 7 -> 7, of which waited for: 3 -> 3; matrix products, arithmetic and copies ran while one was open for 0% -> 0% of each run, Pallas kernels for 33% -> 35%
where the time goes in v17:
time: 28.1 us; the launch traced here: 27.9 us
  Pallas kernels  12.9 us (46%)
  starting transfers between devices  10.6 us (38%)
  waiting for transfers between devices  4.29 us (15%)
    pallas_call x9, Pallas kernels, call(): pl.pallas_call(kernel, out_shape=out_shape, in_specs=in_specs, scratch_sh...  12.9 us
    ppermute x6, starting transfers between devices, exchanged(): lax.ppermute(value, axis, [(source, source ^ flip) for source in range(co...  9.31 us
    ppermute x6, waiting for transfers between devices, exchanged(): lax.ppermute(value, axis, [(source, source ^ flip) for source in range(co...  4.29 us
    ppermute x1, starting transfers between devices, passed_back(): lax.ppermute(value, axis, [(source, source - 1) for source in range(1, co...  1.29 us
  transfers between devices with their start and end apart: 7, of which 3 were waited for; matrix products, arithmetic and copies ran while one was open for 0% of the time, Pallas kernels for 35%

profile of v17, /device:TPU:0, one launch (start us, length us, event | category | flops | bytes accessed | tf_op | source)
XLA Modules:
  0.0 27.9 jit_solution(8487259836182766823)
XLA Ops:
  0.0 1.8 %shard_map.47.refs_0_ = bf16[144,128]{1,0:T(8,128)(2,1)S(1)} custom-call(s32[1,1024]{1,0:T(1,128)} %bitcast.8, bf16[1024,256]{1,0:T(8,128)(2,1)} %bitcast.7), custom_call_target="tpu_custom_call" | custom-call | bytes 1048576 | tf_op jit(solution)/shard_map/pallas_call | solution.py:249
  1.8 5.1 %collective-permute-start.2 = (bf16[144,128]{1,0:T(8,128)(2,1)S(1)}, bf16[144,128]{1,0:T(8,128)(2,1)S(1)}, u32[]{:S(2)}, u32[]{:S(2)}) collective-permute-start(bf16[144,128]{1,0:T(8,128)(2,1)S(1)} %shard_map.47.refs_0_), channel_id=1, source_target_pairs={{0,24},{2,26},{4,28},{6,30},{8,16},{10,18},{12,20},{14,22},{16,8},... | collective-permute-start | bytes 110600 | tf_op jit(solution)/shard_map/ppermute | solution.py:32
  6.9 0.0 collective-permute-start.1
  6.9 0.6 %collective-permute-start = (bf16[144,128]{1,0:T(8,128)(2,1)S(1)}, bf16[144,128]{1,0:T(8,128)(2,1)S(1)}, u32[]{:S(2)}, u32[]{:S(2)}) collective-permute-start(bf16[144,128]{1,0:T(8,128)(2,1)S(1)} %shard_map.47.refs_0_), channel_id=1, source_target_pairs={{0,8},{2,10},{4,12},{6,14},{8,0},{10,2},{12,4},{14,6},{16,24},{18,... | collective-permute-start | bytes 110600 | tf_op jit(solution)/shard_map/ppermute | solution.py:32
  7.6 1.3 %shard_map.46 = (bf16[256,1024]{1,0:T(8,128)(2,1)S(1)}, f32[8,128]{1,0:T(8,128)S(1)}, f32[1024,128]{1,0:T(8,128)S(1)}) custom-call(s32[8]{0:T(128)} %widths_ref.1, s32[128,1024]{1,0:T(8,128)} %offsets_ref.1), custom_call_target="tpu_custom_call" | custom-call | bytes 1048576 | tf_op jit(solution)/shard_map/pallas_call | solution.py:249
  8.9 0.0 collective-permute-done.2.refs_3_
  8.9 2.9 %collective-permute-done.1.refs_2_ = bf16[144,128]{1,0:T(8,128)(2,1)S(1)} collective-permute-done((bf16[144,128]{1,0:T(8,128)(2,1)S(1)}, bf16[144,128]{1,0:T(8,128)(2,1)S(1)}, u32[]{:S(2)}, u32[]{:S(2)}) %collective-permute-start.1) | collective-permute-done | bytes 36896 | tf_op jit(solution)/shard_map/ppermute | solution.py:32
  11.8 0.0 collective-permute-done.refs_1_
  11.8 0.1 shard_map.48.joined_ref
  11.9 1.6 %collective-permute-start.5 = (bf16[272,256]{1,0:T(8,128)(2,1)S(1)}, bf16[272,256]{1,0:T(8,128)(2,1)S(1)}, u32[]{:S(2)}, u32[]{:S(2)}) collective-permute-start(bf16[272,256]{1,0:T(8,128)(2,1)S(1)} %shard_map.48.joined_ref), channel_id=1, source_target_pairs={{0,2},{2,0},{4,6},{6,4},{8,10},{10,8},{12,14},{14,12},{16,18},{18,... | collective-permute-start | bytes 417800 | tf_op jit(solution)/shard_map/ppermute | solution.py:32
  13.5 1.5 %collective-permute-start.4 = (bf16[272,256]{1,0:T(8,128)(2,1)S(1)}, bf16[272,256]{1,0:T(8,128)(2,1)S(1)}, u32[]{:S(2)}, u32[]{:S(2)}) collective-permute-start(bf16[272,256]{1,0:T(8,128)(2,1)S(1)} %shard_map.48.joined_ref), channel_id=1, source_target_pairs={{0,4},{2,6},{4,0},{6,2},{8,12},{10,14},{12,8},{14,10},{16,20},{18,... | collective-permute-start | bytes 417800 | tf_op jit(solution)/shard_map/ppermute | solution.py:32
  15.0 0.5 %collective-permute-start.3 = (bf16[272,256]{1,0:T(8,128)(2,1)S(1)}, bf16[272,256]{1,0:T(8,128)(2,1)S(1)}, u32[]{:S(2)}, u32[]{:S(2)}) collective-permute-start(bf16[272,256]{1,0:T(8,128)(2,1)S(1)} %shard_map.48.joined_ref), channel_id=1, source_target_pairs={{0,6},{2,4},{4,2},{6,0},{8,14},{10,12},{12,10},{14,8},{16,22},{18,... | collective-permute-start | bytes 417800 | tf_op jit(solution)/shard_map/ppermute | solution.py:32
  15.5 2.1 %shard_map.49.refs_0_ = f32[368,128]{1,0:T(8,128)S(1)} custom-call(s32[1]{0:T(128)} %bitcast.me_ref, s32[1]{0:T(128)} %bitcast.1.tm_ref, bf16[272,256]{1,0:T(8,128)(2,1)S(1)} %shard_map.48.joined_ref, f32[1024,128]{1,0:T(8,128)S(1)} %get-tuple-element.12.refs_4_.table_ref), custom_call_target="tpu_custom_call" | custom-call | flops 1849688064 | bytes 1048576 | tf_op jit(solution)/shard_map/pallas_call | solution.py:249
  17.5 0.8 %collective-permute-done.5.joined_ref = bf16[272,256]{1,0:T(8,128)(2,1)S(1)} collective-permute-done((bf16[272,256]{1,0:T(8,128)(2,1)S(1)}, bf16[272,256]{1,0:T(8,128)(2,1)S(1)}, u32[]{:S(2)}, u32[]{:S(2)}) %collective-permute-start.5) | collective-permute-done | bytes 139296 | tf_op jit(solution)/shard_map/ppermute | solution.py:32
  18.3 2.1 %shard_map.50.refs_0_ = f32[368,128]{1,0:T(8,128)S(1)} custom-call(s32[1]{0:T(128)} %bitcast.me_ref, s32[1]{0:T(128)} %bitcast.1.tm_ref, bf16[272,256]{1,0:T(8,128)(2,1)S(1)} %collective-permute-done.5.joined_ref, f32[1024,128]{1,0:T(8,128)S(1)} %get-tuple-element.12.refs_4_.table_ref, f32[368,128]{1,0:T(8,128)S(1)} %shard_map.49.refs_0_), custom_call_target="tpu_custom_call" | custom-call | flops 1849688064 | bytes 1048576 | tf_op jit(solution)/shard_map/pallas_call | solution.py:249
  20.4 0.6 %collective-permute-done.4.joined_ref = bf16[272,256]{1,0:T(8,128)(2,1)S(1)} collective-permute-done((bf16[272,256]{1,0:T(8,128)(2,1)S(1)}, bf16[272,256]{1,0:T(8,128)(2,1)S(1)}, u32[]{:S(2)}, u32[]{:S(2)}) %collective-permute-start.4) | collective-permute-done | bytes 139296 | tf_op jit(solution)/shard_map/ppermute | solution.py:32
  21.1 2.1 %shard_map.51.refs_0_ = f32[368,128]{1,0:T(8,128)S(1)} custom-call(s32[1]{0:T(128)} %bitcast.me_ref, s32[1]{0:T(128)} %bitcast.1.tm_ref, bf16[272,256]{1,0:T(8,128)(2,1)S(1)} %collective-permute-done.4.joined_ref, f32[1024,128]{1,0:T(8,128)S(1)} %get-tuple-element.12.refs_4_.table_ref, f32[368,128]{1,0:T(8,128)S(1)} %shard_map.50.refs_0_), custom_call_target="tpu_custom_call" | custom-call | flops 1849688064 | bytes 1048576 | tf_op jit(solution)/shard_map/pallas_call | solution.py:249
  23.2 0.0 collective-permute-done.3.joined_ref
  23.2 1.3 %collective-permute-start.6 = (f32[240,128]{1,0:T(8,128)S(1)}, f32[240,128]{1,0:T(8,128)S(1)}, u32[]{:S(2)}, u32[]{:S(2)}) collective-permute-start(f32[240,128]{1,0:T(8,128)S(1)} %get-tuple-element.14), channel_id=1, source_target_pairs={{1,0},{3,2},{5,4},{7,6},{9,8},{11,10},{13,12},{15,14},{17,16},{19,... | collective-permute-start | bytes 368648 | tf_op jit(solution)/shard_map/ppermute | solution.py:27
  24.5 2.1 %shard_map.53.sums_ref = f32[368,128]{1,0:T(8,128)S(1)} custom-call(s32[1]{0:T(128)} %bitcast.me_ref, s32[1]{0:T(128)} %bitcast.1.tm_ref, bf16[272,256]{1,0:T(8,128)(2,1)S(1)} %collective-permute-done.3.joined_ref, f32[1024,128]{1,0:T(8,128)S(1)} %get-tuple-element.12.refs_4_.table_ref, f32[368,128]{1,0:T(8,128)S(1)} %get-tuple-element.13.refs_0_), custom_call_target="tpu_custom_call" | custom-call | flops 1849688064 | bytes 1048576 | tf_op jit(solution)/shard_map/pallas_call | solution.py:249
  26.6 0.0 collective-permute-done.6.later_ref
  26.6 1.3 %shard_map.54 = f32[128,8,256]{2,1,0:T(8,128)} custom-call(f32[8,128]{1,0:T(8,128)S(1)} %get-tuple-element.10.shares_ref, bf16[256,1024]{1,0:T(8,128)(2,1)S(1)} %get-tuple-element.11.refs_5_.bands_ref, f32[368,128]{1,0:T(8,128)S(1)} %shard_map.53.sums_ref, f32[240,128]{1,0:T(8,128)S(1)} %collective-permute-done.6.later_ref), custom_call_target="tpu_custom_call" | custom-call | bytes 1048576 | tf_op jit(solution)/shard_map/pallas_call | solution.py:249
  (1 shorter events, 0.0 us)
Async XLA Ops:
  1.8 7.1 %collective-permute-start.2 = (bf16[144,128]{1,0:T(8,128)(2,1)S(1)}, bf16[144,128]{1,0:T(8,128)(2,1)S(1)}, u32[]{:S(2)}, u32[]{:S(2)}) collective-permute-start(bf16[144,128]{1,0:T(8,128)(2,1)S(1)} %shard_map.47.refs_0_), channel_id=1, source_target_pairs={{0,24},{2,26},{4,28},{6,30},{8,16},{10,18},{12,20},{14,22},{16,8},... | collective-permute-start | bytes 110600 | tf_op jit(solution)/shard_map/ppermute | solution.py:32
  6.9 4.9 %collective-permute-start.1 = (bf16[144,128]{1,0:T(8,128)(2,1)S(1)}, bf16[144,128]{1,0:T(8,128)(2,1)S(1)}, u32[]{:S(2)}, u32[]{:S(2)}) collective-permute-start(bf16[144,128]{1,0:T(8,128)(2,1)S(1)} %shard_map.47.refs_0_), channel_id=1, source_target_pairs={{0,16},{2,18},{4,20},{6,22},{8,24},{10,26},{12,28},{14,30},{16,0},... | collective-permute-start | bytes 110600 | tf_op jit(solution)/shard_map/ppermute | solution.py:32
  6.9 4.9 %collective-permute-start = (bf16[144,128]{1,0:T(8,128)(2,1)S(1)}, bf16[144,128]{1,0:T(8,128)(2,1)S(1)}, u32[]{:S(2)}, u32[]{:S(2)}) collective-permute-start(bf16[144,128]{1,0:T(8,128)(2,1)S(1)} %shard_map.47.refs_0_), channel_id=1, source_target_pairs={{0,8},{2,10},{4,12},{6,14},{8,0},{10,2},{12,4},{14,6},{16,24},{18,... | collective-permute-start | bytes 110600 | tf_op jit(solution)/shard_map/ppermute | solution.py:32
  11.9 6.4 %collective-permute-start.5 = (bf16[272,256]{1,0:T(8,128)(2,1)S(1)}, bf16[272,256]{1,0:T(8,128)(2,1)S(1)}, u32[]{:S(2)}, u32[]{:S(2)}) collective-permute-start(bf16[272,256]{1,0:T(8,128)(2,1)S(1)} %shard_map.48.joined_ref), channel_id=1, source_target_pairs={{0,2},{2,0},{4,6},{6,4},{8,10},{10,8},{12,14},{14,12},{16,18},{18,... | collective-permute-start | bytes 417800 | tf_op jit(solution)/shard_map/ppermute | solution.py:32
  13.5 7.6 %collective-permute-start.4 = (bf16[272,256]{1,0:T(8,128)(2,1)S(1)}, bf16[272,256]{1,0:T(8,128)(2,1)S(1)}, u32[]{:S(2)}, u32[]{:S(2)}) collective-permute-start(bf16[272,256]{1,0:T(8,128)(2,1)S(1)} %shard_map.48.joined_ref), channel_id=1, source_target_pairs={{0,4},{2,6},{4,0},{6,2},{8,12},{10,14},{12,8},{14,10},{16,20},{18,... | collective-permute-start | bytes 417800 | tf_op jit(solution)/shard_map/ppermute | solution.py:32
  15.0 8.2 %collective-permute-start.3 = (bf16[272,256]{1,0:T(8,128)(2,1)S(1)}, bf16[272,256]{1,0:T(8,128)(2,1)S(1)}, u32[]{:S(2)}, u32[]{:S(2)}) collective-permute-start(bf16[272,256]{1,0:T(8,128)(2,1)S(1)} %shard_map.48.joined_ref), channel_id=1, source_target_pairs={{0,6},{2,4},{4,2},{6,0},{8,14},{10,12},{12,10},{14,8},{16,22},{18,... | collective-permute-start | bytes 417800 | tf_op jit(solution)/shard_map/ppermute | solution.py:32
  23.2 3.4 %collective-permute-start.6 = (f32[240,128]{1,0:T(8,128)S(1)}, f32[240,128]{1,0:T(8,128)S(1)}, u32[]{:S(2)}, u32[]{:S(2)}) collective-permute-start(f32[240,128]{1,0:T(8,128)S(1)} %get-tuple-element.14), channel_id=1, source_target_pairs={{1,0},{3,2},{5,4},{7,6},{9,8},{11,10},{13,12},{15,14},{17,16},{19,... | collective-permute-start | bytes 368648 | tf_op jit(solution)/shard_map/ppermute | solution.py:27

commit v18 on v17

--- a/solution.py
+++ b/solution.py
@@ -266,7 +266,7 @@
     span = length + DCH
     packed = 2 * sub_dev == LANES
     series_shape = (-(-span // 32) * 16, LANES) if packed else (sub_dev, length + LANES)
-    steps = 4
+    steps = 8
     series = call(
         functools.partial(series_kernel, per_sub, packed),
         jax.ShapeDtypeStruct(series_shape, jnp.bfloat16),
@@ -329,7 +329,7 @@
         if rest:
             later = passed_back(rest[0], "tm")
     parts = length // LANES
-    pieces = 2
+    pieces = 4
     return call(
         functools.partial(boxcars_kernel, scale),
         jax.ShapeDtypeStruct((padded, filters, length), jnp.float32),

time: 28.1 us -> 28.2 us (level)
  no operation moved by 1% of the time
where the time goes in v18:
time: 28.2 us; the launch traced here: 28 us
  Pallas kernels  13 us (46%)
  starting transfers between devices  10.6 us (38%)
  waiting for transfers between devices  4.29 us (15%)
    pallas_call x9, Pallas kernels, call(): pl.pallas_call(kernel, out_shape=out_shape, in_specs=in_specs, scratch_sh...  13 us
    ppermute x6, starting transfers between devices, exchanged(): lax.ppermute(value, axis, [(source, source ^ flip) for source in range(co...  9.31 us
    ppermute x6, waiting for transfers between devices, exchanged(): lax.ppermute(value, axis, [(source, source ^ flip) for source in range(co...  4.29 us
    ppermute x1, starting transfers between devices, passed_back(): lax.ppermute(value, axis, [(source, source - 1) for source in range(1, co...  1.29 us
  transfers between devices with their start and end apart: 7, of which 3 were waited for; matrix products, arithmetic and copies ran while one was open for 0% of the time, Pallas kernels for 35%

profile of v18, /device:TPU:0, one launch (start us, length us, event | category | flops | bytes accessed | tf_op | source)
XLA Modules:
  0.0 28.0 jit_solution(7453483210748665983)
XLA Ops:
  0.0 1.8 %shard_map.47.refs_0_ = bf16[144,128]{1,0:T(8,128)(2,1)S(1)} custom-call(s32[1,1024]{1,0:T(1,128)} %bitcast.8, bf16[1024,256]{1,0:T(8,128)(2,1)} %bitcast.7), custom_call_target="tpu_custom_call" | custom-call | bytes 1048576 | tf_op jit(solution)/shard_map/pallas_call | solution.py:249
  1.8 5.1 %collective-permute-start.2 = (bf16[144,128]{1,0:T(8,128)(2,1)S(1)}, bf16[144,128]{1,0:T(8,128)(2,1)S(1)}, u32[]{:S(2)}, u32[]{:S(2)}) collective-permute-start(bf16[144,128]{1,0:T(8,128)(2,1)S(1)} %shard_map.47.refs_0_), channel_id=1, source_target_pairs={{0,24},{2,26},{4,28},{6,30},{8,16},{10,18},{12,20},{14,22},{16,8},... | collective-permute-start | bytes 110600 | tf_op jit(solution)/shard_map/ppermute | solution.py:32
  6.9 0.0 collective-permute-start.1
  6.9 0.6 %collective-permute-start = (bf16[144,128]{1,0:T(8,128)(2,1)S(1)}, bf16[144,128]{1,0:T(8,128)(2,1)S(1)}, u32[]{:S(2)}, u32[]{:S(2)}) collective-permute-start(bf16[144,128]{1,0:T(8,128)(2,1)S(1)} %shard_map.47.refs_0_), channel_id=1, source_target_pairs={{0,8},{2,10},{4,12},{6,14},{8,0},{10,2},{12,4},{14,6},{16,24},{18,... | collective-permute-start | bytes 110600 | tf_op jit(solution)/shard_map/ppermute | solution.py:32
  7.6 1.3 %shard_map.46 = (bf16[256,1024]{1,0:T(8,128)(2,1)S(1)}, f32[8,128]{1,0:T(8,128)S(1)}, f32[1024,128]{1,0:T(8,128)S(1)}) custom-call(s32[8]{0:T(128)} %widths_ref.1, s32[128,1024]{1,0:T(8,128)} %offsets_ref.1), custom_call_target="tpu_custom_call" | custom-call | bytes 1048576 | tf_op jit(solution)/shard_map/pallas_call | solution.py:249
  8.9 0.0 collective-permute-done.2.refs_3_
  8.9 2.9 %collective-permute-done.1.refs_2_ = bf16[144,128]{1,0:T(8,128)(2,1)S(1)} collective-permute-done((bf16[144,128]{1,0:T(8,128)(2,1)S(1)}, bf16[144,128]{1,0:T(8,128)(2,1)S(1)}, u32[]{:S(2)}, u32[]{:S(2)}) %collective-permute-start.1) | collective-permute-done | bytes 36896 | tf_op jit(solution)/shard_map/ppermute | solution.py:32
  11.8 0.0 collective-permute-done.refs_1_
  11.8 0.1 shard_map.48.joined_ref
  11.9 1.6 %collective-permute-start.5 = (bf16[272,256]{1,0:T(8,128)(2,1)S(1)}, bf16[272,256]{1,0:T(8,128)(2,1)S(1)}, u32[]{:S(2)}, u32[]{:S(2)}) collective-permute-start(bf16[272,256]{1,0:T(8,128)(2,1)S(1)} %shard_map.48.joined_ref), channel_id=1, source_target_pairs={{0,2},{2,0},{4,6},{6,4},{8,10},{10,8},{12,14},{14,12},{16,18},{18,... | collective-permute-start | bytes 417800 | tf_op jit(solution)/shard_map/ppermute | solution.py:32
  13.5 1.5 %collective-permute-start.4 = (bf16[272,256]{1,0:T(8,128)(2,1)S(1)}, bf16[272,256]{1,0:T(8,128)(2,1)S(1)}, u32[]{:S(2)}, u32[]{:S(2)}) collective-permute-start(bf16[272,256]{1,0:T(8,128)(2,1)S(1)} %shard_map.48.joined_ref), channel_id=1, source_target_pairs={{0,4},{2,6},{4,0},{6,2},{8,12},{10,14},{12,8},{14,10},{16,20},{18,... | collective-permute-start | bytes 417800 | tf_op jit(solution)/shard_map/ppermute | solution.py:32
  15.0 0.5 %collective-permute-start.3 = (bf16[272,256]{1,0:T(8,128)(2,1)S(1)}, bf16[272,256]{1,0:T(8,128)(2,1)S(1)}, u32[]{:S(2)}, u32[]{:S(2)}) collective-permute-start(bf16[272,256]{1,0:T(8,128)(2,1)S(1)} %shard_map.48.joined_ref), channel_id=1, source_target_pairs={{0,6},{2,4},{4,2},{6,0},{8,14},{10,12},{12,10},{14,8},{16,22},{18,... | collective-permute-start | bytes 417800 | tf_op jit(solution)/shard_map/ppermute | solution.py:32
  15.5 2.1 %shard_map.49.refs_0_ = f32[368,128]{1,0:T(8,128)S(1)} custom-call(s32[1]{0:T(128)} %bitcast.me_ref, s32[1]{0:T(128)} %bitcast.1.tm_ref, bf16[272,256]{1,0:T(8,128)(2,1)S(1)} %shard_map.48.joined_ref, f32[1024,128]{1,0:T(8,128)S(1)} %get-tuple-element.12.refs_4_.table_ref), custom_call_target="tpu_custom_call" | custom-call | flops 1849688064 | bytes 1048576 | tf_op jit(solution)/shard_map/pallas_call | solution.py:249
  17.5 0.8 %collective-permute-done.5.joined_ref = bf16[272,256]{1,0:T(8,128)(2,1)S(1)} collective-permute-done((bf16[272,256]{1,0:T(8,128)(2,1)S(1)}, bf16[272,256]{1,0:T(8,128)(2,1)S(1)}, u32[]{:S(2)}, u32[]{:S(2)}) %collective-permute-start.5) | collective-permute-done | bytes 139296 | tf_op jit(solution)/shard_map/ppermute | solution.py:32
  18.3 2.1 %shard_map.50.refs_0_ = f32[368,128]{1,0:T(8,128)S(1)} custom-call(s32[1]{0:T(128)} %bitcast.me_ref, s32[1]{0:T(128)} %bitcast.1.tm_ref, bf16[272,256]{1,0:T(8,128)(2,1)S(1)} %collective-permute-done.5.joined_ref, f32[1024,128]{1,0:T(8,128)S(1)} %get-tuple-element.12.refs_4_.table_ref, f32[368,128]{1,0:T(8,128)S(1)} %shard_map.49.refs_0_), custom_call_target="tpu_custom_call" | custom-call | flops 1849688064 | bytes 1048576 | tf_op jit(solution)/shard_map/pallas_call | solution.py:249
  20.4 0.6 %collective-permute-done.4.joined_ref = bf16[272,256]{1,0:T(8,128)(2,1)S(1)} collective-permute-done((bf16[272,256]{1,0:T(8,128)(2,1)S(1)}, bf16[272,256]{1,0:T(8,128)(2,1)S(1)}, u32[]{:S(2)}, u32[]{:S(2)}) %collective-permute-start.4) | collective-permute-done | bytes 139296 | tf_op jit(solution)/shard_map/ppermute | solution.py:32
  21.1 2.1 %shard_map.51.refs_0_ = f32[368,128]{1,0:T(8,128)S(1)} custom-call(s32[1]{0:T(128)} %bitcast.me_ref, s32[1]{0:T(128)} %bitcast.1.tm_ref, bf16[272,256]{1,0:T(8,128)(2,1)S(1)} %collective-permute-done.4.joined_ref, f32[1024,128]{1,0:T(8,128)S(1)} %get-tuple-element.12.refs_4_.table_ref, f32[368,128]{1,0:T(8,128)S(1)} %shard_map.50.refs_0_), custom_call_target="tpu_custom_call" | custom-call | flops 1849688064 | bytes 1048576 | tf_op jit(solution)/shard_map/pallas_call | solution.py:249
  23.2 0.0 collective-permute-done.3.joined_ref
  23.2 1.3 %collective-permute-start.6 = (f32[240,128]{1,0:T(8,128)S(1)}, f32[240,128]{1,0:T(8,128)S(1)}, u32[]{:S(2)}, u32[]{:S(2)}) collective-permute-start(f32[240,128]{1,0:T(8,128)S(1)} %get-tuple-element.14), channel_id=1, source_target_pairs={{1,0},{3,2},{5,4},{7,6},{9,8},{11,10},{13,12},{15,14},{17,16},{19,... | collective-permute-start | bytes 368648 | tf_op jit(solution)/shard_map/ppermute | solution.py:27
  24.5 2.1 %shard_map.53.sums_ref = f32[368,128]{1,0:T(8,128)S(1)} custom-call(s32[1]{0:T(128)} %bitcast.me_ref, s32[1]{0:T(128)} %bitcast.1.tm_ref, bf16[272,256]{1,0:T(8,128)(2,1)S(1)} %collective-permute-done.3.joined_ref, f32[1024,128]{1,0:T(8,128)S(1)} %get-tuple-element.12.refs_4_.table_ref, f32[368,128]{1,0:T(8,128)S(1)} %get-tuple-element.13.refs_0_), custom_call_target="tpu_custom_call" | custom-call | flops 1849688064 | bytes 1048576 | tf_op jit(solution)/shard_map/pallas_call | solution.py:249
  26.6 0.0 collective-permute-done.6.later_ref
  26.6 1.3 %shard_map.54 = f32[128,8,256]{2,1,0:T(8,128)} custom-call(f32[8,128]{1,0:T(8,128)S(1)} %get-tuple-element.10.shares_ref, bf16[256,1024]{1,0:T(8,128)(2,1)S(1)} %get-tuple-element.11.refs_5_.bands_ref, f32[368,128]{1,0:T(8,128)S(1)} %shard_map.53.sums_ref, f32[240,128]{1,0:T(8,128)S(1)} %collective-permute-done.6.later_ref), custom_call_target="tpu_custom_call" | custom-call | bytes 1048576 | tf_op jit(solution)/shard_map/pallas_call | solution.py:249
  (1 shorter events, 0.0 us)
Async XLA Ops:
  1.8 7.1 %collective-permute-start.2 = (bf16[144,128]{1,0:T(8,128)(2,1)S(1)}, bf16[144,128]{1,0:T(8,128)(2,1)S(1)}, u32[]{:S(2)}, u32[]{:S(2)}) collective-permute-start(bf16[144,128]{1,0:T(8,128)(2,1)S(1)} %shard_map.47.refs_0_), channel_id=1, source_target_pairs={{0,24},{2,26},{4,28},{6,30},{8,16},{10,18},{12,20},{14,22},{16,8},... | collective-permute-start | bytes 110600 | tf_op jit(solution)/shard_map/ppermute | solution.py:32
  6.9 4.9 %collective-permute-start.1 = (bf16[144,128]{1,0:T(8,128)(2,1)S(1)}, bf16[144,128]{1,0:T(8,128)(2,1)S(1)}, u32[]{:S(2)}, u32[]{:S(2)}) collective-permute-start(bf16[144,128]{1,0:T(8,128)(2,1)S(1)} %shard_map.47.refs_0_), channel_id=1, source_target_pairs={{0,16},{2,18},{4,20},{6,22},{8,24},{10,26},{12,28},{14,30},{16,0},... | collective-permute-start | bytes 110600 | tf_op jit(solution)/shard_map/ppermute | solution.py:32
  6.9 4.9 %collective-permute-start = (bf16[144,128]{1,0:T(8,128)(2,1)S(1)}, bf16[144,128]{1,0:T(8,128)(2,1)S(1)}, u32[]{:S(2)}, u32[]{:S(2)}) collective-permute-start(bf16[144,128]{1,0:T(8,128)(2,1)S(1)} %shard_map.47.refs_0_), channel_id=1, source_target_pairs={{0,8},{2,10},{4,12},{6,14},{8,0},{10,2},{12,4},{14,6},{16,24},{18,... | collective-permute-start | bytes 110600 | tf_op jit(solution)/shard_map/ppermute | solution.py:32
  11.9 6.4 %collective-permute-start.5 = (bf16[272,256]{1,0:T(8,128)(2,1)S(1)}, bf16[272,256]{1,0:T(8,128)(2,1)S(1)}, u32[]{:S(2)}, u32[]{:S(2)}) collective-permute-start(bf16[272,256]{1,0:T(8,128)(2,1)S(1)} %shard_map.48.joined_ref), channel_id=1, source_target_pairs={{0,2},{2,0},{4,6},{6,4},{8,10},{10,8},{12,14},{14,12},{16,18},{18,... | collective-permute-start | bytes 417800 | tf_op jit(solution)/shard_map/ppermute | solution.py:32
  13.5 7.6 %collective-permute-start.4 = (bf16[272,256]{1,0:T(8,128)(2,1)S(1)}, bf16[272,256]{1,0:T(8,128)(2,1)S(1)}, u32[]{:S(2)}, u32[]{:S(2)}) collective-permute-start(bf16[272,256]{1,0:T(8,128)(2,1)S(1)} %shard_map.48.joined_ref), channel_id=1, source_target_pairs={{0,4},{2,6},{4,0},{6,2},{8,12},{10,14},{12,8},{14,10},{16,20},{18,... | collective-permute-start | bytes 417800 | tf_op jit(solution)/shard_map/ppermute | solution.py:32
  15.0 8.2 %collective-permute-start.3 = (bf16[272,256]{1,0:T(8,128)(2,1)S(1)}, bf16[272,256]{1,0:T(8,128)(2,1)S(1)}, u32[]{:S(2)}, u32[]{:S(2)}) collective-permute-start(bf16[272,256]{1,0:T(8,128)(2,1)S(1)} %shard_map.48.joined_ref), channel_id=1, source_target_pairs={{0,6},{2,4},{4,2},{6,0},{8,14},{10,12},{12,10},{14,8},{16,22},{18,... | collective-permute-start | bytes 417800 | tf_op jit(solution)/shard_map/ppermute | solution.py:32
  23.2 3.4 %collective-permute-start.6 = (f32[240,128]{1,0:T(8,128)S(1)}, f32[240,128]{1,0:T(8,128)S(1)}, u32[]{:S(2)}, u32[]{:S(2)}) collective-permute-start(f32[240,128]{1,0:T(8,128)S(1)} %get-tuple-element.14), channel_id=1, source_target_pairs={{1,0},{3,2},{5,4},{7,6},{9,8},{11,10},{13,12},{15,14},{17,16},{19,... | collective-permute-start | bytes 368648 | tf_op jit(solution)/shard_map/ppermute | solution.py:27

commit v19 on v17

--- a/solution.py
+++ b/solution.py
@@ -159,8 +159,6 @@
             shift(lag)
         for first in range(0, STEP + 1, TOGETHER):
             lags = range(first, min(first + TOGETHER, STEP + 1))
-            for lag in range(first + TOGETHER, min(first + 2 * TOGETHER, STEP + 1)):
-                shift(lag)
             for pair in range(pairs - 1 if first == STEP else 0, pairs):
                 both = jnp.dot(
                     shifted[:, pl.ds(first * nsub, len(lags) * nsub)],
@@ -171,6 +169,9 @@
                     totals[pair][...] += both
                 else:
                     totals[pair][...] = both
+                if pair == 0:
+                    for lag in range(first + TOGETHER, min(first + 2 * TOGETHER, STEP + 1)):
+                        shift(lag)
         for pair in range(pairs):
             add_pair(sums_ref, pair, totals[pair][...])
 

time: 28.1 us -> 28.1 us (level)
  no operation moved by 1% of the time
where the time goes in v19:
time: 28.1 us; the launch traced here: 27.9 us
  Pallas kernels  12.9 us (46%)
  starting transfers between devices  10.6 us (38%)
  waiting for transfers between devices  4.29 us (15%)
    pallas_call x9, Pallas kernels, call(): pl.pallas_call(kernel, out_shape=out_shape, in_specs=in_specs, scratch_sh...  12.9 us
    ppermute x6, starting transfers between devices, exchanged(): lax.ppermute(value, axis, [(source, source ^ flip) for source in range(co...  9.31 us
    ppermute x6, waiting for transfers between devices, exchanged(): lax.ppermute(value, axis, [(source, source ^ flip) for source in range(co...  4.29 us
    ppermute x1, starting transfers between devices, passed_back(): lax.ppermute(value, axis, [(source, source - 1) for source in range(1, co...  1.29 us
  transfers between devices with their start and end apart: 7, of which 3 were waited for; matrix products, arithmetic and copies ran while one was open for 0% of the time, Pallas kernels for 35%

profile of v19, /device:TPU:0, one launch (start us, length us, event | category | flops | bytes accessed | tf_op | source)
XLA Modules:
  0.0 27.9 jit_solution(8487259836182766823)
XLA Ops:
  0.0 1.8 %shard_map.47.refs_0_ = bf16[144,128]{1,0:T(8,128)(2,1)S(1)} custom-call(s32[1,1024]{1,0:T(1,128)} %bitcast.8, bf16[1024,256]{1,0:T(8,128)(2,1)} %bitcast.7), custom_call_target="tpu_custom_call" | custom-call | bytes 1048576 | tf_op jit(solution)/shard_map/pallas_call | solution.py:250
  1.8 5.1 %collective-permute-start.2 = (bf16[144,128]{1,0:T(8,128)(2,1)S(1)}, bf16[144,128]{1,0:T(8,128)(2,1)S(1)}, u32[]{:S(2)}, u32[]{:S(2)}) collective-permute-start(bf16[144,128]{1,0:T(8,128)(2,1)S(1)} %shard_map.47.refs_0_), channel_id=1, source_target_pairs={{0,24},{2,26},{4,28},{6,30},{8,16},{10,18},{12,20},{14,22},{16,8},... | collective-permute-start | bytes 110600 | tf_op jit(solution)/shard_map/ppermute | solution.py:32
  6.9 0.0 collective-permute-start.1
  6.9 0.6 %collective-permute-start = (bf16[144,128]{1,0:T(8,128)(2,1)S(1)}, bf16[144,128]{1,0:T(8,128)(2,1)S(1)}, u32[]{:S(2)}, u32[]{:S(2)}) collective-permute-start(bf16[144,128]{1,0:T(8,128)(2,1)S(1)} %shard_map.47.refs_0_), channel_id=1, source_target_pairs={{0,8},{2,10},{4,12},{6,14},{8,0},{10,2},{12,4},{14,6},{16,24},{18,... | collective-permute-start | bytes 110600 | tf_op jit(solution)/shard_map/ppermute | solution.py:32
  7.6 1.3 %shard_map.46 = (bf16[256,1024]{1,0:T(8,128)(2,1)S(1)}, f32[8,128]{1,0:T(8,128)S(1)}, f32[1024,128]{1,0:T(8,128)S(1)}) custom-call(s32[8]{0:T(128)} %widths_ref.1, s32[128,1024]{1,0:T(8,128)} %offsets_ref.1), custom_call_target="tpu_custom_call" | custom-call | bytes 1048576 | tf_op jit(solution)/shard_map/pallas_call | solution.py:250
  8.9 0.0 collective-permute-done.2.refs_3_
  8.9 2.9 %collective-permute-done.1.refs_2_ = bf16[144,128]{1,0:T(8,128)(2,1)S(1)} collective-permute-done((bf16[144,128]{1,0:T(8,128)(2,1)S(1)}, bf16[144,128]{1,0:T(8,128)(2,1)S(1)}, u32[]{:S(2)}, u32[]{:S(2)}) %collective-permute-start.1) | collective-permute-done | bytes 36896 | tf_op jit(solution)/shard_map/ppermute | solution.py:32
  11.8 0.0 collective-permute-done.refs_1_
  11.8 0.1 shard_map.48.joined_ref
  11.9 1.6 %collective-permute-start.5 = (bf16[272,256]{1,0:T(8,128)(2,1)S(1)}, bf16[272,256]{1,0:T(8,128)(2,1)S(1)}, u32[]{:S(2)}, u32[]{:S(2)}) collective-permute-start(bf16[272,256]{1,0:T(8,128)(2,1)S(1)} %shard_map.48.joined_ref), channel_id=1, source_target_pairs={{0,2},{2,0},{4,6},{6,4},{8,10},{10,8},{12,14},{14,12},{16,18},{18,... | collective-permute-start | bytes 417800 | tf_op jit(solution)/shard_map/ppermute | solution.py:32
  13.5 1.5 %collective-permute-start.4 = (bf16[272,256]{1,0:T(8,128)(2,1)S(1)}, bf16[272,256]{1,0:T(8,128)(2,1)S(1)}, u32[]{:S(2)}, u32[]{:S(2)}) collective-permute-start(bf16[272,256]{1,0:T(8,128)(2,1)S(1)} %shard_map.48.joined_ref), channel_id=1, source_target_pairs={{0,4},{2,6},{4,0},{6,2},{8,12},{10,14},{12,8},{14,10},{16,20},{18,... | collective-permute-start | bytes 417800 | tf_op jit(solution)/shard_map/ppermute | solution.py:32
  15.0 0.5 %collective-permute-start.3 = (bf16[272,256]{1,0:T(8,128)(2,1)S(1)}, bf16[272,256]{1,0:T(8,128)(2,1)S(1)}, u32[]{:S(2)}, u32[]{:S(2)}) collective-permute-start(bf16[272,256]{1,0:T(8,128)(2,1)S(1)} %shard_map.48.joined_ref), channel_id=1, source_target_pairs={{0,6},{2,4},{4,2},{6,0},{8,14},{10,12},{12,10},{14,8},{16,22},{18,... | collective-permute-start | bytes 417800 | tf_op jit(solution)/shard_map/ppermute | solution.py:32
  15.5 2.1 %shard_map.49.refs_0_ = f32[368,128]{1,0:T(8,128)S(1)} custom-call(s32[1]{0:T(128)} %bitcast.me_ref, s32[1]{0:T(128)} %bitcast.1.tm_ref, bf16[272,256]{1,0:T(8,128)(2,1)S(1)} %shard_map.48.joined_ref, f32[1024,128]{1,0:T(8,128)S(1)} %get-tuple-element.12.refs_4_.table_ref), custom_call_target="tpu_custom_call" | custom-call | flops 1849688064 | bytes 1048576 | tf_op jit(solution)/shard_map/pallas_call | solution.py:250
  17.5 0.8 %collective-permute-done.5.joined_ref = bf16[272,256]{1,0:T(8,128)(2,1)S(1)} collective-permute-done((bf16[272,256]{1,0:T(8,128)(2,1)S(1)}, bf16[272,256]{1,0:T(8,128)(2,1)S(1)}, u32[]{:S(2)}, u32[]{:S(2)}) %collective-permute-start.5) | collective-permute-done | bytes 139296 | tf_op jit(solution)/shard_map/ppermute | solution.py:32
  18.3 2.1 %shard_map.50.refs_0_ = f32[368,128]{1,0:T(8,128)S(1)} custom-call(s32[1]{0:T(128)} %bitcast.me_ref, s32[1]{0:T(128)} %bitcast.1.tm_ref, bf16[272,256]{1,0:T(8,128)(2,1)S(1)} %collective-permute-done.5.joined_ref, f32[1024,128]{1,0:T(8,128)S(1)} %get-tuple-element.12.refs_4_.table_ref, f32[368,128]{1,0:T(8,128)S(1)} %shard_map.49.refs_0_), custom_call_target="tpu_custom_call" | custom-call | flops 1849688064 | bytes 1048576 | tf_op jit(solution)/shard_map/pallas_call | solution.py:250
  20.4 0.6 %collective-permute-done.4.joined_ref = bf16[272,256]{1,0:T(8,128)(2,1)S(1)} collective-permute-done((bf16[272,256]{1,0:T(8,128)(2,1)S(1)}, bf16[272,256]{1,0:T(8,128)(2,1)S(1)}, u32[]{:S(2)}, u32[]{:S(2)}) %collective-permute-start.4) | collective-permute-done | bytes 139296 | tf_op jit(solution)/shard_map/ppermute | solution.py:32
  21.1 2.1 %shard_map.51.refs_0_ = f32[368,128]{1,0:T(8,128)S(1)} custom-call(s32[1]{0:T(128)} %bitcast.me_ref, s32[1]{0:T(128)} %bitcast.1.tm_ref, bf16[272,256]{1,0:T(8,128)(2,1)S(1)} %collective-permute-done.4.joined_ref, f32[1024,128]{1,0:T(8,128)S(1)} %get-tuple-element.12.refs_4_.table_ref, f32[368,128]{1,0:T(8,128)S(1)} %shard_map.50.refs_0_), custom_call_target="tpu_custom_call" | custom-call | flops 1849688064 | bytes 1048576 | tf_op jit(solution)/shard_map/pallas_call | solution.py:250
  23.2 0.0 collective-permute-done.3.joined_ref
  23.2 1.3 %collective-permute-start.6 = (f32[240,128]{1,0:T(8,128)S(1)}, f32[240,128]{1,0:T(8,128)S(1)}, u32[]{:S(2)}, u32[]{:S(2)}) collective-permute-start(f32[240,128]{1,0:T(8,128)S(1)} %get-tuple-element.14), channel_id=1, source_target_pairs={{1,0},{3,2},{5,4},{7,6},{9,8},{11,10},{13,12},{15,14},{17,16},{19,... | collective-permute-start | bytes 368648 | tf_op jit(solution)/shard_map/ppermute | solution.py:27
  24.5 2.1 %shard_map.53.sums_ref = f32[368,128]{1,0:T(8,128)S(1)} custom-call(s32[1]{0:T(128)} %bitcast.me_ref, s32[1]{0:T(128)} %bitcast.1.tm_ref, bf16[272,256]{1,0:T(8,128)(2,1)S(1)} %collective-permute-done.3.joined_ref, f32[1024,128]{1,0:T(8,128)S(1)} %get-tuple-element.12.refs_4_.table_ref, f32[368,128]{1,0:T(8,128)S(1)} %get-tuple-element.13.refs_0_), custom_call_target="tpu_custom_call" | custom-call | flops 1849688064 | bytes 1048576 | tf_op jit(solution)/shard_map/pallas_call | solution.py:250
  26.6 0.0 collective-permute-done.6.later_ref
  26.6 1.3 %shard_map.54 = f32[128,8,256]{2,1,0:T(8,128)} custom-call(f32[8,128]{1,0:T(8,128)S(1)} %get-tuple-element.10.shares_ref, bf16[256,1024]{1,0:T(8,128)(2,1)S(1)} %get-tuple-element.11.refs_5_.bands_ref, f32[368,128]{1,0:T(8,128)S(1)} %shard_map.53.sums_ref, f32[240,128]{1,0:T(8,128)S(1)} %collective-permute-done.6.later_ref), custom_call_target="tpu_custom_call" | custom-call | bytes 1048576 | tf_op jit(solution)/shard_map/pallas_call | solution.py:250
  (1 shorter events, 0.0 us)
Async XLA Ops:
  1.8 7.1 %collective-permute-start.2 = (bf16[144,128]{1,0:T(8,128)(2,1)S(1)}, bf16[144,128]{1,0:T(8,128)(2,1)S(1)}, u32[]{:S(2)}, u32[]{:S(2)}) collective-permute-start(bf16[144,128]{1,0:T(8,128)(2,1)S(1)} %shard_map.47.refs_0_), channel_id=1, source_target_pairs={{0,24},{2,26},{4,28},{6,30},{8,16},{10,18},{12,20},{14,22},{16,8},... | collective-permute-start | bytes 110600 | tf_op jit(solution)/shard_map/ppermute | solution.py:32
  6.9 4.9 %collective-permute-start.1 = (bf16[144,128]{1,0:T(8,128)(2,1)S(1)}, bf16[144,128]{1,0:T(8,128)(2,1)S(1)}, u32[]{:S(2)}, u32[]{:S(2)}) collective-permute-start(bf16[144,128]{1,0:T(8,128)(2,1)S(1)} %shard_map.47.refs_0_), channel_id=1, source_target_pairs={{0,16},{2,18},{4,20},{6,22},{8,24},{10,26},{12,28},{14,30},{16,0},... | collective-permute-start | bytes 110600 | tf_op jit(solution)/shard_map/ppermute | solution.py:32
  6.9 4.9 %collective-permute-start = (bf16[144,128]{1,0:T(8,128)(2,1)S(1)}, bf16[144,128]{1,0:T(8,128)(2,1)S(1)}, u32[]{:S(2)}, u32[]{:S(2)}) collective-permute-start(bf16[144,128]{1,0:T(8,128)(2,1)S(1)} %shard_map.47.refs_0_), channel_id=1, source_target_pairs={{0,8},{2,10},{4,12},{6,14},{8,0},{10,2},{12,4},{14,6},{16,24},{18,... | collective-permute-start | bytes 110600 | tf_op jit(solution)/shard_map/ppermute | solution.py:32
  11.9 6.4 %collective-permute-start.5 = (bf16[272,256]{1,0:T(8,128)(2,1)S(1)}, bf16[272,256]{1,0:T(8,128)(2,1)S(1)}, u32[]{:S(2)}, u32[]{:S(2)}) collective-permute-start(bf16[272,256]{1,0:T(8,128)(2,1)S(1)} %shard_map.48.joined_ref), channel_id=1, source_target_pairs={{0,2},{2,0},{4,6},{6,4},{8,10},{10,8},{12,14},{14,12},{16,18},{18,... | collective-permute-start | bytes 417800 | tf_op jit(solution)/shard_map/ppermute | solution.py:32
  13.5 7.6 %collective-permute-start.4 = (bf16[272,256]{1,0:T(8,128)(2,1)S(1)}, bf16[272,256]{1,0:T(8,128)(2,1)S(1)}, u32[]{:S(2)}, u32[]{:S(2)}) collective-permute-start(bf16[272,256]{1,0:T(8,128)(2,1)S(1)} %shard_map.48.joined_ref), channel_id=1, source_target_pairs={{0,4},{2,6},{4,0},{6,2},{8,12},{10,14},{12,8},{14,10},{16,20},{18,... | collective-permute-start | bytes 417800 | tf_op jit(solution)/shard_map/ppermute | solution.py:32
  15.0 8.2 %collective-permute-start.3 = (bf16[272,256]{1,0:T(8,128)(2,1)S(1)}, bf16[272,256]{1,0:T(8,128)(2,1)S(1)}, u32[]{:S(2)}, u32[]{:S(2)}) collective-permute-start(bf16[272,256]{1,0:T(8,128)(2,1)S(1)} %shard_map.48.joined_ref), channel_id=1, source_target_pairs={{0,6},{2,4},{4,2},{6,0},{8,14},{10,12},{12,10},{14,8},{16,22},{18,... | collective-permute-start | bytes 417800 | tf_op jit(solution)/shard_map/ppermute | solution.py:32
  23.2 3.4 %collective-permute-start.6 = (f32[240,128]{1,0:T(8,128)S(1)}, f32[240,128]{1,0:T(8,128)S(1)}, u32[]{:S(2)}, u32[]{:S(2)}) collective-permute-start(f32[240,128]{1,0:T(8,128)S(1)} %get-tuple-element.14), channel_id=1, source_target_pairs={{1,0},{3,2},{5,4},{7,6},{9,8},{11,10},{13,12},{15,14},{17,16},{19,... | collective-permute-start | bytes 368648 | tf_op jit(solution)/shard_map/ppermute | solution.py:27

commit v20 on v17

--- a/solution.py
+++ b/solution.py
@@ -49,7 +49,7 @@
         copies[-1].start()
     rows = lax.broadcasted_iota(jnp.int32, (DCH * subs, block), 0)
     owner = lax.broadcasted_iota(jnp.int32, (1, block), 1) // per_sub
-    blank = jnp.zeros((subs, LANES), jnp.float32)
+    lane = lax.broadcasted_iota(jnp.int32, (subs, length), 1)
     first_copy.wait()
     members = [
         jnp.where(rows == delays[:, at * block : (at + 1) * block] * subs + owner, 1.0, 0.0).astype(jnp.bfloat16)
@@ -60,11 +60,14 @@
     parts = []
     for at, member in enumerate(members):
         picked = jnp.dot(member, held[pl.ds(at * block, block), :], preferred_element_type=jnp.float32)
-        total = None
+        early, late = None, None
         for delay in range(DCH):
-            late = jnp.concatenate([picked[delay * subs : (delay + 1) * subs, :], blank], axis=1)
-            late = pltpu.roll(late, DCH - delay, 1)
-            total = late if total is None else total + late
+            turned = pltpu.roll(picked[delay * subs : (delay + 1) * subs, :], DCH - delay, 1)
+            inside = jnp.where(lane >= DCH - delay, turned, 0.0)
+            beyond = jnp.where(lane[:, :LANES] < DCH - delay, turned[:, :LANES], 0.0)
+            early = inside if early is None else early + inside
+            late = beyond if late is None else late + beyond
+        total = jnp.concatenate([early, late], axis=1)
         parts.append(total)
     total = jnp.concatenate(parts, axis=0)
     if packed:

time: 28.1 us -> 28.1 us (level)
  no operation moved by 1% of the time
where the time goes in v20:
time: 28.1 us; the launch traced here: 27.9 us
  Pallas kernels  12.9 us (46%)
  starting transfers between devices  10.6 us (38%)
  waiting for transfers between devices  4.29 us (15%)
    pallas_call x9, Pallas kernels, call(): pl.pallas_call(kernel, out_shape=out_shape, in_specs=in_specs, scratch_sh...  12.9 us
    ppermute x6, starting transfers between devices, exchanged(): lax.ppermute(value, axis, [(source, source ^ flip) for source in range(co...  9.31 us
    ppermute x6, waiting for transfers between devices, exchanged(): lax.ppermute(value, axis, [(source, source ^ flip) for source in range(co...  4.29 us
    ppermute x1, starting transfers between devices, passed_back(): lax.ppermute(value, axis, [(source, source - 1) for source in range(1, co...  1.29 us
  transfers between devices with their start and end apart: 7, of which 3 were waited for; matrix products, arithmetic and copies ran while one was open for 0% of the time, Pallas kernels for 35%

profile of v20, /device:TPU:0, one launch (start us, length us, event | category | flops | bytes accessed | tf_op | source)
XLA Modules:
  0.0 27.9 jit_solution(841886790895263256)
XLA Ops:
  0.0 1.8 %shard_map.47.refs_0_ = bf16[144,128]{1,0:T(8,128)(2,1)S(1)} custom-call(s32[1,1024]{1,0:T(1,128)} %bitcast.8, bf16[1024,256]{1,0:T(8,128)(2,1)} %bitcast.7), custom_call_target="tpu_custom_call" | custom-call | bytes 1048576 | tf_op jit(solution)/shard_map/pallas_call | solution.py:252
  1.8 5.1 %collective-permute-start.2 = (bf16[144,128]{1,0:T(8,128)(2,1)S(1)}, bf16[144,128]{1,0:T(8,128)(2,1)S(1)}, u32[]{:S(2)}, u32[]{:S(2)}) collective-permute-start(bf16[144,128]{1,0:T(8,128)(2,1)S(1)} %shard_map.47.refs_0_), channel_id=1, source_target_pairs={{0,24},{2,26},{4,28},{6,30},{8,16},{10,18},{12,20},{14,22},{16,8},... | collective-permute-start | bytes 110600 | tf_op jit(solution)/shard_map/ppermute | solution.py:32
  6.9 0.0 collective-permute-start.1
  6.9 0.6 %collective-permute-start = (bf16[144,128]{1,0:T(8,128)(2,1)S(1)}, bf16[144,128]{1,0:T(8,128)(2,1)S(1)}, u32[]{:S(2)}, u32[]{:S(2)}) collective-permute-start(bf16[144,128]{1,0:T(8,128)(2,1)S(1)} %shard_map.47.refs_0_), channel_id=1, source_target_pairs={{0,8},{2,10},{4,12},{6,14},{8,0},{10,2},{12,4},{14,6},{16,24},{18,... | collective-permute-start | bytes 110600 | tf_op jit(solution)/shard_map/ppermute | solution.py:32
  7.6 1.3 %shard_map.46 = (bf16[256,1024]{1,0:T(8,128)(2,1)S(1)}, f32[8,128]{1,0:T(8,128)S(1)}, f32[1024,128]{1,0:T(8,128)S(1)}) custom-call(s32[8]{0:T(128)} %widths_ref.1, s32[128,1024]{1,0:T(8,128)} %offsets_ref.1), custom_call_target="tpu_custom_call" | custom-call | bytes 1048576 | tf_op jit(solution)/shard_map/pallas_call | solution.py:252
  8.9 0.0 collective-permute-done.2.refs_3_
  8.9 2.9 %collective-permute-done.1.refs_2_ = bf16[144,128]{1,0:T(8,128)(2,1)S(1)} collective-permute-done((bf16[144,128]{1,0:T(8,128)(2,1)S(1)}, bf16[144,128]{1,0:T(8,128)(2,1)S(1)}, u32[]{:S(2)}, u32[]{:S(2)}) %collective-permute-start.1) | collective-permute-done | bytes 36896 | tf_op jit(solution)/shard_map/ppermute | solution.py:32
  11.8 0.0 collective-permute-done.refs_1_
  11.8 0.1 shard_map.48.joined_ref
  11.9 1.6 %collective-permute-start.5 = (bf16[272,256]{1,0:T(8,128)(2,1)S(1)}, bf16[272,256]{1,0:T(8,128)(2,1)S(1)}, u32[]{:S(2)}, u32[]{:S(2)}) collective-permute-start(bf16[272,256]{1,0:T(8,128)(2,1)S(1)} %shard_map.48.joined_ref), channel_id=1, source_target_pairs={{0,2},{2,0},{4,6},{6,4},{8,10},{10,8},{12,14},{14,12},{16,18},{18,... | collective-permute-start | bytes 417800 | tf_op jit(solution)/shard_map/ppermute | solution.py:32
  13.5 1.5 %collective-permute-start.4 = (bf16[272,256]{1,0:T(8,128)(2,1)S(1)}, bf16[272,256]{1,0:T(8,128)(2,1)S(1)}, u32[]{:S(2)}, u32[]{:S(2)}) collective-permute-start(bf16[272,256]{1,0:T(8,128)(2,1)S(1)} %shard_map.48.joined_ref), channel_id=1, source_target_pairs={{0,4},{2,6},{4,0},{6,2},{8,12},{10,14},{12,8},{14,10},{16,20},{18,... | collective-permute-start | bytes 417800 | tf_op jit(solution)/shard_map/ppermute | solution.py:32
  15.0 0.5 %collective-permute-start.3 = (bf16[272,256]{1,0:T(8,128)(2,1)S(1)}, bf16[272,256]{1,0:T(8,128)(2,1)S(1)}, u32[]{:S(2)}, u32[]{:S(2)}) collective-permute-start(bf16[272,256]{1,0:T(8,128)(2,1)S(1)} %shard_map.48.joined_ref), channel_id=1, source_target_pairs={{0,6},{2,4},{4,2},{6,0},{8,14},{10,12},{12,10},{14,8},{16,22},{18,... | collective-permute-start | bytes 417800 | tf_op jit(solution)/shard_map/ppermute | solution.py:32
  15.5 2.1 %shard_map.49.refs_0_ = f32[368,128]{1,0:T(8,128)S(1)} custom-call(s32[1]{0:T(128)} %bitcast.me_ref, s32[1]{0:T(128)} %bitcast.1.tm_ref, bf16[272,256]{1,0:T(8,128)(2,1)S(1)} %shard_map.48.joined_ref, f32[1024,128]{1,0:T(8,128)S(1)} %get-tuple-element.12.refs_4_.table_ref), custom_call_target="tpu_custom_call" | custom-call | flops 1849688064 | bytes 1048576 | tf_op jit(solution)/shard_map/pallas_call | solution.py:252
  17.6 0.8 %collective-permute-done.5.joined_ref = bf16[272,256]{1,0:T(8,128)(2,1)S(1)} collective-permute-done((bf16[272,256]{1,0:T(8,128)(2,1)S(1)}, bf16[272,256]{1,0:T(8,128)(2,1)S(1)}, u32[]{:S(2)}, u32[]{:S(2)}) %collective-permute-start.5) | collective-permute-done | bytes 139296 | tf_op jit(solution)/shard_map/ppermute | solution.py:32
  18.4 2.1 %shard_map.50.refs_0_ = f32[368,128]{1,0:T(8,128)S(1)} custom-call(s32[1]{0:T(128)} %bitcast.me_ref, s32[1]{0:T(128)} %bitcast.1.tm_ref, bf16[272,256]{1,0:T(8,128)(2,1)S(1)} %collective-permute-done.5.joined_ref, f32[1024,128]{1,0:T(8,128)S(1)} %get-tuple-element.12.refs_4_.table_ref, f32[368,128]{1,0:T(8,128)S(1)} %shard_map.49.refs_0_), custom_call_target="tpu_custom_call" | custom-call | flops 1849688064 | bytes 1048576 | tf_op jit(solution)/shard_map/pallas_call | solution.py:252
  20.4 0.6 %collective-permute-done.4.joined_ref = bf16[272,256]{1,0:T(8,128)(2,1)S(1)} collective-permute-done((bf16[272,256]{1,0:T(8,128)(2,1)S(1)}, bf16[272,256]{1,0:T(8,128)(2,1)S(1)}, u32[]{:S(2)}, u32[]{:S(2)}) %collective-permute-start.4) | collective-permute-done | bytes 139296 | tf_op jit(solution)/shard_map/ppermute | solution.py:32
  21.1 2.1 %shard_map.51.refs_0_ = f32[368,128]{1,0:T(8,128)S(1)} custom-call(s32[1]{0:T(128)} %bitcast.me_ref, s32[1]{0:T(128)} %bitcast.1.tm_ref, bf16[272,256]{1,0:T(8,128)(2,1)S(1)} %collective-permute-done.4.joined_ref, f32[1024,128]{1,0:T(8,128)S(1)} %get-tuple-element.12.refs_4_.table_ref, f32[368,128]{1,0:T(8,128)S(1)} %shard_map.50.refs_0_), custom_call_target="tpu_custom_call" | custom-call | flops 1849688064 | bytes 1048576 | tf_op jit(solution)/shard_map/pallas_call | solution.py:252
  23.2 0.0 collective-permute-done.3.joined_ref
  23.2 1.3 %collective-permute-start.6 = (f32[240,128]{1,0:T(8,128)S(1)}, f32[240,128]{1,0:T(8,128)S(1)}, u32[]{:S(2)}, u32[]{:S(2)}) collective-permute-start(f32[240,128]{1,0:T(8,128)S(1)} %get-tuple-element.14), channel_id=1, source_target_pairs={{1,0},{3,2},{5,4},{7,6},{9,8},{11,10},{13,12},{15,14},{17,16},{19,... | collective-permute-start | bytes 368648 | tf_op jit(solution)/shard_map/ppermute | solution.py:27
  24.5 2.1 %shard_map.53.sums_ref = f32[368,128]{1,0:T(8,128)S(1)} custom-call(s32[1]{0:T(128)} %bitcast.me_ref, s32[1]{0:T(128)} %bitcast.1.tm_ref, bf16[272,256]{1,0:T(8,128)(2,1)S(1)} %collective-permute-done.3.joined_ref, f32[1024,128]{1,0:T(8,128)S(1)} %get-tuple-element.12.refs_4_.table_ref, f32[368,128]{1,0:T(8,128)S(1)} %get-tuple-element.13.refs_0_), custom_call_target="tpu_custom_call" | custom-call | flops 1849688064 | bytes 1048576 | tf_op jit(solution)/shard_map/pallas_call | solution.py:252
  26.6 0.0 collective-permute-done.6.later_ref
  26.6 1.3 %shard_map.54 = f32[128,8,256]{2,1,0:T(8,128)} custom-call(f32[8,128]{1,0:T(8,128)S(1)} %get-tuple-element.10.shares_ref, bf16[256,1024]{1,0:T(8,128)(2,1)S(1)} %get-tuple-element.11.refs_5_.bands_ref, f32[368,128]{1,0:T(8,128)S(1)} %shard_map.53.sums_ref, f32[240,128]{1,0:T(8,128)S(1)} %collective-permute-done.6.later_ref), custom_call_target="tpu_custom_call" | custom-call | bytes 1048576 | tf_op jit(solution)/shard_map/pallas_call | solution.py:252
  (1 shorter events, 0.0 us)
Async XLA Ops:
  1.8 7.1 %collective-permute-start.2 = (bf16[144,128]{1,0:T(8,128)(2,1)S(1)}, bf16[144,128]{1,0:T(8,128)(2,1)S(1)}, u32[]{:S(2)}, u32[]{:S(2)}) collective-permute-start(bf16[144,128]{1,0:T(8,128)(2,1)S(1)} %shard_map.47.refs_0_), channel_id=1, source_target_pairs={{0,24},{2,26},{4,28},{6,30},{8,16},{10,18},{12,20},{14,22},{16,8},... | collective-permute-start | bytes 110600 | tf_op jit(solution)/shard_map/ppermute | solution.py:32
  6.9 4.9 %collective-permute-start.1 = (bf16[144,128]{1,0:T(8,128)(2,1)S(1)}, bf16[144,128]{1,0:T(8,128)(2,1)S(1)}, u32[]{:S(2)}, u32[]{:S(2)}) collective-permute-start(bf16[144,128]{1,0:T(8,128)(2,1)S(1)} %shard_map.47.refs_0_), channel_id=1, source_target_pairs={{0,16},{2,18},{4,20},{6,22},{8,24},{10,26},{12,28},{14,30},{16,0},... | collective-permute-start | bytes 110600 | tf_op jit(solution)/shard_map/ppermute | solution.py:32
  6.9 4.9 %collective-permute-start = (bf16[144,128]{1,0:T(8,128)(2,1)S(1)}, bf16[144,128]{1,0:T(8,128)(2,1)S(1)}, u32[]{:S(2)}, u32[]{:S(2)}) collective-permute-start(bf16[144,128]{1,0:T(8,128)(2,1)S(1)} %shard_map.47.refs_0_), channel_id=1, source_target_pairs={{0,8},{2,10},{4,12},{6,14},{8,0},{10,2},{12,4},{14,6},{16,24},{18,... | collective-permute-start | bytes 110600 | tf_op jit(solution)/shard_map/ppermute | solution.py:32
  11.9 6.4 %collective-permute-start.5 = (bf16[272,256]{1,0:T(8,128)(2,1)S(1)}, bf16[272,256]{1,0:T(8,128)(2,1)S(1)}, u32[]{:S(2)}, u32[]{:S(2)}) collective-permute-start(bf16[272,256]{1,0:T(8,128)(2,1)S(1)} %shard_map.48.joined_ref), channel_id=1, source_target_pairs={{0,2},{2,0},{4,6},{6,4},{8,10},{10,8},{12,14},{14,12},{16,18},{18,... | collective-permute-start | bytes 417800 | tf_op jit(solution)/shard_map/ppermute | solution.py:32
  13.5 7.6 %collective-permute-start.4 = (bf16[272,256]{1,0:T(8,128)(2,1)S(1)}, bf16[272,256]{1,0:T(8,128)(2,1)S(1)}, u32[]{:S(2)}, u32[]{:S(2)}) collective-permute-start(bf16[272,256]{1,0:T(8,128)(2,1)S(1)} %shard_map.48.joined_ref), channel_id=1, source_target_pairs={{0,4},{2,6},{4,0},{6,2},{8,12},{10,14},{12,8},{14,10},{16,20},{18,... | collective-permute-start | bytes 417800 | tf_op jit(solution)/shard_map/ppermute | solution.py:32
  15.0 8.2 %collective-permute-start.3 = (bf16[272,256]{1,0:T(8,128)(2,1)S(1)}, bf16[272,256]{1,0:T(8,128)(2,1)S(1)}, u32[]{:S(2)}, u32[]{:S(2)}) collective-permute-start(bf16[272,256]{1,0:T(8,128)(2,1)S(1)} %shard_map.48.joined_ref), channel_id=1, source_target_pairs={{0,6},{2,4},{4,2},{6,0},{8,14},{10,12},{12,10},{14,8},{16,22},{18,... | collective-permute-start | bytes 417800 | tf_op jit(solution)/shard_map/ppermute | solution.py:32
  23.2 3.4 %collective-permute-start.6 = (f32[240,128]{1,0:T(8,128)S(1)}, f32[240,128]{1,0:T(8,128)S(1)}, u32[]{:S(2)}, u32[]{:S(2)}) collective-permute-start(f32[240,128]{1,0:T(8,128)S(1)} %get-tuple-element.14), channel_id=1, source_target_pairs={{1,0},{3,2},{5,4},{7,6},{9,8},{11,10},{13,12},{15,14},{17,16},{19,... | collective-permute-start | bytes 368648 | tf_op jit(solution)/shard_map/ppermute | solution.py:27
